TPU v7x, 32 devices: a whole 2x2x4 slice. The times are simulated.
32 devices in a mesh: depth: 4 (over y, x), rows: 8 (over z, core).
Axes of the slice: x: 2, y: 2, z: 4, core: 2. Of those that a mesh axis runs over, the one named last changes fastest.
Arguments:
- hologram: bfloat16 [4096, 4096], P('rows'), may hold values from 0.25 to 1.75
- background: bfloat16 [4096, 4096], P('rows'), may hold values from 0.5 to 2
Outputs:
- focus: float32 [4096, 4096], P('rows')
All inputs are finite; a program needn't handle non-finite values.
Results may differ from a plain program's by a relative error of at most 0.025.
Values may be sent and summed in bfloat16 or wider, within the bound.
No kernel may reach another device: no remote copies, remote signals or barrier semaphores. Data moves between devices by JAX's collectives and lax.ppermute only.
A program may use at most 128 MiB of HBM per device.

v0:
```python
import math

import jax
import jax.numpy as jnp
from jax import lax
from jax.sharding import PartitionSpec as P

N = 4096
RADIX = 64
PL_DEV = 1


wave_number = 0.6
depth_start = 8.0
depth_step = 2.0


def padded_2(block, sides, width):
    for axis, dim in sides:
        count = lax.axis_size(axis)
        forward = [(i, i + 1) for i in range(count - 1)]
        backward = [(target, source) for source, target in forward]
        low = lax.ppermute(
            lax.slice_in_dim(block, block.shape[dim] - width, None, axis=dim), axis, forward
        )
        high = lax.ppermute(lax.slice_in_dim(block, 0, width, axis=dim), axis, backward)
        block = jnp.concatenate([low, block, high], axis=dim)
    return block


def fourier_tables(radix_size, sign_value):
    indices = jnp.arange(radix_size, dtype=jnp.int32)
    products = indices[:, None] * indices[None, :] % radix_size
    angles = products.astype(jnp.float32) * (sign_value * 2.0 * math.pi / radix_size)
    scaling = 1.0 / math.sqrt(radix_size)
    cosine_part = jnp.cos(angles) * scaling
    sine_part = jnp.sin(angles) * scaling
    matrix = jnp.stack([jnp.stack([cosine_part, -sine_part]), jnp.stack([sine_part, cosine_part])])
    return matrix.astype(jnp.bfloat16)


def twiddle_table(radix_size, sign_value):
    indices = jnp.arange(radix_size, dtype=jnp.int32)
    total = radix_size * radix_size
    products = indices[:, None] * indices[None, :] % total
    angles = products.astype(jnp.float32) * (sign_value * 2.0 * math.pi / total)
    return (jnp.cos(angles), jnp.sin(angles))


def rotate(data, cosine_part, sine_part):
    return jnp.stack(
        [data[0] * cosine_part - data[1] * sine_part, data[0] * sine_part + data[1] * cosine_part]
    )


def contract(form, matrix, data):
    return jnp.einsum(form, matrix, data, preferred_element_type=jnp.float32)


def forward_real(data):
    batch_size = data.shape[1]
    shaped = data.reshape(RADIX, RADIX, batch_size)
    matrix = fourier_tables(RADIX, -1.0)
    cosine_part, sine_part = twiddle_table(RADIX, -1.0)
    opening = contract("oka,abm->okbm", matrix[:, 0], shaped)
    sectioned = rotate(opening, cosine_part[:, :, None], sine_part[:, :, None]).astype(jnp.bfloat16)
    closing = contract("ocjb,ckbm->okjm", matrix, sectioned)
    return closing.reshape(2, N, batch_size).astype(jnp.bfloat16)


def forward_first(data):
    batch_size = data.shape[2]
    shaped = data.reshape(2, RADIX, RADIX, batch_size)
    matrix = fourier_tables(RADIX, -1.0)
    cosine_part, sine_part = twiddle_table(RADIX, -1.0)
    opening = contract("ocka,cabm->okbm", matrix, shaped)
    sectioned = rotate(opening, cosine_part[:, :, None], sine_part[:, :, None]).astype(jnp.bfloat16)
    closing = contract("ocjb,ckbm->okjm", matrix, sectioned)
    return closing.reshape(2, N, batch_size).astype(jnp.bfloat16)


def inverse_first(data):
    batch_size = data.shape[2]
    shaped = data.reshape(2, RADIX, RADIX, batch_size)
    matrix = fourier_tables(RADIX, 1.0)
    cosine_part, sine_part = twiddle_table(RADIX, 1.0)
    opening = contract("ocbj,ckjm->okbm", matrix, shaped)
    sectioned = rotate(opening, cosine_part[:, :, None], sine_part[:, :, None]).astype(jnp.bfloat16)
    closing = contract("ocak,ckbm->oabm", matrix, sectioned)
    return closing.reshape(2, N, batch_size)


def frequencies(positions):
    natural = positions // RADIX + RADIX * (positions % RADIX)
    signed_freq = jnp.where(natural >= N // 2, natural - N, natural)
    return signed_freq.astype(jnp.float32) / N


def propagator(freq_whole, freq_own, distance):
    radial = freq_whole[:, None] ** 2 + freq_own[None, :] ** 2
    limit = wave_number * wave_number
    amplitude = jnp.exp(-2.0 * math.pi * distance * jnp.sqrt(jnp.maximum(radial - limit, 0.0)))
    phase_angle = (
        2.0 * math.pi * distance * (jnp.sqrt(jnp.maximum(limit - radial, 0.0)) - wave_number)
    )
    return (amplitude * jnp.cos(phase_angle), amplitude * jnp.sin(phase_angle))


def propagate(spectrum, cosine_part, sine_part):
    return rotate(spectrum.astype(jnp.float32), cosine_part, sine_part).astype(jnp.bfloat16)


def shards(hologram, background):
    row_count = hologram.shape[0]
    contrast = (hologram.astype(jnp.float32) / background.astype(jnp.float32) - 1.0).astype(
        jnp.bfloat16
    )
    along_rows = forward_real(contrast.T)
    columns = lax.all_to_all(
        jnp.swapaxes(along_rows, 1, 2), "rows", split_axis=2, concat_axis=1, tiled=True
    )
    spectrum = forward_first(columns)
    row_index = lax.axis_index("rows")
    own_positions = row_index * row_count + jnp.arange(row_count, dtype=jnp.int32)
    freq_own = frequencies(own_positions)
    freq_whole = frequencies(jnp.arange(N, dtype=jnp.int32))
    depth_index = lax.axis_index("depth")
    distance = depth_start + depth_step * (depth_index * PL_DEV + 0).astype(jnp.float32)
    cosine_part, sine_part = propagator(freq_whole, freq_own, distance)
    propagated = propagate(spectrum, cosine_part, sine_part)
    halfway = inverse_first(propagated).astype(jnp.bfloat16)
    restored = lax.all_to_all(
        jnp.swapaxes(halfway, 1, 2), "rows", split_axis=2, concat_axis=1, tiled=True
    )
    result_field = inverse_first(restored)
    intensities = [
        (result_field[0] * result_field[0] + result_field[1] * result_field[1]).astype(jnp.bfloat16)
    ]
    stacked = jnp.stack(intensities)
    padded = padded_2(stacked, (("depth", 0), ("rows", 2)), 1)
    centre_block = padded[1:-1, :, 1:-1]
    plane_ids = jnp.arange(PL_DEV, dtype=jnp.int32)[:, None, None]
    row_ids = jnp.arange(row_count, dtype=jnp.int32)[None, None, :]
    depth_count = lax.axis_size("depth")
    row_groups = lax.axis_size("rows")
    lower_plane = jnp.where(
        (depth_index == 0) & (plane_ids == 0), centre_block, padded[:-2, :, 1:-1]
    )
    upper_plane = jnp.where(
        (depth_index == depth_count - 1) & (plane_ids == PL_DEV - 1),
        centre_block,
        padded[2:, :, 1:-1],
    )
    north_row = jnp.where((row_index == 0) & (row_ids == 0), centre_block, padded[1:-1, :, :-2])
    south_row = jnp.where(
        (row_index == row_groups - 1) & (row_ids == row_count - 1),
        centre_block,
        padded[1:-1, :, 2:],
    )
    centre = centre_block.astype(jnp.float32)
    east_col = jnp.concatenate([centre[:, 1:], centre[:, -1:]], axis=1)
    west_col = jnp.concatenate([centre[:, :1], centre[:, :-1]], axis=1)
    depth_diff = upper_plane.astype(jnp.float32) - lower_plane.astype(jnp.float32)
    row_diff = south_row.astype(jnp.float32) - north_row.astype(jnp.float32)
    col_diff = east_col - west_col
    scores = (depth_diff * depth_diff + row_diff * row_diff + col_diff * col_diff) / 8.0
    sharpest = jnp.max(scores, axis=0)
    merged = lax.pmax(sharpest.astype(jnp.bfloat16), "depth").astype(sharpest.dtype)
    return merged.T


def solution(mesh):
    in_specs = (P("rows", None), P("rows", None))
    out_specs = P("rows", None)
    return jax.shard_map(shards, mesh=mesh, in_specs=in_specs, out_specs=out_specs, check_vma=False)
```

profile of v0, /device:TPU:0, one launch (start us, length us, event | category | flops | bytes accessed | tf_op | source)
XLA Modules:
  0.0 1027.4 jit_solution(12877251649909888343)
XLA Ops:
  7.0 6.4 copy.62
  13.4 6.5 copy.61
  19.9 5.0 add_convert_fusion.5
  24.9 6.2 fusion.47
  31.1 3.7 subtract_convert_fusion.4
  34.9 6.3 maximum_bitcast_fusion
  41.2 17.2 %fusion.42 = bf16[2,64,64,512]{3,2,0,1:T(8,128)(2,1)} fusion(bf16[2,64,64,512,1]{3,1,2,0,4:T(8,128)(2,1)} %maximum_bitcast_fusion, bf16[2,2,64,64]{3,2,0,1:T(8,128)(2,1)S(1)} %get-tuple-element.24), kind=kOutput, calls=%fused_computation.61 | convolution fusion | flops 1077936128 | bytes 16809984 | tf_op jit(solution)/shard_map/ocjb,ckbm->okjm/dot_general | solution.py:57
  58.4 7.9 copy.66
  66.3 16.4 %copy.67 = bf16[2,512,4096]{1,0,2:T(2,128)(2,1)} copy(bf16[2,512,4096]{1,2,0:T(8,128)(2,1)} %bitcast.126) | data formatting | bytes 16777216 | tf_op jit(solution)/shard_map/transpose | solution.py:120
  82.7 6.3 all-to-all-start
  89.9 183.1 %all-to-all-done = bf16[2,512,4096]{1,0,2:T(2,128)(2,1)} async-done(((bf16[2,512,4096]{1,0,2:T(2,128)(2,1)}), bf16[2,512,4096]{1,0,2:T(2,128)(2,1)}, u32[]{:S(2)}, u32[]{:S(2)}) %all-to-all-start) | async-done | bytes 8388640 | tf_op jit(solution)/shard_map/all_to_all | solution.py:119
  273.0 8.1 copy.68
  281.1 11.9 %copy.69 = bf16[2,8,512,512]{3,2,1,0:T(8,128)(2,1)} copy(bf16[2,8,512,512]{2,3,1,0:T(8,128)(2,1)} %bitcast.127) | data formatting | bytes 16777216 | tf_op jit(solution)/shard_map/all_to_all | solution.py:119
  293.0 14.0 %fusion.34 = f32[2,64,64,512]{3,1,2,0:T(8,128)S(1)} fusion(bf16[2,64,64,512]{3,2,1,0:T(8,128)(2,1)} %bitcast.125, bf16[2,2,64,64,1]{3,2,0,1,4:T(8,128)(2,1)S(1)} %get-tuple-element.23), kind=kOutput, calls=%fused_computation.59 | convolution fusion | flops 1073741824 | bytes 25198592 | tf_op jit(solution)/shard_map/ocka,cabm->okbm/dot_general | solution.py:57
  307.0 3.7 subtract_convert_fusion.3
  310.7 6.3 maximum_bitcast_fusion.1
  317.1 10.4 %convert_bitcast_fusion = f32[2,64,64,512]{3,2,0,1:T(8,128)S(1)} fusion(bf16[2,64,64,512,1]{3,1,2,0,4:T(8,128)(2,1)} %maximum_bitcast_fusion.1, bf16[2,2,64,64]{3,2,0,1:T(8,128)(2,1)S(1)} %get-tuple-element.24), kind=kOutput, calls=%fused_computation.3 | convolution fusion | flops 1082130432 | bytes 25198592 | tf_op jit(solution)/shard_map/ocjb,ckbm->okjm/dot_general | solution.py:57
  327.5 7.0 fusion.96
  334.5 43.4 %subtract_convert_fusion.2 = (bf16[1,4096,512]{2,1,0:T(8,128)(2,1)S(1)}, bf16[1,4096,512]{2,1,0:T(8,128)(2,1)}) fusion(f32[1,4096,512]{2,1,0:T(8,128)} %bitcast.131, f32[1,4096,512]{2,1,0:T(8,128)} %bitcast.130, f32[]{:T(128)S(6)} %mul_shard_map.11, f32[512]{0:T(512)S(1)} %multiply_multiply_fusion, f32[4096]{0:T(1024)S(1)} %fusion.86, f32[]{:T(128)S(6)} %mul_shard_map.10), kind=kLoop, calls=%fused_computation.53 | loop fusion | flops 37748736 | bytes 25184264 | tf_op jit(solution)/shard_map/convert.9
  377.9 4.9 convolution_bitcast_fusion.1
  382.8 4.1 subtract_convert_fusion.1
  386.9 6.4 pad_maximum_fusion
  393.3 17.2 %bitcast_convert_fusion = bf16[2,64,64,512]{3,1,2,0:T(8,128)(2,1)} fusion(bf16[2,64,64,512]{3,2,0,1:T(8,128)(2,1)} %pad_maximum_fusion, bf16[1,2,64,64]{3,2,1,0:T(8,128)(2,1)S(1)} %get-tuple-element.26, bf16[1,2,64,64]{3,2,1,0:T(8,128)(2,1)S(1)} %get-tuple-element.25), kind=kOutput, calls=%fused_computation | convolution fusion | flops 1078001664 | bytes 16809984 | tf_op jit(solution)/shard_map/ocak,ckbm->oabm/dot_general | solution.py:57
  410.6 11.7 %copy.77 = bf16[2,64,64,512]{3,2,1,0:T(8,128)(2,1)} copy(bf16[2,64,64,512]{3,1,2,0:T(8,128)(2,1)} %bitcast_convert_fusion) | data formatting | bytes 16777216 | tf_op jit(solution)/shard_map/convert_element_type | solution.py:131
  422.3 14.5 %copy.78 = bf16[2,512,4096]{1,0,2:T(2,128)(2,1)S(1)} copy(bf16[2,512,4096]{1,2,0:T(8,128)(2,1)} %bitcast.128) | data formatting | bytes 16777216 | tf_op jit(solution)/shard_map/transpose | solution.py:133
  436.8 187.6 %all_to_all.30 = bf16[2,512,4096]{1,0,2:T(2,128)(2,1)} all-to-all(bf16[2,512,4096]{1,0,2:T(2,128)(2,1)S(1)} %copy.78), channel_id=1, replica_groups=mesh['depth'=4,'rows'=8] {'rows'}, dimensions={2} | all-to-all | bytes 16777216 | tf_op jit(solution)/shard_map/all_to_all | solution.py:132
  624.4 8.1 copy.79
  632.5 11.7 %copy.80 = bf16[2,8,512,512]{3,2,1,0:T(8,128)(2,1)} copy(bf16[2,8,512,512]{2,3,1,0:T(8,128)(2,1)} %bitcast.129) | data formatting | bytes 16777216 | tf_op jit(solution)/shard_map/all_to_all | solution.py:132
  644.2 5.1 convolution_bitcast_fusion
  649.3 3.9 subtract_convert_fusion
  653.2 6.4 pad_maximum_fusion.1
  659.6 14.0 %fusion.37 = f32[2,64,64,512]{3,1,2,0:T(8,128)S(1)} fusion(bf16[2,64,64,512]{3,2,0,1:T(8,128)(2,1)} %pad_maximum_fusion.1, bf16[1,2,64,64]{3,2,1,0:T(8,128)(2,1)S(1)} %get-tuple-element.26, bf16[1,2,64,64]{3,2,1,0:T(8,128)(2,1)S(1)} %get-tuple-element.25), kind=kOutput, calls=%fused_computation.60 | convolution fusion | flops 1073807360 | bytes 25198592 | tf_op jit(solution)/shard_map/ocak,ckbm->oabm/dot_general | solution.py:57
  673.6 2.7 fusion.13
  676.3 4.3 copy.83
  681.9 6.5 collective-permute-start.1
  688.4 3.4 bitcast_convert_fusion.3
  691.8 7.0 fusion.97
  698.8 1.4 copy-done
  700.2 76.1 %collective-permute-done = bf16[1,4096,512]{2,1,0:T(8,128)(2,1)} collective-permute-done((bf16[1,4096,512]{2,1,0:T(8,128)(2,1)}, bf16[1,4096,512]{2,1,0:T(8,128)(2,1)}, u32[]{:S(2)}, u32[]{:S(2)}) %collective-permute-start) | collective-permute-done | bytes 4194336 | tf_op jit(solution)/shard_map/ppermute | solution.py:26
  776.3 5.6 pad_maximum_fusion.10
  781.9 3.5 copy.86
  786.6 2.3 copy.84
  788.9 1.3 collective-permute-start.2
  791.0 2.2 copy.87
  793.2 2.9 copy.85
  796.1 22.5 %fusion.50 = bf16[512,4096]{0,1:T(8,128)(2,1)} fusion(f32[1,4095,512]{2,1,0:T(8,128)} %get-tuple-element.20, f32[1,1,512]{2,1,0:T(1,128)S(1)} %get-tuple-element.22, f32[1,1,512]{2,1,0:T(1,128)S(1)} %get-tuple-element.21, f32[1,4095,512]{2,1,0:T(8,128)} %get-tuple-element.19, bf16[1,4096,512]{2,1,0:T(8,128)(2,1)} %bitcast.59, ...), kind=kLoop, calls=%fused_computation.73 | loop fusion | flops 75497472 | bytes 33604608 | tf_op jit(solution)/shard_map/transpose | solution.py:169
  818.6 194.5 %all-reduce.2.cloned.1.call-done = bf16[512,4096]{0,1:T(8,128)(2,1)} async-done(((bf16[512,4096]{0,1:T(8,128)(2,1)}), bf16[512,4096]{0,1:T(8,128)(2,1)}) %all-reduce.2.cloned.1.call-update) | async-done | bytes 4194320 | tf_op jit(solution)/shard_map/pmax | solution.py:168
  1013.1 7.0 copy.88
  (24 shorter events, 4.7 us)
Async XLA Ops:
  82.7 190.3 %all-to-all-start = ((bf16[2,512,4096]{1,0,2:T(2,128)(2,1)}), bf16[2,512,4096]{1,0,2:T(2,128)(2,1)}, u32[]{:S(2)}, u32[]{:S(2)}) async-start(bf16[2,512,4096]{1,0,2:T(2,128)(2,1)} %copy.67), calls=%async_computation | async-start | bytes 16777216 | tf_op jit(solution)/shard_map/all_to_all | solution.py:119
  89.0 924.1 %all-reduce.2.cloned.1.call-start = ((), (), s32[]{:S(2)}) async-start(), calls=%async_computation.2 | async-start | bytes 8388608 | tf_op jit(solution)/shard_map/pmax | solution.py:168
  680.6 95.7 %collective-permute-start = (bf16[1,4096,512]{2,1,0:T(8,128)(2,1)}, bf16[1,4096,512]{2,1,0:T(8,128)(2,1)}, u32[]{:S(2)}, u32[]{:S(2)}) collective-permute-start(bf16[1,4096,512]{2,1,0:T(8,128)(2,1)} %bitcast.59), channel_id=1, source_target_pairs={{8,0},{16,8},{24,16},{9,1},{17,9},{25,17},{10,2},{18,10},{26,18},{... | collective-permute-start | bytes 12582920 | tf_op jit(solution)/shard_map/ppermute | solution.py:26
  681.9 94.4 %collective-permute-start.1 = (bf16[1,4096,512]{2,1,0:T(8,128)(2,1)}, bf16[1,4096,512]{2,1,0:T(8,128)(2,1)}, u32[]{:S(2)}, u32[]{:S(2)}) collective-permute-start(bf16[1,4096,512]{2,1,0:T(8,128)(2,1)} %bitcast.59), channel_id=1, source_target_pairs={{0,8},{8,16},{16,24},{1,9},{9,17},{17,25},{2,10},{10,18},{18,26},{... | collective-permute-start | bytes 12582920 | tf_op jit(solution)/shard_map/ppermute | solution.py:23
  691.8 8.4 copy-start
  785.3 5.6 collective-permute-start.3
  788.9 4.2 collective-permute-start.2
Sparse Core Ops, SparseCore 0:
  818.7 194.3 all-reduce.1
where the time goes:
time: 1040 us; the launch traced here: 1030 us
  waiting for transfers between devices  454 us (44%)
  blocking collectives  188 us (18%)
  local copies, waits for them, and re-layouts  142 us (14%)
  other arithmetic  125 us (12%)
  matrix products  89 us (9%)
  starting transfers between devices  16.8 us (2%)
  between operations  14.1 us (1%)
    pmax x1, waiting for transfers between devices, shards(): lax.pmax(sharpest.astype(jnp.bfloat16), 'depth').astype(sharpest.dtype)  195 us
    all_to_all x1, blocking collectives, shards(): lax.all_to_all(jnp.swapaxes(halfway, 1, 2), 'rows', split_axis=2, concat_...  188 us
    all_to_all x1, waiting for transfers between devices, shards(): lax.all_to_all(jnp.swapaxes(along_rows, 1, 2), 'rows', split_axis=2, conc...  183 us
    dot_general x8, matrix products, contract(): return jnp.einsum(form, matrix, data, preferred_element_type=jnp.float32)  89 us
    ppermute x2, waiting for transfers between devices, padded_2(): lax.ppermute(lax.slice_in_dim(block, 0, width, axis=dim), axis, backward)  76.1 us
    another operation x9, other arithmetic  59.5 us
    another operation x4, other arithmetic, rotate(): jnp.stack([data[0] * cosine_part - data[1] * sine_part, data[0] * sine_pa...  25.5 us
    transpose x1, other arithmetic, shards(): return merged.T  22.5 us
  transfers between devices with their start and end apart: 6, of which 3 were waited for; matrix products, arithmetic and copies ran while one was open for 2% of the time, Pallas kernels for 0%

commit v1 on v0

--- a/solution.py
+++ b/solution.py
@@ -1,8 +1,13 @@
+import functools
 import math
 
 import jax
 import jax.numpy as jnp
+import numpy as np
 from jax import lax
+from jax.experimental import pallas as pl
+from jax.experimental.pallas import tpu as pltpu
+from jax.sharding import Mesh
 from jax.sharding import PartitionSpec as P
 
 N = 4096
@@ -169,7 +174,536 @@
     return merged.T
 
 
+OUT = 16
+INN = 256
+CLS = 8
+LANE = 128
+
+
+def slot_frequencies():
+    table = np.arange(CLS)[:, None] + OUT * np.arange(INN)[None, :]
+    half = np.arange(INN // 2)
+    table[0] = np.concatenate([OUT * half, CLS + OUT * half])
+    return table
+
+
+def angles(products):
+    return 2.0 * np.pi * (products % N) / N
+
+
+def row_forward_tables():
+    freq = slot_frequencies()
+    theta = angles(np.arange(INN)[None, :, None] * freq[:, None, :])
+    cos, sin = np.cos(theta) / 64.0, np.sin(theta) / 64.0
+    top = np.stack([cos, -sin], axis=2)
+    low = np.stack([sin, cos], axis=2)
+    first = np.arange(INN) < INN // 2
+    low[0] = np.where(first, 0.0, top[0])
+    top[0] = np.where(first, top[0], 0.0)
+    full = np.concatenate([top, low], axis=1)
+    full = full.reshape(CLS, 2 * INN, 2, 2, LANE).transpose(0, 1, 3, 2, 4)
+    return full.reshape(CLS, 2 * INN, 2 * INN).astype(jnp.bfloat16)
+
+
+def row_forward_weights():
+    turn = 2.0 * np.pi * np.arange(CLS)[:, None] * np.arange(OUT)[None, :] / OUT
+    re, im = np.cos(turn), -np.sin(turn)
+    im[0] = (-1.0) ** np.arange(OUT)
+    return np.stack([re, im], axis=1).reshape(-1).astype(np.float32)
+
+
+def row_inverse_tables():
+    freq = slot_frequencies()
+    theta = angles(freq[:, :, None] * np.arange(INN)[None, None, :])
+    cos, sin = np.cos(theta) / 32.0, np.sin(theta) / 32.0
+    full = np.zeros((CLS, 2, INN, 2, INN))
+    full[:, 0, :, 0], full[:, 0, :, 1] = cos, sin
+    full[:, 1, :, 0], full[:, 1, :, 1] = -sin, cos
+    half = INN // 2
+    full[0] = 0.0
+    full[0, 0, :half, 0], full[0, 1, :half, 0] = cos[0, :half], -sin[0, :half]
+    full[0, 0, half:, 1], full[0, 1, half:, 1] = cos[0, half:], -sin[0, half:]
+    full[0, 0, 0, 0] = 1.0 / 64.0
+    full[0, 1, 0, 0] = (-1.0) ** np.arange(INN) / 64.0
+    full = full.reshape(CLS, 2, 2, LANE, 2 * INN).transpose(0, 2, 1, 3, 4)
+    return full.reshape(CLS, 2 * INN, 2 * INN).astype(jnp.bfloat16)
+
+
+def column_tables():
+    turn = 2.0 * np.pi * np.arange(OUT)[:, None] * np.arange(OUT)[None, :] / OUT
+    eye = np.eye(16)
+    outer_cos, outer_sin = np.kron(np.cos(turn), eye) / 4.0, np.kron(np.sin(turn), eye) / 4.0
+    outer = np.concatenate([outer_cos, -outer_sin])
+    half_rows = outer_cos.shape[0] // 2
+    back = np.stack(
+        [
+            np.concatenate([outer_cos[i * half_rows :][:half_rows], outer_sin[i * half_rows :][:half_rows]])
+            for i in range(2)
+        ]
+    )
+    freq = np.arange(OUT)[:, None] + OUT * np.arange(INN)[None, :]
+    theta = angles(freq[:, :, None] * np.arange(INN)[None, None, :])
+    inner = np.concatenate([np.cos(theta), -np.sin(theta)], axis=1) / 16.0
+    theta = theta.transpose(0, 2, 1)
+    inner_back = np.concatenate([np.cos(theta), np.sin(theta)], axis=1) / 16.0
+    cast = lambda table: table.astype(jnp.bfloat16)
+    return cast(outer), cast(inner), cast(inner_back), cast(back)
+
+
+def dot(left, right):
+    return jnp.dot(left, right, preferred_element_type=jnp.float32)
+
+
+def split_complex(both, width):
+    rows = both.shape[0] // 2
+    top, low = both[:rows], both[rows:]
+    return top[:, :width] - low[:, width:], top[:, width:] + low[:, :width]
+
+
+def quarter_kernel(radial):
+    gap = wave_number * wave_number - radial
+    root = jnp.sqrt(jnp.abs(gap))
+    inside = gap > 0.0
+    half_pi = 0.5 * math.pi
+    angle = half_pi * (jnp.where(inside, root, 0.0) - wave_number)
+    decay = jnp.exp(jnp.where(inside, 0.0, -half_pi * root))
+    square = angle * angle
+    sine = 1.0 / 362880.0
+    for c in (-1.0 / 5040.0, 1.0 / 120.0, -1.0 / 6.0, 1.0):
+        sine = sine * square + c
+    cosine = -1.0 / 3628800.0
+    for c in (1.0 / 40320.0, -1.0 / 720.0, 1.0 / 24.0, -0.5, 1.0):
+        cosine = cosine * square + c
+    return decay * cosine, decay * (sine * angle)
+
+
+def squared(re, im):
+    return (re - im) * (re + im), 2.0 * re * im
+
+
+def start_and_step(radial):
+    value = quarter_kernel(radial)
+    distance = 0.25
+    step = None
+    while distance < depth_start:
+        value = squared(*value)
+        distance *= 2.0
+        if distance == depth_step:
+            step = value
+    return value, step
+
+
+def signed_fraction(natural):
+    return jnp.where(natural >= N // 2, natural - N, natural).astype(jnp.float32) * (1.0 / N)
+
+
+def row_forward_kernel(own, weights, holo, back, table, out, nyquist, acc):
+    rows = holo.shape[0]
+    group = own[0]
+    lane = lax.broadcasted_iota(jnp.int32, (16, INN), 1)
+    sign = jnp.where(lane % 2 == 0, 1.0, -1.0)
+
+    def strip(i, carry):
+        here = pl.ds(pl.multiple_of(i * 16, 16), 16)
+        sums = [jnp.zeros((16, INN), jnp.float32) for _ in range(5)]
+        for a in range(OUT):
+            there = pl.ds(a * INN, INN)
+            value = holo[here, there].astype(jnp.float32) / back[here, there].astype(jnp.float32)
+            value = (value - 1.0).astype(jnp.bfloat16).astype(jnp.float32)
+            for q in range(4):
+                w = weights[(group * 2 + q // 2) * (2 * OUT) + (q % 2) * OUT + a]
+                sums[q] = sums[q] + value * w
+            sums[4] = sums[4] + value
+        for q in range(4):
+            acc[q // 2, here, pl.ds((q % 2) * INN, INN)] = sums[q].astype(jnp.bfloat16)
+        turned = sums[4] * sign
+        nyquist[here, :] = turned[:, :LANE] + turned[:, LANE:]
+        return carry
+
+    lax.fori_loop(0, rows // 16, strip, 0)
+    for q in range(2):
+        result = dot(acc[q], table[q]).astype(jnp.bfloat16)
+        for low in range(2):
+            part = result[:, low * 2 * LANE : (low + 1) * 2 * LANE]
+            for high in range(2):
+                out[high, low, q] = part
+
+
+def row_forward(own, hologram, background):
+    rows = hologram.shape[0]
+    block = 128
+    table = jnp.asarray(row_forward_tables())
+    weights = jnp.asarray(row_forward_weights())
+    return pl.pallas_call(
+        row_forward_kernel,
+        grid_spec=pltpu.PrefetchScalarGridSpec(
+            num_scalar_prefetch=2,
+            grid=(rows // block,),
+            in_specs=[
+                pl.BlockSpec((block, N), lambda i, o, w: (i, 0)),
+                pl.BlockSpec((block, N), lambda i, o, w: (i, 0)),
+                pl.BlockSpec((2, 2 * INN, 2 * INN), lambda i, o, w: (o[0], 0, 0)),
+            ],
+            out_specs=[
+                pl.BlockSpec((2, 2, 2, block, 2 * LANE), lambda i, o, w: (0, 0, 0, i, 0)),
+                pl.BlockSpec((block, LANE), lambda i, o, w: (i, 0)),
+            ],
+            scratch_shapes=[pltpu.VMEM((2, block, 2 * INN), jnp.bfloat16)],
+        ),
+        out_shape=[
+            jax.ShapeDtypeStruct((2, 2, 2, rows, 2 * LANE), jnp.bfloat16),
+            jax.ShapeDtypeStruct((rows, LANE), jnp.float32),
+        ],
+        compiler_params=pltpu.CompilerParams(vmem_limit_bytes=40 * 1024 * 1024),
+        cost_estimate=pl.CostEstimate(flops=10**10, bytes_accessed=12 * 2**20, transcendentals=0),
+        name="row_forward",
+    )(own, weights, hologram, background, table)
+
+
+def column_kernel(planes, data, fx2, outer, inner, inner_back, back, out, first, mixed, second):
+    step = pl.program_id(0)
+    width = LANE
+
+    @pl.when(step == 0)
+    def _():
+        def chunk(i, carry):
+            here = pl.ds(pl.multiple_of(i * 16, 16), 16)
+            block = data[:, here, :].reshape(OUT * 16, 2 * width)
+            re, im = split_complex(dot(outer[...], block), width)
+            value = jnp.concatenate([re, im], axis=1).astype(jnp.bfloat16)
+            first[:, here, :] = value.reshape(OUT, 16, 2 * width)
+            return carry
+
+        lax.fori_loop(0, INN // 16, chunk, 0)
+
+    @pl.when(step < OUT)
+    def _():
+        both = dot(inner[0], first[step])
+        strip = 32
+        for i in range(INN // strip):
+            rows = slice(i * strip, (i + 1) * strip)
+            low_rows = slice(INN + i * strip, INN + (i + 1) * strip)
+            yr = both[rows, :width] - both[low_rows, width:]
+            yi = both[rows, width:] + both[low_rows, :width]
+            position = lax.broadcasted_iota(jnp.int32, (strip, width), 0) + i * strip
+            fy = signed_fraction(step + OUT * position)
+            (kr, ki), (sr, si) = start_and_step(fy * fy + fx2[...])
+            for g in range(planes):
+                for part, factor in enumerate((kr, ki)):
+                    at = (g * 2 + part) * 2 * width
+                    mixed[rows, at : at + width] = (yr * factor).astype(jnp.bfloat16)
+                    mixed[rows, at + width : at + 2 * width] = (yi * factor).astype(jnp.bfloat16)
+                if g + 1 < planes:
+                    kr, ki = kr * sr - ki * si, kr * si + ki * sr
+        for g in range(2 * planes):
+            lanes = slice(g * 2 * width, (g + 1) * 2 * width)
+            re, im = split_complex(dot(inner_back[0], mixed[:, lanes]), width)
+            second[step, :, lanes] = jnp.concatenate([re, im], axis=1).astype(jnp.bfloat16)
+
+    @pl.when(step >= OUT)
+    def _():
+        here = pl.ds(pl.multiple_of((step - OUT) * 16, 16), 16)
+        for g in range(2 * planes):
+            lanes = slice(g * 2 * width, (g + 1) * 2 * width)
+            block = second[:, here, lanes].reshape(OUT * 16, 2 * width)
+            re, im = split_complex(dot(back[0], block), width)
+            value = jnp.concatenate([re, im], axis=1).astype(jnp.bfloat16)
+            value = value.reshape(2, 2, 2, 16, 2 * width)
+            for low in range(2):
+                for core in range(2):
+                    for high in range(2):
+                        out[high, 0, low, core, :, lanes] = value[low, core, high]
+
+
+def columns(half, planes, data, fx2):
+    outer, inner, inner_back, back = (jnp.asarray(t) for t in column_tables())
+    lanes = planes * 4 * LANE
+    mib = 2**20
+    inner_at = lambda i, o: (jnp.minimum(i, OUT - 1), 0, 0)
+    chunk = lambda i: jnp.maximum(i - OUT, 0)
+    return pl.pallas_call(
+        lambda o, *refs: column_kernel(planes, *refs),
+        grid_spec=pltpu.PrefetchScalarGridSpec(
+            num_scalar_prefetch=1,
+            grid=(2 * OUT,),
+            in_specs=[
+                pl.BlockSpec((OUT, INN, 2 * LANE), lambda i, o: (0, 0, 0)),
+                pl.BlockSpec((1, LANE), lambda i, o: (0, 0)),
+                pl.BlockSpec((2 * INN, INN), lambda i, o: (0, 0)),
+                pl.BlockSpec((1, 2 * INN, INN), inner_at),
+                pl.BlockSpec((1, 2 * INN, INN), inner_at),
+                pl.BlockSpec((1, INN, INN), lambda i, o: (o[0], 0, 0)),
+            ],
+            out_specs=pl.BlockSpec(
+                (2, 1, 2, 2, 16, lanes), lambda i, o: (0, chunk(i) // 8, 0, 0, chunk(i) % 8, 0)
+            ),
+            scratch_shapes=[
+                pltpu.VMEM((OUT, INN, 2 * LANE), jnp.bfloat16),
+                pltpu.VMEM((INN, lanes), jnp.bfloat16),
+                pltpu.VMEM((OUT, INN, lanes), jnp.bfloat16),
+            ],
+        ),
+        out_shape=jax.ShapeDtypeStruct((2, 2, 2, 2, LANE, lanes), jnp.bfloat16),
+        compiler_params=pltpu.CompilerParams(vmem_limit_bytes=48 * mib),
+        cost_estimate=pl.CostEstimate(flops=2 * 10**10, bytes_accessed=20 * mib, transcendentals=0),
+        name="columns",
+    )(half, data, fx2, outer, inner, inner_back, back)
+
+
+def sixteen_points(re, im):
+    c = math.sqrt(0.5)
+    c1, c3 = math.cos(math.pi / 8), math.cos(3 * math.pi / 8)
+    r0, r1, r2, r3, r4, r5, r6, r7 = re
+    r8, i1, i2, i3, i4, i5, i6, i7 = im
+    sum08, dif08, sum26, dif26 = r0 + r8, r0 - r8, r2 + r6, c * (r2 - r6)
+    base = sum08 + r4
+    even = [base + sum26, dif08 + dif26, sum08 - r4, dif08 - dif26, base - sum26]
+    sum17, dif17, sum35, dif35 = r1 + r7, r1 - r7, r3 + r5, r3 - r5
+    odd = [sum17 + sum35, c1 * dif17 + c3 * dif35, c * (sum17 - sum35), c3 * dif17 - c1 * dif35]
+    cosines = [even[a] + odd[a] for a in range(4)] + [even[4]]
+    cosines += [even[8 - a] - odd[8 - a] for a in range(5, 9)]
+    s17, d17, s35, d35 = i1 + i7, i1 - i7, i3 + i5, i3 - i5
+    sines_odd = [None, c3 * s17 + c1 * s35, c * (d17 + d35), c1 * s17 - c3 * s35, d17 - d35]
+    s26 = c * (i2 + i6)
+    sines_even = [None, s26 + i4, i2 - i6, s26 - i4]
+    sines = [None] + [sines_odd[a] + sines_even[a] for a in (1, 2, 3)] + [sines_odd[4]]
+    sines += [sines_odd[8 - a] - sines_even[8 - a] for a in (5, 6, 7)]
+    result = [cosines[0]] + [cosines[a] - sines[a] for a in range(1, 8)] + [cosines[8]]
+    return result + [cosines[16 - a] + sines[16 - a] for a in range(9, 16)]
+
+
+def row_inverse_kernel(parts, nyquist, table, out, opened):
+    plane = pl.program_id(0)
+    rows = out.shape[1]
+    lane = lax.broadcasted_iota(jnp.int32, (rows, LANE), 1)
+    for part in range(2):
+        at = part * 2 * LANE
+        column = jnp.sum(jnp.where(lane == plane * 2 + part, nyquist[...], 0.0), axis=1, keepdims=True)
+        for group in range(CLS):
+            pieces = [parts[group // 2, low, group % 2, :, pl.ds(at, 2 * LANE)] for low in range(2)]
+            block = jnp.concatenate(pieces, axis=1)
+            if group == 0:
+                first = jnp.where(lane == 0, column.astype(jnp.bfloat16), block[:, LANE : 2 * LANE])
+                block = jnp.concatenate([block[:, :LANE], first, block[:, 2 * LANE :]], axis=1)
+            opened[part, group] = dot(block, table[group])
+
+    def strip(i, carry):
+        here = pl.ds(pl.multiple_of(i * 16, 16), 16)
+        for tile in range(INN // LANE):
+            total = None
+            for part in range(2):
+                re = [opened[part, g, here, pl.ds(tile * LANE, LANE)] for g in range(CLS)]
+                im = [opened[part, g, here, pl.ds(INN + tile * LANE, LANE)] for g in range(CLS)]
+                values = sixteen_points(re, im)
+                if total is None:
+                    total = [v * v for v in values]
+                else:
+                    total = [t + v * v for t, v in zip(total, values)]
+            for a in range(OUT):
+                out[0, here, pl.ds(a * INN + tile * LANE, LANE)] = total[a].astype(jnp.bfloat16)
+        return carry
+
+    lax.fori_loop(0, rows // 16, strip, 0)
+
+
+def row_inverse(planes, parts, nyquist):
+    rows = parts.shape[3]
+    table = jnp.asarray(row_inverse_tables())
+    mib = 2**20
+    return pl.pallas_call(
+        row_inverse_kernel,
+        grid=(planes,),
+        in_specs=[
+            pl.BlockSpec((4, 2, 2, rows, 4 * LANE), lambda g: (0, 0, 0, 0, g)),
+            pl.BlockSpec((rows, LANE), lambda g: (0, 0)),
+            pl.BlockSpec((CLS, 2 * INN, 2 * INN), lambda g: (0, 0, 0)),
+        ],
+        out_specs=pl.BlockSpec((1, rows, N), lambda g: (g, 0, 0)),
+        out_shape=jax.ShapeDtypeStruct((planes, rows, N), jnp.bfloat16),
+        scratch_shapes=[pltpu.VMEM((2, CLS, rows, 2 * INN), jnp.float32)],
+        compiler_params=pltpu.CompilerParams(vmem_limit_bytes=40 * mib),
+        cost_estimate=pl.CostEstimate(flops=10**10, bytes_accessed=20 * mib, transcendentals=0),
+        name="row_inverse",
+    )(parts, nyquist, table)
+
+
+def nyquist_kernel(planes, data, out):
+    size = RADIX
+    row = lax.broadcasted_iota(jnp.int32, (size, size), 0)
+    col = lax.broadcasted_iota(jnp.int32, (size, size), 1)
+    turn = (row * col % size).astype(jnp.float32) * (2.0 * math.pi / size)
+    wr, wi = jnp.cos(turn) * (1.0 / 8.0), jnp.sin(turn) * (1.0 / 8.0)
+    twist = (row * col).astype(jnp.float32) * (2.0 * math.pi / (size * size))
+    vr, vi = jnp.cos(twist), jnp.sin(twist)
+
+    def exact(left, right):
+        return jnp.dot(left, right, preferred_element_type=jnp.float32, precision=lax.Precision.HIGHEST)
+
+    def product(xr, xi, yr, yi):
+        return exact(xr, yr) - exact(xi, yi), exact(xr, yi) + exact(xi, yr)
+
+    def rotated(xr, xi, yr, yi):
+        return xr * yr - xi * yi, xr * yi + xi * yr
+
+    ar, ai = rotated(exact(wr, data[...]), exact(-wi, data[...]), vr, -vi)
+    yr, yi = product(ar, ai, wr, -wi)
+    fy = signed_fraction(row + size * col)
+    (kr, ki), (sr, si) = start_and_step(fy * fy + 0.25)
+    for g in range(planes):
+        pr, pi = rotated(yr, yi, kr, ki)
+        br, bi = rotated(*product(pr, pi, wr, wi), vr, vi)
+        ur, ui = product(wr, wi, br, bi)
+        out[2 * g] = ur
+        out[2 * g + 1] = ui
+        kr, ki = rotated(kr, ki, sr, si)
+
+
+def nyquist_column(planes, data):
+    return pl.pallas_call(
+        functools.partial(nyquist_kernel, planes),
+        out_shape=jax.ShapeDtypeStruct((2 * planes, RADIX, RADIX), jnp.float32),
+        cost_estimate=pl.CostEstimate(flops=10**7, bytes_accessed=2**18, transcendentals=0),
+        name="nyquist",
+    )(data)
+
+
+def focus_kernel(intensity, north, south, out, held):
+    planes, rows = intensity.shape[0], intensity.shape[1]
+    for g in range(planes):
+        held[g, 8 : 8 + rows, :] = intensity[g].astype(jnp.float32)
+        held[g, 0:8, :] = jnp.broadcast_to(north[g : g + 1].astype(jnp.float32), (8, N))
+        held[g, 8 + rows : 16 + rows, :] = jnp.broadcast_to(south[g : g + 1].astype(jnp.float32), (8, N))
+    tile = 512
+    lane = lax.broadcasted_iota(jnp.int32, (16, tile), 1)
+    for i in range(rows // 16):
+        r = 8 + i * 16
+        for t in range(N // tile):
+            lanes = slice(t * tile, (t + 1) * tile)
+            centre = [held[g, r : r + 16, lanes] for g in range(planes)]
+            best = None
+            for g in range(planes):
+                depth = centre[min(g + 1, planes - 1)] - centre[max(g - 1, 0)]
+                down = held[g, r + 1 : r + 17, lanes] - held[g, r - 1 : r + 15, lanes]
+                first, last = max(t * tile - 1, 0), min((t + 1) * tile, N - 1)
+                right = pltpu.roll(centre[g], tile - 1, 1)
+                right = jnp.where(lane == tile - 1, held[g, r : r + 16, last : last + 1], right)
+                left = pltpu.roll(centre[g], 1, 1)
+                left = jnp.where(lane == 0, held[g, r : r + 16, first : first + 1], left)
+                across = right - left
+                score = depth * depth + down * down + across * across
+                best = score if best is None else jnp.maximum(best, score)
+            out[i * 16 : (i + 1) * 16, lanes] = (best * 0.125).astype(jnp.bfloat16)
+
+
+def focus_measure(intensity, north, south):
+    planes, rows, _ = intensity.shape
+    mib = 2**20
+    return pl.pallas_call(
+        focus_kernel,
+        out_shape=jax.ShapeDtypeStruct((rows, N), jnp.bfloat16),
+        scratch_shapes=[pltpu.VMEM((planes, rows + 16, N), jnp.float32)],
+        compiler_params=pltpu.CompilerParams(vmem_limit_bytes=40 * mib),
+        cost_estimate=pl.CostEstimate(flops=10**8, bytes_accessed=6 * mib, transcendentals=0),
+        name="focus",
+    )(intensity, north, south)
+
+
+def assemble_kernel(own, mine, ax, ay, axy, bx, by, byx, out):
+    slot = pl.program_id(0)
+    half = ax.shape[0]
+    for s, (a, b) in enumerate(((None, None), (ax, bx), (ay, by), (axy, byx))):
+
+        @pl.when(slot == s)
+        def _():
+            if a is None:
+                out[...] = mine[...].astype(jnp.float32)
+            else:
+                out[:half] = a[...].astype(jnp.float32)
+                out[half:] = b[...].astype(jnp.float32)
+
+
+def assemble(depth_index, mine, halves):
+    rows = mine.shape[0]
+    whole = lambda shape: pl.BlockSpec(shape, lambda s, o: (0, 0))
+    return pl.pallas_call(
+        assemble_kernel,
+        grid_spec=pltpu.PrefetchScalarGridSpec(
+            num_scalar_prefetch=1,
+            grid=(4,),
+            in_specs=[whole((rows, N))] + [whole((rows // 2, N))] * 6,
+            out_specs=pl.BlockSpec((rows, N), lambda s, o: (jnp.bitwise_xor(s, o[0]), 0)),
+        ),
+        out_shape=jax.ShapeDtypeStruct((4 * rows, N), jnp.float32),
+        compiler_params=pltpu.CompilerParams(vmem_limit_bytes=40 * 2**20),
+        cost_estimate=pl.CostEstimate(flops=10**6, bytes_accessed=12 * 2**20, transcendentals=0),
+        name="assemble",
+    )(depth_index, mine, *halves)
+
+
+def exchange_depth(mine):
+    half = mine.shape[0] // 2
+    a, b = mine[:half], mine[half:]
+    over_x = [(i, i ^ 1) for i in range(4)]
+    over_y = [(i, i ^ 2) for i in range(4)]
+    ax, by = lax.ppermute(a, "depth", over_x), lax.ppermute(b, "depth", over_y)
+    ay, axy = lax.ppermute(a, "depth", over_y), lax.ppermute(ax, "depth", over_y)
+    bx, byx = lax.ppermute(b, "depth", over_x), lax.ppermute(by, "depth", over_x)
+    return ax, ay, axy, bx, by, byx
+
+
+def half_spectrum_shards(hologram, background):
+    rows = hologram.shape[0]
+    planes = lax.axis_size("depth") * PL_DEV
+    depth, high = lax.axis_index("depth"), lax.axis_index("high")
+    low, core = lax.axis_index("low"), lax.axis_index("core")
+    as_scalar = lambda value: jnp.reshape(value, (1,)).astype(jnp.int32)
+    everyone = ("depth", "high", "low", "core")
+    slab = ("high", "low", "core")
+
+    sections, alternating = row_forward(as_scalar(depth), hologram, background)
+    column_sum = lax.all_gather(jnp.sum(alternating, axis=1) * (1.0 / 64.0), slab, tiled=True)
+    data = lax.all_to_all(
+        sections.reshape(8, rows, 2 * LANE), slab, split_axis=0, concat_axis=0, tiled=True
+    )
+
+    group = depth * 2 + core
+    slot = low * LANE + jnp.arange(LANE, dtype=jnp.int32)
+    special = jnp.where(low == 0, 0, CLS) + OUT * jnp.arange(LANE, dtype=jnp.int32)
+    fx = signed_fraction(jnp.where(group == 0, special, group + OUT * slot))
+    halfway = columns(as_scalar(high), planes, data.reshape(OUT, INN, 2 * LANE), (fx * fx)[None])
+    own = rows // 4
+    parts = lax.all_to_all(
+        halfway.reshape(16, own, -1), ("depth", "low", "core"), split_axis=0, concat_axis=0, tiled=True
+    )
+    first_row = ((high * 2 + low) * 2 + core) * rows + depth * own
+    middle = nyquist_column(planes, column_sum.reshape(RADIX, RADIX)).reshape(2 * planes, N)
+    middle = lax.dynamic_slice_in_dim(middle, first_row, own, axis=1).T
+    middle = jnp.pad(middle, ((0, 0), (0, LANE - 2 * planes)))
+    intensity = row_inverse(planes, parts.reshape(4, 2, 2, own, -1), middle)
+
+    order = [
+        ((d * 2 + h) * 2 + l) * 2 + c
+        for h in range(2)
+        for l in range(2)
+        for c in range(2)
+        for d in range(4)
+    ]
+    down = list(zip(order[:-1], order[1:]))
+    up = [(target, source) for source, target in down]
+    north = lax.ppermute(intensity[:, -1], everyone, down)
+    south = lax.ppermute(intensity[:, 0], everyone, up)
+    north = jnp.where(first_row == 0, intensity[:, 0], north)
+    south = jnp.where(first_row == N - own, intensity[:, -1], south)
+    mine = focus_measure(intensity, north, south)
+    return assemble(as_scalar(depth), mine, exchange_depth(mine))
+
+
 def solution(mesh):
-    in_specs = (P("rows", None), P("rows", None))
-    out_specs = P("rows", None)
-    return jax.shard_map(shards, mesh=mesh, in_specs=in_specs, out_specs=out_specs, check_vma=False)
+    spec = P("rows", None)
+    if mesh.shape["depth"] == 4 and mesh.shape["rows"] == 8:
+        split = Mesh(mesh.devices.reshape(4, 2, 2, 2), ("depth", "high", "low", "core"))
+        spec = P(("high", "low", "core"), None)
+        body = half_spectrum_shards
+    else:
+        split, body = mesh, shards
+    return jax.shard_map(body, mesh=split, in_specs=(spec, spec), out_specs=spec, check_vma=False)

time: 1040 us -> 305 us (0.29); the launches traced: 1030 us -> 304 us
  waiting for transfers between devices: 454 us -> 82.7 us
  local copies, waits for them, and re-layouts: 142 us -> 15.2 us
  other arithmetic: 125 us -> 0.32 us
  matrix products: 89 us -> 0 us
  blocking collectives: 188 us -> 110 us
  Pallas kernels: 0 us -> 71.1 us
  between operations: 14.1 us -> 0.19 us
    pmax x1 -> x0, waiting for transfers between devices: 195 us -> none  [shards(): lax.pmax(sharpest.astype(jnp.bfloat16), 'depth').astype(sharpest.dtype)]
    all_to_all x1 -> x0, blocking collectives: 188 us -> none  [shards(): lax.all_to_all(jnp.swapaxes(halfway, 1, 2), 'rows', split_axis=2, concat_...]
    all_to_all x1 -> x2, waiting for transfers between devices: 183 us -> 49.1 us  [the longest x1 49.1 us: half_spectrum_shards(): lax.all_to_all(sections.reshape(8, rows, 2 * LANE), slab, split_axis=0, c...]
    all_gather x0 -> x1, blocking collectives: none -> 110 us  [half_spectrum_shards(): lax.all_gather(jnp.sum(alternating, axis=1) * (1.0 / 64.0), slab, tiled=T...]
    dot_general x8 -> x0, matrix products: 89 us -> none  [contract(): return jnp.einsum(form, matrix, data, preferred_element_type=jnp.float32)]
    another operation x16 -> x0, other arithmetic: 85.1 us -> none
    pallas_call x0 -> x6, Pallas kernels: none -> 71.1 us  [the longest x1 37.5 us: columns(): pl.pallas_call(lambda o, *refs: column_kernel(planes, *refs), grid_spec=p...]
    ppermute x4 -> x8, waiting for transfers between devices: 76.1 us -> 33.7 us  [the longest x1 9.78 us: exchange_depth(): lax.ppermute(a, 'depth', over_y)]
  transfers between devices with their start and end apart: 6 -> 10, of which waited for: 3 -> 6; matrix products, arithmetic and copies ran while one was open for 2% -> 1% of each run, Pallas kernels for 0% -> 1%
where the time goes in v1:
time: 305 us; the launch traced here: 304 us
  blocking collectives  110 us (36%)
  waiting for transfers between devices  82.7 us (27%)
  Pallas kernels  71.1 us (23%)
  starting transfers between devices  25 us (8%)
  local copies, waits for them, and re-layouts  15.2 us (5%)
    all_gather x1, blocking collectives, half_spectrum_shards(): lax.all_gather(jnp.sum(alternating, axis=1) * (1.0 / 64.0), slab, tiled=T...  110 us
    all_to_all x1, waiting for transfers between devices, half_spectrum_shards(): lax.all_to_all(sections.reshape(8, rows, 2 * LANE), slab, split_axis=0, c...  49.1 us
    pallas_call x1, Pallas kernels, columns(): pl.pallas_call(lambda o, *refs: column_kernel(planes, *refs), grid_spec=p...  37.5 us
    unnamed x19, local copies, waits for them, and re-layouts  12.8 us
    pallas_call x1, Pallas kernels, row_inverse(): pl.pallas_call(row_inverse_kernel, grid=(planes,), in_specs=[pl.BlockSpec...  11.1 us
    ppermute x1, waiting for transfers between devices, exchange_depth(): lax.ppermute(a, 'depth', over_y)  9.78 us
    ppermute x1, waiting for transfers between devices, exchange_depth(): lax.ppermute(a, 'depth', over_x)  9.18 us
    ppermute x1, waiting for transfers between devices, exchange_depth(): lax.ppermute(ax, 'depth', over_y)  8.83 us
  transfers between devices with their start and end apart: 10, of which 6 were waited for; matrix products, arithmetic and copies ran while one was open for 1% of the time, Pallas kernels for 1%

profile of v1, /device:TPU:0, one launch (start us, length us, event | category | flops | bytes accessed | tf_op | source)
XLA Modules:
  0.0 304.3 jit_solution(7275504719447624936)
XLA Ops:
  0.0 0.0 copy-start.3
  0.0 2.2 copy-done.3
  2.2 2.2 copy-done.4
  4.4 0.7 copy-done.8
  5.1 8.0 %row_forward.1 = (bf16[2,2,2,512,256]{4,3,2,1,0:T(8,128)(2,1)S(1)}, f32[512,128]{1,0:T(8,128)S(1)}) custom-call(s32[1]{0:T(128)} %bitcast.own, f32[256]{0:T(256)S(1)} %copy-done.8, bf16[512,4096]{1,0:T(8,128)(2,1)S(1)} %copy-done.3, bf16[512,4096]{1,0:T(8,128)(2,1)S(1)} %copy-done.4, bf16[8,512,512]{2,1,0:T(8,128)(2,1)} %constant.56.clone.table), custom_call_target="tpu_custom_call" | custom-call | flops 10000000000 | bytes 12582912 | tf_op jit(solution)/shard_map/row_forward/pallas_call | solution.py:337
  13.1 0.0 copy-start.2
  13.1 1.3 copy-done.2
  14.4 6.5 %all-to-all-start = ((bf16[8,512,256]{2,1,0:T(8,128)(2,1)}), bf16[8,512,256]{2,1,0:T(8,128)(2,1)S(1)}, u32[]{:S(2)}, u32[]{:S(2)}) async-start(bf16[8,512,256]{2,1,0:T(8,128)(2,1)} %bitcast.19), calls=%async_computation | async-start | bytes 4194304 | tf_op jit(solution)/shard_map/all_to_all | solution.py:665
  20.9 49.1 %all-to-all-done = bf16[8,512,256]{2,1,0:T(8,128)(2,1)S(1)} async-done(((bf16[8,512,256]{2,1,0:T(8,128)(2,1)}), bf16[8,512,256]{2,1,0:T(8,128)(2,1)S(1)}, u32[]{:S(2)}, u32[]{:S(2)}) %all-to-all-start) | async-done | bytes 2097184 | tf_op jit(solution)/shard_map/all_to_all | solution.py:665
  69.9 0.0 copy-done.6
  69.9 0.0 copy-done.7
  69.9 37.5 %columns.1 = bf16[2,2,2,2,128,2048]{5,4,3,2,1,0:T(8,128)(2,1)} custom-call(s32[1]{0:T(128)} %bitcast.1.o, bf16[16,256,256]{2,1,0:T(8,128)(2,1)S(1)} %bitcast.18, f32[1,128]{1,0:T(1,128)S(1)} %multiply_multiply_fusion.refs_1_, bf16[512,256]{1,0:T(8,128)(2,1)S(1)} %copy-done.6, bf16[16,512,256]{2,1,0:T(8,128)(2,1)} %constant.59.clone.refs_3_, ...), custom_call_target="tpu_custom_call" | custom-call | flops 20000000000 | bytes 20971520 | tf_op jit(solution)/shard_map/columns/pallas_call | solution.py:424
  107.4 4.8 %all-to-all-start.1 = ((bf16[16,128,2048]{2,1,0:T(8,128)(2,1)}), bf16[16,128,2048]{2,1,0:T(8,128)(2,1)}, u32[]{:S(2)}, u32[]{:S(2)}) async-start(bf16[16,128,2048]{2,1,0:T(8,128)(2,1)} %bitcast.20), calls=%async_computation.1 | async-start | bytes 16777216 | tf_op jit(solution)/shard_map/all_to_all | solution.py:675
  112.2 0.1 reduce_sum.9
  112.3 109.7 %all-gather = f32[8,1,512]{2,1,0:T(1,128)S(1)} all-gather(f32[1,1,512]{2,1,0:T(1,128)S(1)} %bitcast.23), channel_id=1, replica_groups=mesh['depth'=4,'high'=2,'low'=2,'core'=2] {'high','low','core'}, dimensions={0}, use_global_device_ids=true | all-gather | bytes 18432 | tf_op jit(solution)/shard_map/all_gather | solution.py:664
  222.0 0.7 reshape.75.data
  222.7 3.7 %nyquist.1 = f32[8,64,64]{2,1,0:T(8,128)} custom-call(f32[64,64]{1,0:T(8,128)} %reshape.75.data), custom_call_target="tpu_custom_call" | custom-call | flops 10000000 | bytes 262144 | tf_op jit(solution)/shard_map/nyquist/pallas_call | solution.py:562
  226.4 1.6 copy.13
  228.0 0.0 all-to-all-done.1
  228.0 0.0 copy-start.5
  228.0 2.2 copy-done.5
  230.2 11.1 %row_inverse.1.intensity = bf16[4,128,4096]{2,1,0:T(8,128)(2,1)S(1)} custom-call(bf16[4,2,2,128,2048]{4,3,2,1,0:T(8,128)(2,1)} %bitcast.5.parts, f32[128,128]{1,0:T(8,128)S(1)} %pad.4.nyquist, bf16[8,512,512]{2,1,0:T(8,128)(2,1)S(1)} %copy-done.5), custom_call_target="tpu_custom_call" | custom-call | flops 10000000000 | bytes 20971520 | tf_op jit(solution)/shard_map/row_inverse/pallas_call | solution.py:513
  241.4 0.1 fusion
  241.5 0.0 copy-start
  241.5 2.0 copy-done
  243.5 1.3 collective-permute-start.1
  244.8 4.5 %collective-permute-done.1 = bf16[4,4096]{1,0:T(4,128)(2,1)S(1)} collective-permute-done((bf16[4,4096]{1,0:T(4,128)(2,1)S(1)}, bf16[4,4096]{1,0:T(4,128)(2,1)S(1)}, u32[]{:S(2)}, u32[]{:S(2)}) %collective-permute-start.1) | collective-permute-done | bytes 32800 | tf_op jit(solution)/shard_map/ppermute | solution.py:694
  249.4 0.1 broadcast_select_fusion
  249.4 3.0 collective-permute-start
  252.4 1.4 collective-permute-done
  253.8 0.1 broadcast_select_fusion.1.north
  253.9 0.0 copy-start.1
  253.9 2.2 copy-done.1
  256.1 7.2 %focus.1.mine = bf16[128,4096]{1,0:T(8,128)(2,1)S(1)} custom-call(bf16[4,128,4096]{2,1,0:T(8,128)(2,1)S(1)} %copy-done.1, bf16[4,4096]{1,0:T(4,128)(2,1)S(1)} %broadcast_select_fusion.1.north, bf16[4,4096]{1,0:T(4,128)(2,1)S(1)} %get-tuple-element.9.south), custom_call_target="tpu_custom_call" | custom-call | flops 100000000 | bytes 6291456 | tf_op jit(solution)/shard_map/focus/pallas_call | solution.py:601
  263.3 0.1 fusion.1
  263.4 2.4 collective-permute-start.2
  265.8 1.5 collective-permute-start.6
  267.3 0.5 collective-permute-start.3
  267.8 1.5 collective-permute-start.5
  269.3 9.2 %collective-permute-done.2.ax = bf16[64,4096]{1,0:T(8,128)(2,1)S(1)} collective-permute-done((bf16[64,4096]{1,0:T(8,128)(2,1)S(1)}, bf16[64,4096]{1,0:T(8,128)(2,1)S(1)}, u32[]{:S(2)}, u32[]{:S(2)}) %collective-permute-start.2) | collective-permute-done | bytes 524320 | tf_op jit(solution)/shard_map/ppermute | solution.py:648
  278.4 3.6 %collective-permute-start.4 = (bf16[64,4096]{1,0:T(8,128)(2,1)S(1)}, bf16[64,4096]{1,0:T(8,128)(2,1)S(1)}, u32[]{:S(2)}, u32[]{:S(2)}) collective-permute-start(bf16[64,4096]{1,0:T(8,128)(2,1)S(1)} %collective-permute-done.2.ax), channel_id=1, source_target_pairs={{0,16},{8,24},{16,0},{24,8},{1,17},{9,25},{17,1},{25,9},{2,18},{10... | collective-permute-start | bytes 1572872 | tf_op jit(solution)/shard_map/ppermute | solution.py:649
  282.1 0.0 collective-permute-done.6.by
  282.1 0.0 collective-permute-start.7
  282.1 9.8 %collective-permute-done.3.ay = bf16[64,4096]{1,0:T(8,128)(2,1)S(1)} collective-permute-done((bf16[64,4096]{1,0:T(8,128)(2,1)S(1)}, bf16[64,4096]{1,0:T(8,128)(2,1)S(1)}, u32[]{:S(2)}, u32[]{:S(2)}) %collective-permute-start.3) | collective-permute-done | bytes 524320 | tf_op jit(solution)/shard_map/ppermute | solution.py:649
  291.9 0.0 collective-permute-done.5.bx
  291.9 8.8 %collective-permute-done.4.axy = bf16[64,4096]{1,0:T(8,128)(2,1)S(1)} collective-permute-done((bf16[64,4096]{1,0:T(8,128)(2,1)S(1)}, bf16[64,4096]{1,0:T(8,128)(2,1)S(1)}, u32[]{:S(2)}, u32[]{:S(2)}) %collective-permute-start.4) | collective-permute-done | bytes 524320 | tf_op jit(solution)/shard_map/ppermute | solution.py:649
  300.7 0.0 collective-permute-done.7.byx
  300.7 3.6 %assemble.1 = f32[512,4096]{1,0:T(8,128)} custom-call(s32[1]{0:T(128)} %bitcast.own, bf16[128,4096]{1,0:T(8,128)(2,1)S(1)} %focus.1.mine, bf16[64,4096]{1,0:T(8,128)(2,1)S(1)} %collective-permute-done.2.ax, bf16[64,4096]{1,0:T(8,128)(2,1)S(1)} %collective-permute-done.3.ay, bf16[64,4096]{1,0:T(8,128)(2,1)S(1)} %collective-permute-done.4.axy, ...), custom_call_target="tpu_custom_call" | custom-call | flops 1000000 | bytes 12582912 | tf_op jit(solution)/shard_map/assemble/pallas_call | solution.py:628
  (10 shorter events, 0.1 us)
Async XLA Ops:
  0.0 2.2 copy-start.3
  2.2 2.2 copy-start.4
  4.4 0.7 copy-start.8
  13.1 1.3 copy-start.2
  14.4 55.5 %copy-start.6 = (bf16[512,256]{1,0:T(8,128)(2,1)S(1)}, bf16[512,256]{1,0:T(8,128)(2,1)}, u32[]{:S(2)}) copy-start(bf16[512,256]{1,0:T(8,128)(2,1)} %constant.58.clone.refs_2_) | copy-start | bytes 786436
  14.4 55.5 %copy-start.7 = (bf16[2,256,256]{2,1,0:T(8,128)(2,1)S(1)}, bf16[2,256,256]{2,1,0:T(8,128)(2,1)}, u32[]{:S(2)}) copy-start(bf16[2,256,256]{2,1,0:T(8,128)(2,1)} %constant.61.clone.refs_5_) | copy-start | bytes 786436
  14.4 55.5 %all-to-all-start = ((bf16[8,512,256]{2,1,0:T(8,128)(2,1)}), bf16[8,512,256]{2,1,0:T(8,128)(2,1)S(1)}, u32[]{:S(2)}, u32[]{:S(2)}) async-start(bf16[8,512,256]{2,1,0:T(8,128)(2,1)} %bitcast.19), calls=%async_computation | async-start | bytes 4194304 | tf_op jit(solution)/shard_map/all_to_all | solution.py:665
  107.4 120.6 %all-to-all-start.1 = ((bf16[16,128,2048]{2,1,0:T(8,128)(2,1)}), bf16[16,128,2048]{2,1,0:T(8,128)(2,1)}, u32[]{:S(2)}, u32[]{:S(2)}) async-start(bf16[16,128,2048]{2,1,0:T(8,128)(2,1)} %bitcast.20), calls=%async_computation.1 | async-start | bytes 16777216 | tf_op jit(solution)/shard_map/all_to_all | solution.py:675
  228.0 2.2 copy-start.5
  241.5 2.0 copy-start
  243.5 5.8 %collective-permute-start.1 = (bf16[4,4096]{1,0:T(4,128)(2,1)S(1)}, bf16[4,4096]{1,0:T(4,128)(2,1)S(1)}, u32[]{:S(2)}, u32[]{:S(2)}) collective-permute-start(bf16[4,4096]{1,0:T(4,128)(2,1)S(1)} %bitcast.22), channel_id=1, source_target_pairs={{8,0},{16,8},{24,16},{1,24},{9,1},{17,9},{25,17},{2,25},{10,2},{18... | collective-permute-start | bytes 98312 | tf_op jit(solution)/shard_map/ppermute | solution.py:694
  249.4 4.4 %collective-permute-start = (bf16[4,4096]{1,0:T(4,128)(2,1)S(1)}, bf16[4,4096]{1,0:T(4,128)(2,1)S(1)}, u32[]{:S(2)}, u32[]{:S(2)}) collective-permute-start(bf16[4,4096]{1,0:T(4,128)(2,1)S(1)} %get-tuple-element.10), channel_id=1, source_target_pairs={{0,8},{8,16},{16,24},{24,1},{1,9},{9,17},{17,25},{25,2},{2,10},{10... | collective-permute-start | bytes 98312 | tf_op jit(solution)/shard_map/ppermute | solution.py:693
  253.9 2.2 copy-start.1
  263.4 15.1 %collective-permute-start.2 = (bf16[64,4096]{1,0:T(8,128)(2,1)S(1)}, bf16[64,4096]{1,0:T(8,128)(2,1)S(1)}, u32[]{:S(2)}, u32[]{:S(2)}) collective-permute-start(bf16[64,4096]{1,0:T(8,128)(2,1)S(1)} %get-tuple-element.14), channel_id=1, source_target_pairs={{0,8},{8,0},{16,24},{24,16},{1,9},{9,1},{17,25},{25,17},{2,10},{10... | collective-permute-start | bytes 1572872 | tf_op jit(solution)/shard_map/ppermute | solution.py:648
  265.8 16.3 %collective-permute-start.6 = (bf16[64,4096]{1,0:T(8,128)(2,1)S(1)}, bf16[64,4096]{1,0:T(8,128)(2,1)S(1)}, u32[]{:S(2)}, u32[]{:S(2)}) collective-permute-start(bf16[64,4096]{1,0:T(8,128)(2,1)S(1)} %get-tuple-element.13), channel_id=1, source_target_pairs={{0,16},{8,24},{16,0},{24,8},{1,17},{9,25},{17,1},{25,9},{2,18},{10... | collective-permute-start | bytes 1572872 | tf_op jit(solution)/shard_map/ppermute | solution.py:648
  267.3 24.6 %collective-permute-start.3 = (bf16[64,4096]{1,0:T(8,128)(2,1)S(1)}, bf16[64,4096]{1,0:T(8,128)(2,1)S(1)}, u32[]{:S(2)}, u32[]{:S(2)}) collective-permute-start(bf16[64,4096]{1,0:T(8,128)(2,1)S(1)} %get-tuple-element.14), channel_id=1, source_target_pairs={{0,16},{8,24},{16,0},{24,8},{1,17},{9,25},{17,1},{25,9},{2,18},{10... | collective-permute-start | bytes 1572872 | tf_op jit(solution)/shard_map/ppermute | solution.py:649
  267.8 24.1 %collective-permute-start.5 = (bf16[64,4096]{1,0:T(8,128)(2,1)S(1)}, bf16[64,4096]{1,0:T(8,128)(2,1)S(1)}, u32[]{:S(2)}, u32[]{:S(2)}) collective-permute-start(bf16[64,4096]{1,0:T(8,128)(2,1)S(1)} %get-tuple-element.13), channel_id=1, source_target_pairs={{0,8},{8,0},{16,24},{24,16},{1,9},{9,1},{17,25},{25,17},{2,10},{10... | collective-permute-start | bytes 1572872 | tf_op jit(solution)/shard_map/ppermute | solution.py:650
  278.4 22.2 %collective-permute-start.4 = (bf16[64,4096]{1,0:T(8,128)(2,1)S(1)}, bf16[64,4096]{1,0:T(8,128)(2,1)S(1)}, u32[]{:S(2)}, u32[]{:S(2)}) collective-permute-start(bf16[64,4096]{1,0:T(8,128)(2,1)S(1)} %collective-permute-done.2.ax), channel_id=1, source_target_pairs={{0,16},{8,24},{16,0},{24,8},{1,17},{9,25},{17,1},{25,9},{2,18},{10... | collective-permute-start | bytes 1572872 | tf_op jit(solution)/shard_map/ppermute | solution.py:649
  282.1 18.6 %collective-permute-start.7 = (bf16[64,4096]{1,0:T(8,128)(2,1)S(1)}, bf16[64,4096]{1,0:T(8,128)(2,1)S(1)}, u32[]{:S(2)}, u32[]{:S(2)}) collective-permute-start(bf16[64,4096]{1,0:T(8,128)(2,1)S(1)} %collective-permute-done.6.by), channel_id=1, source_target_pairs={{0,8},{8,0},{16,24},{24,16},{1,9},{9,1},{17,25},{25,17},{2,10},{10... | collective-permute-start | bytes 1572872 | tf_op jit(solution)/shard_map/ppermute | solution.py:650

commit v2 on v1

--- a/solution.py
+++ b/solution.py
@@ -178,6 +178,8 @@
 INN = 256
 CLS = 8
 LANE = 128
+MIB = 2**20
+VMEM = 60 * MIB
 
 
 def slot_frequencies():
@@ -234,6 +236,7 @@
     eye = np.eye(16)
     outer_cos, outer_sin = np.kron(np.cos(turn), eye) / 4.0, np.kron(np.sin(turn), eye) / 4.0
     outer = np.concatenate([outer_cos, -outer_sin])
+    outer = outer.reshape(-1, 8, 2, 16).swapaxes(1, 2).reshape(outer.shape)
     half_rows = outer_cos.shape[0] // 2
     back = np.stack(
         [
@@ -297,11 +300,12 @@
     return jnp.where(natural >= N // 2, natural - N, natural).astype(jnp.float32) * (1.0 / N)
 
 
-def row_forward_kernel(own, weights, holo, back, table, out, nyquist, acc):
+def row_forward_kernel(own, weights, holo, back, table, out, acc, held):
+    step = pl.program_id(0)
     rows = holo.shape[0]
     group = own[0]
     lane = lax.broadcasted_iota(jnp.int32, (16, INN), 1)
-    sign = jnp.where(lane % 2 == 0, 1.0, -1.0)
+    sign = jnp.where(lane % 2 == 0, 1.0, -1.0).astype(jnp.bfloat16)
 
     def strip(i, carry):
         here = pl.ds(pl.multiple_of(i * 16, 16), 16)
@@ -316,24 +320,39 @@
             sums[4] = sums[4] + value
         for q in range(4):
             acc[q // 2, here, pl.ds((q % 2) * INN, INN)] = sums[q].astype(jnp.bfloat16)
-        turned = sums[4] * sign
-        nyquist[here, :] = turned[:, :LANE] + turned[:, LANE:]
+        acc[2, here, pl.ds(0, INN)] = sums[4].astype(jnp.bfloat16)
         return carry
 
     lax.fori_loop(0, rows // 16, strip, 0)
+    here = pl.ds(pl.multiple_of(step * rows, rows), rows)
     for q in range(2):
         result = dot(acc[q], table[q]).astype(jnp.bfloat16)
         for low in range(2):
             part = result[:, low * 2 * LANE : (low + 1) * 2 * LANE]
             for high in range(2):
-                out[high, low, q] = part
+                out[high, low, q, here, :] = part
+    alternating = lax.dot_general(
+        sign, acc[2, :, :INN], (((1,), (1,)), ((), ())), preferred_element_type=jnp.float32
+    )
+    held[step] = alternating * (1.0 / 64.0)
+
+    @pl.when(step == pl.num_programs(0) - 1)
+    def _():
+        rows_of = [jnp.concatenate([held[2 * r], held[2 * r + 1]], axis=1) for r in range(2)]
+        extra = jnp.where(lax.broadcasted_iota(jnp.int32, (16, INN), 0) == 0, rows_of[0], rows_of[1])
+        extra = extra.astype(jnp.bfloat16)
+        for high in range(2):
+            for low in range(2):
+                for q in range(2):
+                    out[high, low, q, pl.ds(4 * rows, 16), :] = extra
 
 
 def row_forward(own, hologram, background):
     rows = hologram.shape[0]
-    block = 128
+    block = LANE
     table = jnp.asarray(row_forward_tables())
     weights = jnp.asarray(row_forward_weights())
+    shape = (2, 2, 2, rows + 16, 2 * LANE)
     return pl.pallas_call(
         row_forward_kernel,
         grid_spec=pltpu.PrefetchScalarGridSpec(
@@ -344,110 +363,209 @@
                 pl.BlockSpec((block, N), lambda i, o, w: (i, 0)),
                 pl.BlockSpec((2, 2 * INN, 2 * INN), lambda i, o, w: (o[0], 0, 0)),
             ],
-            out_specs=[
-                pl.BlockSpec((2, 2, 2, block, 2 * LANE), lambda i, o, w: (0, 0, 0, i, 0)),
-                pl.BlockSpec((block, LANE), lambda i, o, w: (i, 0)),
+            out_specs=pl.BlockSpec(shape, lambda i, o, w: (0, 0, 0, 0, 0)),
+            scratch_shapes=[
+                pltpu.VMEM((3, block, 2 * INN), jnp.bfloat16),
+                pltpu.VMEM((rows // block, 16, LANE), jnp.float32),
             ],
-            scratch_shapes=[pltpu.VMEM((2, block, 2 * INN), jnp.bfloat16)],
         ),
-        out_shape=[
-            jax.ShapeDtypeStruct((2, 2, 2, rows, 2 * LANE), jnp.bfloat16),
-            jax.ShapeDtypeStruct((rows, LANE), jnp.float32),
-        ],
-        compiler_params=pltpu.CompilerParams(vmem_limit_bytes=40 * 1024 * 1024),
-        cost_estimate=pl.CostEstimate(flops=10**10, bytes_accessed=12 * 2**20, transcendentals=0),
+        out_shape=jax.ShapeDtypeStruct(shape, jnp.bfloat16),
+        compiler_params=pltpu.CompilerParams(vmem_limit_bytes=VMEM),
+        cost_estimate=pl.CostEstimate(flops=10**10, bytes_accessed=12 * MIB, transcendentals=0),
         name="row_forward",
     )(own, weights, hologram, background, table)
 
 
-def column_kernel(planes, data, fx2, outer, inner, inner_back, back, out, first, mixed, second):
+def propagator_kernel(planes, fx2, out):
     step = pl.program_id(0)
+    strip = 32
+    for i in range(INN // strip):
+        rows = slice(i * strip, (i + 1) * strip)
+        position = lax.broadcasted_iota(jnp.int32, (strip, LANE), 0) + i * strip
+        fy = signed_fraction(step + OUT * position)
+        (kr, ki), (sr, si) = start_and_step(fy * fy + fx2[...])
+        for g in range(planes):
+            out[g, 0, rows, :LANE] = kr
+            out[g, 0, rows, LANE:] = ki
+            if g + 1 < planes:
+                kr, ki = kr * sr - ki * si, kr * si + ki * sr
+
+
+def propagators(planes, fx2):
+    return pl.pallas_call(
+        functools.partial(propagator_kernel, planes),
+        grid=(OUT,),
+        in_specs=[pl.BlockSpec((1, LANE), lambda i: (0, 0))],
+        out_specs=pl.BlockSpec((planes, 1, INN, 2 * LANE), lambda i: (0, i, 0, 0)),
+        out_shape=jax.ShapeDtypeStruct((planes, OUT, INN, 2 * LANE), jnp.float32),
+        compiler_params=pltpu.CompilerParams(vmem_limit_bytes=VMEM),
+        cost_estimate=pl.CostEstimate(flops=10**9, bytes_accessed=16 * MIB, transcendentals=10**6),
+        name="propagators",
+    )(fx2)
+
+
+PER = 4
+
+
+def mix_and_open(k, slot, yr, yi, kernels, inner_back, mixed, second):
     width = LANE
-
-    @pl.when(step == 0)
-    def _():
-        def chunk(i, carry):
-            here = pl.ds(pl.multiple_of(i * 16, 16), 16)
-            block = data[:, here, :].reshape(OUT * 16, 2 * width)
-            re, im = split_complex(dot(outer[...], block), width)
-            value = jnp.concatenate([re, im], axis=1).astype(jnp.bfloat16)
-            first[:, here, :] = value.reshape(OUT, 16, 2 * width)
-            return carry
-
-        lax.fori_loop(0, INN // 16, chunk, 0)
-
-    @pl.when(step < OUT)
-    def _():
-        both = dot(inner[0], first[step])
-        strip = 32
-        for i in range(INN // strip):
-            rows = slice(i * strip, (i + 1) * strip)
-            low_rows = slice(INN + i * strip, INN + (i + 1) * strip)
-            yr = both[rows, :width] - both[low_rows, width:]
-            yi = both[rows, width:] + both[low_rows, :width]
-            position = lax.broadcasted_iota(jnp.int32, (strip, width), 0) + i * strip
-            fy = signed_fraction(step + OUT * position)
-            (kr, ki), (sr, si) = start_and_step(fy * fy + fx2[...])
-            for g in range(planes):
-                for part, factor in enumerate((kr, ki)):
-                    at = (g * 2 + part) * 2 * width
-                    mixed[rows, at : at + width] = (yr * factor).astype(jnp.bfloat16)
-                    mixed[rows, at + width : at + 2 * width] = (yi * factor).astype(jnp.bfloat16)
-                if g + 1 < planes:
-                    kr, ki = kr * sr - ki * si, kr * si + ki * sr
-        for g in range(2 * planes):
-            lanes = slice(g * 2 * width, (g + 1) * 2 * width)
-            re, im = split_complex(dot(inner_back[0], mixed[:, lanes]), width)
-            second[step, :, lanes] = jnp.concatenate([re, im], axis=1).astype(jnp.bfloat16)
-
-    @pl.when(step >= OUT)
-    def _():
-        here = pl.ds(pl.multiple_of((step - OUT) * 16, 16), 16)
-        for g in range(2 * planes):
-            lanes = slice(g * 2 * width, (g + 1) * 2 * width)
-            block = second[:, here, lanes].reshape(OUT * 16, 2 * width)
-            re, im = split_complex(dot(back[0], block), width)
+    for part in range(2):
+        factor = kernels[:, part * width : (part + 1) * width]
+        at = part * 2 * width
+        mixed[slot, :, at : at + width] = (yr * factor).astype(jnp.bfloat16)
+        mixed[slot, :, at + width : at + 2 * width] = (yi * factor).astype(jnp.bfloat16)
+    both = dot(inner_back, mixed[slot])
+    for part in range(2):
+        lanes = slice(part * 2 * width, (part + 1) * 2 * width)
+        re, im = split_complex(both[:, lanes], width)
+        second[k, :, lanes] = jnp.concatenate([re, im], axis=1).astype(jnp.bfloat16)
+
+
+def close_columns(start, back, second, out):
+    width = LANE
+    for c in range(PER):
+        here = pl.ds(pl.multiple_of((start + c) * 16, 16), 16)
+        both = dot(back[0], second[:, here, :].reshape(OUT * 16, 4 * width))
+        rows = slice(c * 16, (c + 1) * 16)
+        for part in range(2):
+            lanes = slice(part * 2 * width, (part + 1) * 2 * width)
+            re, im = split_complex(both[:, lanes], width)
             value = jnp.concatenate([re, im], axis=1).astype(jnp.bfloat16)
             value = value.reshape(2, 2, 2, 16, 2 * width)
             for low in range(2):
                 for core in range(2):
                     for high in range(2):
-                        out[high, 0, low, core, :, lanes] = value[low, core, high]
-
-
-def columns(half, planes, data, fx2):
+                        out[high, 0, low, core, rows, lanes] = value[low, core, high]
+
+
+def first_columns_kernel(
+    half, data, kernels, outer, inner, inner_back, back, out, spectrum, first, mixed, second
+):
+    step = pl.program_id(0)
+    width = LANE
+
+    @pl.when(step == 0)
+    def _():
+        for i in range(INN // 16):
+            here = slice(i * 16, (i + 1) * 16)
+            there = slice(INN + i * 16, INN + (i + 1) * 16)
+            block = jnp.concatenate([data[:, here, :], data[:, there, :]], axis=0)
+            re, im = split_complex(dot(outer[...], block.reshape(OUT * 16, 2 * width)), width)
+            value = jnp.concatenate([re, im], axis=1).astype(jnp.bfloat16)
+            first[:, here, :] = value.reshape(OUT, 16, 2 * width)
+
+    @pl.when(step < OUT // PER)
+    def _():
+        for c in range(PER):
+            k = step * PER + c
+            yr, yi = split_complex(dot(inner[c], first[k]), width)
+            spectrum[c] = jnp.concatenate([yr, yi], axis=1).astype(jnp.bfloat16)
+            mix_and_open(k, c, yr, yi, kernels[0, c], inner_back[c], mixed, second)
+
+    @pl.when(step >= OUT // PER)
+    def _():
+        close_columns((step - OUT // PER) * PER, back, second, out)
+
+
+def next_columns_kernel(half, spectrum, kernels, inner_back, back, out, mixed, second):
+    step = pl.program_id(1)
+    width = LANE
+
+    @pl.when(step < OUT // PER)
+    def _():
+        for c in range(PER):
+            values = spectrum[c].astype(jnp.float32)
+            yr, yi = values[:, :width], values[:, width:]
+            mix_and_open(step * PER + c, c, yr, yi, kernels[0, c], inner_back[c], mixed, second)
+
+    @pl.when(step >= OUT // PER)
+    def _():
+        close_columns((step - OUT // PER) * PER, back, second, out)
+
+
+STEPS = OUT // PER
+
+
+def opening_step(s):
+    return jnp.minimum(s, STEPS - 1)
+
+
+def closing_step(s):
+    return jnp.maximum(s - STEPS, 0)
+
+
+def first_columns(half, data, kernels):
     outer, inner, inner_back, back = (jnp.asarray(t) for t in column_tables())
-    lanes = planes * 4 * LANE
-    mib = 2**20
-    inner_at = lambda i, o: (jnp.minimum(i, OUT - 1), 0, 0)
-    chunk = lambda i: jnp.maximum(i - OUT, 0)
+    rows = data.shape[1] - 16
+    opening = lambda i, o: (opening_step(i), 0, 0)
     return pl.pallas_call(
-        lambda o, *refs: column_kernel(planes, *refs),
+        first_columns_kernel,
         grid_spec=pltpu.PrefetchScalarGridSpec(
             num_scalar_prefetch=1,
-            grid=(2 * OUT,),
+            grid=(2 * STEPS,),
             in_specs=[
-                pl.BlockSpec((OUT, INN, 2 * LANE), lambda i, o: (0, 0, 0)),
-                pl.BlockSpec((1, LANE), lambda i, o: (0, 0)),
+                pl.BlockSpec((8, rows, 2 * LANE), lambda i, o: (0, 0, 0)),
+                pl.BlockSpec((1, PER, INN, 2 * LANE), lambda i, o: (0, opening_step(i), 0, 0)),
                 pl.BlockSpec((2 * INN, INN), lambda i, o: (0, 0)),
-                pl.BlockSpec((1, 2 * INN, INN), inner_at),
-                pl.BlockSpec((1, 2 * INN, INN), inner_at),
+                pl.BlockSpec((PER, 2 * INN, INN), opening),
+                pl.BlockSpec((PER, 2 * INN, INN), opening),
                 pl.BlockSpec((1, INN, INN), lambda i, o: (o[0], 0, 0)),
             ],
+            out_specs=[
+                pl.BlockSpec(
+                    (2, 1, 2, 2, PER * 16, 4 * LANE),
+                    lambda i, o: (0, closing_step(i) // 2, 0, 0, closing_step(i) % 2, 0),
+                ),
+                pl.BlockSpec((PER, INN, 2 * LANE), opening),
+            ],
+            scratch_shapes=[
+                pltpu.VMEM((OUT, INN, 2 * LANE), jnp.bfloat16),
+                pltpu.VMEM((PER, INN, 4 * LANE), jnp.bfloat16),
+                pltpu.VMEM((OUT, INN, 4 * LANE), jnp.bfloat16),
+            ],
+        ),
+        out_shape=[
+            jax.ShapeDtypeStruct((2, 2, 2, 2, LANE, 4 * LANE), jnp.bfloat16),
+            jax.ShapeDtypeStruct((OUT, INN, 2 * LANE), jnp.bfloat16),
+        ],
+        compiler_params=pltpu.CompilerParams(vmem_limit_bytes=VMEM),
+        cost_estimate=pl.CostEstimate(flops=10**10, bytes_accessed=20 * MIB, transcendentals=0),
+        name="first_columns",
+    )(half, data, kernels, outer, inner, inner_back, back)
+
+
+def next_columns(half, plane, count, spectrum, kernels):
+    _, _, inner_back, back = (jnp.asarray(t) for t in column_tables())
+    opening = lambda g, i, o: (opening_step(i), 0, 0)
+    return pl.pallas_call(
+        next_columns_kernel,
+        grid_spec=pltpu.PrefetchScalarGridSpec(
+            num_scalar_prefetch=1,
+            grid=(count, 2 * STEPS),
+            in_specs=[
+                pl.BlockSpec((PER, INN, 2 * LANE), opening),
+                pl.BlockSpec(
+                    (1, PER, INN, 2 * LANE), lambda g, i, o: (plane + g, opening_step(i), 0, 0)
+                ),
+                pl.BlockSpec((PER, 2 * INN, INN), opening),
+                pl.BlockSpec((1, INN, INN), lambda g, i, o: (o[0], 0, 0)),
+            ],
             out_specs=pl.BlockSpec(
-                (2, 1, 2, 2, 16, lanes), lambda i, o: (0, chunk(i) // 8, 0, 0, chunk(i) % 8, 0)
+                (2, 1, 2, 2, PER * 16, 4 * LANE),
+                lambda g, i, o: (0, closing_step(i) // 2, 0, 0, closing_step(i) % 2, g),
             ),
             scratch_shapes=[
-                pltpu.VMEM((OUT, INN, 2 * LANE), jnp.bfloat16),
-                pltpu.VMEM((INN, lanes), jnp.bfloat16),
-                pltpu.VMEM((OUT, INN, lanes), jnp.bfloat16),
+                pltpu.VMEM((PER, INN, 4 * LANE), jnp.bfloat16),
+                pltpu.VMEM((OUT, INN, 4 * LANE), jnp.bfloat16),
             ],
         ),
-        out_shape=jax.ShapeDtypeStruct((2, 2, 2, 2, LANE, lanes), jnp.bfloat16),
-        compiler_params=pltpu.CompilerParams(vmem_limit_bytes=48 * mib),
-        cost_estimate=pl.CostEstimate(flops=2 * 10**10, bytes_accessed=20 * mib, transcendentals=0),
-        name="columns",
-    )(half, data, fx2, outer, inner, inner_back, back)
+        out_shape=jax.ShapeDtypeStruct((2, 2, 2, 2, LANE, count * 4 * LANE), jnp.bfloat16),
+        compiler_params=pltpu.CompilerParams(vmem_limit_bytes=VMEM),
+        cost_estimate=pl.CostEstimate(
+            flops=count * 7 * 10**9, bytes_accessed=count * 16 * MIB, transcendentals=0
+        ),
+        name="next_columns",
+    )(half, spectrum, kernels, inner_back, back)
 
 
 def sixteen_points(re, im):
@@ -472,69 +590,82 @@
     return result + [cosines[16 - a] + sines[16 - a] for a in range(9, 16)]
 
 
-def row_inverse_kernel(parts, nyquist, table, out, opened):
-    plane = pl.program_id(0)
-    rows = out.shape[1]
+def row_inverse_kernel(plane, parts, nyquist, table, out, edges, opened):
+    current = plane + pl.program_id(0)
+    rows = parts.shape[3]
     lane = lax.broadcasted_iota(jnp.int32, (rows, LANE), 1)
     for part in range(2):
         at = part * 2 * LANE
-        column = jnp.sum(jnp.where(lane == plane * 2 + part, nyquist[...], 0.0), axis=1, keepdims=True)
+        mine = jnp.where(lane == current * 2 + part, nyquist[...], 0.0)
+        column = jnp.sum(mine, axis=1, keepdims=True).astype(jnp.bfloat16)
         for group in range(CLS):
-            pieces = [parts[group // 2, low, group % 2, :, pl.ds(at, 2 * LANE)] for low in range(2)]
-            block = jnp.concatenate(pieces, axis=1)
+            low, high = (parts[group // 2, i, group % 2, :, at : at + 2 * LANE] for i in range(2))
             if group == 0:
-                first = jnp.where(lane == 0, column.astype(jnp.bfloat16), block[:, LANE : 2 * LANE])
-                block = jnp.concatenate([block[:, :LANE], first, block[:, 2 * LANE :]], axis=1)
-            opened[part, group] = dot(block, table[group])
+                first = jnp.where(lane == 0, column, low[:, LANE:])
+                low = jnp.concatenate([low[:, :LANE], first], axis=1)
+            opened[part, group] = dot(jnp.concatenate([low, high], axis=1), table[group])
 
     def strip(i, carry):
         here = pl.ds(pl.multiple_of(i * 16, 16), 16)
         for tile in range(INN // LANE):
             total = None
             for part in range(2):
-                re = [opened[part, g, here, pl.ds(tile * LANE, LANE)] for g in range(CLS)]
-                im = [opened[part, g, here, pl.ds(INN + tile * LANE, LANE)] for g in range(CLS)]
+                re = [opened[part, g, here, tile * LANE : (tile + 1) * LANE] for g in range(CLS)]
+                im = [
+                    opened[part, g, here, INN + tile * LANE : INN + (tile + 1) * LANE]
+                    for g in range(CLS)
+                ]
                 values = sixteen_points(re, im)
                 if total is None:
                     total = [v * v for v in values]
                 else:
                     total = [t + v * v for t, v in zip(total, values)]
             for a in range(OUT):
-                out[0, here, pl.ds(a * INN + tile * LANE, LANE)] = total[a].astype(jnp.bfloat16)
+                lanes = slice(a * INN + tile * LANE, a * INN + (tile + 1) * LANE)
+                out[0, here, lanes] = total[a].astype(jnp.bfloat16)
         return carry
 
     lax.fori_loop(0, rows // 16, strip, 0)
-
-
-def row_inverse(planes, parts, nyquist):
+    edges[0, 0:8, :] = out[0, 0:16, :].astype(jnp.float32)[0:8]
+    edges[0, 8:16, :] = out[0, rows - 16 :, :].astype(jnp.float32)[8:16]
+
+
+def row_inverse(plane, count, parts, nyquist):
     rows = parts.shape[3]
     table = jnp.asarray(row_inverse_tables())
-    mib = 2**20
     return pl.pallas_call(
-        row_inverse_kernel,
-        grid=(planes,),
+        functools.partial(row_inverse_kernel, plane),
+        grid=(count,),
         in_specs=[
             pl.BlockSpec((4, 2, 2, rows, 4 * LANE), lambda g: (0, 0, 0, 0, g)),
             pl.BlockSpec((rows, LANE), lambda g: (0, 0)),
             pl.BlockSpec((CLS, 2 * INN, 2 * INN), lambda g: (0, 0, 0)),
         ],
-        out_specs=pl.BlockSpec((1, rows, N), lambda g: (g, 0, 0)),
-        out_shape=jax.ShapeDtypeStruct((planes, rows, N), jnp.bfloat16),
+        out_specs=[
+            pl.BlockSpec((1, rows, N), lambda g: (g, 0, 0)),
+            pl.BlockSpec((1, 16, N), lambda g: (g, 0, 0)),
+        ],
+        out_shape=[
+            jax.ShapeDtypeStruct((count, rows, N), jnp.bfloat16),
+            jax.ShapeDtypeStruct((count, 16, N), jnp.float32),
+        ],
         scratch_shapes=[pltpu.VMEM((2, CLS, rows, 2 * INN), jnp.float32)],
-        compiler_params=pltpu.CompilerParams(vmem_limit_bytes=40 * mib),
-        cost_estimate=pl.CostEstimate(flops=10**10, bytes_accessed=20 * mib, transcendentals=0),
+        compiler_params=pltpu.CompilerParams(vmem_limit_bytes=VMEM),
+        cost_estimate=pl.CostEstimate(
+            flops=count * 3 * 10**9, bytes_accessed=count * 8 * MIB, transcendentals=0
+        ),
         name="row_inverse",
     )(parts, nyquist, table)
 
 
-def nyquist_kernel(planes, data, out):
-    size = RADIX
-    row = lax.broadcasted_iota(jnp.int32, (size, size), 0)
-    col = lax.broadcasted_iota(jnp.int32, (size, size), 1)
-    turn = (row * col % size).astype(jnp.float32) * (2.0 * math.pi / size)
-    wr, wi = jnp.cos(turn) * (1.0 / 8.0), jnp.sin(turn) * (1.0 / 8.0)
-    twist = (row * col).astype(jnp.float32) * (2.0 * math.pi / (size * size))
-    vr, vi = jnp.cos(twist), jnp.sin(twist)
+def nyquist_kernel(planes, own, data, out):
+    wide = lambda axis: lax.broadcasted_iota(jnp.int32, (INN, INN), axis)
+    tall = lambda axis: lax.broadcasted_iota(jnp.int32, (OUT, INN), axis)
+    small = lambda axis: lax.broadcasted_iota(jnp.int32, (OUT, OUT), axis)
+
+    def wave(products, period):
+        turn = (products % period).astype(jnp.float32) * (2.0 * math.pi / period)
+        return jnp.cos(turn), jnp.sin(turn)
 
     def exact(left, right):
         return jnp.dot(left, right, preferred_element_type=jnp.float32, precision=lax.Precision.HIGHEST)
@@ -545,37 +676,49 @@
     def rotated(xr, xi, yr, yi):
         return xr * yr - xi * yi, xr * yi + xi * yr
 
-    ar, ai = rotated(exact(wr, data[...]), exact(-wi, data[...]), vr, -vi)
-    yr, yi = product(ar, ai, wr, -wi)
-    fy = signed_fraction(row + size * col)
+    column = jnp.concatenate([data[i, 0:2, :].astype(jnp.float32) for i in range(8)], axis=0)
+    wr, wi = wave(small(0) * small(1), OUT)
+    inner_r, inner_i = wave(wide(0) * wide(1), INN)
+    vr, vi = wave(tall(0) * tall(1), N)
+    ar, ai = rotated(exact(wr, column), exact(-wi, column), vr, -vi)
+    yr, yi = product(ar, ai, inner_r, -inner_i)
+    fy = signed_fraction(tall(0) + OUT * tall(1))
     (kr, ki), (sr, si) = start_and_step(fy * fy + 0.25)
+    block = own[0]
+    k = lax.broadcasted_iota(jnp.int32, (8, OUT), 1)
+    hr, hi = wave(k * (block // 2), OUT)
+    result = []
     for g in range(planes):
         pr, pi = rotated(yr, yi, kr, ki)
-        br, bi = rotated(*product(pr, pi, wr, wi), vr, vi)
-        ur, ui = product(wr, wi, br, bi)
-        out[2 * g] = ur
-        out[2 * g + 1] = ui
+        br, bi = rotated(*product(pr, pi, inner_r, inner_i), vr, vi)
+        for value in product(hr, hi, br, bi):
+            half = jnp.where(block % 2 == 0, value[:, :LANE], value[:, LANE:])
+            result.append(half[0:1] * (1.0 / N))
         kr, ki = rotated(kr, ki, sr, si)
-
-
-def nyquist_column(planes, data):
+    result.append(jnp.zeros((LANE - 2 * planes, LANE), jnp.float32))
+    out[...] = jnp.concatenate(result, axis=0).T
+
+
+def nyquist_column(own, planes, data):
+    rows = data.shape[1] - 16
     return pl.pallas_call(
         functools.partial(nyquist_kernel, planes),
-        out_shape=jax.ShapeDtypeStruct((2 * planes, RADIX, RADIX), jnp.float32),
-        cost_estimate=pl.CostEstimate(flops=10**7, bytes_accessed=2**18, transcendentals=0),
+        grid_spec=pltpu.PrefetchScalarGridSpec(
+            num_scalar_prefetch=1,
+            grid=(1,),
+            in_specs=[pl.BlockSpec((8, 16, 2 * LANE), lambda i, o: (0, rows // 16, 0))],
+            out_specs=pl.BlockSpec((LANE, LANE), lambda i, o: (0, 0)),
+        ),
+        out_shape=jax.ShapeDtypeStruct((LANE, LANE), jnp.float32),
+        cost_estimate=pl.CostEstimate(flops=10**9, bytes_accessed=2**18, transcendentals=0),
         name="nyquist",
-    )(data)
-
-
-def focus_kernel(intensity, north, south, out, held):
-    planes, rows = intensity.shape[0], intensity.shape[1]
-    for g in range(planes):
-        held[g, 8 : 8 + rows, :] = intensity[g].astype(jnp.float32)
-        held[g, 0:8, :] = jnp.broadcast_to(north[g : g + 1].astype(jnp.float32), (8, N))
-        held[g, 8 + rows : 16 + rows, :] = jnp.broadcast_to(south[g : g + 1].astype(jnp.float32), (8, N))
+    )(own, data)
+
+
+def focus_of(held, planes, count, out):
     tile = 512
     lane = lax.broadcasted_iota(jnp.int32, (16, tile), 1)
-    for i in range(rows // 16):
+    for i in range(count // 16):
         r = 8 + i * 16
         for t in range(N // tile):
             lanes = slice(t * tile, (t + 1) * tile)
@@ -595,49 +738,97 @@
             out[i * 16 : (i + 1) * 16, lanes] = (best * 0.125).astype(jnp.bfloat16)
 
 
-def focus_measure(intensity, north, south):
-    planes, rows, _ = intensity.shape
-    mib = 2**20
+def inner_focus_kernel(sizes, begin, count, *refs):
+    blocks, out, held = refs[: len(sizes)], refs[-2], refs[-1]
+    plane = 0
+    for block, size in zip(blocks, sizes):
+        for g in range(size):
+            held[plane, 0 : count + 16, :] = block[g, begin - 16 : begin + count + 16, :].astype(
+                jnp.float32
+            )[8 : count + 24]
+            plane += 1
+    focus_of(held, plane, count, out)
+
+
+def inner_focus(intensities, begin, count):
+    sizes = [block.shape[0] for block in intensities]
     return pl.pallas_call(
-        focus_kernel,
-        out_shape=jax.ShapeDtypeStruct((rows, N), jnp.bfloat16),
-        scratch_shapes=[pltpu.VMEM((planes, rows + 16, N), jnp.float32)],
-        compiler_params=pltpu.CompilerParams(vmem_limit_bytes=40 * mib),
-        cost_estimate=pl.CostEstimate(flops=10**8, bytes_accessed=6 * mib, transcendentals=0),
-        name="focus",
-    )(intensity, north, south)
-
-
-def assemble_kernel(own, mine, ax, ay, axy, bx, by, byx, out):
-    slot = pl.program_id(0)
-    half = ax.shape[0]
-    for s, (a, b) in enumerate(((None, None), (ax, bx), (ay, by), (axy, byx))):
+        functools.partial(inner_focus_kernel, sizes, begin, count),
+        out_shape=jax.ShapeDtypeStruct((count, N), jnp.bfloat16),
+        scratch_shapes=[pltpu.VMEM((sum(sizes), count + 16, N), jnp.float32)],
+        compiler_params=pltpu.CompilerParams(vmem_limit_bytes=VMEM),
+        cost_estimate=pl.CostEstimate(flops=10**8, bytes_accessed=6 * MIB, transcendentals=0),
+        name="inner_focus",
+    )(*intensities)
+
+
+def outer_focus_kernel(sizes, count, *refs):
+    blocks, north, south, out, held = refs[: len(sizes)], refs[-4], refs[-3], refs[-2], refs[-1]
+    planes = sum(sizes)
+    for side in range(2):
+        plane = 0
+        for block, size in zip(blocks, sizes):
+            rows = block.shape[1]
+            for g in range(size):
+                if side == 0:
+                    held[plane, 8 : 24 + count, :] = block[g, : count + 16, :].astype(jnp.float32)
+                    held[plane, 0:8, :] = jnp.broadcast_to(north[plane : plane + 1, :], (8, N))
+                else:
+                    value = block[g, rows - count - 16 :, :].astype(jnp.float32)
+                    held[plane, 0 : count + 8, :] = value[8:]
+                    held[plane, count + 8 : count + 16, :] = jnp.broadcast_to(
+                        south[plane : plane + 1, :], (8, N)
+                    )
+                plane += 1
+        focus_of(held, planes, count, out.at[side * count : (side + 1) * count])
+
+
+def outer_focus(intensities, north, south, count):
+    sizes = [block.shape[0] for block in intensities]
+    return pl.pallas_call(
+        functools.partial(outer_focus_kernel, sizes, count),
+        out_shape=jax.ShapeDtypeStruct((2 * count, N), jnp.bfloat16),
+        scratch_shapes=[pltpu.VMEM((sum(sizes), count + 24, N), jnp.float32)],
+        compiler_params=pltpu.CompilerParams(vmem_limit_bytes=VMEM),
+        cost_estimate=pl.CostEstimate(flops=10**8, bytes_accessed=6 * MIB, transcendentals=0),
+        name="outer_focus",
+    )(*intensities, north, south)
+
+
+def assemble_kernel(own, *refs):
+    slot, out = pl.program_id(0), refs[-1]
+    inner, outer = refs[:7], refs[7:14]
+    part = inner[1].shape[0]
+    for s in range(4):
 
         @pl.when(slot == s)
         def _():
-            if a is None:
-                out[...] = mine[...].astype(jnp.float32)
-            else:
-                out[:half] = a[...].astype(jnp.float32)
-                out[half:] = b[...].astype(jnp.float32)
-
-
-def assemble(depth_index, mine, halves):
-    rows = mine.shape[0]
+            for both, places in ((inner, (part, 2 * part)), (outer, (0, 3 * part))):
+                if s == 0:
+                    a, b = both[0][:part], both[0][part:]
+                else:
+                    a, b = both[s][...], both[3 + s][...]
+                out[places[0] : places[0] + part] = a.astype(jnp.float32)
+                out[places[1] : places[1] + part] = b.astype(jnp.float32)
+
+
+def assemble(depth_index, inner, outer):
+    part = inner[1].shape[0]
     whole = lambda shape: pl.BlockSpec(shape, lambda s, o: (0, 0))
+    specs = [whole((2 * part, N))] + [whole((part, N))] * 6
     return pl.pallas_call(
         assemble_kernel,
         grid_spec=pltpu.PrefetchScalarGridSpec(
             num_scalar_prefetch=1,
             grid=(4,),
-            in_specs=[whole((rows, N))] + [whole((rows // 2, N))] * 6,
-            out_specs=pl.BlockSpec((rows, N), lambda s, o: (jnp.bitwise_xor(s, o[0]), 0)),
+            in_specs=specs * 2,
+            out_specs=pl.BlockSpec((4 * part, N), lambda s, o: (jnp.bitwise_xor(s, o[0]), 0)),
         ),
-        out_shape=jax.ShapeDtypeStruct((4 * rows, N), jnp.float32),
-        compiler_params=pltpu.CompilerParams(vmem_limit_bytes=40 * 2**20),
-        cost_estimate=pl.CostEstimate(flops=10**6, bytes_accessed=12 * 2**20, transcendentals=0),
+        out_shape=jax.ShapeDtypeStruct((16 * part, N), jnp.float32),
+        compiler_params=pltpu.CompilerParams(vmem_limit_bytes=VMEM),
+        cost_estimate=pl.CostEstimate(flops=10**6, bytes_accessed=12 * MIB, transcendentals=0),
         name="assemble",
-    )(depth_index, mine, *halves)
+    )(depth_index, *inner, *outer)
 
 
 def exchange_depth(mine):
@@ -648,7 +839,7 @@
     ax, by = lax.ppermute(a, "depth", over_x), lax.ppermute(b, "depth", over_y)
     ay, axy = lax.ppermute(a, "depth", over_y), lax.ppermute(ax, "depth", over_y)
     bx, byx = lax.ppermute(b, "depth", over_x), lax.ppermute(by, "depth", over_x)
-    return ax, ay, axy, bx, by, byx
+    return mine, ax, ay, axy, bx, by, byx
 
 
 def half_spectrum_shards(hologram, background):
@@ -658,28 +849,48 @@
     low, core = lax.axis_index("low"), lax.axis_index("core")
     as_scalar = lambda value: jnp.reshape(value, (1,)).astype(jnp.int32)
     everyone = ("depth", "high", "low", "core")
-    slab = ("high", "low", "core")
-
-    sections, alternating = row_forward(as_scalar(depth), hologram, background)
-    column_sum = lax.all_gather(jnp.sum(alternating, axis=1) * (1.0 / 64.0), slab, tiled=True)
+    own = rows // 4
+    block = ((high * 2 + low) * 2 + core) * 4 + depth
+
+    sections = row_forward(as_scalar(depth), hologram, background)
     data = lax.all_to_all(
-        sections.reshape(8, rows, 2 * LANE), slab, split_axis=0, concat_axis=0, tiled=True
+        sections.reshape(8, rows + 16, 2 * LANE),
+        ("high", "low", "core"),
+        split_axis=0,
+        concat_axis=0,
+        tiled=True,
     )
 
     group = depth * 2 + core
     slot = low * LANE + jnp.arange(LANE, dtype=jnp.int32)
     special = jnp.where(low == 0, 0, CLS) + OUT * jnp.arange(LANE, dtype=jnp.int32)
     fx = signed_fraction(jnp.where(group == 0, special, group + OUT * slot))
-    halfway = columns(as_scalar(high), planes, data.reshape(OUT, INN, 2 * LANE), (fx * fx)[None])
-    own = rows // 4
-    parts = lax.all_to_all(
-        halfway.reshape(16, own, -1), ("depth", "low", "core"), split_axis=0, concat_axis=0, tiled=True
-    )
-    first_row = ((high * 2 + low) * 2 + core) * rows + depth * own
-    middle = nyquist_column(planes, column_sum.reshape(RADIX, RADIX)).reshape(2 * planes, N)
-    middle = lax.dynamic_slice_in_dim(middle, first_row, own, axis=1).T
-    middle = jnp.pad(middle, ((0, 0), (0, LANE - 2 * planes)))
-    intensity = row_inverse(planes, parts.reshape(4, 2, 2, own, -1), middle)
+    kernels = propagators(planes, (fx * fx)[None])
+
+    def to_rows(halfway):
+        parts = lax.all_to_all(
+            halfway.reshape(16, own, -1),
+            ("depth", "low", "core"),
+            split_axis=0,
+            concat_axis=0,
+            tiled=True,
+        )
+        return parts.reshape(4, 2, 2, own, -1)
+
+    halfway, spectrum = first_columns(as_scalar(high), data, kernels)
+    parts = [to_rows(halfway)]
+    cuts = [(1, 2), (3, planes - 3)]
+    for plane, count in cuts:
+        halfway = next_columns(as_scalar(high), plane, count, spectrum, kernels)
+        if plane > 1:
+            halfway, parts[-1] = lax.optimization_barrier((halfway, parts[-1]))
+        parts.append(to_rows(halfway))
+    middle = nyquist_column(as_scalar(block), planes, data)
+    intensities, edges = [], []
+    for (plane, count), part in zip([(0, 1)] + cuts, parts):
+        intensity, edge = row_inverse(plane, count, part, middle)
+        intensities.append(intensity)
+        edges.append(edge)
 
     order = [
         ((d * 2 + h) * 2 + l) * 2 + c
@@ -690,12 +901,15 @@
     ]
     down = list(zip(order[:-1], order[1:]))
     up = [(target, source) for source, target in down]
-    north = lax.ppermute(intensity[:, -1], everyone, down)
-    south = lax.ppermute(intensity[:, 0], everyone, up)
-    north = jnp.where(first_row == 0, intensity[:, 0], north)
-    south = jnp.where(first_row == N - own, intensity[:, -1], south)
-    mine = focus_measure(intensity, north, south)
-    return assemble(as_scalar(depth), mine, exchange_depth(mine))
+    first = jnp.concatenate([edge[:, 0] for edge in edges])
+    last = jnp.concatenate([edge[:, 15] for edge in edges])
+    north = lax.ppermute(last, everyone, down)
+    south = lax.ppermute(first, everyone, up)
+    inner = exchange_depth(inner_focus(intensities, own // 4, own // 2))
+    north = jnp.where(block == 0, first, north)
+    south = jnp.where(block == N // own - 1, last, south)
+    outer = exchange_depth(outer_focus(intensities, north, south, own // 4))
+    return assemble(as_scalar(depth), inner, outer)
 
 
 def solution(mesh):

time: 305 us -> 291 us (0.954)
  blocking collectives: 110 us -> 54.4 us
  Pallas kernels: 71.1 us -> 111 us
  starting transfers between devices: 25 us -> 34.2 us
  local copies, waits for them, and re-layouts: 15.2 us -> 10.1 us
  waiting for transfers between devices: 82.7 us -> 78.2 us
    all_gather x1 -> x0, blocking collectives: 110 us -> none  [half_spectrum_shards(): lax.all_gather(jnp.sum(alternating, axis=1) * (1.0 / 64.0), slab, tiled=T...]
    all_to_all x0 -> x1, blocking collectives: none -> 54.4 us  [to_rows(): lax.all_to_all(halfway.reshape(16, own, -1), ('depth', 'low', 'core'), sp...]
    pallas_call x4 -> x10, Pallas kernels: 59.5 us -> 95.3 us  [the longest x2 27.4 us: next_columns(): pl.pallas_call(next_columns_kernel, grid_spec=pltpu.PrefetchScalarGridSpe...]
    all_to_all x2 -> x3, waiting for transfers between devices: 49.1 us -> 61.1 us  [the longest x1 38 us: half_spectrum_shards(): lax.all_to_all(sections.reshape(8, rows + 16, 2 * LANE), ('high', 'low',...]
    ppermute x1 -> x2, waiting for transfers between devices: 9.78 us -> 0.01 us  [exchange_depth(): lax.ppermute(a, 'depth', over_y)]
    unnamed x19 -> x30, local copies, waits for them, and re-layouts: 12.8 us -> 5.42 us
    ppermute x2, waiting for transfers between devices: 5.9 us -> 0.01 us  [the longest x1 0.01 us: half_spectrum_shards(): south = lax.ppermute(first, everyone, up)]
    ppermute x1 -> x2, waiting for transfers between devices: 9.18 us -> 4.02 us  [exchange_depth(): lax.ppermute(a, 'depth', over_x)]
  transfers between devices with their start and end apart: 10 -> 17, of which waited for: 6 -> 7; matrix products, arithmetic and copies ran while one was open for 1% -> 2% of each run, Pallas kernels for 1% -> 19%
where the time goes in v2:
time: 291 us; the launch traced here: 290 us
  Pallas kernels  111 us (38%)
  waiting for transfers between devices  78.2 us (27%)
  blocking collectives  54.4 us (19%)
  starting transfers between devices  34.2 us (12%)
  local copies, waits for them, and re-layouts  10.1 us (3%)
    all_to_all x1, blocking collectives, to_rows(): lax.all_to_all(halfway.reshape(16, own, -1), ('depth', 'low', 'core'), sp...  54.4 us
    all_to_all x1, waiting for transfers between devices, half_spectrum_shards(): lax.all_to_all(sections.reshape(8, rows + 16, 2 * LANE), ('high', 'low',...  38 us
    pallas_call x2, Pallas kernels, next_columns(): pl.pallas_call(next_columns_kernel, grid_spec=pltpu.PrefetchScalarGridSpe...  27.4 us
    all_to_all x2, waiting for transfers between devices, to_rows(): lax.all_to_all(halfway.reshape(16, own, -1), ('depth', 'low', 'core'), sp...  23.1 us
    pallas_call x3, Pallas kernels, row_inverse(): pl.pallas_call(functools.partial(row_inverse_kernel, plane), grid=(count,...  21.7 us
    pallas_call x1, Pallas kernels, first_columns(): pl.pallas_call(first_columns_kernel, grid_spec=pltpu.PrefetchScalarGridSp...  15 us
    pallas_call x1, Pallas kernels, propagators(): pl.pallas_call(functools.partial(propagator_kernel, planes), grid=(OUT,),...  11.9 us
    pallas_call x1, Pallas kernels, row_forward(): pl.pallas_call(row_forward_kernel, grid_spec=pltpu.PrefetchScalarGridSpec...  10 us
  transfers between devices with their start and end apart: 17, of which 7 were waited for; matrix products, arithmetic and copies ran while one was open for 2% of the time, Pallas kernels for 19%

profile of v2, /device:TPU:0, one launch (start us, length us, event | category | flops | bytes accessed | tf_op | source)
XLA Modules:
  0.0 290.2 jit_solution(15701628519999632462)
XLA Ops:
  0.0 10.0 %row_forward.1 = bf16[2,2,2,528,256]{4,3,2,1,0:T(8,128)(2,1)} custom-call(s32[1]{0:T(128)} %bitcast.own, f32[256]{0:T(256)} %constant.50.clone.weights, bf16[512,4096]{1,0:T(8,128)(2,1)} %holo.1, bf16[512,4096]{1,0:T(8,128)(2,1)} %back.4, bf16[8,512,512]{2,1,0:T(8,128)(2,1)} %constant.49.clone.table), custom_call_target="tpu_custom_call" | custom-call | flops 10000000000 | bytes 12582912 | tf_op jit(solution)/shard_map/row_forward/pallas_call | solution.py:356
  10.0 6.3 %all-to-all-start = ((bf16[8,528,256]{2,1,0:T(8,128)(2,1)}), bf16[8,528,256]{2,1,0:T(8,128)(2,1)S(1)}, u32[]{:S(2)}, u32[]{:S(2)}) async-start(bf16[8,528,256]{2,1,0:T(8,128)(2,1)} %bitcast.24), calls=%async_computation | async-start | bytes 4325376 | tf_op jit(solution)/shard_map/all_to_all | solution.py:856
  16.3 0.5 multiply_multiply_fusion.fx2
  16.9 11.9 %propagators.1.kernels = f32[4,16,256,256]{3,2,1,0:T(8,128)} custom-call(f32[1,128]{1,0:T(1,128)} %multiply_multiply_fusion.fx2), custom_call_target="tpu_custom_call" | custom-call | flops 1000000000 | bytes 16777216 | tf_op jit(solution)/shard_map/propagators/pallas_call | solution.py:395
  28.8 38.0 %all-to-all-done.data = bf16[8,528,256]{2,1,0:T(8,128)(2,1)S(1)} async-done(((bf16[8,528,256]{2,1,0:T(8,128)(2,1)}), bf16[8,528,256]{2,1,0:T(8,128)(2,1)S(1)}, u32[]{:S(2)}, u32[]{:S(2)}) %all-to-all-start) | async-done | bytes 2162720 | tf_op jit(solution)/shard_map/all_to_all | solution.py:856
  66.8 1.4 copy-done
  68.2 15.0 %first_columns.1 = (bf16[2,2,2,2,128,512]{5,4,3,2,1,0:T(8,128)(2,1)}, bf16[16,256,256]{2,1,0:T(8,128)(2,1)}) custom-call(s32[1]{0:T(128)} %bitcast.1.half, bf16[8,528,256]{2,1,0:T(8,128)(2,1)} %copy-done, f32[4,16,256,256]{3,2,1,0:T(8,128)} %propagators.1.kernels, bf16[512,256]{1,0:T(8,128)(2,1)} %constant.51.clone.outer, ...), custom_call_target="tpu_custom_call" | custom-call | flops 10000000000 | bytes 20971520 | tf_op jit(solution)/shard_map/first_columns/pallas_call | solution.py:501
  83.2 17.8 %next_columns.3 = bf16[2,2,2,2,128,1024]{5,4,3,2,1,0:T(8,128)(2,1)} custom-call(s32[1]{0:T(128)} %bitcast.1.half, bf16[16,256,256]{2,1,0:T(8,128)(2,1)} %get-tuple-element.17.spectrum, f32[4,16,256,256]{3,2,1,0:T(8,128)} %propagators.1.kernels, bf16[16,512,256]{2,1,0:T(8,128)(2,1)} %constant.53.clone.inner_back, bf16[2,256,256]{2,1,0:T(8,128)(2,1)} %constant.54.clone.back), custom_call_target="tpu_custom_call" | custom-call | flops 14000000000 | bytes 33554432 | tf_op jit(solution)/shard_map/next_columns/pallas_call | solution.py:540
  101.0 54.4 %all_to_all.20 = bf16[16,128,1024]{2,1,0:T(8,128)(2,1)} all-to-all(bf16[16,128,1024]{2,1,0:T(8,128)(2,1)} %bitcast.23), channel_id=1, replica_groups=mesh['depth'=4,'high'=2,'low'=2,'core'=2] {'depth','low','core'}, dimensions={0} | all-to-all | bytes 8388608 | tf_op jit(solution)/shard_map/all_to_all | solution.py:871
  155.4 3.7 %all-to-all-start.1 = ((bf16[16,128,512]{2,1,0:T(8,128)(2,1)}), bf16[16,128,512]{2,1,0:T(8,128)(2,1)S(1)}, u32[]{:S(2)}, u32[]{:S(2)}) async-start(bf16[16,128,512]{2,1,0:T(8,128)(2,1)} %bitcast.28), calls=%async_computation.1 | async-start | bytes 4194304 | tf_op jit(solution)/shard_map/all_to_all | solution.py:871
  159.1 9.5 %next_columns.2 = bf16[2,2,2,2,128,512]{5,4,3,2,1,0:T(8,128)(2,1)} custom-call(s32[1]{0:T(128)} %bitcast.1.half, bf16[16,256,256]{2,1,0:T(8,128)(2,1)} %get-tuple-element.17.spectrum, f32[4,16,256,256]{3,2,1,0:T(8,128)} %propagators.1.kernels, bf16[16,512,256]{2,1,0:T(8,128)(2,1)} %constant.53.clone.inner_back, bf16[2,256,256]{2,1,0:T(8,128)(2,1)} %constant.54.clone.back), custom_call_target="tpu_custom_call" | custom-call | flops 7000000000 | bytes 16777216 | tf_op jit(solution)/shard_map/next_columns/pallas_call | solution.py:540
  168.7 18.1 %all-to-all-done.1 = bf16[16,128,512]{2,1,0:T(8,128)(2,1)S(1)} async-done(((bf16[16,128,512]{2,1,0:T(8,128)(2,1)}), bf16[16,128,512]{2,1,0:T(8,128)(2,1)S(1)}, u32[]{:S(2)}, u32[]{:S(2)}) %all-to-all-start.1) | async-done | bytes 2097184 | tf_op jit(solution)/shard_map/all_to_all | solution.py:871
  186.8 1.3 copy-done.2
  188.1 4.4 %all-to-all-start.3 = ((bf16[16,128,512]{2,1,0:T(8,128)(2,1)}), bf16[16,128,512]{2,1,0:T(8,128)(2,1)S(1)}, u32[]{:S(2)}, u32[]{:S(2)}) async-start(bf16[16,128,512]{2,1,0:T(8,128)(2,1)} %bitcast.25), calls=%async_computation.3 | async-start | bytes 4194304 | tf_op jit(solution)/shard_map/all_to_all | solution.py:871
  192.6 6.1 %nyquist.1 = f32[128,128]{1,0:T(8,128)} custom-call(s32[1]{0:T(128)} %bitcast.5.own, bf16[8,528,256]{2,1,0:T(8,128)(2,1)} %copy-done), custom_call_target="tpu_custom_call" | custom-call | flops 1000000000 | bytes 262144 | tf_op jit(solution)/shard_map/nyquist/pallas_call | solution.py:704
  198.6 6.4 %row_inverse.3 = (bf16[1,128,4096]{2,1,0:T(8,128)(2,1)}, f32[1,16,4096]{2,1,0:T(8,128)}) custom-call(bf16[4,2,2,128,512]{4,3,2,1,0:T(8,128)(2,1)} %bitcast.27, f32[128,128]{1,0:T(8,128)} %nyquist.1, bf16[8,512,512]{2,1,0:T(8,128)(2,1)} %constant.55.clone.table), custom_call_target="tpu_custom_call" | custom-call | flops 3000000000 | bytes 8388608 | tf_op jit(solution)/shard_map/row_inverse/pallas_call | solution.py:636
  205.1 8.8 %row_inverse.4 = (bf16[2,128,4096]{2,1,0:T(8,128)(2,1)}, f32[2,16,4096]{2,1,0:T(8,128)}) custom-call(bf16[4,2,2,128,1024]{4,3,2,1,0:T(8,128)(2,1)} %bitcast.22, f32[128,128]{1,0:T(8,128)} %nyquist.1, bf16[8,512,512]{2,1,0:T(8,128)(2,1)} %constant.55.clone.table), custom_call_target="tpu_custom_call" | custom-call | flops 6000000000 | bytes 16777216 | tf_op jit(solution)/shard_map/row_inverse/pallas_call | solution.py:636
  213.9 1.4 copy.16
  215.4 4.9 %all-to-all-done.3 = bf16[16,128,512]{2,1,0:T(8,128)(2,1)S(1)} async-done(((bf16[16,128,512]{2,1,0:T(8,128)(2,1)}), bf16[16,128,512]{2,1,0:T(8,128)(2,1)S(1)}, u32[]{:S(2)}, u32[]{:S(2)}) %all-to-all-start.3) | async-done | bytes 2097184 | tf_op jit(solution)/shard_map/all_to_all | solution.py:871
  220.3 1.4 copy-done.1
  221.7 6.4 %row_inverse.5 = (bf16[1,128,4096]{2,1,0:T(8,128)(2,1)}, f32[1,16,4096]{2,1,0:T(8,128)}) custom-call(bf16[4,2,2,128,512]{4,3,2,1,0:T(8,128)(2,1)} %bitcast.26, f32[128,128]{1,0:T(8,128)} %nyquist.1, bf16[8,512,512]{2,1,0:T(8,128)(2,1)} %constant.55.clone.table), custom_call_target="tpu_custom_call" | custom-call | flops 3000000000 | bytes 8388608 | tf_op jit(solution)/shard_map/row_inverse/pallas_call | solution.py:636
  228.1 1.1 slice_bitcast_fusion.4
  229.3 1.3 collective-permute-start.7
  230.6 6.6 %inner_focus.1.refs_0_ = bf16[64,4096]{1,0:T(8,128)(2,1)} custom-call(bf16[1,128,4096]{2,1,0:T(8,128)(2,1)} %get-tuple-element.16.refs_0_, bf16[2,128,4096]{2,1,0:T(8,128)(2,1)} %get-tuple-element.19.refs_1_, bf16[1,128,4096]{2,1,0:T(8,128)(2,1)} %get-tuple-element.21.refs_2_), custom_call_target="tpu_custom_call" | custom-call | flops 100000000 | bytes 6291456 | tf_op jit(solution)/shard_map/inner_focus/pallas_call | solution.py:755
  237.1 0.7 broadcast_select_fusion
  237.8 4.9 %collective-permute-start.6 = (f32[4,4096]{1,0:T(4,128)S(1)}, f32[4,4096]{1,0:T(4,128)S(1)}, u32[]{:S(2)}, u32[]{:S(2)}) collective-permute-start(f32[4,4096]{1,0:T(4,128)S(1)} %get-tuple-element.36), channel_id=1, source_target_pairs={{0,8},{8,16},{16,24},{24,1},{1,9},{9,17},{17,25},{25,2},{2,10},{10... | collective-permute-start | bytes 196616 | tf_op jit(solution)/shard_map/ppermute | solution.py:906
  242.7 1.1 fusion.1
  243.8 3.0 %collective-permute-start = (bf16[32,4096]{1,0:T(8,128)(2,1)S(1)}, bf16[32,4096]{1,0:T(8,128)(2,1)S(1)}, u32[]{:S(2)}, u32[]{:S(2)}) collective-permute-start(bf16[32,4096]{1,0:T(8,128)(2,1)S(1)} %get-tuple-element.30), channel_id=1, source_target_pairs={{0,8},{8,0},{16,24},{24,16},{1,9},{9,1},{17,25},{25,17},{2,10},{10... | collective-permute-start | bytes 786440 | tf_op jit(solution)/shard_map/ppermute | solution.py:839
  246.8 1.1 collective-permute-start.1
  248.0 0.9 collective-permute-start.4
  248.9 0.7 broadcast_select_fusion.1.refs_3_
  249.6 6.7 %outer_focus.1.refs_7_ = bf16[64,4096]{1,0:T(8,128)(2,1)} custom-call(bf16[1,128,4096]{2,1,0:T(8,128)(2,1)} %get-tuple-element.16.refs_0_, bf16[2,128,4096]{2,1,0:T(8,128)(2,1)} %get-tuple-element.19.refs_1_, bf16[1,128,4096]{2,1,0:T(8,128)(2,1)} %get-tuple-element.21.refs_2_, f32[4,4096]{1,0:T(4,128)} %broadcast_select_fusion.1.refs_3_, ...), custom_call_target="tpu_custom_call" | custom-call | flops 100000000 | bytes 6291456 | tf_op jit(solution)/shard_map/outer_focus/pallas_call | solution.py:788
  256.3 1.1 fusion
  257.4 2.0 collective-permute-start.8
  259.4 1.1 collective-permute-start.9
  260.5 0.9 collective-permute-start.12
  261.4 0.1 collective-permute-start.11
  261.5 1.1 collective-permute-start.2
  262.7 4.0 %collective-permute-done.8.refs_8_ = bf16[32,4096]{1,0:T(8,128)(2,1)S(1)} collective-permute-done((bf16[32,4096]{1,0:T(8,128)(2,1)S(1)}, bf16[32,4096]{1,0:T(8,128)(2,1)S(1)}, u32[]{:S(2)}, u32[]{:S(2)}) %collective-permute-start.8) | collective-permute-done | bytes 262176 | tf_op jit(solution)/shard_map/ppermute | solution.py:839
  266.7 1.9 collective-permute-start.5
  268.6 1.1 collective-permute-start.10
  269.8 4.5 %collective-permute-done.12.refs_12_ = bf16[32,4096]{1,0:T(8,128)(2,1)S(1)} collective-permute-done((bf16[32,4096]{1,0:T(8,128)(2,1)S(1)}, bf16[32,4096]{1,0:T(8,128)(2,1)S(1)}, u32[]{:S(2)}, u32[]{:S(2)}) %collective-permute-start.12) | collective-permute-done | bytes 262176 | tf_op jit(solution)/shard_map/ppermute | solution.py:839
  274.3 0.1 collective-permute-start.13
  274.4 5.5 %collective-permute-done.2.refs_3_ = bf16[32,4096]{1,0:T(8,128)(2,1)S(1)} collective-permute-done((bf16[32,4096]{1,0:T(8,128)(2,1)S(1)}, bf16[32,4096]{1,0:T(8,128)(2,1)S(1)}, u32[]{:S(2)}, u32[]{:S(2)}) %collective-permute-start.2) | collective-permute-done | bytes 262176 | tf_op jit(solution)/shard_map/ppermute | solution.py:840
  279.9 3.1 %collective-permute-done.10.refs_10_ = bf16[32,4096]{1,0:T(8,128)(2,1)S(1)} collective-permute-done((bf16[32,4096]{1,0:T(8,128)(2,1)S(1)}, bf16[32,4096]{1,0:T(8,128)(2,1)S(1)}, u32[]{:S(2)}, u32[]{:S(2)}) %collective-permute-start.10) | collective-permute-done | bytes 262176 | tf_op jit(solution)/shard_map/ppermute | solution.py:840
  283.1 0.6 copy-done.13
  283.7 0.7 copy-done.14
  284.4 5.7 %assemble.1 = f32[512,4096]{1,0:T(8,128)} custom-call(s32[1]{0:T(128)} %bitcast.own, bf16[64,4096]{1,0:T(8,128)(2,1)} %inner_focus.1.refs_0_, bf16[32,4096]{1,0:T(8,128)(2,1)} %copy-done.3, bf16[32,4096]{1,0:T(8,128)(2,1)} %copy-done.4, bf16[32,4096]{1,0:T(8,128)(2,1)} %copy-done.11, bf16[32,4096]{1,0:T(8,128)(2,1)} %copy-done.5, ...), custom_call_target="tpu_custom_call" | custom-call | flops 1000000 | bytes 12582912 | tf_op jit(solution)/shard_map/assemble/pallas_call | solution.py:819
  (38 shorter events, 0.2 us)
Async XLA Ops:
  10.0 56.8 %all-to-all-start = ((bf16[8,528,256]{2,1,0:T(8,128)(2,1)}), bf16[8,528,256]{2,1,0:T(8,128)(2,1)S(1)}, u32[]{:S(2)}, u32[]{:S(2)}) async-start(bf16[8,528,256]{2,1,0:T(8,128)(2,1)} %bitcast.24), calls=%async_computation | async-start | bytes 4325376 | tf_op jit(solution)/shard_map/all_to_all | solution.py:856
  66.8 1.4 copy-start
  155.4 31.4 %all-to-all-start.1 = ((bf16[16,128,512]{2,1,0:T(8,128)(2,1)}), bf16[16,128,512]{2,1,0:T(8,128)(2,1)S(1)}, u32[]{:S(2)}, u32[]{:S(2)}) async-start(bf16[16,128,512]{2,1,0:T(8,128)(2,1)} %bitcast.28), calls=%async_computation.1 | async-start | bytes 4194304 | tf_op jit(solution)/shard_map/all_to_all | solution.py:871
  186.8 1.3 copy-start.2
  188.1 32.2 %all-to-all-start.3 = ((bf16[16,128,512]{2,1,0:T(8,128)(2,1)}), bf16[16,128,512]{2,1,0:T(8,128)(2,1)S(1)}, u32[]{:S(2)}, u32[]{:S(2)}) async-start(bf16[16,128,512]{2,1,0:T(8,128)(2,1)} %bitcast.25), calls=%async_computation.3 | async-start | bytes 4194304 | tf_op jit(solution)/shard_map/all_to_all | solution.py:871
  220.3 1.4 copy-start.1
  229.3 7.9 %collective-permute-start.7 = (f32[4,4096]{1,0:T(4,128)S(1)}, f32[4,4096]{1,0:T(4,128)S(1)}, u32[]{:S(2)}, u32[]{:S(2)}) collective-permute-start(f32[4,4096]{1,0:T(4,128)S(1)} %pad_maximum_fusion), channel_id=1, source_target_pairs={{8,0},{16,8},{24,16},{1,24},{9,1},{17,9},{25,17},{2,25},{10,2},{18... | collective-permute-start | bytes 196616 | tf_op jit(solution)/shard_map/ppermute | solution.py:907
  237.8 11.1 %collective-permute-start.6 = (f32[4,4096]{1,0:T(4,128)S(1)}, f32[4,4096]{1,0:T(4,128)S(1)}, u32[]{:S(2)}, u32[]{:S(2)}) collective-permute-start(f32[4,4096]{1,0:T(4,128)S(1)} %get-tuple-element.36), channel_id=1, source_target_pairs={{0,8},{8,16},{16,24},{24,1},{1,9},{9,17},{17,25},{25,2},{2,10},{10... | collective-permute-start | bytes 196616 | tf_op jit(solution)/shard_map/ppermute | solution.py:906
  243.8 15.6 %collective-permute-start = (bf16[32,4096]{1,0:T(8,128)(2,1)S(1)}, bf16[32,4096]{1,0:T(8,128)(2,1)S(1)}, u32[]{:S(2)}, u32[]{:S(2)}) collective-permute-start(bf16[32,4096]{1,0:T(8,128)(2,1)S(1)} %get-tuple-element.30), channel_id=1, source_target_pairs={{0,8},{8,0},{16,24},{24,16},{1,9},{9,1},{17,25},{25,17},{2,10},{10... | collective-permute-start | bytes 786440 | tf_op jit(solution)/shard_map/ppermute | solution.py:839
  246.8 13.7 %collective-permute-start.1 = (bf16[32,4096]{1,0:T(8,128)(2,1)S(1)}, bf16[32,4096]{1,0:T(8,128)(2,1)S(1)}, u32[]{:S(2)}, u32[]{:S(2)}) collective-permute-start(bf16[32,4096]{1,0:T(8,128)(2,1)S(1)} %get-tuple-element.30), channel_id=1, source_target_pairs={{0,16},{8,24},{16,0},{24,8},{1,17},{9,25},{17,1},{25,9},{2,18},{10... | collective-permute-start | bytes 786440 | tf_op jit(solution)/shard_map/ppermute | solution.py:840
  247.9 13.5 %collective-permute-start.3 = (bf16[32,4096]{1,0:T(8,128)(2,1)S(1)}, bf16[32,4096]{1,0:T(8,128)(2,1)S(1)}, u32[]{:S(2)}, u32[]{:S(2)}) collective-permute-start(bf16[32,4096]{1,0:T(8,128)(2,1)S(1)} %get-tuple-element.29), channel_id=1, source_target_pairs={{0,8},{8,0},{16,24},{24,16},{1,9},{9,1},{17,25},{25,17},{2,10},{10... | collective-permute-start | bytes 786440 | tf_op jit(solution)/shard_map/ppermute | solution.py:841
  248.0 13.5 %collective-permute-start.4 = (bf16[32,4096]{1,0:T(8,128)(2,1)S(1)}, bf16[32,4096]{1,0:T(8,128)(2,1)S(1)}, u32[]{:S(2)}, u32[]{:S(2)}) collective-permute-start(bf16[32,4096]{1,0:T(8,128)(2,1)S(1)} %get-tuple-element.29), channel_id=1, source_target_pairs={{0,16},{8,24},{16,0},{24,8},{1,17},{9,25},{17,1},{25,9},{2,18},{10... | collective-permute-start | bytes 786440 | tf_op jit(solution)/shard_map/ppermute | solution.py:839
  257.4 9.3 %collective-permute-start.8 = (bf16[32,4096]{1,0:T(8,128)(2,1)S(1)}, bf16[32,4096]{1,0:T(8,128)(2,1)S(1)}, u32[]{:S(2)}, u32[]{:S(2)}) collective-permute-start(bf16[32,4096]{1,0:T(8,128)(2,1)S(1)} %get-tuple-element.26), channel_id=1, source_target_pairs={{0,8},{8,0},{16,24},{24,16},{1,9},{9,1},{17,25},{25,17},{2,10},{10... | collective-permute-start | bytes 786440 | tf_op jit(solution)/shard_map/ppermute | solution.py:839
  259.4 23.6 %copy-start.3 = (bf16[32,4096]{1,0:T(8,128)(2,1)}, bf16[32,4096]{1,0:T(8,128)(2,1)S(1)}, u32[]{:S(2)}) copy-start(bf16[32,4096]{1,0:T(8,128)(2,1)S(1)} %collective-permute-done.refs_1_) | copy-start | bytes 786436
  259.4 9.2 %collective-permute-start.9 = (bf16[32,4096]{1,0:T(8,128)(2,1)S(1)}, bf16[32,4096]{1,0:T(8,128)(2,1)S(1)}, u32[]{:S(2)}, u32[]{:S(2)}) collective-permute-start(bf16[32,4096]{1,0:T(8,128)(2,1)S(1)} %get-tuple-element.26), channel_id=1, source_target_pairs={{0,16},{8,24},{16,0},{24,8},{1,17},{9,25},{17,1},{25,9},{2,18},{10... | collective-permute-start | bytes 786440 | tf_op jit(solution)/shard_map/ppermute | solution.py:840
  260.5 22.5 %copy-start.4 = (bf16[32,4096]{1,0:T(8,128)(2,1)}, bf16[32,4096]{1,0:T(8,128)(2,1)S(1)}, u32[]{:S(2)}) copy-start(bf16[32,4096]{1,0:T(8,128)(2,1)S(1)} %collective-permute-done.1.refs_2_) | copy-start | bytes 786436
  260.5 13.7 %collective-permute-start.12 = (bf16[32,4096]{1,0:T(8,128)(2,1)S(1)}, bf16[32,4096]{1,0:T(8,128)(2,1)S(1)}, u32[]{:S(2)}, u32[]{:S(2)}) collective-permute-start(bf16[32,4096]{1,0:T(8,128)(2,1)S(1)} %get-tuple-element.25), channel_id=1, source_target_pairs={{0,16},{8,24},{16,0},{24,8},{1,17},{9,25},{17,1},{25,9},{2,18},{10... | collective-permute-start | bytes 786440 | tf_op jit(solution)/shard_map/ppermute | solution.py:839
  261.4 21.6 %copy-start.5 = (bf16[32,4096]{1,0:T(8,128)(2,1)}, bf16[32,4096]{1,0:T(8,128)(2,1)S(1)}, u32[]{:S(2)}) copy-start(bf16[32,4096]{1,0:T(8,128)(2,1)S(1)} %collective-permute-done.3.refs_4_) | copy-start | bytes 786436
  261.4 12.9 %collective-permute-start.11 = (bf16[32,4096]{1,0:T(8,128)(2,1)S(1)}, bf16[32,4096]{1,0:T(8,128)(2,1)S(1)}, u32[]{:S(2)}, u32[]{:S(2)}) collective-permute-start(bf16[32,4096]{1,0:T(8,128)(2,1)S(1)} %get-tuple-element.25), channel_id=1, source_target_pairs={{0,8},{8,0},{16,24},{24,16},{1,9},{9,1},{17,25},{25,17},{2,10},{10... | collective-permute-start | bytes 786440 | tf_op jit(solution)/shard_map/ppermute | solution.py:841
  261.5 21.5 %copy-start.6 = (bf16[32,4096]{1,0:T(8,128)(2,1)}, bf16[32,4096]{1,0:T(8,128)(2,1)S(1)}, u32[]{:S(2)}) copy-start(bf16[32,4096]{1,0:T(8,128)(2,1)S(1)} %collective-permute-done.4.refs_5_) | copy-start | bytes 786436
  261.5 18.3 %collective-permute-start.2 = (bf16[32,4096]{1,0:T(8,128)(2,1)S(1)}, bf16[32,4096]{1,0:T(8,128)(2,1)S(1)}, u32[]{:S(2)}, u32[]{:S(2)}) collective-permute-start(bf16[32,4096]{1,0:T(8,128)(2,1)S(1)} %collective-permute-done.refs_1_), channel_id=1, source_target_pairs={{0,16},{8,24},{16,0},{24,8},{1,17},{9,25},{17,1},{25,9},{2,18},{10... | collective-permute-start | bytes 786440 | tf_op jit(solution)/shard_map/ppermute | solution.py:840
  266.7 16.3 %copy-start.7 = (bf16[32,4096]{1,0:T(8,128)(2,1)}, bf16[32,4096]{1,0:T(8,128)(2,1)S(1)}, u32[]{:S(2)}) copy-start(bf16[32,4096]{1,0:T(8,128)(2,1)S(1)} %collective-permute-done.8.refs_8_) | copy-start | bytes 786436
  266.7 13.2 %collective-permute-start.5 = (bf16[32,4096]{1,0:T(8,128)(2,1)S(1)}, bf16[32,4096]{1,0:T(8,128)(2,1)S(1)}, u32[]{:S(2)}, u32[]{:S(2)}) collective-permute-start(bf16[32,4096]{1,0:T(8,128)(2,1)S(1)} %collective-permute-done.4.refs_5_), channel_id=1, source_target_pairs={{0,8},{8,0},{16,24},{24,16},{1,9},{9,1},{17,25},{25,17},{2,10},{10... | collective-permute-start | bytes 786440 | tf_op jit(solution)/shard_map/ppermute | solution.py:841
  268.6 14.4 %copy-start.8 = (bf16[32,4096]{1,0:T(8,128)(2,1)}, bf16[32,4096]{1,0:T(8,128)(2,1)S(1)}, u32[]{:S(2)}) copy-start(bf16[32,4096]{1,0:T(8,128)(2,1)S(1)} %collective-permute-done.9.refs_9_) | copy-start | bytes 786436
  268.6 14.3 %collective-permute-start.10 = (bf16[32,4096]{1,0:T(8,128)(2,1)S(1)}, bf16[32,4096]{1,0:T(8,128)(2,1)S(1)}, u32[]{:S(2)}, u32[]{:S(2)}) collective-permute-start(bf16[32,4096]{1,0:T(8,128)(2,1)S(1)} %collective-permute-done.8.refs_8_), channel_id=1, source_target_pairs={{0,16},{8,24},{16,0},{24,8},{1,17},{9,25},{17,1},{25,9},{2,18},{10... | collective-permute-start | bytes 786440 | tf_op jit(solution)/shard_map/ppermute | solution.py:840
  274.3 8.8 %copy-start.9 = (bf16[32,4096]{1,0:T(8,128)(2,1)}, bf16[32,4096]{1,0:T(8,128)(2,1)S(1)}, u32[]{:S(2)}) copy-start(bf16[32,4096]{1,0:T(8,128)(2,1)S(1)} %collective-permute-done.12.refs_12_) | copy-start | bytes 786436
  274.3 8.7 %collective-permute-start.13 = (bf16[32,4096]{1,0:T(8,128)(2,1)S(1)}, bf16[32,4096]{1,0:T(8,128)(2,1)S(1)}, u32[]{:S(2)}, u32[]{:S(2)}) collective-permute-start(bf16[32,4096]{1,0:T(8,128)(2,1)S(1)} %collective-permute-done.12.refs_12_), channel_id=1, source_target_pairs={{0,8},{8,0},{16,24},{24,16},{1,9},{9,1},{17,25},{25,17},{2,10},{10... | collective-permute-start | bytes 786440 | tf_op jit(solution)/shard_map/ppermute | solution.py:841
  274.4 8.7 %copy-start.10 = (bf16[32,4096]{1,0:T(8,128)(2,1)}, bf16[32,4096]{1,0:T(8,128)(2,1)S(1)}, u32[]{:S(2)}) copy-start(bf16[32,4096]{1,0:T(8,128)(2,1)S(1)} %collective-permute-done.11.refs_11_) | copy-start | bytes 786436
  279.9 3.2 %copy-start.11 = (bf16[32,4096]{1,0:T(8,128)(2,1)}, bf16[32,4096]{1,0:T(8,128)(2,1)S(1)}, u32[]{:S(2)}) copy-start(bf16[32,4096]{1,0:T(8,128)(2,1)S(1)} %collective-permute-done.2.refs_3_) | copy-start | bytes 786436
  279.9 3.2 %copy-start.12 = (bf16[32,4096]{1,0:T(8,128)(2,1)}, bf16[32,4096]{1,0:T(8,128)(2,1)S(1)}, u32[]{:S(2)}) copy-start(bf16[32,4096]{1,0:T(8,128)(2,1)S(1)} %collective-permute-done.5.refs_6_) | copy-start | bytes 786436
  283.0 0.7 copy-start.13
  283.7 0.7 copy-start.14

commit v3 on v2

--- a/solution.py
+++ b/solution.py
@@ -179,7 +179,8 @@
 CLS = 8
 LANE = 128
 MIB = 2**20
-VMEM = 60 * MIB
+VMEM = 63 * MIB
+SHARED = 36 * MIB
 
 
 def slot_frequencies():
@@ -244,13 +245,16 @@
             for i in range(2)
         ]
     )
+    beyond = np.stack(
+        [np.concatenate([outer_cos[a * 16 :][:16], outer_sin[a * 16 :][:16]]) for a in (8, 7)]
+    )
     freq = np.arange(OUT)[:, None] + OUT * np.arange(INN)[None, :]
     theta = angles(freq[:, :, None] * np.arange(INN)[None, None, :])
     inner = np.concatenate([np.cos(theta), -np.sin(theta)], axis=1) / 16.0
     theta = theta.transpose(0, 2, 1)
     inner_back = np.concatenate([np.cos(theta), np.sin(theta)], axis=1) / 16.0
     cast = lambda table: table.astype(jnp.bfloat16)
-    return cast(outer), cast(inner), cast(inner_back), cast(back)
+    return cast(outer), cast(inner), cast(inner_back), cast(back), cast(beyond)
 
 
 def dot(left, right):
@@ -421,8 +425,19 @@
         second[k, :, lanes] = jnp.concatenate([re, im], axis=1).astype(jnp.bfloat16)
 
 
-def close_columns(start, back, second, out):
+def close_columns(half, step, back, beyond, second, out, outside):
     width = LANE
+    start = step * PER
+
+    @pl.when(step == 0)
+    def _():
+        here = pl.ds(pl.multiple_of(half[0] * (INN - 16), 16), 16)
+        both = dot(beyond[0], second[:, here, :].reshape(OUT * 16, 4 * width))
+        for part in range(2):
+            lanes = slice(part * 2 * width, (part + 1) * 2 * width)
+            re, im = split_complex(both[:, lanes], width)
+            outside[0, :, lanes] = jnp.concatenate([re, im], axis=1).astype(jnp.bfloat16)
+
     for c in range(PER):
         here = pl.ds(pl.multiple_of((start + c) * 16, 16), 16)
         both = dot(back[0], second[:, here, :].reshape(OUT * 16, 4 * width))
@@ -439,7 +454,8 @@
 
 
 def first_columns_kernel(
-    half, data, kernels, outer, inner, inner_back, back, out, spectrum, first, mixed, second
+    half, data, kernels, outer, inner, inner_back, back, beyond,
+    out, outside, spectrum, first, mixed, second,
 ):
     step = pl.program_id(0)
     width = LANE
@@ -464,10 +480,12 @@
 
     @pl.when(step >= OUT // PER)
     def _():
-        close_columns((step - OUT // PER) * PER, back, second, out)
-
-
-def next_columns_kernel(half, spectrum, kernels, inner_back, back, out, mixed, second):
+        close_columns(half, step - OUT // PER, back, beyond, second, out, outside)
+
+
+def next_columns_kernel(
+    half, spectrum, kernels, inner_back, back, beyond, out, outside, mixed, second
+):
     step = pl.program_id(1)
     width = LANE
 
@@ -480,7 +498,7 @@
 
     @pl.when(step >= OUT // PER)
     def _():
-        close_columns((step - OUT // PER) * PER, back, second, out)
+        close_columns(half, step - OUT // PER, back, beyond, second, out, outside)
 
 
 STEPS = OUT // PER
@@ -495,7 +513,7 @@
 
 
 def first_columns(half, data, kernels):
-    outer, inner, inner_back, back = (jnp.asarray(t) for t in column_tables())
+    outer, inner, inner_back, back, beyond = (jnp.asarray(t) for t in column_tables())
     rows = data.shape[1] - 16
     opening = lambda i, o: (opening_step(i), 0, 0)
     return pl.pallas_call(
@@ -510,12 +528,14 @@
                 pl.BlockSpec((PER, 2 * INN, INN), opening),
                 pl.BlockSpec((PER, 2 * INN, INN), opening),
                 pl.BlockSpec((1, INN, INN), lambda i, o: (o[0], 0, 0)),
+                pl.BlockSpec((1, 32, INN), lambda i, o: (o[0], 0, 0)),
             ],
             out_specs=[
                 pl.BlockSpec(
                     (2, 1, 2, 2, PER * 16, 4 * LANE),
                     lambda i, o: (0, closing_step(i) // 2, 0, 0, closing_step(i) % 2, 0),
                 ),
+                pl.BlockSpec((1, 16, 4 * LANE), lambda i, o: (0, 0, 0)),
                 pl.BlockSpec((PER, INN, 2 * LANE), opening),
             ],
             scratch_shapes=[
@@ -526,16 +546,17 @@
         ),
         out_shape=[
             jax.ShapeDtypeStruct((2, 2, 2, 2, LANE, 4 * LANE), jnp.bfloat16),
+            jax.ShapeDtypeStruct((1, 16, 4 * LANE), jnp.bfloat16),
             jax.ShapeDtypeStruct((OUT, INN, 2 * LANE), jnp.bfloat16),
         ],
         compiler_params=pltpu.CompilerParams(vmem_limit_bytes=VMEM),
         cost_estimate=pl.CostEstimate(flops=10**10, bytes_accessed=20 * MIB, transcendentals=0),
         name="first_columns",
-    )(half, data, kernels, outer, inner, inner_back, back)
+    )(half, data, kernels, outer, inner, inner_back, back, beyond)
 
 
 def next_columns(half, plane, count, spectrum, kernels):
-    _, _, inner_back, back = (jnp.asarray(t) for t in column_tables())
+    inner_back, back, beyond = (jnp.asarray(t) for t in column_tables()[2:])
     opening = lambda g, i, o: (opening_step(i), 0, 0)
     return pl.pallas_call(
         next_columns_kernel,
@@ -549,23 +570,30 @@
                 ),
                 pl.BlockSpec((PER, 2 * INN, INN), opening),
                 pl.BlockSpec((1, INN, INN), lambda g, i, o: (o[0], 0, 0)),
+                pl.BlockSpec((1, 32, INN), lambda g, i, o: (o[0], 0, 0)),
             ],
-            out_specs=pl.BlockSpec(
-                (2, 1, 2, 2, PER * 16, 4 * LANE),
-                lambda g, i, o: (0, closing_step(i) // 2, 0, 0, closing_step(i) % 2, g),
-            ),
+            out_specs=[
+                pl.BlockSpec(
+                    (2, 1, 2, 2, PER * 16, 4 * LANE),
+                    lambda g, i, o: (0, closing_step(i) // 2, 0, 0, closing_step(i) % 2, g),
+                ),
+                pl.BlockSpec((1, 16, 4 * LANE), lambda g, i, o: (g, 0, 0)),
+            ],
             scratch_shapes=[
                 pltpu.VMEM((PER, INN, 4 * LANE), jnp.bfloat16),
                 pltpu.VMEM((OUT, INN, 4 * LANE), jnp.bfloat16),
             ],
         ),
-        out_shape=jax.ShapeDtypeStruct((2, 2, 2, 2, LANE, count * 4 * LANE), jnp.bfloat16),
+        out_shape=[
+            jax.ShapeDtypeStruct((2, 2, 2, 2, LANE, count * 4 * LANE), jnp.bfloat16),
+            jax.ShapeDtypeStruct((count, 16, 4 * LANE), jnp.bfloat16),
+        ],
         compiler_params=pltpu.CompilerParams(vmem_limit_bytes=VMEM),
         cost_estimate=pl.CostEstimate(
             flops=count * 7 * 10**9, bytes_accessed=count * 16 * MIB, transcendentals=0
         ),
         name="next_columns",
-    )(half, spectrum, kernels, inner_back, back)
+    )(half, spectrum, kernels, inner_back, back, beyond)
 
 
 def sixteen_points(re, im):
@@ -590,6 +618,19 @@
     return result + [cosines[16 - a] + sines[16 - a] for a in range(9, 16)]
 
 
+def strip_intensity(opened, here, tile):
+    total = None
+    for part in range(2):
+        re = [opened[part, g, here, tile * LANE : (tile + 1) * LANE] for g in range(CLS)]
+        im = [opened[part, g, here, INN + tile * LANE : INN + (tile + 1) * LANE] for g in range(CLS)]
+        values = sixteen_points(re, im)
+        if total is None:
+            total = [v * v for v in values]
+        else:
+            total = [t + v * v for t, v in zip(total, values)]
+    return total
+
+
 def row_inverse_kernel(plane, parts, nyquist, table, out, edges, opened):
     current = plane + pl.program_id(0)
     rows = parts.shape[3]
@@ -608,18 +649,7 @@
     def strip(i, carry):
         here = pl.ds(pl.multiple_of(i * 16, 16), 16)
         for tile in range(INN // LANE):
-            total = None
-            for part in range(2):
-                re = [opened[part, g, here, tile * LANE : (tile + 1) * LANE] for g in range(CLS)]
-                im = [
-                    opened[part, g, here, INN + tile * LANE : INN + (tile + 1) * LANE]
-                    for g in range(CLS)
-                ]
-                values = sixteen_points(re, im)
-                if total is None:
-                    total = [v * v for v in values]
-                else:
-                    total = [t + v * v for t, v in zip(total, values)]
+            total = strip_intensity(opened, here, tile)
             for a in range(OUT):
                 lanes = slice(a * INN + tile * LANE, a * INN + (tile + 1) * LANE)
                 out[0, here, lanes] = total[a].astype(jnp.bfloat16)
@@ -684,19 +714,28 @@
     yr, yi = product(ar, ai, inner_r, -inner_i)
     fy = signed_fraction(tall(0) + OUT * tall(1))
     (kr, ki), (sr, si) = start_and_step(fy * fy + 0.25)
-    block = own[0]
+    block, blocks = own[0], own[1]
     k = lax.broadcasted_iota(jnp.int32, (8, OUT), 1)
-    hr, hi = wave(k * (block // 2), OUT)
-    result = []
+    section = block // 2 + lax.broadcasted_iota(jnp.int32, (8, OUT), 0) + (OUT - 1)
+    hr, hi = wave(k * (section % OUT), OUT)
+    even = block % 2 == 0
+    lane = lax.broadcasted_iota(jnp.int32, (1, LANE), 1)
+    result, beside = [], []
     for g in range(planes):
         pr, pi = rotated(yr, yi, kr, ki)
         br, bi = rotated(*product(pr, pi, inner_r, inner_i), vr, vi)
         for value in product(hr, hi, br, bi):
-            half = jnp.where(block % 2 == 0, value[:, :LANE], value[:, LANE:])
-            result.append(half[0:1] * (1.0 / N))
+            value = value * (1.0 / N)
+            result.append(jnp.where(even, value[1:2, :LANE], value[1:2, LANE:]))
+            above = jnp.where(even, value[0:1, INN - 1 :], value[1:2, LANE - 1 : LANE])
+            above = jnp.where(block == 0, value[1:2, 0:1], above)
+            below = jnp.where(even, value[1:2, LANE : LANE + 1], value[2:3, 0:1])
+            below = jnp.where(block == blocks - 1, value[1:2, INN - 1 :], below)
+            beside.append(jnp.where(lane == 0, above, jnp.where(lane == 1, below, 0.0)))
         kr, ki = rotated(kr, ki, sr, si)
-    result.append(jnp.zeros((LANE - 2 * planes, LANE), jnp.float32))
-    out[...] = jnp.concatenate(result, axis=0).T
+    rest = [jnp.zeros((LANE - 2 * planes, LANE), jnp.float32)]
+    out[:LANE, :] = jnp.concatenate(result + rest, axis=0).T
+    out[LANE:, :] = jnp.concatenate(beside + rest, axis=0).T
 
 
 def nyquist_column(own, planes, data):
@@ -707,139 +746,241 @@
             num_scalar_prefetch=1,
             grid=(1,),
             in_specs=[pl.BlockSpec((8, 16, 2 * LANE), lambda i, o: (0, rows // 16, 0))],
-            out_specs=pl.BlockSpec((LANE, LANE), lambda i, o: (0, 0)),
+            out_specs=pl.BlockSpec((2 * LANE, LANE), lambda i, o: (0, 0)),
         ),
-        out_shape=jax.ShapeDtypeStruct((LANE, LANE), jnp.float32),
+        out_shape=jax.ShapeDtypeStruct((2 * LANE, LANE), jnp.float32),
+        compiler_params=pltpu.CompilerParams(vmem_limit_bytes=VMEM),
         cost_estimate=pl.CostEstimate(flops=10**9, bytes_accessed=2**18, transcendentals=0),
         name="nyquist",
     )(own, data)
 
 
-def focus_of(held, planes, count, out):
-    tile = 512
-    lane = lax.broadcasted_iota(jnp.int32, (16, tile), 1)
-    for i in range(count // 16):
+TILE = 512
+
+
+def across(centre, tile, west, east):
+    lane = lax.broadcasted_iota(jnp.int32, centre.shape, 1)
+    right = jnp.where(lane == TILE - 1, east, pltpu.roll(centre, TILE - 1, 1))
+    left = jnp.where(lane == 0, west, pltpu.roll(centre, 1, 1))
+    return (right - left) * (right - left)
+
+
+def spatial_term(held, r, t):
+    lanes = slice(t * TILE, (t + 1) * TILE)
+    centre = held[r : r + 16, lanes]
+    down = held[r + 1 : r + 17, lanes] - held[r - 1 : r + 15, lanes]
+    first, last = max(t * TILE - 1, 0), min((t + 1) * TILE, N - 1)
+    west, east = held[r : r + 16, first : first + 1], held[r : r + 16, last : last + 1]
+    return centre, down * down + across(centre, TILE, west, east)
+
+
+def hold(held, block, rows):
+    held[8 : 8 + rows, :] = block.astype(jnp.float32)
+    held[7:8, :] = held[8:9, :]
+    held[8 + rows : 9 + rows, :] = held[7 + rows : 8 + rows, :]
+
+
+def early_focus_kernel(first, others, best, spatial, held):
+    rows = first.shape[1]
+    for g in range(3):
+        hold(held.at[g], first[0] if g == 0 else others[g - 1], rows)
+    for i in range(rows // 16):
         r = 8 + i * 16
-        for t in range(N // tile):
-            lanes = slice(t * tile, (t + 1) * tile)
-            centre = [held[g, r : r + 16, lanes] for g in range(planes)]
-            best = None
-            for g in range(planes):
-                depth = centre[min(g + 1, planes - 1)] - centre[max(g - 1, 0)]
-                down = held[g, r + 1 : r + 17, lanes] - held[g, r - 1 : r + 15, lanes]
-                first, last = max(t * tile - 1, 0), min((t + 1) * tile, N - 1)
-                right = pltpu.roll(centre[g], tile - 1, 1)
-                right = jnp.where(lane == tile - 1, held[g, r : r + 16, last : last + 1], right)
-                left = pltpu.roll(centre[g], 1, 1)
-                left = jnp.where(lane == 0, held[g, r : r + 16, first : first + 1], left)
-                across = right - left
-                score = depth * depth + down * down + across * across
-                best = score if best is None else jnp.maximum(best, score)
-            out[i * 16 : (i + 1) * 16, lanes] = (best * 0.125).astype(jnp.bfloat16)
-
-
-def inner_focus_kernel(sizes, begin, count, *refs):
-    blocks, out, held = refs[: len(sizes)], refs[-2], refs[-1]
-    plane = 0
-    for block, size in zip(blocks, sizes):
-        for g in range(size):
-            held[plane, 0 : count + 16, :] = block[g, begin - 16 : begin + count + 16, :].astype(
-                jnp.float32
-            )[8 : count + 24]
-            plane += 1
-    focus_of(held, plane, count, out)
-
-
-def inner_focus(intensities, begin, count):
-    sizes = [block.shape[0] for block in intensities]
+        for t in range(N // TILE):
+            lanes = slice(t * TILE, (t + 1) * TILE)
+            (c0, s0), (c1, s1), (c2, s2) = (spatial_term(held.at[g], r, t) for g in range(3))
+            d0, d1 = c1 - c0, c2 - c0
+            score = jnp.maximum(d0 * d0 + s0, d1 * d1 + s1)
+            best[r - 8 : r + 8, lanes] = (score * 0.125).astype(jnp.bfloat16)
+            spatial[r - 8 : r + 8, lanes] = s2
+
+
+def early_focus(first, others):
+    rows = first.shape[1]
     return pl.pallas_call(
-        functools.partial(inner_focus_kernel, sizes, begin, count),
-        out_shape=jax.ShapeDtypeStruct((count, N), jnp.bfloat16),
-        scratch_shapes=[pltpu.VMEM((sum(sizes), count + 16, N), jnp.float32)],
+        early_focus_kernel,
+        out_shape=[
+            jax.ShapeDtypeStruct((rows, N), jnp.bfloat16),
+            jax.ShapeDtypeStruct((rows, N), jnp.float32),
+        ],
+        scratch_shapes=[pltpu.VMEM((3, rows + 16, N), jnp.float32)],
         compiler_params=pltpu.CompilerParams(vmem_limit_bytes=VMEM),
-        cost_estimate=pl.CostEstimate(flops=10**8, bytes_accessed=6 * MIB, transcendentals=0),
-        name="inner_focus",
-    )(*intensities)
-
-
-def outer_focus_kernel(sizes, count, *refs):
-    blocks, north, south, out, held = refs[: len(sizes)], refs[-4], refs[-3], refs[-2], refs[-1]
-    planes = sum(sizes)
-    for side in range(2):
-        plane = 0
-        for block, size in zip(blocks, sizes):
-            rows = block.shape[1]
-            for g in range(size):
-                if side == 0:
-                    held[plane, 8 : 24 + count, :] = block[g, : count + 16, :].astype(jnp.float32)
-                    held[plane, 0:8, :] = jnp.broadcast_to(north[plane : plane + 1, :], (8, N))
-                else:
-                    value = block[g, rows - count - 16 :, :].astype(jnp.float32)
-                    held[plane, 0 : count + 8, :] = value[8:]
-                    held[plane, count + 8 : count + 16, :] = jnp.broadcast_to(
-                        south[plane : plane + 1, :], (8, N)
-                    )
-                plane += 1
-        focus_of(held, planes, count, out.at[side * count : (side + 1) * count])
-
-
-def outer_focus(intensities, north, south, count):
-    sizes = [block.shape[0] for block in intensities]
+        cost_estimate=pl.CostEstimate(flops=10**9, bytes_accessed=12 * MIB, transcendentals=0),
+        name="early_focus",
+    )(first, others)
+
+
+def edge_rows(edges, halo, out_upper, out_lower):
+    lane = lax.broadcasted_iota(jnp.int32, (2, N), 1)
+    pair = lambda a, b: jnp.concatenate([a, b], axis=0)
+    centre = [pair(e[0:1, :], e[15:16, :]) for e in edges]
+    best = None
+    for g, e in enumerate(edges):
+        depth = centre[min(g + 1, 3)] - centre[max(g - 1, 0)]
+        above, below = halo[2 * g : 2 * g + 1, :], halo[2 * g + 1 : 2 * g + 2, :]
+        down = pair(e[1:2, :], below) - pair(above, e[14:15, :])
+        c = centre[g]
+        right = jnp.where(lane == N - 1, c, jnp.concatenate([c[:, 1:], c[:, :1]], axis=1))
+        left = jnp.where(lane == 0, c, jnp.concatenate([c[:, -1:], c[:, :-1]], axis=1))
+        score = depth * depth + down * down + (right - left) * (right - left)
+        best = score if best is None else jnp.maximum(best, score)
+    best = best * 0.125
+    rows = out_upper.shape[0]
+    index = lax.broadcasted_iota(jnp.int32, (16, N), 0)
+    top = out_upper[0:16, :].astype(jnp.float32)
+    out_upper[0:16, :] = jnp.where(index == 0, best[0:1], top).astype(jnp.bfloat16)
+    low = out_lower[rows - 16 :, :].astype(jnp.float32)
+    out_lower[rows - 16 :, :] = jnp.where(index == 15, best[1:2], low).astype(jnp.bfloat16)
+
+
+def last_rows_kernel(
+    parts, nyquist, table, best, spatial, others, edge0, edge12,
+    upper, lower,
+    part_buf, table_buf, best_buf, spatial_buf, others_buf, opened, held, halo, edge, sems,
+):
+    rows = upper.shape[0] * 2
+    loads = []
+    for group in range(CLS):
+        source = parts.at[group // 2, :, group % 2]
+        loads.append(pltpu.make_async_copy(source, part_buf.at[group], sems.at[0, group]))
+        loads.append(pltpu.make_async_copy(table.at[group], table_buf.at[group], sems.at[1, group]))
+    for i, (source, target) in enumerate(
+        ((best, best_buf), (spatial, spatial_buf), (others, others_buf))
+    ):
+        loads.append(pltpu.make_async_copy(source, target, sems.at[2, i]))
+    for load in loads:
+        load.start()
+    lane = lax.broadcasted_iota(jnp.int32, (rows, LANE), 1)
+    few_lane = lax.broadcasted_iota(jnp.int32, (16, LANE), 1)
+    few_row = lax.broadcasted_iota(jnp.int32, (16, LANE), 0)
+    beside = jnp.where(few_row % 2 == 0, nyquist[rows : rows + 1, :], nyquist[rows + 1 : rows + 2, :])
+    for group in range(CLS):
+        loads[2 * group].wait()
+        loads[2 * group + 1].wait()
+        for part in range(2):
+            at = part * 2 * LANE
+            low, high = (part_buf[group, i, :, at : at + 2 * LANE] for i in range(2))
+            if group == 0:
+                mine = jnp.where(lane == 6 + part, nyquist[:rows, :], 0.0)
+                few = jnp.where(few_lane == (few_row // 2) * 2 + part, beside, 0.0)
+                column = jnp.sum(jnp.concatenate([mine, few], axis=0), axis=1, keepdims=True)
+                column = column.astype(jnp.bfloat16)
+                every = lax.broadcasted_iota(jnp.int32, (rows + 16, LANE), 1)
+                first = jnp.where(every == 0, column, low[:, LANE:])
+                low = jnp.concatenate([low[:, :LANE], first], axis=1)
+            opened[part, group] = dot(jnp.concatenate([low, high], axis=1), table_buf[group])
+
+    def strip(i, carry):
+        base = pl.multiple_of(i * 8, 8)
+        for tile in range(INN // LANE):
+            for a, value in enumerate(strip_intensity(opened, pl.ds(base, 8), tile)):
+                lanes = slice(a * INN + tile * LANE, a * INN + (tile + 1) * LANE)
+                value = value.astype(jnp.bfloat16).astype(jnp.float32)
+                held[pl.ds(pl.multiple_of(base + 8, 8), 8), lanes] = value
+        return carry
+
+    lax.fori_loop(0, rows // 8 + 1, strip, 0)
+    halo[...] = held[8 + rows : 16 + rows, :]
+    held[7:8, :] = held[8:9, :]
+    held[8 + rows : 9 + rows, :] = held[7 + rows : 8 + rows, :]
+    edge[0:8, :] = held[8:16, :]
+    edge[8:16, :] = held[rows : rows + 8, :]
+    for load in loads[2 * CLS :]:
+        load.wait()
+    for i in range(rows // 16):
+        r = 8 + i * 16
+        here = slice(r - 8, r + 8)
+        out, at = (upper, r - 8) if 2 * i < rows // 16 else (lower, r - 8 - rows // 2)
+        for t in range(N // TILE):
+            lanes = slice(t * TILE, (t + 1) * TILE)
+            centre, term = spatial_term(held, r, t)
+            d2 = centre - others_buf[0, here, lanes].astype(jnp.float32)
+            d3 = centre - others_buf[1, here, lanes].astype(jnp.float32)
+            score = jnp.maximum(d2 * d2 + spatial_buf[here, lanes], d3 * d3 + term)
+            score = jnp.maximum(score * 0.125, best_buf[here, lanes].astype(jnp.float32))
+            out[at : at + 16, lanes] = score.astype(jnp.bfloat16)
+    edge_rows([edge0.at[0], edge12.at[0], edge12.at[1], edge], halo, upper, lower)
+
+
+def last_rows(parts, nyquist, best, spatial, others, edge0, edge12):
+    rows = best.shape[0]
+    table = jnp.asarray(row_inverse_tables())
+    vmem, hbm = pl.BlockSpec(memory_space=pltpu.VMEM), pl.BlockSpec(memory_space=pl.ANY)
+    bf16, f32 = jnp.bfloat16, jnp.float32
     return pl.pallas_call(
-        functools.partial(outer_focus_kernel, sizes, count),
-        out_shape=jax.ShapeDtypeStruct((2 * count, N), jnp.bfloat16),
-        scratch_shapes=[pltpu.VMEM((sum(sizes), count + 24, N), jnp.float32)],
+        last_rows_kernel,
+        in_specs=[hbm, vmem, hbm, hbm, hbm, hbm, vmem, vmem],
+        out_specs=[vmem] * 2,
+        out_shape=[jax.ShapeDtypeStruct((rows // 2, N), bf16)] * 2,
+        scratch_shapes=[
+            pltpu.VMEM((CLS, 2, rows + 16, 4 * LANE), bf16),
+            pltpu.VMEM((CLS, 2 * INN, 2 * INN), bf16),
+            pltpu.VMEM((rows, N), bf16),
+            pltpu.VMEM((rows, N), f32),
+            pltpu.VMEM((2, rows, N), bf16),
+            pltpu.VMEM((2, CLS, rows + 16, 2 * INN), f32),
+            pltpu.VMEM((rows + 16, N), f32),
+            pltpu.VMEM((8, N), f32),
+            pltpu.VMEM((16, N), f32),
+            pltpu.SemaphoreType.DMA((3, CLS)),
+        ],
         compiler_params=pltpu.CompilerParams(vmem_limit_bytes=VMEM),
-        cost_estimate=pl.CostEstimate(flops=10**8, bytes_accessed=6 * MIB, transcendentals=0),
-        name="outer_focus",
-    )(*intensities, north, south)
+        cost_estimate=pl.CostEstimate(flops=3 * 10**9, bytes_accessed=16 * MIB, transcendentals=0),
+        name="last_rows",
+    )(parts, nyquist, table, best, spatial, others, edge0, edge12)
 
 
 def assemble_kernel(own, *refs):
     slot, out = pl.program_id(0), refs[-1]
-    inner, outer = refs[:7], refs[7:14]
-    part = inner[1].shape[0]
+    half = refs[0].shape[0]
     for s in range(4):
 
         @pl.when(slot == s)
         def _():
-            for both, places in ((inner, (part, 2 * part)), (outer, (0, 3 * part))):
-                if s == 0:
-                    a, b = both[0][:part], both[0][part:]
-                else:
-                    a, b = both[s][...], both[3 + s][...]
-                out[places[0] : places[0] + part] = a.astype(jnp.float32)
-                out[places[1] : places[1] + part] = b.astype(jnp.float32)
-
-
-def assemble(depth_index, inner, outer):
-    part = inner[1].shape[0]
-    whole = lambda shape: pl.BlockSpec(shape, lambda s, o: (0, 0))
-    specs = [whole((2 * part, N))] + [whole((part, N))] * 6
+            out[:half] = refs[s][...].astype(jnp.float32)
+            out[half:] = refs[4 + s][...].astype(jnp.float32)
+
+
+def assemble(depth_index, upper, lower):
+    half = upper[0].shape[0]
+    whole = pl.BlockSpec((half, N), lambda s, o: (0, 0))
     return pl.pallas_call(
         assemble_kernel,
         grid_spec=pltpu.PrefetchScalarGridSpec(
             num_scalar_prefetch=1,
             grid=(4,),
-            in_specs=specs * 2,
-            out_specs=pl.BlockSpec((4 * part, N), lambda s, o: (jnp.bitwise_xor(s, o[0]), 0)),
+            in_specs=[whole] * 8,
+            out_specs=pl.BlockSpec((2 * half, N), lambda s, o: (jnp.bitwise_xor(s, o[0]), 0)),
         ),
-        out_shape=jax.ShapeDtypeStruct((16 * part, N), jnp.float32),
-        compiler_params=pltpu.CompilerParams(vmem_limit_bytes=VMEM),
+        out_shape=jax.ShapeDtypeStruct((8 * half, N), jnp.float32),
+        compiler_params=pltpu.CompilerParams(vmem_limit_bytes=SHARED),
         cost_estimate=pl.CostEstimate(flops=10**6, bytes_accessed=12 * MIB, transcendentals=0),
         name="assemble",
-    )(depth_index, *inner, *outer)
-
-
-def exchange_depth(mine):
-    half = mine.shape[0] // 2
-    a, b = mine[:half], mine[half:]
-    over_x = [(i, i ^ 1) for i in range(4)]
-    over_y = [(i, i ^ 2) for i in range(4)]
-    ax, by = lax.ppermute(a, "depth", over_x), lax.ppermute(b, "depth", over_y)
-    ay, axy = lax.ppermute(a, "depth", over_y), lax.ppermute(ax, "depth", over_y)
-    bx, byx = lax.ppermute(b, "depth", over_x), lax.ppermute(by, "depth", over_x)
-    return mine, ax, ay, axy, bx, by, byx
+    )(depth_index, *upper, *lower)
+
+
+OVER_X = [(i, i ^ 1) for i in range(4)]
+OVER_Y = [(i, i ^ 2) for i in range(4)]
+
+
+def exchange_depth(a, b):
+    ax, by = lax.ppermute(a, "depth", OVER_X), lax.ppermute(b, "depth", OVER_Y)
+    ay, axy = lax.ppermute(a, "depth", OVER_Y), lax.ppermute(ax, "depth", OVER_Y)
+    bx, byx = lax.ppermute(b, "depth", OVER_X), lax.ppermute(by, "depth", OVER_X)
+    return (a, ax, ay, axy), (b, bx, by, byx)
+
+
+def border_rows(halfway, outside, high):
+    lanes = 4 * LANE
+    count = halfway.shape[-1] // lanes
+    natural = lambda rows: rows.reshape(4, 2, 2, count, lanes).transpose(1, 2, 0, 3, 4).reshape(16, count, lanes)
+    first, last = natural(halfway[..., 0, :]), natural(halfway[..., -1, :])
+    above = jnp.where(high == 0, first[:1], outside[None, :, 15])
+    below = jnp.where(high == 0, outside[None, :, 0], last[-1:])
+    above = jnp.concatenate([above, last[:-1]])
+    below = jnp.concatenate([first[1:], below])
+    both = jnp.stack([above, below], axis=2).reshape(2, 2, 4, 2 * count, lanes)
+    return both.transpose(2, 0, 1, 3, 4).reshape(16, 2 * count, lanes)
 
 
 def half_spectrum_shards(hologram, background):
@@ -848,9 +989,9 @@
     depth, high = lax.axis_index("depth"), lax.axis_index("high")
     low, core = lax.axis_index("low"), lax.axis_index("core")
     as_scalar = lambda value: jnp.reshape(value, (1,)).astype(jnp.int32)
-    everyone = ("depth", "high", "low", "core")
     own = rows // 4
     block = ((high * 2 + low) * 2 + core) * 4 + depth
+    place = jnp.stack([block, jnp.int32(N // own)]).astype(jnp.int32)
 
     sections = row_forward(as_scalar(depth), hologram, background)
     data = lax.all_to_all(
@@ -869,47 +1010,41 @@
 
     def to_rows(halfway):
         parts = lax.all_to_all(
-            halfway.reshape(16, own, -1),
+            halfway.reshape(16, -1, halfway.shape[-1]),
             ("depth", "low", "core"),
             split_axis=0,
             concat_axis=0,
             tiled=True,
         )
-        return parts.reshape(4, 2, 2, own, -1)
-
-    halfway, spectrum = first_columns(as_scalar(high), data, kernels)
-    parts = [to_rows(halfway)]
-    cuts = [(1, 2), (3, planes - 3)]
-    for plane, count in cuts:
-        halfway = next_columns(as_scalar(high), plane, count, spectrum, kernels)
-        if plane > 1:
-            halfway, parts[-1] = lax.optimization_barrier((halfway, parts[-1]))
+        return parts.reshape(4, 2, 2, -1, halfway.shape[-1])
+
+    halfway, outside, spectrum = first_columns(as_scalar(high), data, kernels)
+    parts, borders = [to_rows(halfway)], [border_rows(halfway, outside, high)]
+    for plane, count in ((1, 2), (3, 1)):
+        halfway, outside = next_columns(as_scalar(high), plane, count, spectrum, kernels)
+        borders.append(border_rows(halfway, outside, high))
+        halfway = halfway.reshape(16, own, -1)
+        if plane == 3:
+            below = jnp.concatenate(borders, axis=1)
+            below = jnp.pad(below, ((0, 0), (0, 16 - 2 * planes), (0, 0)))
+            halfway = jnp.concatenate([halfway, below], axis=1)
+        ready = parts[-1]
+        if plane == 3:
+            first, first_edge = row_inverse(0, 1, parts[0], middle)
+            ready = ready, first, first_edge
+        elif plane == 1:
+            middle = nyquist_column(place, planes, data)
+            ready = ready, middle
+        halfway, ready = lax.optimization_barrier((halfway, ready))
+        if plane == 3:
+            parts[-1], first, first_edge = ready
+        else:
+            parts[-1], middle = ready
         parts.append(to_rows(halfway))
-    middle = nyquist_column(as_scalar(block), planes, data)
-    intensities, edges = [], []
-    for (plane, count), part in zip([(0, 1)] + cuts, parts):
-        intensity, edge = row_inverse(plane, count, part, middle)
-        intensities.append(intensity)
-        edges.append(edge)
-
-    order = [
-        ((d * 2 + h) * 2 + l) * 2 + c
-        for h in range(2)
-        for l in range(2)
-        for c in range(2)
-        for d in range(4)
-    ]
-    down = list(zip(order[:-1], order[1:]))
-    up = [(target, source) for source, target in down]
-    first = jnp.concatenate([edge[:, 0] for edge in edges])
-    last = jnp.concatenate([edge[:, 15] for edge in edges])
-    north = lax.ppermute(last, everyone, down)
-    south = lax.ppermute(first, everyone, up)
-    inner = exchange_depth(inner_focus(intensities, own // 4, own // 2))
-    north = jnp.where(block == 0, first, north)
-    south = jnp.where(block == N // own - 1, last, south)
-    outer = exchange_depth(outer_focus(intensities, north, south, own // 4))
-    return assemble(as_scalar(depth), inner, outer)
+    others, others_edge = row_inverse(1, 2, parts[1], middle)
+    best, spatial = early_focus(first, others)
+    upper, lower = last_rows(parts[2], middle, best, spatial, others, first_edge, others_edge)
+    return assemble(as_scalar(depth), *exchange_depth(upper, lower))
 
 
 def solution(mesh):

time: 291 us -> 263 us (0.904)
  blocking collectives: 54.4 us -> 0 us
  waiting for transfers between devices: 78.2 us -> 111 us
  starting transfers between devices: 34.2 us -> 28.9 us
  local copies, waits for them, and re-layouts: 10.1 us -> 6.95 us
    all_to_all x1 -> x0, blocking collectives: 54.4 us -> none  [to_rows(): lax.all_to_all(halfway.reshape(16, own, -1), ('depth', 'low', 'core'), sp...]
    all_to_all x2 -> x3, waiting for transfers between devices: 23.1 us -> 42.5 us  [to_rows(): lax.all_to_all(halfway.reshape(16, -1, halfway.shape[-1]), ('depth', 'low...]
    ppermute x14 -> x6, waiting for transfers between devices: 17.1 us -> 30.9 us  [the longest x1 10.9 us: exchange_depth(): lax.ppermute(a, 'depth', OVER_X)]
    ppermute x14 -> x6, starting transfers between devices: 19.7 us -> 7.74 us  [the longest x1 2.79 us: exchange_depth(): lax.ppermute(a, 'depth', OVER_X)]
    all_to_all x2 -> x3, starting transfers between devices: 8.17 us -> 14.8 us  [to_rows(): lax.all_to_all(halfway.reshape(16, -1, halfway.shape[-1]), ('depth', 'low...]
    pallas_call x3 -> x2, Pallas kernels: 21.7 us -> 15.3 us  [row_inverse(): pl.pallas_call(functools.partial(row_inverse_kernel, plane), grid=(count,...]
    pallas_call x2, Pallas kernels: 13.3 us -> 19 us  [the longest x1 9.94 us: last_rows(): pl.pallas_call(last_rows_kernel, in_specs=[hbm, vmem, hbm, hbm, hbm, hbm,...]
    unnamed x30 -> x10, local copies, waits for them, and re-layouts: 5.42 us -> 2.16 us
  transfers between devices with their start and end apart: 17 -> 10, of which waited for: 7 -> 8; matrix products, arithmetic and copies ran while one was open for 2% -> 3% of each run, Pallas kernels for 19% -> 27%
where the time goes in v3:
time: 263 us; the launch traced here: 262 us
  waiting for transfers between devices  111 us (42%)
  Pallas kernels  110 us (42%)
  starting transfers between devices  28.9 us (11%)
  local copies, waits for them, and re-layouts  6.95 us (3%)
  other arithmetic  3.99 us (2%)
    all_to_all x3, waiting for transfers between devices, to_rows(): lax.all_to_all(halfway.reshape(16, -1, halfway.shape[-1]), ('depth', 'low...  42.5 us
    all_to_all x1, waiting for transfers between devices, half_spectrum_shards(): lax.all_to_all(sections.reshape(8, rows + 16, 2 * LANE), ('high', 'low',...  38 us
    pallas_call x2, Pallas kernels, next_columns(): pl.pallas_call(next_columns_kernel, grid_spec=pltpu.PrefetchScalarGridSpe...  28.1 us
    pallas_call x2, Pallas kernels, row_inverse(): pl.pallas_call(functools.partial(row_inverse_kernel, plane), grid=(count,...  15.3 us
    pallas_call x1, Pallas kernels, first_columns(): pl.pallas_call(first_columns_kernel, grid_spec=pltpu.PrefetchScalarGridSp...  15.3 us
    all_to_all x3, starting transfers between devices, to_rows(): lax.all_to_all(halfway.reshape(16, -1, halfway.shape[-1]), ('depth', 'low...  14.8 us
    pallas_call x1, Pallas kernels, propagators(): pl.pallas_call(functools.partial(propagator_kernel, planes), grid=(OUT,),...  12 us
    ppermute x1, waiting for transfers between devices, exchange_depth(): lax.ppermute(a, 'depth', OVER_X)  10.9 us
  transfers between devices with their start and end apart: 10, of which 8 were waited for; matrix products, arithmetic and copies ran while one was open for 3% of the time, Pallas kernels for 27%

profile of v3, /device:TPU:0, one launch (start us, length us, event | category | flops | bytes accessed | tf_op | source)
XLA Modules:
  0.0 261.7 jit_solution(4008696217609217372)
XLA Ops:
  0.0 10.0 %row_forward.1 = bf16[2,2,2,528,256]{4,3,2,1,0:T(8,128)(2,1)} custom-call(s32[1]{0:T(128)} %bitcast.own, f32[256]{0:T(256)} %constant.54.clone.weights, bf16[512,4096]{1,0:T(8,128)(2,1)} %holo.1, bf16[512,4096]{1,0:T(8,128)(2,1)} %back.4, bf16[8,512,512]{2,1,0:T(8,128)(2,1)} %constant.53.clone.table), custom_call_target="tpu_custom_call" | custom-call | flops 10000000000 | bytes 12582912 | tf_op jit(solution)/shard_map/row_forward/pallas_call | solution.py:360
  10.0 6.3 %all-to-all-start = ((bf16[8,528,256]{2,1,0:T(8,128)(2,1)}), bf16[8,528,256]{2,1,0:T(8,128)(2,1)}, u32[]{:S(2)}, u32[]{:S(2)}) async-start(bf16[8,528,256]{2,1,0:T(8,128)(2,1)} %bitcast.91), calls=%async_computation | async-start | bytes 4325376 | tf_op jit(solution)/shard_map/all_to_all | solution.py:997
  16.3 0.5 multiply_multiply_fusion.fx2
  16.9 12.0 %propagators.1.kernels = f32[4,16,256,256]{3,2,1,0:T(8,128)} custom-call(f32[1,128]{1,0:T(1,128)} %multiply_multiply_fusion.fx2), custom_call_target="tpu_custom_call" | custom-call | flops 1000000000 | bytes 16777216 | tf_op jit(solution)/shard_map/propagators/pallas_call | solution.py:399
  28.9 38.0 %all-to-all-done.data = bf16[8,528,256]{2,1,0:T(8,128)(2,1)} async-done(((bf16[8,528,256]{2,1,0:T(8,128)(2,1)}), bf16[8,528,256]{2,1,0:T(8,128)(2,1)}, u32[]{:S(2)}, u32[]{:S(2)}) %all-to-all-start) | async-done | bytes 2162720 | tf_op jit(solution)/shard_map/all_to_all | solution.py:997
  66.9 15.3 %first_columns.1 = (bf16[2,2,2,2,128,512]{5,4,3,2,1,0:T(8,128)(2,1)}, bf16[1,16,512]{2,1,0:T(8,128)(2,1)}, bf16[16,256,256]{2,1,0:T(8,128)(2,1)}) custom-call(s32[1]{0:T(128)} %bitcast.1.half, bf16[8,528,256]{2,1,0:T(8,128)(2,1)} %all-to-all-done.data, f32[4,16,256,256]{3,2,1,0:T(8,128)} %propagators.1.kernels, bf16[512,256]{1,0:T(8,128)(2,1)} %constant.55.clone.outer, ...), custom_call_target="tpu_custom_call" | custom-call | flops 10000000000 | bytes 20971520 | tf_op jit(solution)/shard_map/first_columns/pallas_call | solution.py:519
  82.2 4.4 %all-to-all-start.1 = ((bf16[16,128,512]{2,1,0:T(8,128)(2,1)}), bf16[16,128,512]{2,1,0:T(8,128)(2,1)}, u32[]{:S(2)}, u32[]{:S(2)}) async-start(bf16[16,128,512]{2,1,0:T(8,128)(2,1)} %bitcast.90), calls=%async_computation.1 | async-start | bytes 4194304 | tf_op jit(solution)/shard_map/all_to_all | solution.py:1012
  86.7 0.6 pad_add_fusion.own
  87.3 6.9 %nyquist.1 = f32[256,128]{1,0:T(8,128)} custom-call(s32[2]{0:T(128)} %pad_add_fusion.own, bf16[8,528,256]{2,1,0:T(8,128)(2,1)} %all-to-all-done.data), custom_call_target="tpu_custom_call" | custom-call | flops 1000000000 | bytes 262144 | tf_op jit(solution)/shard_map/nyquist/pallas_call | solution.py:743
  94.2 18.3 %next_columns.3 = (bf16[2,2,2,2,128,1024]{5,4,3,2,1,0:T(8,128)(2,1)}, bf16[2,16,512]{2,1,0:T(8,128)(2,1)}) custom-call(s32[1]{0:T(128)} %bitcast.1.half, bf16[16,256,256]{2,1,0:T(8,128)(2,1)} %get-tuple-element.27.spectrum, f32[4,16,256,256]{3,2,1,0:T(8,128)} %propagators.1.kernels, bf16[16,512,256]{2,1,0:T(8,128)(2,1)} %constant.57.clone.inner_back, ...), custom_call_target="tpu_custom_call" | custom-call | flops 14000000000 | bytes 33554432 | tf_op jit(solution)/shard_map/next_columns/pallas_call | solution.py:561
  112.4 1.9 all-to-all-done.1
  114.3 4.7 %all-to-all-start.2 = ((bf16[16,128,1024]{2,1,0:T(8,128)(2,1)}), bf16[16,128,1024]{2,1,0:T(8,128)(2,1)}, u32[]{:S(2)}, u32[]{:S(2)}) async-start(bf16[16,128,1024]{2,1,0:T(8,128)(2,1)} %bitcast.88), calls=%async_computation.2 | async-start | bytes 8388608 | tf_op jit(solution)/shard_map/all_to_all | solution.py:1012
  119.1 1.0 fusion.9
  120.3 9.8 %next_columns.2 = (bf16[2,2,2,2,128,512]{5,4,3,2,1,0:T(8,128)(2,1)}, bf16[1,16,512]{2,1,0:T(8,128)(2,1)}) custom-call(s32[1]{0:T(128)} %bitcast.1.half, bf16[16,256,256]{2,1,0:T(8,128)(2,1)} %get-tuple-element.27.spectrum, f32[4,16,256,256]{3,2,1,0:T(8,128)} %propagators.1.kernels, bf16[16,512,256]{2,1,0:T(8,128)(2,1)} %constant.57.clone.inner_back, ...), custom_call_target="tpu_custom_call" | custom-call | flops 7000000000 | bytes 16777216 | tf_op jit(solution)/shard_map/next_columns/pallas_call | solution.py:561
  130.0 0.0 copy-start.2
  130.0 1.2 fusion.10
  131.4 0.8 fusion.5
  132.4 1.4 slice_reduce_fusion.1
  134.0 0.7 fusion.11
  134.9 0.1 pad_maximum_fusion.1
  135.0 0.1 copy.70
  135.1 0.1 fusion.4
  135.2 0.0 copy-done.2
  135.2 1.6 pad_maximum_fusion
  136.9 6.4 %row_inverse.2 = (bf16[1,128,4096]{2,1,0:T(8,128)(2,1)}, f32[1,16,4096]{2,1,0:T(8,128)}) custom-call(bf16[4,2,2,128,512]{4,3,2,1,0:T(8,128)(2,1)} %bitcast.26.parts, f32[256,128]{1,0:T(8,128)} %nyquist.1, bf16[8,512,512]{2,1,0:T(8,128)(2,1)} %constant.60.clone.table), custom_call_target="tpu_custom_call" | custom-call | flops 3000000000 | bytes 8388608 | tf_op jit(solution)/shard_map/row_inverse/pallas_call | solution.py:666
  143.3 27.9 %all-to-all-done.2 = bf16[16,128,1024]{2,1,0:T(8,128)(2,1)} async-done(((bf16[16,128,1024]{2,1,0:T(8,128)(2,1)}), bf16[16,128,1024]{2,1,0:T(8,128)(2,1)}, u32[]{:S(2)}, u32[]{:S(2)}) %all-to-all-start.2) | async-done | bytes 4194336 | tf_op jit(solution)/shard_map/all_to_all | solution.py:1012
  171.3 5.6 %all-to-all-start.3 = ((bf16[16,144,512]{2,1,0:T(8,128)(2,1)}), bf16[16,144,512]{2,1,0:T(8,128)(2,1)}, u32[]{:S(2)}, u32[]{:S(2)}) async-start(bf16[16,144,512]{2,1,0:T(8,128)(2,1)} %pad_maximum_fusion), calls=%async_computation.3 | async-start | bytes 4718592 | tf_op jit(solution)/shard_map/all_to_all | solution.py:1012
  176.9 8.9 %row_inverse.3 = (bf16[2,128,4096]{2,1,0:T(8,128)(2,1)}, f32[2,16,4096]{2,1,0:T(8,128)}) custom-call(bf16[4,2,2,128,1024]{4,3,2,1,0:T(8,128)(2,1)} %bitcast.28.parts, f32[256,128]{1,0:T(8,128)} %nyquist.1, bf16[8,512,512]{2,1,0:T(8,128)(2,1)} %constant.60.clone.table), custom_call_target="tpu_custom_call" | custom-call | flops 6000000000 | bytes 16777216 | tf_op jit(solution)/shard_map/row_inverse/pallas_call | solution.py:666
  185.7 9.0 %early_focus.1 = (bf16[128,4096]{1,0:T(8,128)(2,1)}, f32[128,4096]{1,0:T(8,128)}) custom-call(bf16[1,128,4096]{2,1,0:T(8,128)(2,1)} %get-tuple-element.40.first, bf16[2,128,4096]{2,1,0:T(8,128)(2,1)} %get-tuple-element.42.others), custom_call_target="tpu_custom_call" | custom-call | flops 1000000000 | bytes 12582912 | tf_op jit(solution)/shard_map/early_focus/pallas_call | solution.py:800
  194.8 12.6 %all-to-all-done.3 = bf16[16,144,512]{2,1,0:T(8,128)(2,1)} async-done(((bf16[16,144,512]{2,1,0:T(8,128)(2,1)}), bf16[16,144,512]{2,1,0:T(8,128)(2,1)}, u32[]{:S(2)}, u32[]{:S(2)}) %all-to-all-start.3) | async-done | bytes 2359328 | tf_op jit(solution)/shard_map/all_to_all | solution.py:1012
  207.4 9.9 %last_rows.1 = (bf16[64,4096]{1,0:T(8,128)(2,1)}, bf16[64,4096]{1,0:T(8,128)(2,1)}) custom-call(bf16[4,2,2,144,512]{4,3,2,1,0:T(8,128)(2,1)} %bitcast.29.parts, f32[256,128]{1,0:T(8,128)} %nyquist.1, bf16[8,512,512]{2,1,0:T(8,128)(2,1)} %constant.60.clone.table, bf16[128,4096]{1,0:T(8,128)(2,1)} %get-tuple-element.43.best, ...), custom_call_target="tpu_custom_call" | custom-call | flops 3000000000 | bytes 16777216 | tf_op jit(solution)/shard_map/last_rows/pallas_call | solution.py:910
  217.4 2.8 %collective-permute-start = (bf16[64,4096]{1,0:T(8,128)(2,1)}, bf16[64,4096]{1,0:T(8,128)(2,1)S(1)}, u32[]{:S(2)}, u32[]{:S(2)}) collective-permute-start(bf16[64,4096]{1,0:T(8,128)(2,1)} %get-tuple-element.47.refs_0_), channel_id=1, source_target_pairs={{0,8},{8,0},{16,24},{24,16},{1,9},{9,1},{17,25},{25,17},{2,10},{10... | collective-permute-start | bytes 1572872 | tf_op jit(solution)/shard_map/ppermute | solution.py:967
  220.1 1.4 collective-permute-start.4
  221.6 0.6 collective-permute-start.1
  222.2 0.1 collective-permute-start.3
  222.3 10.9 %collective-permute-done.refs_1_ = bf16[64,4096]{1,0:T(8,128)(2,1)S(1)} collective-permute-done((bf16[64,4096]{1,0:T(8,128)(2,1)}, bf16[64,4096]{1,0:T(8,128)(2,1)S(1)}, u32[]{:S(2)}, u32[]{:S(2)}) %collective-permute-start) | collective-permute-done | bytes 524320 | tf_op jit(solution)/shard_map/ppermute | solution.py:967
  233.1 1.4 collective-permute-start.2
  234.6 0.7 collective-permute-done.4.refs_6_
  235.2 1.4 collective-permute-start.5
  236.6 9.8 %collective-permute-done.1.refs_2_ = bf16[64,4096]{1,0:T(8,128)(2,1)S(1)} collective-permute-done((bf16[64,4096]{1,0:T(8,128)(2,1)}, bf16[64,4096]{1,0:T(8,128)(2,1)S(1)}, u32[]{:S(2)}, u32[]{:S(2)}) %collective-permute-start.1) | collective-permute-done | bytes 524320 | tf_op jit(solution)/shard_map/ppermute | solution.py:968
  246.5 0.0 collective-permute-done.3.refs_5_
  246.5 9.6 %collective-permute-done.2.refs_3_ = bf16[64,4096]{1,0:T(8,128)(2,1)S(1)} collective-permute-done((bf16[64,4096]{1,0:T(8,128)(2,1)S(1)}, bf16[64,4096]{1,0:T(8,128)(2,1)S(1)}, u32[]{:S(2)}, u32[]{:S(2)}) %collective-permute-start.2) | collective-permute-done | bytes 524320 | tf_op jit(solution)/shard_map/ppermute | solution.py:968
  256.0 0.0 collective-permute-done.5.refs_7_
  256.0 0.0 copy-start
  256.0 1.0 copy-done
  257.1 0.0 copy-start.1
  257.1 1.0 copy-done.1
  258.1 3.6 %assemble.1 = f32[512,4096]{1,0:T(8,128)} custom-call(s32[1]{0:T(128)} %bitcast.own, bf16[64,4096]{1,0:T(8,128)(2,1)S(1)} %copy-done, bf16[64,4096]{1,0:T(8,128)(2,1)S(1)} %collective-permute-done.refs_1_, bf16[64,4096]{1,0:T(8,128)(2,1)S(1)} %collective-permute-done.1.refs_2_, bf16[64,4096]{1,0:T(8,128)(2,1)S(1)} %collective-permute-done.2.refs_3_, ...), custom_call_target="tpu_custom_call" | custom-call | flops 1000000 | bytes 12582912 | tf_op jit(solution)/shard_map/assemble/pallas_call | solution.py:947
  (37 shorter events, 0.7 us)
Async XLA Ops:
  10.0 56.9 %all-to-all-start = ((bf16[8,528,256]{2,1,0:T(8,128)(2,1)}), bf16[8,528,256]{2,1,0:T(8,128)(2,1)}, u32[]{:S(2)}, u32[]{:S(2)}) async-start(bf16[8,528,256]{2,1,0:T(8,128)(2,1)} %bitcast.91), calls=%async_computation | async-start | bytes 4325376 | tf_op jit(solution)/shard_map/all_to_all | solution.py:997
  82.2 32.2 %all-to-all-start.1 = ((bf16[16,128,512]{2,1,0:T(8,128)(2,1)}), bf16[16,128,512]{2,1,0:T(8,128)(2,1)}, u32[]{:S(2)}, u32[]{:S(2)}) async-start(bf16[16,128,512]{2,1,0:T(8,128)(2,1)} %bitcast.90), calls=%async_computation.1 | async-start | bytes 4194304 | tf_op jit(solution)/shard_map/all_to_all | solution.py:1012
  114.3 56.9 %all-to-all-start.2 = ((bf16[16,128,1024]{2,1,0:T(8,128)(2,1)}), bf16[16,128,1024]{2,1,0:T(8,128)(2,1)}, u32[]{:S(2)}, u32[]{:S(2)}) async-start(bf16[16,128,1024]{2,1,0:T(8,128)(2,1)} %bitcast.88), calls=%async_computation.2 | async-start | bytes 8388608 | tf_op jit(solution)/shard_map/all_to_all | solution.py:1012
  130.0 5.2 %copy-start.2 = (bf16[2,2,2,2,128,512]{5,4,3,2,1,0:T(8,128)(2,1)S(1)}, bf16[2,2,2,2,128,512]{5,4,3,2,1,0:T(8,128)(2,1)}, u32[]{:S(2)}) copy-start(bf16[2,2,2,2,128,512]{5,4,3,2,1,0:T(8,128)(2,1)} %get-tuple-element.28) | copy-start | bytes 6291460
  171.3 36.2 %all-to-all-start.3 = ((bf16[16,144,512]{2,1,0:T(8,128)(2,1)}), bf16[16,144,512]{2,1,0:T(8,128)(2,1)}, u32[]{:S(2)}, u32[]{:S(2)}) async-start(bf16[16,144,512]{2,1,0:T(8,128)(2,1)} %pad_maximum_fusion), calls=%async_computation.3 | async-start | bytes 4718592 | tf_op jit(solution)/shard_map/all_to_all | solution.py:1012
  217.4 15.8 %collective-permute-start = (bf16[64,4096]{1,0:T(8,128)(2,1)}, bf16[64,4096]{1,0:T(8,128)(2,1)S(1)}, u32[]{:S(2)}, u32[]{:S(2)}) collective-permute-start(bf16[64,4096]{1,0:T(8,128)(2,1)} %get-tuple-element.47.refs_0_), channel_id=1, source_target_pairs={{0,8},{8,0},{16,24},{24,16},{1,9},{9,1},{17,25},{25,17},{2,10},{10... | collective-permute-start | bytes 1572872 | tf_op jit(solution)/shard_map/ppermute | solution.py:967
  220.1 15.1 %collective-permute-start.4 = (bf16[64,4096]{1,0:T(8,128)(2,1)}, bf16[64,4096]{1,0:T(8,128)(2,1)S(1)}, u32[]{:S(2)}, u32[]{:S(2)}) collective-permute-start(bf16[64,4096]{1,0:T(8,128)(2,1)} %get-tuple-element.48.refs_4_), channel_id=1, source_target_pairs={{0,16},{8,24},{16,0},{24,8},{1,17},{9,25},{17,1},{25,9},{2,18},{10... | collective-permute-start | bytes 1572872 | tf_op jit(solution)/shard_map/ppermute | solution.py:967
  221.6 24.9 %collective-permute-start.1 = (bf16[64,4096]{1,0:T(8,128)(2,1)}, bf16[64,4096]{1,0:T(8,128)(2,1)S(1)}, u32[]{:S(2)}, u32[]{:S(2)}) collective-permute-start(bf16[64,4096]{1,0:T(8,128)(2,1)} %get-tuple-element.47.refs_0_), channel_id=1, source_target_pairs={{0,16},{8,24},{16,0},{24,8},{1,17},{9,25},{17,1},{25,9},{2,18},{10... | collective-permute-start | bytes 1572872 | tf_op jit(solution)/shard_map/ppermute | solution.py:968
  222.2 24.3 %collective-permute-start.3 = (bf16[64,4096]{1,0:T(8,128)(2,1)}, bf16[64,4096]{1,0:T(8,128)(2,1)S(1)}, u32[]{:S(2)}, u32[]{:S(2)}) collective-permute-start(bf16[64,4096]{1,0:T(8,128)(2,1)} %get-tuple-element.48.refs_4_), channel_id=1, source_target_pairs={{0,8},{8,0},{16,24},{24,16},{1,9},{9,1},{17,25},{25,17},{2,10},{10... | collective-permute-start | bytes 1572872 | tf_op jit(solution)/shard_map/ppermute | solution.py:969
  233.1 22.9 %collective-permute-start.2 = (bf16[64,4096]{1,0:T(8,128)(2,1)S(1)}, bf16[64,4096]{1,0:T(8,128)(2,1)S(1)}, u32[]{:S(2)}, u32[]{:S(2)}) collective-permute-start(bf16[64,4096]{1,0:T(8,128)(2,1)S(1)} %collective-permute-done.refs_1_), channel_id=1, source_target_pairs={{0,16},{8,24},{16,0},{24,8},{1,17},{9,25},{17,1},{25,9},{2,18},{10... | collective-permute-start | bytes 1572872 | tf_op jit(solution)/shard_map/ppermute | solution.py:968
  235.2 20.8 %collective-permute-start.5 = (bf16[64,4096]{1,0:T(8,128)(2,1)S(1)}, bf16[64,4096]{1,0:T(8,128)(2,1)S(1)}, u32[]{:S(2)}, u32[]{:S(2)}) collective-permute-start(bf16[64,4096]{1,0:T(8,128)(2,1)S(1)} %collective-permute-done.4.refs_6_), channel_id=1, source_target_pairs={{0,8},{8,0},{16,24},{24,16},{1,9},{9,1},{17,25},{25,17},{2,10},{10... | collective-permute-start | bytes 1572872 | tf_op jit(solution)/shard_map/ppermute | solution.py:969
  256.0 1.0 copy-start
  257.1 1.0 copy-start.1

commit v4 on v3

--- a/solution.py
+++ b/solution.py
@@ -209,52 +209,64 @@
 
 
 def row_forward_weights():
-    turn = 2.0 * np.pi * np.arange(CLS)[:, None] * np.arange(OUT)[None, :] / OUT
-    re, im = np.cos(turn), -np.sin(turn)
-    im[0] = (-1.0) ** np.arange(OUT)
-    return np.stack([re, im], axis=1).reshape(-1).astype(np.float32)
+    a = np.arange(1, 5)
+    rows = []
+    for d in range(CLS // 2):
+        even, odd = (2.0 * np.pi * c * a / OUT for c in (2 * d, 2 * d + 1))
+        parts = np.cos(even), -np.sin(even[:3]), [float(d == 0)], np.cos(odd[:3]), -np.sin(odd), [0.0]
+        rows.append(np.concatenate(parts))
+    return np.concatenate(rows).astype(np.float32)
 
 
 def row_inverse_tables():
-    freq = slot_frequencies()
-    theta = angles(freq[:, :, None] * np.arange(INN)[None, None, :])
-    cos, sin = np.cos(theta) / 32.0, np.sin(theta) / 32.0
-    full = np.zeros((CLS, 2, INN, 2, INN))
-    full[:, 0, :, 0], full[:, 0, :, 1] = cos, sin
-    full[:, 1, :, 0], full[:, 1, :, 1] = -sin, cos
-    half = INN // 2
-    full[0] = 0.0
-    full[0, 0, :half, 0], full[0, 1, :half, 0] = cos[0, :half], -sin[0, :half]
-    full[0, 0, half:, 1], full[0, 1, half:, 1] = cos[0, half:], -sin[0, half:]
-    full[0, 0, 0, 0] = 1.0 / 64.0
-    full[0, 1, 0, 0] = (-1.0) ** np.arange(INN) / 64.0
-    full = full.reshape(CLS, 2, 2, LANE, 2 * INN).transpose(0, 2, 1, 3, 4)
-    return full.reshape(CLS, 2 * INN, 2 * INN).astype(jnp.bfloat16)
+    half = np.arange(INN // 2)
+    position = np.arange(INN)[None, :]
+    full = np.zeros((2, 2, INN, 2, INN))
+    for first, place in ((0, 0), (CLS, 1)):
+        theta = angles((first + OUT * half)[:, None] * position)
+        rows = slice(place * INN // 2, (place + 1) * INN // 2)
+        full[0, 0, rows, place], full[0, 1, rows, place] = np.cos(theta), -np.sin(theta)
+    full[0, 0, 0, 0] = 0.5
+    full[0, 1, 0, 0] = 0.5 * (-1.0) ** np.arange(INN)
+    theta = angles(OUT * np.arange(INN)[:, None] * position)
+    full[1, 0, :, 0], full[1, 0, :, 1] = np.cos(theta), np.sin(theta)
+    full[1, 1, :, 0], full[1, 1, :, 1] = -np.sin(theta), np.cos(theta)
+    full = full.reshape(2, 2, 2, LANE, 2 * INN).transpose(0, 2, 1, 3, 4) / 32.0
+    turn = angles(np.arange(CLS)[:, None] * position)
+    turn = np.concatenate([np.cos(turn), np.sin(turn)]).astype(np.float32)
+    return full.reshape(2, 2 * INN, 2 * INN).astype(jnp.bfloat16), turn
 
 
 def column_tables():
     turn = 2.0 * np.pi * np.arange(OUT)[:, None] * np.arange(OUT)[None, :] / OUT
     eye = np.eye(16)
     outer_cos, outer_sin = np.kron(np.cos(turn), eye) / 4.0, np.kron(np.sin(turn), eye) / 4.0
-    outer = np.concatenate([outer_cos, -outer_sin])
-    outer = outer.reshape(-1, 8, 2, 16).swapaxes(1, 2).reshape(outer.shape)
+    complex_form = lambda cos, sin: np.concatenate(
+        [np.concatenate([cos, -sin], axis=-1), np.concatenate([sin, cos], axis=-1)], axis=-2
+    )
+    slabs = lambda table: table.reshape(-1, 8, 2, 16).swapaxes(1, 2).reshape(table.shape)
+    outer = complex_form(slabs(outer_cos), slabs(-outer_sin))
     half_rows = outer_cos.shape[0] // 2
+    cut = lambda table, begin, size: table[begin : begin + size]
     back = np.stack(
         [
-            np.concatenate([outer_cos[i * half_rows :][:half_rows], outer_sin[i * half_rows :][:half_rows]])
-            for i in range(2)
+            complex_form(cut(outer_cos, begin, half_rows), cut(outer_sin, begin, half_rows))
+            for begin in (0, half_rows)
         ]
     )
     beyond = np.stack(
-        [np.concatenate([outer_cos[a * 16 :][:16], outer_sin[a * 16 :][:16]]) for a in (8, 7)]
+        [complex_form(cut(outer_cos, a * 16, 16), cut(outer_sin, a * 16, 16)) for a in (8, 7)]
     )
-    freq = np.arange(OUT)[:, None] + OUT * np.arange(INN)[None, :]
-    theta = angles(freq[:, :, None] * np.arange(INN)[None, None, :])
-    inner = np.concatenate([np.cos(theta), -np.sin(theta)], axis=1) / 16.0
-    theta = theta.transpose(0, 2, 1)
-    inner_back = np.concatenate([np.cos(theta), np.sin(theta)], axis=1) / 16.0
+    theta = angles(OUT * np.arange(INN)[:, None] * np.arange(INN)[None, :])
+    inner = complex_form(np.cos(theta), -np.sin(theta)) / 16.0
+    inner_back = complex_form(np.cos(theta), np.sin(theta)) / 16.0
+    turn = angles(np.arange(OUT)[:, None] * np.arange(INN)[None, :])
+    by_chunk = turn.reshape(OUT, 16, 16).swapaxes(1, 2).reshape(INN, 16)
+    twist = np.zeros((2, INN, LANE), np.float32)
+    for i, table in enumerate((by_chunk, turn.T)):
+        twist[i, :, :16], twist[i, :, 16:32] = np.cos(table), np.sin(table)
     cast = lambda table: table.astype(jnp.bfloat16)
-    return cast(outer), cast(inner), cast(inner_back), cast(back), cast(beyond)
+    return cast(outer), cast(inner), cast(inner_back), cast(back), cast(beyond), twist
 
 
 def dot(left, right):
@@ -304,76 +316,136 @@
     return jnp.where(natural >= N // 2, natural - N, natural).astype(jnp.float32) * (1.0 / N)
 
 
-def row_forward_kernel(own, weights, holo, back, table, out, acc, held):
-    step = pl.program_id(0)
+CHUNK = 64
+
+
+def sixteen_sums(term, w):
+    c0, c8 = term(0), term(8)
+    plus, minus = c0 + c8, c0 - c8
+    c4, c12 = term(4), term(12)
+    e4, o4 = c4 + c12, c4 - c12
+    total = plus + e4
+    eighth = total
+    re_even = plus + w(3) * e4
+    im_even = None
+    re_odd, im_odd = minus, w(14) * o4
+    for a in (1, 2, 3):
+        p, q, r, s = term(a), term(16 - a), term(8 - a), term(8 + a)
+        e, o, f, h = p + q, p - q, r + s, r - s
+        both = e + f
+        total = total + both
+        eighth = eighth - both if a % 2 else eighth + both
+        re_even = re_even + w(a - 1) * both
+        term_im = w(3 + a) * (o - h)
+        im_even = term_im if im_even is None else im_even + term_im
+        re_odd = re_odd + w(7 + a) * (e - f)
+        im_odd = im_odd + w(10 + a) * (o + h)
+    return re_even, im_even + w(7) * eighth, re_odd, im_odd, total
+
+
+def row_forward_kernel(
+    own, weights, holo, back, table, out, holo_buf, back_buf, table_buf, acc, result, held, sems
+):
     rows = holo.shape[0]
     group = own[0]
+    chunks = rows // CHUNK
+    loads = []
+    for i in range(chunks):
+        here = pl.ds(i * CHUNK, CHUNK)
+        loads.append(
+            (
+                pltpu.make_async_copy(holo.at[here], holo_buf.at[here], sems.at[0, i]),
+                pltpu.make_async_copy(back.at[here], back_buf.at[here], sems.at[1, i]),
+            )
+        )
+        for load in loads[-1]:
+            load.start()
+        if i == 0:
+            tables = pltpu.make_async_copy(table.at[pl.ds(2 * group, 2)], table_buf, sems.at[4, 0])
+            tables.start()
     lane = lax.broadcasted_iota(jnp.int32, (16, INN), 1)
     sign = jnp.where(lane % 2 == 0, 1.0, -1.0).astype(jnp.bfloat16)
-
-    def strip(i, carry):
-        here = pl.ds(pl.multiple_of(i * 16, 16), 16)
-        sums = [jnp.zeros((16, INN), jnp.float32) for _ in range(5)]
-        for a in range(OUT):
-            there = pl.ds(a * INN, INN)
-            value = holo[here, there].astype(jnp.float32) / back[here, there].astype(jnp.float32)
-            value = (value - 1.0).astype(jnp.bfloat16).astype(jnp.float32)
+    stores = []
+    for chunk in range(chunks):
+        for load in loads[chunk]:
+            load.wait()
+
+        def strip(i, carry):
+            here = pl.ds(pl.multiple_of(chunk * CHUNK + i * 16, 16), 16)
+
+            def term(a):
+                there = pl.ds(a * INN, INN)
+                below = back_buf[here, there].astype(jnp.float32)
+                inverse = pl.reciprocal(below, approx=True)
+                inverse = inverse * (2.0 - below * inverse)
+                inverse = inverse * (2.0 - below * inverse)
+                value = holo_buf[here, there].astype(jnp.float32) * inverse
+                return (value - 1.0).astype(jnp.bfloat16).astype(jnp.float32)
+
+            sums = sixteen_sums(term, lambda n: weights[group * 16 + n])
             for q in range(4):
-                w = weights[(group * 2 + q // 2) * (2 * OUT) + (q % 2) * OUT + a]
-                sums[q] = sums[q] + value * w
-            sums[4] = sums[4] + value
-        for q in range(4):
-            acc[q // 2, here, pl.ds((q % 2) * INN, INN)] = sums[q].astype(jnp.bfloat16)
-        acc[2, here, pl.ds(0, INN)] = sums[4].astype(jnp.bfloat16)
-        return carry
-
-    lax.fori_loop(0, rows // 16, strip, 0)
-    here = pl.ds(pl.multiple_of(step * rows, rows), rows)
-    for q in range(2):
-        result = dot(acc[q], table[q]).astype(jnp.bfloat16)
-        for low in range(2):
-            part = result[:, low * 2 * LANE : (low + 1) * 2 * LANE]
-            for high in range(2):
-                out[high, low, q, here, :] = part
-    alternating = lax.dot_general(
-        sign, acc[2, :, :INN], (((1,), (1,)), ((), ())), preferred_element_type=jnp.float32
-    )
-    held[step] = alternating * (1.0 / 64.0)
-
-    @pl.when(step == pl.num_programs(0) - 1)
-    def _():
-        rows_of = [jnp.concatenate([held[2 * r], held[2 * r + 1]], axis=1) for r in range(2)]
-        extra = jnp.where(lax.broadcasted_iota(jnp.int32, (16, INN), 0) == 0, rows_of[0], rows_of[1])
-        extra = extra.astype(jnp.bfloat16)
-        for high in range(2):
+                acc[q // 2, here, pl.ds((q % 2) * INN, INN)] = sums[q].astype(jnp.bfloat16)
+            acc[2, here, pl.ds(0, INN)] = sums[4].astype(jnp.bfloat16)
+            return carry
+
+        lax.fori_loop(0, CHUNK // 16, strip, 0)
+        batch = rows // 2 // CHUNK
+        if chunk % batch != batch - 1:
+            continue
+        if chunk < batch:
+            tables.wait()
+        begin, end = (chunk + 1 - batch) * CHUNK, (chunk + 1) * CHUNK
+        for q in range(2):
+            both = dot(acc[q, begin:end], table_buf[q]).astype(jnp.bfloat16)
+            for low in range(2):
+                part = both[:, low * 2 * LANE : (low + 1) * 2 * LANE]
+                result[low, q, begin:end, :] = part
+        held[chunk // batch] = lax.dot_general(
+            sign,
+            acc[2, begin:end, :INN],
+            (((1,), (1,)), ((), ())),
+            preferred_element_type=jnp.float32,
+        )
+        here = pl.ds(begin, end - begin)
+        if chunk == chunks - 1:
+            index = lax.broadcasted_iota(jnp.int32, (16, INN), 0)
+            extra = jnp.where(index == 0, held[0], held[1]) * (1.0 / 64.0)
             for low in range(2):
                 for q in range(2):
-                    out[high, low, q, pl.ds(4 * rows, 16), :] = extra
+                    result[low, q, rows:, :] = extra.astype(jnp.bfloat16)
+            here = pl.ds(begin, end - begin + 16)
+        for high in range(2):
+            source, target = result.at[:, :, here, :], out.at[high, :, :, here, :]
+            stores.append(pltpu.make_async_copy(source, target, sems.at[2 + high, chunk]))
+            stores[-1].start()
+    for store in stores:
+        store.wait()
 
 
 def row_forward(own, hologram, background):
     rows = hologram.shape[0]
-    block = LANE
     table = jnp.asarray(row_forward_tables())
     weights = jnp.asarray(row_forward_weights())
-    shape = (2, 2, 2, rows + 16, 2 * LANE)
+    hbm = pl.BlockSpec(memory_space=pl.ANY)
+    chunks = rows // CHUNK
     return pl.pallas_call(
         row_forward_kernel,
         grid_spec=pltpu.PrefetchScalarGridSpec(
             num_scalar_prefetch=2,
-            grid=(rows // block,),
-            in_specs=[
-                pl.BlockSpec((block, N), lambda i, o, w: (i, 0)),
-                pl.BlockSpec((block, N), lambda i, o, w: (i, 0)),
-                pl.BlockSpec((2, 2 * INN, 2 * INN), lambda i, o, w: (o[0], 0, 0)),
-            ],
-            out_specs=pl.BlockSpec(shape, lambda i, o, w: (0, 0, 0, 0, 0)),
+            grid=(1,),
+            in_specs=[hbm] * 3,
+            out_specs=hbm,
             scratch_shapes=[
-                pltpu.VMEM((3, block, 2 * INN), jnp.bfloat16),
-                pltpu.VMEM((rows // block, 16, LANE), jnp.float32),
+                pltpu.VMEM((rows, N), jnp.bfloat16),
+                pltpu.VMEM((rows, N), jnp.bfloat16),
+                pltpu.VMEM((2, 2 * INN, 2 * INN), jnp.bfloat16),
+                pltpu.VMEM((3, rows, 2 * INN), jnp.bfloat16),
+                pltpu.VMEM((2, 2, rows + 16, 2 * LANE), jnp.bfloat16),
+                pltpu.VMEM((2, 16, INN), jnp.float32),
+                pltpu.SemaphoreType.DMA((5, chunks)),
             ],
         ),
-        out_shape=jax.ShapeDtypeStruct(shape, jnp.bfloat16),
+        out_shape=jax.ShapeDtypeStruct((2, 2, 2, rows + 16, 2 * LANE), jnp.bfloat16),
         compiler_params=pltpu.CompilerParams(vmem_limit_bytes=VMEM),
         cost_estimate=pl.CostEstimate(flops=10**10, bytes_accessed=12 * MIB, transcendentals=0),
         name="row_forward",
@@ -389,8 +461,8 @@
         fy = signed_fraction(step + OUT * position)
         (kr, ki), (sr, si) = start_and_step(fy * fy + fx2[...])
         for g in range(planes):
-            out[g, 0, rows, :LANE] = kr
-            out[g, 0, rows, LANE:] = ki
+            out[g, 0, rows, :LANE] = kr.astype(jnp.bfloat16)
+            out[g, 0, rows, LANE:] = ki.astype(jnp.bfloat16)
             if g + 1 < planes:
                 kr, ki = kr * sr - ki * si, kr * si + ki * sr
 
@@ -401,187 +473,246 @@
         grid=(OUT,),
         in_specs=[pl.BlockSpec((1, LANE), lambda i: (0, 0))],
         out_specs=pl.BlockSpec((planes, 1, INN, 2 * LANE), lambda i: (0, i, 0, 0)),
-        out_shape=jax.ShapeDtypeStruct((planes, OUT, INN, 2 * LANE), jnp.float32),
+        out_shape=jax.ShapeDtypeStruct((planes, OUT, INN, 2 * LANE), jnp.bfloat16),
         compiler_params=pltpu.CompilerParams(vmem_limit_bytes=VMEM),
         cost_estimate=pl.CostEstimate(flops=10**9, bytes_accessed=16 * MIB, transcendentals=10**6),
         name="propagators",
     )(fx2)
 
 
-PER = 4
-
-
-def mix_and_open(k, slot, yr, yi, kernels, inner_back, mixed, second):
-    width = LANE
-    for part in range(2):
-        factor = kernels[:, part * width : (part + 1) * width]
-        at = part * 2 * width
-        mixed[slot, :, at : at + width] = (yr * factor).astype(jnp.bfloat16)
-        mixed[slot, :, at + width : at + 2 * width] = (yi * factor).astype(jnp.bfloat16)
-    both = dot(inner_back, mixed[slot])
-    for part in range(2):
-        lanes = slice(part * 2 * width, (part + 1) * 2 * width)
-        re, im = split_complex(both[:, lanes], width)
-        second[k, :, lanes] = jnp.concatenate([re, im], axis=1).astype(jnp.bfloat16)
-
-
-def close_columns(half, step, back, beyond, second, out, outside):
-    width = LANE
-    start = step * PER
-
-    @pl.when(step == 0)
-    def _():
-        here = pl.ds(pl.multiple_of(half[0] * (INN - 16), 16), 16)
-        both = dot(beyond[0], second[:, here, :].reshape(OUT * 16, 4 * width))
+PAIRS = OUT // 2
+
+
+def mix_and_open(pair, both, kernels, inner_back, twist, mixed, second):
+    wide = 2 * LANE
+    for k in range(2):
+        yr, yi = (both[p * INN : (p + 1) * INN, k * LANE : (k + 1) * LANE] for p in range(2))
         for part in range(2):
-            lanes = slice(part * 2 * width, (part + 1) * 2 * width)
-            re, im = split_complex(both[:, lanes], width)
-            outside[0, :, lanes] = jnp.concatenate([re, im], axis=1).astype(jnp.bfloat16)
-
-    for c in range(PER):
-        here = pl.ds(pl.multiple_of((start + c) * 16, 16), 16)
-        both = dot(back[0], second[:, here, :].reshape(OUT * 16, 4 * width))
-        rows = slice(c * 16, (c + 1) * 16)
+            factor = kernels[k, :, part * LANE : (part + 1) * LANE].astype(jnp.float32)
+            lanes = slice(k * wide + part * LANE, k * wide + (part + 1) * LANE)
+            mixed[:INN, lanes] = (yr * factor).astype(jnp.bfloat16)
+            mixed[INN:, lanes] = (yi * factor).astype(jnp.bfloat16)
+    opened = dot(inner_back[...], mixed[...])
+    for k in range(2):
+        at = pair * 2 + k
+        re, im = (opened[p * INN : (p + 1) * INN, k * wide : (k + 1) * wide] for p in range(2))
+        cos, sin = twist[1, :, at : at + 1], twist[1, :, 16 + at : 17 + at]
+        second[0, at] = (re * cos - im * sin).astype(jnp.bfloat16)
+        second[1, at] = (re * sin + im * cos).astype(jnp.bfloat16)
+
+
+def outer_block(second, here):
+    return second[:, :, here, :].reshape(2 * OUT * 16, 2 * LANE)
+
+
+def spread(both):
+    rows = both.shape[0] // 2
+    re, im = both[:rows], both[rows:]
+    return [re[:, :LANE], im[:, :LANE], re[:, LANE:], im[:, LANE:]]
+
+
+def open_outside(half, beyond, second, outside):
+    here = pl.ds(pl.multiple_of(half[0] * (INN - 16), 16), 16)
+    both = dot(beyond, outer_block(second, here)).astype(jnp.bfloat16)
+    for i, value in enumerate(spread(both)):
+        outside[:, i * LANE : (i + 1) * LANE] = value
+
+
+def close_chunk(here, back, second, store):
+    both = dot(back, outer_block(second, here)).astype(jnp.bfloat16)
+    for i, value in enumerate(spread(both)):
+        value = value.reshape(2, 2, 2, 16, LANE)
+        for low in range(2):
+            for core in range(2):
+                for high in range(2):
+                    store(high, low, core, slice(i * LANE, (i + 1) * LANE), value[low, core, high])
+
+
+def first_columns_kernel(
+    half, data, kernels, outer_in, inner_in, inner_back_in, back_in, beyond_in, twist_in,
+    out, spectrum, outside,
+    data_buf, kernel_buf, outer, inner, inner_back, back, beyond, twist,
+    out_buf, spectrum_buf, first, mixed, second, sems,
+):
+    rows = data_buf.shape[1]
+    early = [
+        pltpu.make_async_copy(source, target, sems.at[3, i])
+        for i, (source, target) in enumerate(
+            (
+                (data.at[:, pl.ds(0, rows), :], data_buf),
+                (outer_in, outer),
+                (twist_in, twist),
+                (inner_in, inner),
+                (inner_back_in, inner_back),
+                (back_in.at[half[0]], back),
+                (beyond_in.at[half[0]], beyond),
+            )
+        )
+    ]
+    for load in early:
+        load.start()
+    loads = []
+    for pair in range(PAIRS):
+        here = pl.ds(2 * pair, 2)
+        loads.append(
+            pltpu.make_async_copy(kernels.at[0, here], kernel_buf.at[here], sems.at[1, pair])
+        )
+        loads[-1].start()
+    for load in early[:3]:
+        load.wait()
+    for i in range(0, INN // 16, 2):
+        pieces = []
         for part in range(2):
-            lanes = slice(part * 2 * width, (part + 1) * 2 * width)
-            re, im = split_complex(both[:, lanes], width)
-            value = jnp.concatenate([re, im], axis=1).astype(jnp.bfloat16)
-            value = value.reshape(2, 2, 2, 16, 2 * width)
-            for low in range(2):
-                for core in range(2):
-                    for high in range(2):
-                        out[high, 0, low, core, rows, lanes] = value[low, core, high]
-
-
-def first_columns_kernel(
-    half, data, kernels, outer, inner, inner_back, back, beyond,
-    out, outside, spectrum, first, mixed, second,
-):
-    step = pl.program_id(0)
-    width = LANE
-
-    @pl.when(step == 0)
-    def _():
-        for i in range(INN // 16):
-            here = slice(i * 16, (i + 1) * 16)
-            there = slice(INN + i * 16, INN + (i + 1) * 16)
-            block = jnp.concatenate([data[:, here, :], data[:, there, :]], axis=0)
-            re, im = split_complex(dot(outer[...], block.reshape(OUT * 16, 2 * width)), width)
-            value = jnp.concatenate([re, im], axis=1).astype(jnp.bfloat16)
-            first[:, here, :] = value.reshape(OUT, 16, 2 * width)
-
-    @pl.when(step < OUT // PER)
-    def _():
-        for c in range(PER):
-            k = step * PER + c
-            yr, yi = split_complex(dot(inner[c], first[k]), width)
-            spectrum[c] = jnp.concatenate([yr, yi], axis=1).astype(jnp.bfloat16)
-            mix_and_open(k, c, yr, yi, kernels[0, c], inner_back[c], mixed, second)
-
-    @pl.when(step >= OUT // PER)
-    def _():
-        close_columns(half, step - OUT // PER, back, beyond, second, out, outside)
+            lanes = slice(part * LANE, (part + 1) * LANE)
+            for parity in range(2):
+                at = parity * INN + i * 16
+                block = data_buf[:, at : at + 32, lanes]
+                block = jnp.concatenate([block[:, :16], block[:, 16:]], axis=2)
+                pieces.append(block.reshape(OUT // 2 * 16, 2 * LANE))
+        both = dot(outer[...], jnp.concatenate(pieces, axis=0))
+        for c in range(2):
+            re, im = (both[p * INN : (p + 1) * INN, c * LANE : (c + 1) * LANE] for p in range(2))
+            cos, sin = (twist[0, :, t + i + c : t + i + c + 1] for t in (0, 16))
+            here = slice((i + c) * 16, (i + c + 1) * 16)
+            for part, value in enumerate((re * cos + im * sin, im * cos - re * sin)):
+                value = value.astype(jnp.bfloat16).reshape(PAIRS, 2, 16, LANE)
+                first[:, part, here, :LANE] = value[:, 0]
+                first[:, part, here, LANE:] = value[:, 1]
+    stores = []
+
+    def transform(pair):
+        both = dot(inner[...], first[pair].reshape(2 * INN, 2 * LANE))
+        spectrum_buf[pair] = both.astype(jnp.bfloat16)
+        stores.append(pltpu.make_async_copy(spectrum_buf.at[pair], spectrum.at[pair], sems.at[2, pair]))
+        stores[-1].start()
+        return both
+
+    early[3].wait()
+    both = transform(0)
+    early[4].wait()
+    for pair in range(PAIRS):
+        following = transform(pair + 1) if pair + 1 < PAIRS else None
+        loads[pair].wait()
+        now = kernel_buf.at[pl.ds(2 * pair, 2)]
+        mix_and_open(pair, both, now, inner_back, twist, mixed.at[pair % 2], second)
+        both = following
+    for load in early[5:]:
+        load.wait()
+    open_outside(half, beyond[...], second, outside.at[0])
+    for chunk in range(INN // 16):
+        side, rows = chunk // 8, slice(chunk % 8 * 16, chunk % 8 * 16 + 16)
+
+        def store(high, low, core, lanes, value):
+            out_buf[side, high, low, core, rows, lanes] = value
+
+        close_chunk(slice(chunk * 16, chunk * 16 + 16), back[...], second, store)
+        if chunk % 4 == 3:
+            here = pl.ds((chunk % 8 - 3) * 16, 64)
+            source = out_buf.at[side, :, :, :, here, :]
+            target = out.at[:, side, :, :, here, :]
+            stores.append(pltpu.make_async_copy(source, target, sems.at[0, chunk // 4]))
+            stores[-1].start()
+    for copy in stores:
+        copy.wait()
 
 
 def next_columns_kernel(
-    half, spectrum, kernels, inner_back, back, beyond, out, outside, mixed, second
+    half, spectrum, kernels, inner_back, back, beyond, twist, out, outside, mixed, second
 ):
     step = pl.program_id(1)
-    width = LANE
-
-    @pl.when(step < OUT // PER)
+    for s in range(2):
+
+        @pl.when(step == s)
+        def _():
+            for i in range(PAIRS // 2):
+                pair = s * (PAIRS // 2) + i
+                both = spectrum[i].astype(jnp.float32)
+                now = kernels.at[0, pl.ds(2 * i, 2)]
+                mix_and_open(pair, both, now, inner_back, twist, mixed.at[i % 2], second)
+            if s == 1:
+                open_outside(half, beyond[0], second, outside.at[0])
+
+    @pl.when(step >= 2)
     def _():
-        for c in range(PER):
-            values = spectrum[c].astype(jnp.float32)
-            yr, yi = values[:, :width], values[:, width:]
-            mix_and_open(step * PER + c, c, yr, yi, kernels[0, c], inner_back[c], mixed, second)
-
-    @pl.when(step >= OUT // PER)
-    def _():
-        close_columns(half, step - OUT // PER, back, beyond, second, out, outside)
-
-
-STEPS = OUT // PER
-
-
-def opening_step(s):
-    return jnp.minimum(s, STEPS - 1)
-
-
-def closing_step(s):
-    return jnp.maximum(s - STEPS, 0)
+        for c in range(8):
+            rows = slice(c * 16, (c + 1) * 16)
+
+            def store(high, low, core, lanes, value):
+                out[high, 0, low, core, rows, lanes] = value
+
+            start = pl.multiple_of(((step - 2) * 8 + c) * 16, 16)
+            close_chunk(pl.ds(start, 16), back[0], second, store)
 
 
 def first_columns(half, data, kernels):
-    outer, inner, inner_back, back, beyond = (jnp.asarray(t) for t in column_tables())
+    tables = [jnp.asarray(t) for t in column_tables()]
     rows = data.shape[1] - 16
-    opening = lambda i, o: (opening_step(i), 0, 0)
+    bf16, f32 = jnp.bfloat16, jnp.float32
+    hbm = pl.BlockSpec(memory_space=pl.ANY)
     return pl.pallas_call(
         first_columns_kernel,
         grid_spec=pltpu.PrefetchScalarGridSpec(
             num_scalar_prefetch=1,
-            grid=(2 * STEPS,),
-            in_specs=[
-                pl.BlockSpec((8, rows, 2 * LANE), lambda i, o: (0, 0, 0)),
-                pl.BlockSpec((1, PER, INN, 2 * LANE), lambda i, o: (0, opening_step(i), 0, 0)),
-                pl.BlockSpec((2 * INN, INN), lambda i, o: (0, 0)),
-                pl.BlockSpec((PER, 2 * INN, INN), opening),
-                pl.BlockSpec((PER, 2 * INN, INN), opening),
-                pl.BlockSpec((1, INN, INN), lambda i, o: (o[0], 0, 0)),
-                pl.BlockSpec((1, 32, INN), lambda i, o: (o[0], 0, 0)),
-            ],
-            out_specs=[
-                pl.BlockSpec(
-                    (2, 1, 2, 2, PER * 16, 4 * LANE),
-                    lambda i, o: (0, closing_step(i) // 2, 0, 0, closing_step(i) % 2, 0),
-                ),
-                pl.BlockSpec((1, 16, 4 * LANE), lambda i, o: (0, 0, 0)),
-                pl.BlockSpec((PER, INN, 2 * LANE), opening),
-            ],
+            grid=(1,),
+            in_specs=[hbm] * 8,
+            out_specs=[hbm, hbm, pl.BlockSpec((1, 16, 4 * LANE), lambda i, o: (0, 0, 0))],
             scratch_shapes=[
-                pltpu.VMEM((OUT, INN, 2 * LANE), jnp.bfloat16),
-                pltpu.VMEM((PER, INN, 4 * LANE), jnp.bfloat16),
-                pltpu.VMEM((OUT, INN, 4 * LANE), jnp.bfloat16),
+                pltpu.VMEM((8, rows, 2 * LANE), bf16),
+                pltpu.VMEM((OUT, INN, 2 * LANE), bf16),
+                pltpu.VMEM((2 * INN, 2 * INN), bf16),
+                pltpu.VMEM((2 * INN, 2 * INN), bf16),
+                pltpu.VMEM((2 * INN, 2 * INN), bf16),
+                pltpu.VMEM((INN, 2 * INN), bf16),
+                pltpu.VMEM((32, 2 * INN), bf16),
+                pltpu.VMEM((2, INN, LANE), f32),
+                pltpu.VMEM((2, 2, 2, 2, LANE, 4 * LANE), bf16),
+                pltpu.VMEM((PAIRS, 2 * INN, 2 * LANE), bf16),
+                pltpu.VMEM((PAIRS, 2, INN, 2 * LANE), bf16),
+                pltpu.VMEM((2, 2 * INN, 4 * LANE), bf16),
+                pltpu.VMEM((2, OUT, INN, 2 * LANE), bf16),
+                pltpu.SemaphoreType.DMA((4, PAIRS)),
             ],
         ),
         out_shape=[
-            jax.ShapeDtypeStruct((2, 2, 2, 2, LANE, 4 * LANE), jnp.bfloat16),
-            jax.ShapeDtypeStruct((1, 16, 4 * LANE), jnp.bfloat16),
-            jax.ShapeDtypeStruct((OUT, INN, 2 * LANE), jnp.bfloat16),
+            jax.ShapeDtypeStruct((2, 2, 2, 2, LANE, 4 * LANE), bf16),
+            jax.ShapeDtypeStruct((PAIRS, 2 * INN, 2 * LANE), bf16),
+            jax.ShapeDtypeStruct((1, 16, 4 * LANE), bf16),
         ],
         compiler_params=pltpu.CompilerParams(vmem_limit_bytes=VMEM),
-        cost_estimate=pl.CostEstimate(flops=10**10, bytes_accessed=20 * MIB, transcendentals=0),
+        cost_estimate=pl.CostEstimate(flops=10**10, bytes_accessed=16 * MIB, transcendentals=0),
         name="first_columns",
-    )(half, data, kernels, outer, inner, inner_back, back, beyond)
+    )(half, data, kernels, *tables)
 
 
 def next_columns(half, plane, count, spectrum, kernels):
-    inner_back, back, beyond = (jnp.asarray(t) for t in column_tables()[2:])
-    opening = lambda g, i, o: (opening_step(i), 0, 0)
+    tables = [jnp.asarray(t) for t in column_tables()[2:]]
+    opening = lambda i: jnp.minimum(i, 1)
+    closing = lambda i: jnp.maximum(i - 2, 0)
+    own = lambda g, i, o: (o[0], 0, 0)
     return pl.pallas_call(
         next_columns_kernel,
         grid_spec=pltpu.PrefetchScalarGridSpec(
             num_scalar_prefetch=1,
-            grid=(count, 2 * STEPS),
+            grid=(count, 4),
             in_specs=[
-                pl.BlockSpec((PER, INN, 2 * LANE), opening),
+                pl.BlockSpec((PAIRS // 2, 2 * INN, 2 * LANE), lambda g, i, o: (opening(i), 0, 0)),
                 pl.BlockSpec(
-                    (1, PER, INN, 2 * LANE), lambda g, i, o: (plane + g, opening_step(i), 0, 0)
+                    (1, OUT // 2, INN, 2 * LANE), lambda g, i, o: (plane + g, opening(i), 0, 0)
                 ),
-                pl.BlockSpec((PER, 2 * INN, INN), opening),
-                pl.BlockSpec((1, INN, INN), lambda g, i, o: (o[0], 0, 0)),
-                pl.BlockSpec((1, 32, INN), lambda g, i, o: (o[0], 0, 0)),
+                pl.BlockSpec((2 * INN, 2 * INN), lambda g, i, o: (0, 0)),
+                pl.BlockSpec((1, INN, 2 * INN), own),
+                pl.BlockSpec((1, 32, 2 * INN), own),
+                pl.BlockSpec((2, INN, LANE), lambda g, i, o: (0, 0, 0)),
             ],
             out_specs=[
                 pl.BlockSpec(
-                    (2, 1, 2, 2, PER * 16, 4 * LANE),
-                    lambda g, i, o: (0, closing_step(i) // 2, 0, 0, closing_step(i) % 2, g),
+                    (2, 1, 2, 2, LANE, 4 * LANE), lambda g, i, o: (0, closing(i), 0, 0, 0, g)
                 ),
                 pl.BlockSpec((1, 16, 4 * LANE), lambda g, i, o: (g, 0, 0)),
             ],
             scratch_shapes=[
-                pltpu.VMEM((PER, INN, 4 * LANE), jnp.bfloat16),
-                pltpu.VMEM((OUT, INN, 4 * LANE), jnp.bfloat16),
+                pltpu.VMEM((2, 2 * INN, 4 * LANE), jnp.bfloat16),
+                pltpu.VMEM((2, OUT, INN, 2 * LANE), jnp.bfloat16),
             ],
         ),
         out_shape=[
@@ -593,7 +724,7 @@
             flops=count * 7 * 10**9, bytes_accessed=count * 16 * MIB, transcendentals=0
         ),
         name="next_columns",
-    )(half, spectrum, kernels, inner_back, back, beyond)
+    )(half, spectrum, kernels, *tables)
 
 
 def sixteen_points(re, im):
@@ -618,6 +749,31 @@
     return result + [cosines[16 - a] + sines[16 - a] for a in range(9, 16)]
 
 
+def open_rows(group, block, table, turn):
+    both = dot(block, table[min(group, 1)])
+    if group == 0:
+        return both
+    re, im = both[:, :INN], both[:, INN:]
+    cos, sin = turn[group : group + 1, :], turn[CLS + group : CLS + group + 1, :]
+    return jnp.concatenate([re * cos - im * sin, re * sin + im * cos], axis=1)
+
+
+def open_class(group, low, high, columns, table, turn, opened):
+    blocks = []
+    for part in range(2):
+        lanes = slice(part * 2 * LANE, (part + 1) * 2 * LANE)
+        first, rest = low[:, lanes], high[:, lanes]
+        if group == 0:
+            lane = lax.broadcasted_iota(jnp.int32, (first.shape[0], LANE), 1)
+            im = jnp.where(lane == 0, columns[part], first[:, LANE:])
+            first = jnp.concatenate([first[:, :LANE], im], axis=1)
+        blocks.append(jnp.concatenate([first, rest], axis=1))
+    rows = blocks[0].shape[0]
+    both = open_rows(group, jnp.concatenate(blocks, axis=0), table, turn)
+    for part in range(2):
+        opened[part, group] = both[part * rows : (part + 1) * rows]
+
+
 def strip_intensity(opened, here, tile):
     total = None
     for part in range(2):
@@ -631,20 +787,17 @@
     return total
 
 
-def row_inverse_kernel(plane, parts, nyquist, table, out, edges, opened):
+def row_inverse_kernel(plane, parts, nyquist, table, turn, out, edges, opened):
     current = plane + pl.program_id(0)
     rows = parts.shape[3]
     lane = lax.broadcasted_iota(jnp.int32, (rows, LANE), 1)
+    columns = []
     for part in range(2):
-        at = part * 2 * LANE
         mine = jnp.where(lane == current * 2 + part, nyquist[...], 0.0)
-        column = jnp.sum(mine, axis=1, keepdims=True).astype(jnp.bfloat16)
-        for group in range(CLS):
-            low, high = (parts[group // 2, i, group % 2, :, at : at + 2 * LANE] for i in range(2))
-            if group == 0:
-                first = jnp.where(lane == 0, column, low[:, LANE:])
-                low = jnp.concatenate([low[:, :LANE], first], axis=1)
-            opened[part, group] = dot(jnp.concatenate([low, high], axis=1), table[group])
+        columns.append(jnp.sum(mine, axis=1, keepdims=True).astype(jnp.bfloat16))
+    for group in range(CLS):
+        low, high = (parts[group // 2, i, group % 2] for i in range(2))
+        open_class(group, low, high, columns, table, turn, opened)
 
     def strip(i, carry):
         here = pl.ds(pl.multiple_of(i * 16, 16), 16)
@@ -662,14 +815,15 @@
 
 def row_inverse(plane, count, parts, nyquist):
     rows = parts.shape[3]
-    table = jnp.asarray(row_inverse_tables())
+    table, turn = (jnp.asarray(t) for t in row_inverse_tables())
     return pl.pallas_call(
         functools.partial(row_inverse_kernel, plane),
         grid=(count,),
         in_specs=[
             pl.BlockSpec((4, 2, 2, rows, 4 * LANE), lambda g: (0, 0, 0, 0, g)),
             pl.BlockSpec((rows, LANE), lambda g: (0, 0)),
-            pl.BlockSpec((CLS, 2 * INN, 2 * INN), lambda g: (0, 0, 0)),
+            pl.BlockSpec((2, 2 * INN, 2 * INN), lambda g: (0, 0, 0)),
+            pl.BlockSpec((2 * CLS, INN), lambda g: (0, 0)),
         ],
         out_specs=[
             pl.BlockSpec((1, rows, N), lambda g: (g, 0, 0)),
@@ -685,7 +839,7 @@
             flops=count * 3 * 10**9, bytes_accessed=count * 8 * MIB, transcendentals=0
         ),
         name="row_inverse",
-    )(parts, nyquist, table)
+    )(parts, nyquist, table, turn)
 
 
 def nyquist_kernel(planes, own, data, out):
@@ -767,10 +921,11 @@
 
 def spatial_term(held, r, t):
     lanes = slice(t * TILE, (t + 1) * TILE)
-    centre = held[r : r + 16, lanes]
-    down = held[r + 1 : r + 17, lanes] - held[r - 1 : r + 15, lanes]
+    around = held[pl.ds(pl.multiple_of(r - 8, 8), 32), lanes]
+    centre, down = around[8:24], around[9:25] - around[7:23]
     first, last = max(t * TILE - 1, 0), min((t + 1) * TILE, N - 1)
-    west, east = held[r : r + 16, first : first + 1], held[r : r + 16, last : last + 1]
+    here = pl.ds(r, 16)
+    west, east = held[here, first : first + 1], held[here, last : last + 1]
     return centre, down * down + across(centre, TILE, west, east)
 
 
@@ -784,15 +939,20 @@
     rows = first.shape[1]
     for g in range(3):
         hold(held.at[g], first[0] if g == 0 else others[g - 1], rows)
-    for i in range(rows // 16):
-        r = 8 + i * 16
+
+    def strip(i, carry):
+        r = pl.multiple_of(8 + i * 16, 8)
+        here = pl.ds(pl.multiple_of(i * 16, 16), 16)
         for t in range(N // TILE):
             lanes = slice(t * TILE, (t + 1) * TILE)
             (c0, s0), (c1, s1), (c2, s2) = (spatial_term(held.at[g], r, t) for g in range(3))
             d0, d1 = c1 - c0, c2 - c0
             score = jnp.maximum(d0 * d0 + s0, d1 * d1 + s1)
-            best[r - 8 : r + 8, lanes] = (score * 0.125).astype(jnp.bfloat16)
-            spatial[r - 8 : r + 8, lanes] = s2
+            best[here, lanes] = (score * 0.125).astype(jnp.bfloat16)
+            spatial[here, lanes] = s2.astype(jnp.bfloat16)
+        return carry
+
+    lax.fori_loop(0, rows // 16, strip, 0)
 
 
 def early_focus(first, others):
@@ -801,7 +961,7 @@
         early_focus_kernel,
         out_shape=[
             jax.ShapeDtypeStruct((rows, N), jnp.bfloat16),
-            jax.ShapeDtypeStruct((rows, N), jnp.float32),
+            jax.ShapeDtypeStruct((rows, N), jnp.bfloat16),
         ],
         scratch_shapes=[pltpu.VMEM((3, rows + 16, N), jnp.float32)],
         compiler_params=pltpu.CompilerParams(vmem_limit_bytes=VMEM),
@@ -810,7 +970,7 @@
     )(first, others)
 
 
-def edge_rows(edges, halo, out_upper, out_lower):
+def edge_rows(edges, halo):
     lane = lax.broadcasted_iota(jnp.int32, (2, N), 1)
     pair = lambda a, b: jnp.concatenate([a, b], axis=0)
     centre = [pair(e[0:1, :], e[15:16, :]) for e in edges]
@@ -824,51 +984,43 @@
         left = jnp.where(lane == 0, c, jnp.concatenate([c[:, -1:], c[:, :-1]], axis=1))
         score = depth * depth + down * down + (right - left) * (right - left)
         best = score if best is None else jnp.maximum(best, score)
-    best = best * 0.125
-    rows = out_upper.shape[0]
-    index = lax.broadcasted_iota(jnp.int32, (16, N), 0)
-    top = out_upper[0:16, :].astype(jnp.float32)
-    out_upper[0:16, :] = jnp.where(index == 0, best[0:1], top).astype(jnp.bfloat16)
-    low = out_lower[rows - 16 :, :].astype(jnp.float32)
-    out_lower[rows - 16 :, :] = jnp.where(index == 15, best[1:2], low).astype(jnp.bfloat16)
+    return best * 0.125
 
 
 def last_rows_kernel(
-    parts, nyquist, table, best, spatial, others, edge0, edge12,
-    upper, lower,
-    part_buf, table_buf, best_buf, spatial_buf, others_buf, opened, held, halo, edge, sems,
+    parts, best, spatial, others, nyquist_in, table_in, turn_in, edge0_in, edge12_in,
+    upper_out, lower_out,
+    both, nyquist, table, turn, edge0, edge12, part_buf, best_buf, spatial_buf, others_buf, opened, held, halo, edge, sems,
 ):
-    rows = upper.shape[0] * 2
+    rows = both.shape[0]
     loads = []
     for group in range(CLS):
         source = parts.at[group // 2, :, group % 2]
         loads.append(pltpu.make_async_copy(source, part_buf.at[group], sems.at[0, group]))
-        loads.append(pltpu.make_async_copy(table.at[group], table_buf.at[group], sems.at[1, group]))
-    for i, (source, target) in enumerate(
-        ((best, best_buf), (spatial, spatial_buf), (others, others_buf))
-    ):
-        loads.append(pltpu.make_async_copy(source, target, sems.at[2, i]))
-    for load in loads:
+    late = (best, best_buf), (spatial, spatial_buf), (others, others_buf)
+    late += (edge0_in, edge0), (edge12_in, edge12)
+    for i, (source, target) in enumerate(late):
+        loads.append(pltpu.make_async_copy(source, target, sems.at[1, i]))
+    early = (nyquist_in, nyquist), (table_in, table), (turn_in, turn)
+    early = [pltpu.make_async_copy(a, b, sems.at[2, i]) for i, (a, b) in enumerate(early)]
+    for load in early + loads:
         load.start()
+    for load in early:
+        load.wait()
     lane = lax.broadcasted_iota(jnp.int32, (rows, LANE), 1)
     few_lane = lax.broadcasted_iota(jnp.int32, (16, LANE), 1)
     few_row = lax.broadcasted_iota(jnp.int32, (16, LANE), 0)
     beside = jnp.where(few_row % 2 == 0, nyquist[rows : rows + 1, :], nyquist[rows + 1 : rows + 2, :])
+    columns = []
+    for part in range(2):
+        mine = jnp.where(lane == 6 + part, nyquist[:rows, :], 0.0)
+        few = jnp.where(few_lane == (few_row // 2) * 2 + part, beside, 0.0)
+        column = jnp.sum(jnp.concatenate([mine, few], axis=0), axis=1, keepdims=True)
+        columns.append(column.astype(jnp.bfloat16))
     for group in range(CLS):
-        loads[2 * group].wait()
-        loads[2 * group + 1].wait()
-        for part in range(2):
-            at = part * 2 * LANE
-            low, high = (part_buf[group, i, :, at : at + 2 * LANE] for i in range(2))
-            if group == 0:
-                mine = jnp.where(lane == 6 + part, nyquist[:rows, :], 0.0)
-                few = jnp.where(few_lane == (few_row // 2) * 2 + part, beside, 0.0)
-                column = jnp.sum(jnp.concatenate([mine, few], axis=0), axis=1, keepdims=True)
-                column = column.astype(jnp.bfloat16)
-                every = lax.broadcasted_iota(jnp.int32, (rows + 16, LANE), 1)
-                first = jnp.where(every == 0, column, low[:, LANE:])
-                low = jnp.concatenate([low[:, :LANE], first], axis=1)
-            opened[part, group] = dot(jnp.concatenate([low, high], axis=1), table_buf[group])
+        loads[group].wait()
+        low, high = part_buf[group, 0], part_buf[group, 1]
+        open_class(group, low, high, columns, table, turn, opened)
 
     def strip(i, carry):
         base = pl.multiple_of(i * 8, 8)
@@ -885,38 +1037,58 @@
     held[8 + rows : 9 + rows, :] = held[7 + rows : 8 + rows, :]
     edge[0:8, :] = held[8:16, :]
     edge[8:16, :] = held[rows : rows + 8, :]
-    for load in loads[2 * CLS :]:
+    for load in loads[CLS:]:
         load.wait()
-    for i in range(rows // 16):
-        r = 8 + i * 16
-        here = slice(r - 8, r + 8)
-        out, at = (upper, r - 8) if 2 * i < rows // 16 else (lower, r - 8 - rows // 2)
+    ends = edge_rows([edge0.at[0], edge12.at[0], edge12.at[1], edge], halo)
+
+    def measure(i, carry):
+        r = pl.multiple_of(8 + i * 16, 8)
+        here = pl.ds(pl.multiple_of(i * 16, 16), 16)
         for t in range(N // TILE):
             lanes = slice(t * TILE, (t + 1) * TILE)
             centre, term = spatial_term(held, r, t)
             d2 = centre - others_buf[0, here, lanes].astype(jnp.float32)
             d3 = centre - others_buf[1, here, lanes].astype(jnp.float32)
-            score = jnp.maximum(d2 * d2 + spatial_buf[here, lanes], d3 * d3 + term)
+            score = jnp.maximum(d2 * d2 + spatial_buf[here, lanes].astype(jnp.float32), d3 * d3 + term)
             score = jnp.maximum(score * 0.125, best_buf[here, lanes].astype(jnp.float32))
-            out[at : at + 16, lanes] = score.astype(jnp.bfloat16)
-    edge_rows([edge0.at[0], edge12.at[0], edge12.at[1], edge], halo, upper, lower)
+            both[here, lanes] = score.astype(jnp.bfloat16)
+        return carry
+
+    half = rows // 2
+    stores = []
+    for side, out in enumerate((upper_out, lower_out)):
+        lax.fori_loop(side * (half // 16), (side + 1) * (half // 16), measure, 0)
+        here = slice(0, 16) if side == 0 else slice(rows - 16, rows)
+        index = lax.broadcasted_iota(jnp.int32, (16, N), 0)
+        value = jnp.where(index == 15 * side, ends[side : side + 1], both[here].astype(jnp.float32))
+        both[here] = value.astype(jnp.bfloat16)
+        source = both.at[pl.ds(side * half, half)]
+        stores.append(pltpu.make_async_copy(source, out, sems.at[2, 3 + side]))
+        stores[-1].start()
+    for store in stores:
+        store.wait()
 
 
 def last_rows(parts, nyquist, best, spatial, others, edge0, edge12):
     rows = best.shape[0]
-    table = jnp.asarray(row_inverse_tables())
-    vmem, hbm = pl.BlockSpec(memory_space=pltpu.VMEM), pl.BlockSpec(memory_space=pl.ANY)
+    table, turn = (jnp.asarray(t) for t in row_inverse_tables())
+    hbm = pl.BlockSpec(memory_space=pl.ANY)
     bf16, f32 = jnp.bfloat16, jnp.float32
     return pl.pallas_call(
         last_rows_kernel,
-        in_specs=[hbm, vmem, hbm, hbm, hbm, hbm, vmem, vmem],
-        out_specs=[vmem] * 2,
+        in_specs=[hbm] * 9,
+        out_specs=[hbm] * 2,
         out_shape=[jax.ShapeDtypeStruct((rows // 2, N), bf16)] * 2,
         scratch_shapes=[
+            pltpu.VMEM((rows, N), bf16),
+            pltpu.VMEM((2 * LANE, LANE), f32),
+            pltpu.VMEM((2, 2 * INN, 2 * INN), bf16),
+            pltpu.VMEM((2 * CLS, INN), f32),
+            pltpu.VMEM((1, 16, N), f32),
+            pltpu.VMEM((2, 16, N), f32),
             pltpu.VMEM((CLS, 2, rows + 16, 4 * LANE), bf16),
-            pltpu.VMEM((CLS, 2 * INN, 2 * INN), bf16),
             pltpu.VMEM((rows, N), bf16),
-            pltpu.VMEM((rows, N), f32),
+            pltpu.VMEM((rows, N), bf16),
             pltpu.VMEM((2, rows, N), bf16),
             pltpu.VMEM((2, CLS, rows + 16, 2 * INN), f32),
             pltpu.VMEM((rows + 16, N), f32),
@@ -927,7 +1099,7 @@
         compiler_params=pltpu.CompilerParams(vmem_limit_bytes=VMEM),
         cost_estimate=pl.CostEstimate(flops=3 * 10**9, bytes_accessed=16 * MIB, transcendentals=0),
         name="last_rows",
-    )(parts, nyquist, table, best, spatial, others, edge0, edge12)
+    )(parts, best, spatial, others, nyquist, table, turn, edge0, edge12)
 
 
 def assemble_kernel(own, *refs):
@@ -1018,7 +1190,7 @@
         )
         return parts.reshape(4, 2, 2, -1, halfway.shape[-1])
 
-    halfway, outside, spectrum = first_columns(as_scalar(high), data, kernels)
+    halfway, spectrum, outside = first_columns(as_scalar(high), data, kernels)
     parts, borders = [to_rows(halfway)], [border_rows(halfway, outside, high)]
     for plane, count in ((1, 2), (3, 1)):
         halfway, outside = next_columns(as_scalar(high), plane, count, spectrum, kernels)

time: 263 us -> 259 us (0.985)
  Pallas kernels: 110 us -> 100 us
  waiting for transfers between devices: 111 us -> 118 us
    all_to_all x3, waiting for transfers between devices: 42.5 us -> 48 us  [to_rows(): lax.all_to_all(halfway.reshape(16, -1, halfway.shape[-1]), ('depth', 'low...]
    pallas_call x2, Pallas kernels: 28.1 us -> 24.1 us  [next_columns(): pl.pallas_call(next_columns_kernel, grid_spec=pltpu.PrefetchScalarGridSpe...]
  transfers between devices with their start and end apart: 10 -> 10, of which waited for: 8 -> 8; matrix products, arithmetic and copies ran while one was open for 3% -> 3% of each run, Pallas kernels for 27% -> 25%
where the time goes in v4:
time: 259 us; the launch traced here: 258 us
  waiting for transfers between devices  118 us (46%)
  Pallas kernels  100 us (39%)
  starting transfers between devices  28.9 us (11%)
  local copies, waits for them, and re-layouts  6.95 us (3%)
  other arithmetic  4.03 us (2%)
    all_to_all x3, waiting for transfers between devices, to_rows(): lax.all_to_all(halfway.reshape(16, -1, halfway.shape[-1]), ('depth', 'low...  48 us
    all_to_all x1, waiting for transfers between devices, half_spectrum_shards(): lax.all_to_all(sections.reshape(8, rows + 16, 2 * LANE), ('high', 'low',...  39 us
    pallas_call x2, Pallas kernels, next_columns(): pl.pallas_call(next_columns_kernel, grid_spec=pltpu.PrefetchScalarGridSpe...  24.1 us
    all_to_all x3, starting transfers between devices, to_rows(): lax.all_to_all(halfway.reshape(16, -1, halfway.shape[-1]), ('depth', 'low...  15 us
    pallas_call x1, Pallas kernels, first_columns(): pl.pallas_call(first_columns_kernel, grid_spec=pltpu.PrefetchScalarGridSp...  13.5 us
    pallas_call x2, Pallas kernels, row_inverse(): pl.pallas_call(functools.partial(row_inverse_kernel, plane), grid=(count,...  13.4 us
    pallas_call x1, Pallas kernels, propagators(): pl.pallas_call(functools.partial(propagator_kernel, planes), grid=(OUT,),...  10.9 us
    ppermute x1, waiting for transfers between devices, exchange_depth(): lax.ppermute(a, 'depth', OVER_X)  10.9 us
  transfers between devices with their start and end apart: 10, of which 8 were waited for; matrix products, arithmetic and copies ran while one was open for 3% of the time, Pallas kernels for 25%

profile of v4, /device:TPU:0, one launch (start us, length us, event | category | flops | bytes accessed | tf_op | source)
XLA Modules:
  0.0 258.1 jit_solution(1683434193366703294)
XLA Ops:
  0.0 9.2 %row_forward.1 = bf16[2,2,2,528,256]{4,3,2,1,0:T(8,128)(2,1)} custom-call(s32[1]{0:T(128)} %bitcast.own, f32[64]{0:T(128)} %constant.58.clone.weights, bf16[512,4096]{1,0:T(8,128)(2,1)} %holo.1, bf16[512,4096]{1,0:T(8,128)(2,1)} %back.3, bf16[8,512,512]{2,1,0:T(8,128)(2,1)} %constant.57.clone.table), custom_call_target="tpu_custom_call" | custom-call | flops 10000000000 | bytes 12582912 | tf_op jit(solution)/shard_map/row_forward/pallas_call | solution.py:431
  9.2 6.3 %all-to-all-start = ((bf16[8,528,256]{2,1,0:T(8,128)(2,1)}), bf16[8,528,256]{2,1,0:T(8,128)(2,1)}, u32[]{:S(2)}, u32[]{:S(2)}) async-start(bf16[8,528,256]{2,1,0:T(8,128)(2,1)} %bitcast.91), calls=%async_computation | async-start | bytes 4325376 | tf_op jit(solution)/shard_map/all_to_all | solution.py:1169
  15.5 0.6 multiply_multiply_fusion.fx2
  16.1 10.9 %propagators.1.kernels = bf16[4,16,256,256]{3,2,1,0:T(8,128)(2,1)} custom-call(f32[1,128]{1,0:T(1,128)} %multiply_multiply_fusion.fx2), custom_call_target="tpu_custom_call" | custom-call | flops 1000000000 | bytes 16777216 | tf_op jit(solution)/shard_map/propagators/pallas_call | solution.py:471
  27.0 39.0 %all-to-all-done.data = bf16[8,528,256]{2,1,0:T(8,128)(2,1)} async-done(((bf16[8,528,256]{2,1,0:T(8,128)(2,1)}), bf16[8,528,256]{2,1,0:T(8,128)(2,1)}, u32[]{:S(2)}, u32[]{:S(2)}) %all-to-all-start) | async-done | bytes 2162720 | tf_op jit(solution)/shard_map/all_to_all | solution.py:1169
  66.1 13.5 %first_columns.1 = (bf16[2,2,2,2,128,512]{5,4,3,2,1,0:T(8,128)(2,1)}, bf16[8,512,256]{2,1,0:T(8,128)(2,1)}, bf16[1,16,512]{2,1,0:T(8,128)(2,1)}) custom-call(s32[1]{0:T(128)} %bitcast.1.half, bf16[8,528,256]{2,1,0:T(8,128)(2,1)} %all-to-all-done.data, bf16[4,16,256,256]{3,2,1,0:T(8,128)(2,1)} %propagators.1.kernels, ...), custom_call_target="tpu_custom_call" | custom-call | flops 10000000000 | bytes 16777216 | tf_op jit(solution)/shard_map/first_columns/pallas_call | solution.py:652
  79.6 4.6 %all-to-all-start.1 = ((bf16[16,128,512]{2,1,0:T(8,128)(2,1)}), bf16[16,128,512]{2,1,0:T(8,128)(2,1)}, u32[]{:S(2)}, u32[]{:S(2)}) async-start(bf16[16,128,512]{2,1,0:T(8,128)(2,1)} %bitcast.90), calls=%async_computation.1 | async-start | bytes 4194304 | tf_op jit(solution)/shard_map/all_to_all | solution.py:1184
  84.2 0.6 pad_add_fusion.own
  84.9 6.9 %nyquist.1.nyquist_in = f32[256,128]{1,0:T(8,128)} custom-call(s32[2]{0:T(128)} %pad_add_fusion.own, bf16[8,528,256]{2,1,0:T(8,128)(2,1)} %all-to-all-done.data), custom_call_target="tpu_custom_call" | custom-call | flops 1000000000 | bytes 262144 | tf_op jit(solution)/shard_map/nyquist/pallas_call | solution.py:897
  91.8 15.7 %next_columns.3 = (bf16[2,2,2,2,128,1024]{5,4,3,2,1,0:T(8,128)(2,1)}, bf16[2,16,512]{2,1,0:T(8,128)(2,1)}) custom-call(s32[1]{0:T(128)} %bitcast.1.half, bf16[8,512,256]{2,1,0:T(8,128)(2,1)} %get-tuple-element.27.spectrum, bf16[4,16,256,256]{3,2,1,0:T(8,128)(2,1)} %propagators.1.kernels, bf16[512,512]{1,0:T(8,128)(2,1)} %constant.61.clone.inner_back_in.inner_back, ...), custom_call_target="tpu_custom_call" | custom-call | flops 14000000000 | bytes 33554432 | tf_op jit(solution)/shard_map/next_columns/pallas_call | solution.py:692
  107.4 4.3 %all-to-all-done.1 = bf16[16,128,512]{2,1,0:T(8,128)(2,1)} async-done(((bf16[16,128,512]{2,1,0:T(8,128)(2,1)}), bf16[16,128,512]{2,1,0:T(8,128)(2,1)}, u32[]{:S(2)}, u32[]{:S(2)}) %all-to-all-start.1) | async-done | bytes 2097184 | tf_op jit(solution)/shard_map/all_to_all | solution.py:1184
  111.8 4.8 %all-to-all-start.2 = ((bf16[16,128,1024]{2,1,0:T(8,128)(2,1)}), bf16[16,128,1024]{2,1,0:T(8,128)(2,1)}, u32[]{:S(2)}, u32[]{:S(2)}) async-start(bf16[16,128,1024]{2,1,0:T(8,128)(2,1)} %bitcast.88), calls=%async_computation.2 | async-start | bytes 8388608 | tf_op jit(solution)/shard_map/all_to_all | solution.py:1184
  116.6 1.0 fusion.9
  117.7 8.4 %next_columns.2 = (bf16[2,2,2,2,128,512]{5,4,3,2,1,0:T(8,128)(2,1)}, bf16[1,16,512]{2,1,0:T(8,128)(2,1)}) custom-call(s32[1]{0:T(128)} %bitcast.1.half, bf16[8,512,256]{2,1,0:T(8,128)(2,1)} %get-tuple-element.27.spectrum, bf16[4,16,256,256]{3,2,1,0:T(8,128)(2,1)} %propagators.1.kernels, bf16[512,512]{1,0:T(8,128)(2,1)} %constant.61.clone.inner_back_in.inner_back, ...), custom_call_target="tpu_custom_call" | custom-call | flops 7000000000 | bytes 16777216 | tf_op jit(solution)/shard_map/next_columns/pallas_call | solution.py:692
  126.1 0.0 copy-start.2
  126.1 1.2 fusion.10
  127.4 0.8 fusion.5
  128.5 1.4 slice_reduce_fusion.1
  130.1 0.7 fusion.11
  131.0 0.1 pad_maximum_fusion.1
  131.1 0.1 copy.76
  131.2 0.1 fusion.4
  131.3 0.0 copy-done.2
  131.3 1.6 pad_maximum_fusion
  132.9 5.4 %row_inverse.2 = (bf16[1,128,4096]{2,1,0:T(8,128)(2,1)}, f32[1,16,4096]{2,1,0:T(8,128)}) custom-call(bf16[4,2,2,128,512]{4,3,2,1,0:T(8,128)(2,1)} %bitcast.26.parts, f32[256,128]{1,0:T(8,128)} %nyquist.1.nyquist_in, bf16[2,512,512]{2,1,0:T(8,128)(2,1)} %constant.65.clone.table.table_in, f32[16,256]{1,0:T(8,128)} %constant.66.clone.turn.turn_in), custom_call_target="tpu_custom_call" | custom-call | flops 3000000000 | bytes 8388608 | tf_op jit(solution)/shard_map/row_inverse/pallas_call | solution.py:819
  138.3 30.4 %all-to-all-done.2 = bf16[16,128,1024]{2,1,0:T(8,128)(2,1)} async-done(((bf16[16,128,1024]{2,1,0:T(8,128)(2,1)}), bf16[16,128,1024]{2,1,0:T(8,128)(2,1)}, u32[]{:S(2)}, u32[]{:S(2)}) %all-to-all-start.2) | async-done | bytes 4194336 | tf_op jit(solution)/shard_map/all_to_all | solution.py:1184
  168.7 5.6 %all-to-all-start.3 = ((bf16[16,144,512]{2,1,0:T(8,128)(2,1)}), bf16[16,144,512]{2,1,0:T(8,128)(2,1)}, u32[]{:S(2)}, u32[]{:S(2)}) async-start(bf16[16,144,512]{2,1,0:T(8,128)(2,1)} %pad_maximum_fusion), calls=%async_computation.3 | async-start | bytes 4718592 | tf_op jit(solution)/shard_map/all_to_all | solution.py:1184
  174.3 8.0 %row_inverse.3 = (bf16[2,128,4096]{2,1,0:T(8,128)(2,1)}, f32[2,16,4096]{2,1,0:T(8,128)}) custom-call(bf16[4,2,2,128,1024]{4,3,2,1,0:T(8,128)(2,1)} %bitcast.28.parts, f32[256,128]{1,0:T(8,128)} %nyquist.1.nyquist_in, bf16[2,512,512]{2,1,0:T(8,128)(2,1)} %constant.65.clone.table.table_in, f32[16,256]{1,0:T(8,128)} %constant.66.clone.turn.turn_in), custom_call_target="tpu_custom_call" | custom-call | flops 6000000000 | bytes 16777216 | tf_op jit(solution)/shard_map/row_inverse/pallas_call | solution.py:819
  182.3 9.3 %early_focus.1 = (bf16[128,4096]{1,0:T(8,128)(2,1)}, bf16[128,4096]{1,0:T(8,128)(2,1)}) custom-call(bf16[1,128,4096]{2,1,0:T(8,128)(2,1)} %get-tuple-element.40.first, bf16[2,128,4096]{2,1,0:T(8,128)(2,1)} %get-tuple-element.42.others), custom_call_target="tpu_custom_call" | custom-call | flops 1000000000 | bytes 12582912 | tf_op jit(solution)/shard_map/early_focus/pallas_call | solution.py:960
  191.5 13.3 %all-to-all-done.3 = bf16[16,144,512]{2,1,0:T(8,128)(2,1)} async-done(((bf16[16,144,512]{2,1,0:T(8,128)(2,1)}), bf16[16,144,512]{2,1,0:T(8,128)(2,1)}, u32[]{:S(2)}, u32[]{:S(2)}) %all-to-all-start.3) | async-done | bytes 2359328 | tf_op jit(solution)/shard_map/all_to_all | solution.py:1184
  204.8 9.1 %last_rows.1 = (bf16[64,4096]{1,0:T(8,128)(2,1)}, bf16[64,4096]{1,0:T(8,128)(2,1)}) custom-call(bf16[4,2,2,144,512]{4,3,2,1,0:T(8,128)(2,1)} %bitcast.29.parts, bf16[128,4096]{1,0:T(8,128)(2,1)} %get-tuple-element.43.best, bf16[128,4096]{1,0:T(8,128)(2,1)} %get-tuple-element.44.spatial, bf16[2,128,4096]{2,1,0:T(8,128)(2,1)} %get-tuple-element.42.others, ...), custom_call_target="tpu_custom_call" | custom-call | flops 3000000000 | bytes 16777216 | tf_op jit(solution)/shard_map/last_rows/pallas_call | solution.py:1077
  213.9 2.6 %collective-permute-start = (bf16[64,4096]{1,0:T(8,128)(2,1)}, bf16[64,4096]{1,0:T(8,128)(2,1)S(1)}, u32[]{:S(2)}, u32[]{:S(2)}) collective-permute-start(bf16[64,4096]{1,0:T(8,128)(2,1)} %get-tuple-element.47.refs_0_), channel_id=1, source_target_pairs={{0,8},{8,0},{16,24},{24,16},{1,9},{9,1},{17,25},{25,17},{2,10},{10... | collective-permute-start | bytes 1572872 | tf_op jit(solution)/shard_map/ppermute | solution.py:1139
  216.5 1.5 collective-permute-start.4
  218.0 0.6 collective-permute-start.1
  218.6 0.1 collective-permute-start.3
  218.7 10.9 %collective-permute-done.refs_1_ = bf16[64,4096]{1,0:T(8,128)(2,1)S(1)} collective-permute-done((bf16[64,4096]{1,0:T(8,128)(2,1)}, bf16[64,4096]{1,0:T(8,128)(2,1)S(1)}, u32[]{:S(2)}, u32[]{:S(2)}) %collective-permute-start) | collective-permute-done | bytes 524320 | tf_op jit(solution)/shard_map/ppermute | solution.py:1139
  229.5 1.5 collective-permute-start.2
  231.0 0.6 collective-permute-done.4.refs_6_
  231.6 1.5 collective-permute-start.5
  233.1 9.8 %collective-permute-done.1.refs_2_ = bf16[64,4096]{1,0:T(8,128)(2,1)S(1)} collective-permute-done((bf16[64,4096]{1,0:T(8,128)(2,1)}, bf16[64,4096]{1,0:T(8,128)(2,1)S(1)}, u32[]{:S(2)}, u32[]{:S(2)}) %collective-permute-start.1) | collective-permute-done | bytes 524320 | tf_op jit(solution)/shard_map/ppermute | solution.py:1140
  242.9 0.0 collective-permute-done.3.refs_5_
  242.9 9.6 %collective-permute-done.2.refs_3_ = bf16[64,4096]{1,0:T(8,128)(2,1)S(1)} collective-permute-done((bf16[64,4096]{1,0:T(8,128)(2,1)S(1)}, bf16[64,4096]{1,0:T(8,128)(2,1)S(1)}, u32[]{:S(2)}, u32[]{:S(2)}) %collective-permute-start.2) | collective-permute-done | bytes 524320 | tf_op jit(solution)/shard_map/ppermute | solution.py:1140
  252.4 0.0 collective-permute-done.5.refs_7_
  252.4 0.0 copy-start
  252.4 1.0 copy-done
  253.5 0.0 copy-start.1
  253.5 1.0 copy-done.1
  254.5 3.6 %assemble.1 = f32[512,4096]{1,0:T(8,128)} custom-call(s32[1]{0:T(128)} %bitcast.own, bf16[64,4096]{1,0:T(8,128)(2,1)S(1)} %copy-done, bf16[64,4096]{1,0:T(8,128)(2,1)S(1)} %collective-permute-done.refs_1_, bf16[64,4096]{1,0:T(8,128)(2,1)S(1)} %collective-permute-done.1.refs_2_, bf16[64,4096]{1,0:T(8,128)(2,1)S(1)} %collective-permute-done.2.refs_3_, ...), custom_call_target="tpu_custom_call" | custom-call | flops 1000000 | bytes 12582912 | tf_op jit(solution)/shard_map/assemble/pallas_call | solution.py:1119
  (37 shorter events, 0.7 us)
Async XLA Ops:
  9.2 56.9 %all-to-all-start = ((bf16[8,528,256]{2,1,0:T(8,128)(2,1)}), bf16[8,528,256]{2,1,0:T(8,128)(2,1)}, u32[]{:S(2)}, u32[]{:S(2)}) async-start(bf16[8,528,256]{2,1,0:T(8,128)(2,1)} %bitcast.91), calls=%async_computation | async-start | bytes 4325376 | tf_op jit(solution)/shard_map/all_to_all | solution.py:1169
  79.6 32.2 %all-to-all-start.1 = ((bf16[16,128,512]{2,1,0:T(8,128)(2,1)}), bf16[16,128,512]{2,1,0:T(8,128)(2,1)}, u32[]{:S(2)}, u32[]{:S(2)}) async-start(bf16[16,128,512]{2,1,0:T(8,128)(2,1)} %bitcast.90), calls=%async_computation.1 | async-start | bytes 4194304 | tf_op jit(solution)/shard_map/all_to_all | solution.py:1184
  111.8 56.9 %all-to-all-start.2 = ((bf16[16,128,1024]{2,1,0:T(8,128)(2,1)}), bf16[16,128,1024]{2,1,0:T(8,128)(2,1)}, u32[]{:S(2)}, u32[]{:S(2)}) async-start(bf16[16,128,1024]{2,1,0:T(8,128)(2,1)} %bitcast.88), calls=%async_computation.2 | async-start | bytes 8388608 | tf_op jit(solution)/shard_map/all_to_all | solution.py:1184
  126.1 5.2 %copy-start.2 = (bf16[2,2,2,2,128,512]{5,4,3,2,1,0:T(8,128)(2,1)S(1)}, bf16[2,2,2,2,128,512]{5,4,3,2,1,0:T(8,128)(2,1)}, u32[]{:S(2)}) copy-start(bf16[2,2,2,2,128,512]{5,4,3,2,1,0:T(8,128)(2,1)} %get-tuple-element.28) | copy-start | bytes 6291460
  168.7 36.1 %all-to-all-start.3 = ((bf16[16,144,512]{2,1,0:T(8,128)(2,1)}), bf16[16,144,512]{2,1,0:T(8,128)(2,1)}, u32[]{:S(2)}, u32[]{:S(2)}) async-start(bf16[16,144,512]{2,1,0:T(8,128)(2,1)} %pad_maximum_fusion), calls=%async_computation.3 | async-start | bytes 4718592 | tf_op jit(solution)/shard_map/all_to_all | solution.py:1184
  213.9 15.6 %collective-permute-start = (bf16[64,4096]{1,0:T(8,128)(2,1)}, bf16[64,4096]{1,0:T(8,128)(2,1)S(1)}, u32[]{:S(2)}, u32[]{:S(2)}) collective-permute-start(bf16[64,4096]{1,0:T(8,128)(2,1)} %get-tuple-element.47.refs_0_), channel_id=1, source_target_pairs={{0,8},{8,0},{16,24},{24,16},{1,9},{9,1},{17,25},{25,17},{2,10},{10... | collective-permute-start | bytes 1572872 | tf_op jit(solution)/shard_map/ppermute | solution.py:1139
  216.5 15.1 %collective-permute-start.4 = (bf16[64,4096]{1,0:T(8,128)(2,1)}, bf16[64,4096]{1,0:T(8,128)(2,1)S(1)}, u32[]{:S(2)}, u32[]{:S(2)}) collective-permute-start(bf16[64,4096]{1,0:T(8,128)(2,1)} %get-tuple-element.48.refs_4_), channel_id=1, source_target_pairs={{0,16},{8,24},{16,0},{24,8},{1,17},{9,25},{17,1},{25,9},{2,18},{10... | collective-permute-start | bytes 1572872 | tf_op jit(solution)/shard_map/ppermute | solution.py:1139
  218.0 24.8 %collective-permute-start.1 = (bf16[64,4096]{1,0:T(8,128)(2,1)}, bf16[64,4096]{1,0:T(8,128)(2,1)S(1)}, u32[]{:S(2)}, u32[]{:S(2)}) collective-permute-start(bf16[64,4096]{1,0:T(8,128)(2,1)} %get-tuple-element.47.refs_0_), channel_id=1, source_target_pairs={{0,16},{8,24},{16,0},{24,8},{1,17},{9,25},{17,1},{25,9},{2,18},{10... | collective-permute-start | bytes 1572872 | tf_op jit(solution)/shard_map/ppermute | solution.py:1140
  218.6 24.3 %collective-permute-start.3 = (bf16[64,4096]{1,0:T(8,128)(2,1)}, bf16[64,4096]{1,0:T(8,128)(2,1)S(1)}, u32[]{:S(2)}, u32[]{:S(2)}) collective-permute-start(bf16[64,4096]{1,0:T(8,128)(2,1)} %get-tuple-element.48.refs_4_), channel_id=1, source_target_pairs={{0,8},{8,0},{16,24},{24,16},{1,9},{9,1},{17,25},{25,17},{2,10},{10... | collective-permute-start | bytes 1572872 | tf_op jit(solution)/shard_map/ppermute | solution.py:1141
  229.5 22.9 %collective-permute-start.2 = (bf16[64,4096]{1,0:T(8,128)(2,1)S(1)}, bf16[64,4096]{1,0:T(8,128)(2,1)S(1)}, u32[]{:S(2)}, u32[]{:S(2)}) collective-permute-start(bf16[64,4096]{1,0:T(8,128)(2,1)S(1)} %collective-permute-done.refs_1_), channel_id=1, source_target_pairs={{0,16},{8,24},{16,0},{24,8},{1,17},{9,25},{17,1},{25,9},{2,18},{10... | collective-permute-start | bytes 1572872 | tf_op jit(solution)/shard_map/ppermute | solution.py:1140
  231.6 20.8 %collective-permute-start.5 = (bf16[64,4096]{1,0:T(8,128)(2,1)S(1)}, bf16[64,4096]{1,0:T(8,128)(2,1)S(1)}, u32[]{:S(2)}, u32[]{:S(2)}) collective-permute-start(bf16[64,4096]{1,0:T(8,128)(2,1)S(1)} %collective-permute-done.4.refs_6_), channel_id=1, source_target_pairs={{0,8},{8,0},{16,24},{24,16},{1,9},{9,1},{17,25},{25,17},{2,10},{10... | collective-permute-start | bytes 1572872 | tf_op jit(solution)/shard_map/ppermute | solution.py:1141
  252.4 1.0 copy-start
  253.5 1.0 copy-start.1

commit v5 on v4

--- a/solution.py
+++ b/solution.py
@@ -378,7 +378,6 @@
                 below = back_buf[here, there].astype(jnp.float32)
                 inverse = pl.reciprocal(below, approx=True)
                 inverse = inverse * (2.0 - below * inverse)
-                inverse = inverse * (2.0 - below * inverse)
                 value = holo_buf[here, there].astype(jnp.float32) * inverse
                 return (value - 1.0).astype(jnp.bfloat16).astype(jnp.float32)
 
@@ -1105,12 +1104,12 @@
 def assemble_kernel(own, *refs):
     slot, out = pl.program_id(0), refs[-1]
     half = refs[0].shape[0]
-    for s in range(4):
+    for s in range(3):
 
         @pl.when(slot == s)
         def _():
             out[:half] = refs[s][...].astype(jnp.float32)
-            out[half:] = refs[4 + s][...].astype(jnp.float32)
+            out[half:] = refs[3 + s][...].astype(jnp.float32)
 
 
 def assemble(depth_index, upper, lower):
@@ -1120,15 +1119,46 @@
         assemble_kernel,
         grid_spec=pltpu.PrefetchScalarGridSpec(
             num_scalar_prefetch=1,
-            grid=(4,),
-            in_specs=[whole] * 8,
+            grid=(3,),
+            in_specs=[whole] * 6,
             out_specs=pl.BlockSpec((2 * half, N), lambda s, o: (jnp.bitwise_xor(s, o[0]), 0)),
         ),
         out_shape=jax.ShapeDtypeStruct((8 * half, N), jnp.float32),
-        compiler_params=pltpu.CompilerParams(vmem_limit_bytes=SHARED),
-        cost_estimate=pl.CostEstimate(flops=10**6, bytes_accessed=12 * MIB, transcendentals=0),
+        compiler_params=pltpu.CompilerParams(vmem_limit_bytes=20 * MIB),
+        cost_estimate=pl.CostEstimate(flops=10**6, bytes_accessed=10 * MIB, transcendentals=0),
         name="assemble",
     )(depth_index, *upper, *lower)
+
+
+def complete_kernel(own, upper, lower, whole, out):
+    half = lower.shape[0] // 2
+    step = pl.program_id(0)
+    for s, ref in enumerate((upper, lower)):
+        for part in range(2):
+
+            @pl.when(step == 2 * s + part)
+            def _():
+                out[...] = ref[part * half : (part + 1) * half].astype(jnp.float32)
+
+
+def complete(depth_index, upper, lower, whole):
+    half = upper.shape[0]
+    both = pl.BlockSpec((half, N), lambda i, o: (0, 0))
+    place = lambda i, o: (jnp.bitwise_xor(3, o[0]) * 4 + i, 0)
+    return pl.pallas_call(
+        complete_kernel,
+        grid_spec=pltpu.PrefetchScalarGridSpec(
+            num_scalar_prefetch=1,
+            grid=(4,),
+            in_specs=[both, both, pl.BlockSpec(memory_space=pl.ANY)],
+            out_specs=pl.BlockSpec((half // 2, N), place),
+        ),
+        out_shape=jax.ShapeDtypeStruct(whole.shape, jnp.float32),
+        input_output_aliases={3: 0},
+        compiler_params=pltpu.CompilerParams(vmem_limit_bytes=20 * MIB),
+        cost_estimate=pl.CostEstimate(flops=10**6, bytes_accessed=3 * MIB, transcendentals=0),
+        name="complete",
+    )(depth_index, upper, lower, whole)
 
 
 OVER_X = [(i, i ^ 1) for i in range(4)]
@@ -1216,7 +1246,9 @@
     others, others_edge = row_inverse(1, 2, parts[1], middle)
     best, spatial = early_focus(first, others)
     upper, lower = last_rows(parts[2], middle, best, spatial, others, first_edge, others_edge)
-    return assemble(as_scalar(depth), *exchange_depth(upper, lower))
+    upper, lower = exchange_depth(upper, lower)
+    whole = assemble(as_scalar(depth), upper[:3], lower[:3])
+    return complete(as_scalar(depth), upper[3], lower[3], whole)
 
 
 def solution(mesh):

time: 259 us -> 254 us (0.981)
  waiting for transfers between devices: 118 us -> 113 us
    ppermute x1, waiting for transfers between devices: 9.55 us -> 4.55 us  [exchange_depth(): lax.ppermute(ax, 'depth', OVER_Y)]
  transfers between devices with their start and end apart: 10 -> 10, of which waited for: 8 -> 8; matrix products, arithmetic and copies ran while one was open for 3% -> 4% of each run, Pallas kernels for 25% -> 27%
where the time goes in v5:
time: 254 us
  waiting for transfers between devices  113 us (44%)
  Pallas kernels  100 us (39%)
  starting transfers between devices  28.9 us (11%)
  local copies, waits for them, and re-layouts  6.95 us (3%)
  other arithmetic  4.03 us (2%)
    all_to_all x3, waiting for transfers between devices, to_rows(): lax.all_to_all(halfway.reshape(16, -1, halfway.shape[-1]), ('depth', 'low...  48 us
    all_to_all x1, waiting for transfers between devices, half_spectrum_shards(): lax.all_to_all(sections.reshape(8, rows + 16, 2 * LANE), ('high', 'low',...  39 us
    pallas_call x2, Pallas kernels, next_columns(): pl.pallas_call(next_columns_kernel, grid_spec=pltpu.PrefetchScalarGridSpe...  24.1 us
    all_to_all x3, starting transfers between devices, to_rows(): lax.all_to_all(halfway.reshape(16, -1, halfway.shape[-1]), ('depth', 'low...  15 us
    pallas_call x1, Pallas kernels, first_columns(): pl.pallas_call(first_columns_kernel, grid_spec=pltpu.PrefetchScalarGridSp...  13.5 us
    pallas_call x2, Pallas kernels, row_inverse(): pl.pallas_call(functools.partial(row_inverse_kernel, plane), grid=(count,...  13.4 us
    pallas_call x1, Pallas kernels, propagators(): pl.pallas_call(functools.partial(propagator_kernel, planes), grid=(OUT,),...  10.9 us
    ppermute x1, waiting for transfers between devices, exchange_depth(): lax.ppermute(a, 'depth', OVER_X)  10.9 us
  transfers between devices with their start and end apart: 10, of which 8 were waited for; matrix products, arithmetic and copies ran while one was open for 4% of the time, Pallas kernels for 27%

profile of v5, /device:TPU:0, one launch (start us, length us, event | category | flops | bytes accessed | tf_op | source)
XLA Modules:
  0.0 253.5 jit_solution(11472919366020694476)
XLA Ops:
  0.0 8.4 %row_forward.1 = bf16[2,2,2,528,256]{4,3,2,1,0:T(8,128)(2,1)} custom-call(s32[1]{0:T(128)} %bitcast.own, f32[64]{0:T(128)} %constant.58.clone.weights, bf16[512,4096]{1,0:T(8,128)(2,1)} %holo.1, bf16[512,4096]{1,0:T(8,128)(2,1)} %back.3, bf16[8,512,512]{2,1,0:T(8,128)(2,1)} %constant.57.clone.table), custom_call_target="tpu_custom_call" | custom-call | flops 10000000000 | bytes 12582912 | tf_op jit(solution)/shard_map/row_forward/pallas_call | solution.py:430
  8.4 6.3 %all-to-all-start = ((bf16[8,528,256]{2,1,0:T(8,128)(2,1)}), bf16[8,528,256]{2,1,0:T(8,128)(2,1)}, u32[]{:S(2)}, u32[]{:S(2)}) async-start(bf16[8,528,256]{2,1,0:T(8,128)(2,1)} %bitcast.91), calls=%async_computation | async-start | bytes 4325376 | tf_op jit(solution)/shard_map/all_to_all | solution.py:1199
  14.8 0.6 multiply_multiply_fusion.fx2
  15.4 10.9 %propagators.1.kernels = bf16[4,16,256,256]{3,2,1,0:T(8,128)(2,1)} custom-call(f32[1,128]{1,0:T(1,128)} %multiply_multiply_fusion.fx2), custom_call_target="tpu_custom_call" | custom-call | flops 1000000000 | bytes 16777216 | tf_op jit(solution)/shard_map/propagators/pallas_call | solution.py:470
  26.3 39.0 %all-to-all-done.data = bf16[8,528,256]{2,1,0:T(8,128)(2,1)} async-done(((bf16[8,528,256]{2,1,0:T(8,128)(2,1)}), bf16[8,528,256]{2,1,0:T(8,128)(2,1)}, u32[]{:S(2)}, u32[]{:S(2)}) %all-to-all-start) | async-done | bytes 2162720 | tf_op jit(solution)/shard_map/all_to_all | solution.py:1199
  65.4 13.5 %first_columns.1 = (bf16[2,2,2,2,128,512]{5,4,3,2,1,0:T(8,128)(2,1)}, bf16[8,512,256]{2,1,0:T(8,128)(2,1)}, bf16[1,16,512]{2,1,0:T(8,128)(2,1)}) custom-call(s32[1]{0:T(128)} %bitcast.1.half, bf16[8,528,256]{2,1,0:T(8,128)(2,1)} %all-to-all-done.data, bf16[4,16,256,256]{3,2,1,0:T(8,128)(2,1)} %propagators.1.kernels, ...), custom_call_target="tpu_custom_call" | custom-call | flops 10000000000 | bytes 16777216 | tf_op jit(solution)/shard_map/first_columns/pallas_call | solution.py:651
  78.9 4.6 %all-to-all-start.1 = ((bf16[16,128,512]{2,1,0:T(8,128)(2,1)}), bf16[16,128,512]{2,1,0:T(8,128)(2,1)}, u32[]{:S(2)}, u32[]{:S(2)}) async-start(bf16[16,128,512]{2,1,0:T(8,128)(2,1)} %bitcast.90), calls=%async_computation.1 | async-start | bytes 4194304 | tf_op jit(solution)/shard_map/all_to_all | solution.py:1214
  83.5 0.6 pad_add_fusion.own
  84.2 6.9 %nyquist.1.nyquist_in = f32[256,128]{1,0:T(8,128)} custom-call(s32[2]{0:T(128)} %pad_add_fusion.own, bf16[8,528,256]{2,1,0:T(8,128)(2,1)} %all-to-all-done.data), custom_call_target="tpu_custom_call" | custom-call | flops 1000000000 | bytes 262144 | tf_op jit(solution)/shard_map/nyquist/pallas_call | solution.py:896
  91.1 15.7 %next_columns.3 = (bf16[2,2,2,2,128,1024]{5,4,3,2,1,0:T(8,128)(2,1)}, bf16[2,16,512]{2,1,0:T(8,128)(2,1)}) custom-call(s32[1]{0:T(128)} %bitcast.1.half, bf16[8,512,256]{2,1,0:T(8,128)(2,1)} %get-tuple-element.27.spectrum, bf16[4,16,256,256]{3,2,1,0:T(8,128)(2,1)} %propagators.1.kernels, bf16[512,512]{1,0:T(8,128)(2,1)} %constant.61.clone.inner_back_in.inner_back, ...), custom_call_target="tpu_custom_call" | custom-call | flops 14000000000 | bytes 33554432 | tf_op jit(solution)/shard_map/next_columns/pallas_call | solution.py:691
  106.7 4.3 %all-to-all-done.1 = bf16[16,128,512]{2,1,0:T(8,128)(2,1)} async-done(((bf16[16,128,512]{2,1,0:T(8,128)(2,1)}), bf16[16,128,512]{2,1,0:T(8,128)(2,1)}, u32[]{:S(2)}, u32[]{:S(2)}) %all-to-all-start.1) | async-done | bytes 2097184 | tf_op jit(solution)/shard_map/all_to_all | solution.py:1214
  111.0 4.8 %all-to-all-start.2 = ((bf16[16,128,1024]{2,1,0:T(8,128)(2,1)}), bf16[16,128,1024]{2,1,0:T(8,128)(2,1)}, u32[]{:S(2)}, u32[]{:S(2)}) async-start(bf16[16,128,1024]{2,1,0:T(8,128)(2,1)} %bitcast.88), calls=%async_computation.2 | async-start | bytes 8388608 | tf_op jit(solution)/shard_map/all_to_all | solution.py:1214
  115.8 1.0 fusion.9
  117.0 8.4 %next_columns.2 = (bf16[2,2,2,2,128,512]{5,4,3,2,1,0:T(8,128)(2,1)}, bf16[1,16,512]{2,1,0:T(8,128)(2,1)}) custom-call(s32[1]{0:T(128)} %bitcast.1.half, bf16[8,512,256]{2,1,0:T(8,128)(2,1)} %get-tuple-element.27.spectrum, bf16[4,16,256,256]{3,2,1,0:T(8,128)(2,1)} %propagators.1.kernels, bf16[512,512]{1,0:T(8,128)(2,1)} %constant.61.clone.inner_back_in.inner_back, ...), custom_call_target="tpu_custom_call" | custom-call | flops 7000000000 | bytes 16777216 | tf_op jit(solution)/shard_map/next_columns/pallas_call | solution.py:691
  125.4 0.0 copy-start.2
  125.4 1.2 fusion.10
  126.7 0.8 fusion.5
  127.8 1.4 slice_reduce_fusion.1
  129.3 0.7 fusion.11
  130.2 0.1 pad_maximum_fusion.1
  130.4 0.1 copy.77
  130.4 0.1 fusion.4
  130.6 0.0 copy-done.2
  130.6 1.6 pad_maximum_fusion
  132.2 5.4 %row_inverse.2 = (bf16[1,128,4096]{2,1,0:T(8,128)(2,1)}, f32[1,16,4096]{2,1,0:T(8,128)}) custom-call(bf16[4,2,2,128,512]{4,3,2,1,0:T(8,128)(2,1)} %bitcast.26.parts, f32[256,128]{1,0:T(8,128)} %nyquist.1.nyquist_in, bf16[2,512,512]{2,1,0:T(8,128)(2,1)} %constant.65.clone.table.table_in, f32[16,256]{1,0:T(8,128)} %constant.66.clone.turn.turn_in), custom_call_target="tpu_custom_call" | custom-call | flops 3000000000 | bytes 8388608 | tf_op jit(solution)/shard_map/row_inverse/pallas_call | solution.py:818
  137.6 30.4 %all-to-all-done.2 = bf16[16,128,1024]{2,1,0:T(8,128)(2,1)} async-done(((bf16[16,128,1024]{2,1,0:T(8,128)(2,1)}), bf16[16,128,1024]{2,1,0:T(8,128)(2,1)}, u32[]{:S(2)}, u32[]{:S(2)}) %all-to-all-start.2) | async-done | bytes 4194336 | tf_op jit(solution)/shard_map/all_to_all | solution.py:1214
  168.0 5.6 %all-to-all-start.3 = ((bf16[16,144,512]{2,1,0:T(8,128)(2,1)}), bf16[16,144,512]{2,1,0:T(8,128)(2,1)}, u32[]{:S(2)}, u32[]{:S(2)}) async-start(bf16[16,144,512]{2,1,0:T(8,128)(2,1)} %pad_maximum_fusion), calls=%async_computation.3 | async-start | bytes 4718592 | tf_op jit(solution)/shard_map/all_to_all | solution.py:1214
  173.5 8.0 %row_inverse.3 = (bf16[2,128,4096]{2,1,0:T(8,128)(2,1)}, f32[2,16,4096]{2,1,0:T(8,128)}) custom-call(bf16[4,2,2,128,1024]{4,3,2,1,0:T(8,128)(2,1)} %bitcast.28.parts, f32[256,128]{1,0:T(8,128)} %nyquist.1.nyquist_in, bf16[2,512,512]{2,1,0:T(8,128)(2,1)} %constant.65.clone.table.table_in, f32[16,256]{1,0:T(8,128)} %constant.66.clone.turn.turn_in), custom_call_target="tpu_custom_call" | custom-call | flops 6000000000 | bytes 16777216 | tf_op jit(solution)/shard_map/row_inverse/pallas_call | solution.py:818
  181.6 9.3 %early_focus.1 = (bf16[128,4096]{1,0:T(8,128)(2,1)}, bf16[128,4096]{1,0:T(8,128)(2,1)}) custom-call(bf16[1,128,4096]{2,1,0:T(8,128)(2,1)} %get-tuple-element.40.first, bf16[2,128,4096]{2,1,0:T(8,128)(2,1)} %get-tuple-element.42.others), custom_call_target="tpu_custom_call" | custom-call | flops 1000000000 | bytes 12582912 | tf_op jit(solution)/shard_map/early_focus/pallas_call | solution.py:959
  190.8 13.3 %all-to-all-done.3 = bf16[16,144,512]{2,1,0:T(8,128)(2,1)} async-done(((bf16[16,144,512]{2,1,0:T(8,128)(2,1)}), bf16[16,144,512]{2,1,0:T(8,128)(2,1)}, u32[]{:S(2)}, u32[]{:S(2)}) %all-to-all-start.3) | async-done | bytes 2359328 | tf_op jit(solution)/shard_map/all_to_all | solution.py:1214
  204.1 9.1 %last_rows.1 = (bf16[64,4096]{1,0:T(8,128)(2,1)}, bf16[64,4096]{1,0:T(8,128)(2,1)}) custom-call(bf16[4,2,2,144,512]{4,3,2,1,0:T(8,128)(2,1)} %bitcast.29.parts, bf16[128,4096]{1,0:T(8,128)(2,1)} %get-tuple-element.43.best, bf16[128,4096]{1,0:T(8,128)(2,1)} %get-tuple-element.44.spatial, bf16[2,128,4096]{2,1,0:T(8,128)(2,1)} %get-tuple-element.42.others, ...), custom_call_target="tpu_custom_call" | custom-call | flops 3000000000 | bytes 16777216 | tf_op jit(solution)/shard_map/last_rows/pallas_call | solution.py:1076
  213.2 2.6 %collective-permute-start = (bf16[64,4096]{1,0:T(8,128)(2,1)}, bf16[64,4096]{1,0:T(8,128)(2,1)S(1)}, u32[]{:S(2)}, u32[]{:S(2)}) collective-permute-start(bf16[64,4096]{1,0:T(8,128)(2,1)} %get-tuple-element.47.refs_0_), channel_id=1, source_target_pairs={{0,8},{8,0},{16,24},{24,16},{1,9},{9,1},{17,25},{25,17},{2,10},{10... | collective-permute-start | bytes 1572872 | tf_op jit(solution)/shard_map/ppermute | solution.py:1169
  215.8 1.5 collective-permute-start.2
  217.3 0.6 collective-permute-start.4
  217.8 0.1 collective-permute-start.5
  217.9 10.9 %collective-permute-done.refs_1_ = bf16[64,4096]{1,0:T(8,128)(2,1)S(1)} collective-permute-done((bf16[64,4096]{1,0:T(8,128)(2,1)}, bf16[64,4096]{1,0:T(8,128)(2,1)S(1)}, u32[]{:S(2)}, u32[]{:S(2)}) %collective-permute-start) | collective-permute-done | bytes 524320 | tf_op jit(solution)/shard_map/ppermute | solution.py:1169
  228.8 1.5 collective-permute-start.1
  230.3 0.6 collective-permute-done.2.refs_5_
  230.9 1.5 collective-permute-start.3
  232.3 9.8 %collective-permute-done.4.refs_2_ = bf16[64,4096]{1,0:T(8,128)(2,1)S(1)} collective-permute-done((bf16[64,4096]{1,0:T(8,128)(2,1)}, bf16[64,4096]{1,0:T(8,128)(2,1)S(1)}, u32[]{:S(2)}, u32[]{:S(2)}) %collective-permute-start.4) | collective-permute-done | bytes 524320 | tf_op jit(solution)/shard_map/ppermute | solution.py:1170
  242.1 0.0 collective-permute-done.5.refs_4_
  242.1 0.0 copy-start
  242.1 1.0 copy-done
  243.2 1.0 copy-done.1
  244.2 2.9 %assemble.1.whole = f32[512,4096]{1,0:T(8,128)} custom-call(s32[1]{0:T(128)} %bitcast.own, bf16[64,4096]{1,0:T(8,128)(2,1)S(1)} %copy-done, bf16[64,4096]{1,0:T(8,128)(2,1)S(1)} %collective-permute-done.refs_1_, bf16[64,4096]{1,0:T(8,128)(2,1)S(1)} %collective-permute-done.4.refs_2_, bf16[64,4096]{1,0:T(8,128)(2,1)S(1)} %copy-done.1, ...), custom_call_target="tpu_custom_call" | custom-call | flops 1000000 | bytes 10485760 | tf_op jit(solution)/shard_map/assemble/pallas_call | solution.py:1118
  247.1 4.5 %collective-permute-done.1.upper = bf16[64,4096]{1,0:T(8,128)(2,1)S(1)} collective-permute-done((bf16[64,4096]{1,0:T(8,128)(2,1)S(1)}, bf16[64,4096]{1,0:T(8,128)(2,1)S(1)}, u32[]{:S(2)}, u32[]{:S(2)}) %collective-permute-start.1) | collective-permute-done | bytes 524320 | tf_op jit(solution)/shard_map/ppermute | solution.py:1170
  251.7 0.0 collective-permute-done.3.lower
  251.7 1.9 complete.1
  (38 shorter events, 0.7 us)
Async XLA Ops:
  8.4 56.9 %all-to-all-start = ((bf16[8,528,256]{2,1,0:T(8,128)(2,1)}), bf16[8,528,256]{2,1,0:T(8,128)(2,1)}, u32[]{:S(2)}, u32[]{:S(2)}) async-start(bf16[8,528,256]{2,1,0:T(8,128)(2,1)} %bitcast.91), calls=%async_computation | async-start | bytes 4325376 | tf_op jit(solution)/shard_map/all_to_all | solution.py:1199
  78.9 32.2 %all-to-all-start.1 = ((bf16[16,128,512]{2,1,0:T(8,128)(2,1)}), bf16[16,128,512]{2,1,0:T(8,128)(2,1)}, u32[]{:S(2)}, u32[]{:S(2)}) async-start(bf16[16,128,512]{2,1,0:T(8,128)(2,1)} %bitcast.90), calls=%async_computation.1 | async-start | bytes 4194304 | tf_op jit(solution)/shard_map/all_to_all | solution.py:1214
  111.0 56.9 %all-to-all-start.2 = ((bf16[16,128,1024]{2,1,0:T(8,128)(2,1)}), bf16[16,128,1024]{2,1,0:T(8,128)(2,1)}, u32[]{:S(2)}, u32[]{:S(2)}) async-start(bf16[16,128,1024]{2,1,0:T(8,128)(2,1)} %bitcast.88), calls=%async_computation.2 | async-start | bytes 8388608 | tf_op jit(solution)/shard_map/all_to_all | solution.py:1214
  125.4 5.2 %copy-start.2 = (bf16[2,2,2,2,128,512]{5,4,3,2,1,0:T(8,128)(2,1)S(1)}, bf16[2,2,2,2,128,512]{5,4,3,2,1,0:T(8,128)(2,1)}, u32[]{:S(2)}) copy-start(bf16[2,2,2,2,128,512]{5,4,3,2,1,0:T(8,128)(2,1)} %get-tuple-element.28) | copy-start | bytes 6291460
  168.0 36.1 %all-to-all-start.3 = ((bf16[16,144,512]{2,1,0:T(8,128)(2,1)}), bf16[16,144,512]{2,1,0:T(8,128)(2,1)}, u32[]{:S(2)}, u32[]{:S(2)}) async-start(bf16[16,144,512]{2,1,0:T(8,128)(2,1)} %pad_maximum_fusion), calls=%async_computation.3 | async-start | bytes 4718592 | tf_op jit(solution)/shard_map/all_to_all | solution.py:1214
  213.2 15.6 %collective-permute-start = (bf16[64,4096]{1,0:T(8,128)(2,1)}, bf16[64,4096]{1,0:T(8,128)(2,1)S(1)}, u32[]{:S(2)}, u32[]{:S(2)}) collective-permute-start(bf16[64,4096]{1,0:T(8,128)(2,1)} %get-tuple-element.47.refs_0_), channel_id=1, source_target_pairs={{0,8},{8,0},{16,24},{24,16},{1,9},{9,1},{17,25},{25,17},{2,10},{10... | collective-permute-start | bytes 1572872 | tf_op jit(solution)/shard_map/ppermute | solution.py:1169
  215.8 15.1 %collective-permute-start.2 = (bf16[64,4096]{1,0:T(8,128)(2,1)}, bf16[64,4096]{1,0:T(8,128)(2,1)S(1)}, u32[]{:S(2)}, u32[]{:S(2)}) collective-permute-start(bf16[64,4096]{1,0:T(8,128)(2,1)} %get-tuple-element.48.refs_3_), channel_id=1, source_target_pairs={{0,16},{8,24},{16,0},{24,8},{1,17},{9,25},{17,1},{25,9},{2,18},{10... | collective-permute-start | bytes 1572872 | tf_op jit(solution)/shard_map/ppermute | solution.py:1169
  217.3 24.8 %collective-permute-start.4 = (bf16[64,4096]{1,0:T(8,128)(2,1)}, bf16[64,4096]{1,0:T(8,128)(2,1)S(1)}, u32[]{:S(2)}, u32[]{:S(2)}) collective-permute-start(bf16[64,4096]{1,0:T(8,128)(2,1)} %get-tuple-element.47.refs_0_), channel_id=1, source_target_pairs={{0,16},{8,24},{16,0},{24,8},{1,17},{9,25},{17,1},{25,9},{2,18},{10... | collective-permute-start | bytes 1572872 | tf_op jit(solution)/shard_map/ppermute | solution.py:1170
  217.8 24.3 %collective-permute-start.5 = (bf16[64,4096]{1,0:T(8,128)(2,1)}, bf16[64,4096]{1,0:T(8,128)(2,1)S(1)}, u32[]{:S(2)}, u32[]{:S(2)}) collective-permute-start(bf16[64,4096]{1,0:T(8,128)(2,1)} %get-tuple-element.48.refs_3_), channel_id=1, source_target_pairs={{0,8},{8,0},{16,24},{24,16},{1,9},{9,1},{17,25},{25,17},{2,10},{10... | collective-permute-start | bytes 1572872 | tf_op jit(solution)/shard_map/ppermute | solution.py:1171
  228.8 22.9 %collective-permute-start.1 = (bf16[64,4096]{1,0:T(8,128)(2,1)S(1)}, bf16[64,4096]{1,0:T(8,128)(2,1)S(1)}, u32[]{:S(2)}, u32[]{:S(2)}) collective-permute-start(bf16[64,4096]{1,0:T(8,128)(2,1)S(1)} %collective-permute-done.refs_1_), channel_id=1, source_target_pairs={{0,16},{8,24},{16,0},{24,8},{1,17},{9,25},{17,1},{25,9},{2,18},{10... | collective-permute-start | bytes 1572872 | tf_op jit(solution)/shard_map/ppermute | solution.py:1170
  230.9 20.8 %collective-permute-start.3 = (bf16[64,4096]{1,0:T(8,128)(2,1)S(1)}, bf16[64,4096]{1,0:T(8,128)(2,1)S(1)}, u32[]{:S(2)}, u32[]{:S(2)}) collective-permute-start(bf16[64,4096]{1,0:T(8,128)(2,1)S(1)} %collective-permute-done.2.refs_5_), channel_id=1, source_target_pairs={{0,8},{8,0},{16,24},{24,16},{1,9},{9,1},{17,25},{25,17},{2,10},{10... | collective-permute-start | bytes 1572872 | tf_op jit(solution)/shard_map/ppermute | solution.py:1171
  242.1 1.0 copy-start
  243.2 1.0 copy-start.1

commit v6 on v5

--- a/solution.py
+++ b/solution.py
@@ -317,6 +317,7 @@
 
 
 CHUNK = 64
+BATCHES = ((0,), (1, 2), (3, 4), (5, 6, 7))
 
 
 def sixteen_sums(term, w):
@@ -580,21 +581,30 @@
     stores = []
 
     def transform(pair):
-        both = dot(inner[...], first[pair].reshape(2 * INN, 2 * LANE))
-        spectrum_buf[pair] = both.astype(jnp.bfloat16)
-        stores.append(pltpu.make_async_copy(spectrum_buf.at[pair], spectrum.at[pair], sems.at[2, pair]))
-        stores[-1].start()
-        return both
+        block = jnp.concatenate(
+            [first[pair + i].reshape(2 * INN, 2 * LANE) for i in range(2)], axis=1
+        )
+        both = dot(inner[...], block)
+        result = []
+        for i in range(2):
+            result.append(both[:, i * 2 * LANE : (i + 1) * 2 * LANE])
+            spectrum_buf[pair + i] = result[i].astype(jnp.bfloat16)
+        here = pl.ds(pair, 2)
+        copy = pltpu.make_async_copy(spectrum_buf.at[here], spectrum.at[here], sems.at[2, pair])
+        stores.append(copy)
+        copy.start()
+        return result
 
     early[3].wait()
     both = transform(0)
     early[4].wait()
     for pair in range(PAIRS):
-        following = transform(pair + 1) if pair + 1 < PAIRS else None
+        if pair % 2 == 0:
+            now_both = both
+            both = transform(pair + 2) if pair + 2 < PAIRS else None
         loads[pair].wait()
         now = kernel_buf.at[pl.ds(2 * pair, 2)]
-        mix_and_open(pair, both, now, inner_back, twist, mixed.at[pair % 2], second)
-        both = following
+        mix_and_open(pair, now_both[pair % 2], now, inner_back, twist, mixed.at[pair % 2], second)
     for load in early[5:]:
         load.wait()
     open_outside(half, beyond[...], second, outside.at[0])
@@ -748,8 +758,7 @@
     return result + [cosines[16 - a] + sines[16 - a] for a in range(9, 16)]
 
 
-def open_rows(group, block, table, turn):
-    both = dot(block, table[min(group, 1)])
+def open_rows(group, both, turn):
     if group == 0:
         return both
     re, im = both[:, :INN], both[:, INN:]
@@ -757,20 +766,23 @@
     return jnp.concatenate([re * cos - im * sin, re * sin + im * cos], axis=1)
 
 
-def open_class(group, low, high, columns, table, turn, opened):
+def open_classes(groups, halves, columns, table, turn, opened):
     blocks = []
-    for part in range(2):
-        lanes = slice(part * 2 * LANE, (part + 1) * 2 * LANE)
-        first, rest = low[:, lanes], high[:, lanes]
-        if group == 0:
-            lane = lax.broadcasted_iota(jnp.int32, (first.shape[0], LANE), 1)
-            im = jnp.where(lane == 0, columns[part], first[:, LANE:])
-            first = jnp.concatenate([first[:, :LANE], im], axis=1)
-        blocks.append(jnp.concatenate([first, rest], axis=1))
+    for group, (low, high) in zip(groups, halves):
+        for part in range(2):
+            lanes = slice(part * 2 * LANE, (part + 1) * 2 * LANE)
+            first, rest = low[:, lanes], high[:, lanes]
+            if group == 0:
+                lane = lax.broadcasted_iota(jnp.int32, (first.shape[0], LANE), 1)
+                im = jnp.where(lane == 0, columns[part], first[:, LANE:])
+                first = jnp.concatenate([first[:, :LANE], im], axis=1)
+            blocks.append(jnp.concatenate([first, rest], axis=1))
     rows = blocks[0].shape[0]
-    both = open_rows(group, jnp.concatenate(blocks, axis=0), table, turn)
-    for part in range(2):
-        opened[part, group] = both[part * rows : (part + 1) * rows]
+    both = dot(jnp.concatenate(blocks, axis=0), table[min(groups[0], 1)])
+    for i, group in enumerate(groups):
+        for part in range(2):
+            at = (2 * i + part) * rows
+            opened[part, group] = open_rows(group, both[at : at + rows], turn)
 
 
 def strip_intensity(opened, here, tile):
@@ -794,9 +806,9 @@
     for part in range(2):
         mine = jnp.where(lane == current * 2 + part, nyquist[...], 0.0)
         columns.append(jnp.sum(mine, axis=1, keepdims=True).astype(jnp.bfloat16))
-    for group in range(CLS):
-        low, high = (parts[group // 2, i, group % 2] for i in range(2))
-        open_class(group, low, high, columns, table, turn, opened)
+    for groups in BATCHES:
+        halves = [[parts[g // 2, i, g % 2] for i in range(2)] for g in groups]
+        open_classes(groups, halves, columns, table, turn, opened)
 
     def strip(i, carry):
         here = pl.ds(pl.multiple_of(i * 16, 16), 16)
@@ -1016,10 +1028,11 @@
         few = jnp.where(few_lane == (few_row // 2) * 2 + part, beside, 0.0)
         column = jnp.sum(jnp.concatenate([mine, few], axis=0), axis=1, keepdims=True)
         columns.append(column.astype(jnp.bfloat16))
-    for group in range(CLS):
-        loads[group].wait()
-        low, high = part_buf[group, 0], part_buf[group, 1]
-        open_class(group, low, high, columns, table, turn, opened)
+    for groups in BATCHES:
+        for group in groups:
+            loads[group].wait()
+        halves = [[part_buf[g, i] for i in range(2)] for g in groups]
+        open_classes(groups, halves, columns, table, turn, opened)
 
     def strip(i, carry):
         base = pl.multiple_of(i * 8, 8)

time: 254 us -> 253 us (level)
  no operation moved by 1% of the time
where the time goes in v6:
time: 253 us; the launch traced here: 252 us
  waiting for transfers between devices  113 us (45%)
  Pallas kernels  99.1 us (39%)
  starting transfers between devices  28.9 us (11%)
  local copies, waits for them, and re-layouts  6.95 us (3%)
  other arithmetic  4.03 us (2%)
    all_to_all x3, waiting for transfers between devices, to_rows(): lax.all_to_all(halfway.reshape(16, -1, halfway.shape[-1]), ('depth', 'low...  48 us
    all_to_all x1, waiting for transfers between devices, half_spectrum_shards(): lax.all_to_all(sections.reshape(8, rows + 16, 2 * LANE), ('high', 'low',...  39 us
    pallas_call x2, Pallas kernels, next_columns(): pl.pallas_call(next_columns_kernel, grid_spec=pltpu.PrefetchScalarGridSpe...  24.1 us
    all_to_all x3, starting transfers between devices, to_rows(): lax.all_to_all(halfway.reshape(16, -1, halfway.shape[-1]), ('depth', 'low...  15 us
    pallas_call x2, Pallas kernels, row_inverse(): pl.pallas_call(functools.partial(row_inverse_kernel, plane), grid=(count,...  13.4 us
    pallas_call x1, Pallas kernels, first_columns(): pl.pallas_call(first_columns_kernel, grid_spec=pltpu.PrefetchScalarGridSp...  12.8 us
    pallas_call x1, Pallas kernels, propagators(): pl.pallas_call(functools.partial(propagator_kernel, planes), grid=(OUT,),...  10.9 us
    ppermute x1, waiting for transfers between devices, exchange_depth(): lax.ppermute(a, 'depth', OVER_X)  10.9 us
  transfers between devices with their start and end apart: 10, of which 8 were waited for; matrix products, arithmetic and copies ran while one was open for 4% of the time, Pallas kernels for 27%

profile of v6, /device:TPU:0, one launch (start us, length us, event | category | flops | bytes accessed | tf_op | source)
XLA Modules:
  0.0 252.2 jit_solution(3847106837788331428)
XLA Ops:
  0.0 8.4 %row_forward.1 = bf16[2,2,2,528,256]{4,3,2,1,0:T(8,128)(2,1)} custom-call(s32[1]{0:T(128)} %bitcast.own, f32[64]{0:T(128)} %constant.58.clone.weights, bf16[512,4096]{1,0:T(8,128)(2,1)} %holo.1, bf16[512,4096]{1,0:T(8,128)(2,1)} %back.3, bf16[8,512,512]{2,1,0:T(8,128)(2,1)} %constant.57.clone.table), custom_call_target="tpu_custom_call" | custom-call | flops 10000000000 | bytes 12582912 | tf_op jit(solution)/shard_map/row_forward/pallas_call | solution.py:431
  8.4 6.3 %all-to-all-start = ((bf16[8,528,256]{2,1,0:T(8,128)(2,1)}), bf16[8,528,256]{2,1,0:T(8,128)(2,1)}, u32[]{:S(2)}, u32[]{:S(2)}) async-start(bf16[8,528,256]{2,1,0:T(8,128)(2,1)} %bitcast.91), calls=%async_computation | async-start | bytes 4325376 | tf_op jit(solution)/shard_map/all_to_all | solution.py:1212
  14.8 0.6 multiply_multiply_fusion.fx2
  15.4 10.9 %propagators.1.kernels = bf16[4,16,256,256]{3,2,1,0:T(8,128)(2,1)} custom-call(f32[1,128]{1,0:T(1,128)} %multiply_multiply_fusion.fx2), custom_call_target="tpu_custom_call" | custom-call | flops 1000000000 | bytes 16777216 | tf_op jit(solution)/shard_map/propagators/pallas_call | solution.py:471
  26.3 39.0 %all-to-all-done.data = bf16[8,528,256]{2,1,0:T(8,128)(2,1)} async-done(((bf16[8,528,256]{2,1,0:T(8,128)(2,1)}), bf16[8,528,256]{2,1,0:T(8,128)(2,1)}, u32[]{:S(2)}, u32[]{:S(2)}) %all-to-all-start) | async-done | bytes 2162720 | tf_op jit(solution)/shard_map/all_to_all | solution.py:1212
  65.4 12.8 %first_columns.1 = (bf16[2,2,2,2,128,512]{5,4,3,2,1,0:T(8,128)(2,1)}, bf16[8,512,256]{2,1,0:T(8,128)(2,1)}, bf16[1,16,512]{2,1,0:T(8,128)(2,1)}) custom-call(s32[1]{0:T(128)} %bitcast.1.half, bf16[8,528,256]{2,1,0:T(8,128)(2,1)} %all-to-all-done.data, bf16[4,16,256,256]{3,2,1,0:T(8,128)(2,1)} %propagators.1.kernels, ...), custom_call_target="tpu_custom_call" | custom-call | flops 10000000000 | bytes 16777216 | tf_op jit(solution)/shard_map/first_columns/pallas_call | solution.py:661
  78.2 4.6 %all-to-all-start.1 = ((bf16[16,128,512]{2,1,0:T(8,128)(2,1)}), bf16[16,128,512]{2,1,0:T(8,128)(2,1)}, u32[]{:S(2)}, u32[]{:S(2)}) async-start(bf16[16,128,512]{2,1,0:T(8,128)(2,1)} %bitcast.90), calls=%async_computation.1 | async-start | bytes 4194304 | tf_op jit(solution)/shard_map/all_to_all | solution.py:1227
  82.9 0.6 pad_add_fusion.own
  83.5 6.9 %nyquist.1.nyquist_in = f32[256,128]{1,0:T(8,128)} custom-call(s32[2]{0:T(128)} %pad_add_fusion.own, bf16[8,528,256]{2,1,0:T(8,128)(2,1)} %all-to-all-done.data), custom_call_target="tpu_custom_call" | custom-call | flops 1000000000 | bytes 262144 | tf_op jit(solution)/shard_map/nyquist/pallas_call | solution.py:908
  90.4 15.7 %next_columns.3 = (bf16[2,2,2,2,128,1024]{5,4,3,2,1,0:T(8,128)(2,1)}, bf16[2,16,512]{2,1,0:T(8,128)(2,1)}) custom-call(s32[1]{0:T(128)} %bitcast.1.half, bf16[8,512,256]{2,1,0:T(8,128)(2,1)} %get-tuple-element.27.spectrum, bf16[4,16,256,256]{3,2,1,0:T(8,128)(2,1)} %propagators.1.kernels, bf16[512,512]{1,0:T(8,128)(2,1)} %constant.61.clone.inner_back_in.inner_back, ...), custom_call_target="tpu_custom_call" | custom-call | flops 14000000000 | bytes 33554432 | tf_op jit(solution)/shard_map/next_columns/pallas_call | solution.py:701
  106.1 4.3 %all-to-all-done.1 = bf16[16,128,512]{2,1,0:T(8,128)(2,1)} async-done(((bf16[16,128,512]{2,1,0:T(8,128)(2,1)}), bf16[16,128,512]{2,1,0:T(8,128)(2,1)}, u32[]{:S(2)}, u32[]{:S(2)}) %all-to-all-start.1) | async-done | bytes 2097184 | tf_op jit(solution)/shard_map/all_to_all | solution.py:1227
  110.4 4.8 %all-to-all-start.2 = ((bf16[16,128,1024]{2,1,0:T(8,128)(2,1)}), bf16[16,128,1024]{2,1,0:T(8,128)(2,1)}, u32[]{:S(2)}, u32[]{:S(2)}) async-start(bf16[16,128,1024]{2,1,0:T(8,128)(2,1)} %bitcast.88), calls=%async_computation.2 | async-start | bytes 8388608 | tf_op jit(solution)/shard_map/all_to_all | solution.py:1227
  115.2 1.0 fusion.9
  116.3 8.4 %next_columns.2 = (bf16[2,2,2,2,128,512]{5,4,3,2,1,0:T(8,128)(2,1)}, bf16[1,16,512]{2,1,0:T(8,128)(2,1)}) custom-call(s32[1]{0:T(128)} %bitcast.1.half, bf16[8,512,256]{2,1,0:T(8,128)(2,1)} %get-tuple-element.27.spectrum, bf16[4,16,256,256]{3,2,1,0:T(8,128)(2,1)} %propagators.1.kernels, bf16[512,512]{1,0:T(8,128)(2,1)} %constant.61.clone.inner_back_in.inner_back, ...), custom_call_target="tpu_custom_call" | custom-call | flops 7000000000 | bytes 16777216 | tf_op jit(solution)/shard_map/next_columns/pallas_call | solution.py:701
  124.7 0.0 copy-start.2
  124.7 1.2 fusion.10
  126.0 0.8 fusion.5
  127.1 1.4 slice_reduce_fusion.1
  128.7 0.7 fusion.11
  129.6 0.1 pad_maximum_fusion.1
  129.7 0.1 copy.77
  129.8 0.1 fusion.4
  129.9 0.0 copy-done.2
  129.9 1.6 pad_maximum_fusion
  131.5 5.4 %row_inverse.2 = (bf16[1,128,4096]{2,1,0:T(8,128)(2,1)}, f32[1,16,4096]{2,1,0:T(8,128)}) custom-call(bf16[4,2,2,128,512]{4,3,2,1,0:T(8,128)(2,1)} %bitcast.26.parts, f32[256,128]{1,0:T(8,128)} %nyquist.1.nyquist_in, bf16[2,512,512]{2,1,0:T(8,128)(2,1)} %constant.65.clone.table.table_in, f32[16,256]{1,0:T(8,128)} %constant.66.clone.turn.turn_in), custom_call_target="tpu_custom_call" | custom-call | flops 3000000000 | bytes 8388608 | tf_op jit(solution)/shard_map/row_inverse/pallas_call | solution.py:830
  137.0 30.4 %all-to-all-done.2 = bf16[16,128,1024]{2,1,0:T(8,128)(2,1)} async-done(((bf16[16,128,1024]{2,1,0:T(8,128)(2,1)}), bf16[16,128,1024]{2,1,0:T(8,128)(2,1)}, u32[]{:S(2)}, u32[]{:S(2)}) %all-to-all-start.2) | async-done | bytes 4194336 | tf_op jit(solution)/shard_map/all_to_all | solution.py:1227
  167.3 5.6 %all-to-all-start.3 = ((bf16[16,144,512]{2,1,0:T(8,128)(2,1)}), bf16[16,144,512]{2,1,0:T(8,128)(2,1)}, u32[]{:S(2)}, u32[]{:S(2)}) async-start(bf16[16,144,512]{2,1,0:T(8,128)(2,1)} %pad_maximum_fusion), calls=%async_computation.3 | async-start | bytes 4718592 | tf_op jit(solution)/shard_map/all_to_all | solution.py:1227
  172.9 8.0 %row_inverse.3 = (bf16[2,128,4096]{2,1,0:T(8,128)(2,1)}, f32[2,16,4096]{2,1,0:T(8,128)}) custom-call(bf16[4,2,2,128,1024]{4,3,2,1,0:T(8,128)(2,1)} %bitcast.28.parts, f32[256,128]{1,0:T(8,128)} %nyquist.1.nyquist_in, bf16[2,512,512]{2,1,0:T(8,128)(2,1)} %constant.65.clone.table.table_in, f32[16,256]{1,0:T(8,128)} %constant.66.clone.turn.turn_in), custom_call_target="tpu_custom_call" | custom-call | flops 6000000000 | bytes 16777216 | tf_op jit(solution)/shard_map/row_inverse/pallas_call | solution.py:830
  180.9 9.3 %early_focus.1 = (bf16[128,4096]{1,0:T(8,128)(2,1)}, bf16[128,4096]{1,0:T(8,128)(2,1)}) custom-call(bf16[1,128,4096]{2,1,0:T(8,128)(2,1)} %get-tuple-element.40.first, bf16[2,128,4096]{2,1,0:T(8,128)(2,1)} %get-tuple-element.42.others), custom_call_target="tpu_custom_call" | custom-call | flops 1000000000 | bytes 12582912 | tf_op jit(solution)/shard_map/early_focus/pallas_call | solution.py:971
  190.2 13.3 %all-to-all-done.3 = bf16[16,144,512]{2,1,0:T(8,128)(2,1)} async-done(((bf16[16,144,512]{2,1,0:T(8,128)(2,1)}), bf16[16,144,512]{2,1,0:T(8,128)(2,1)}, u32[]{:S(2)}, u32[]{:S(2)}) %all-to-all-start.3) | async-done | bytes 2359328 | tf_op jit(solution)/shard_map/all_to_all | solution.py:1227
  203.5 8.4 %last_rows.1 = (bf16[64,4096]{1,0:T(8,128)(2,1)}, bf16[64,4096]{1,0:T(8,128)(2,1)}) custom-call(bf16[4,2,2,144,512]{4,3,2,1,0:T(8,128)(2,1)} %bitcast.29.parts, bf16[128,4096]{1,0:T(8,128)(2,1)} %get-tuple-element.43.best, bf16[128,4096]{1,0:T(8,128)(2,1)} %get-tuple-element.44.spatial, bf16[2,128,4096]{2,1,0:T(8,128)(2,1)} %get-tuple-element.42.others, ...), custom_call_target="tpu_custom_call" | custom-call | flops 3000000000 | bytes 16777216 | tf_op jit(solution)/shard_map/last_rows/pallas_call | solution.py:1089
  211.9 2.6 %collective-permute-start = (bf16[64,4096]{1,0:T(8,128)(2,1)}, bf16[64,4096]{1,0:T(8,128)(2,1)S(1)}, u32[]{:S(2)}, u32[]{:S(2)}) collective-permute-start(bf16[64,4096]{1,0:T(8,128)(2,1)} %get-tuple-element.47.refs_0_), channel_id=1, source_target_pairs={{0,8},{8,0},{16,24},{24,16},{1,9},{9,1},{17,25},{25,17},{2,10},{10... | collective-permute-start | bytes 1572872 | tf_op jit(solution)/shard_map/ppermute | solution.py:1182
  214.5 1.5 collective-permute-start.2
  216.0 0.6 collective-permute-start.4
  216.5 0.1 collective-permute-start.5
  216.6 10.9 %collective-permute-done.refs_1_ = bf16[64,4096]{1,0:T(8,128)(2,1)S(1)} collective-permute-done((bf16[64,4096]{1,0:T(8,128)(2,1)}, bf16[64,4096]{1,0:T(8,128)(2,1)S(1)}, u32[]{:S(2)}, u32[]{:S(2)}) %collective-permute-start) | collective-permute-done | bytes 524320 | tf_op jit(solution)/shard_map/ppermute | solution.py:1182
  227.5 1.5 collective-permute-start.1
  229.0 0.6 collective-permute-done.2.refs_5_
  229.6 1.4 collective-permute-start.3
  231.0 9.8 %collective-permute-done.4.refs_2_ = bf16[64,4096]{1,0:T(8,128)(2,1)S(1)} collective-permute-done((bf16[64,4096]{1,0:T(8,128)(2,1)}, bf16[64,4096]{1,0:T(8,128)(2,1)S(1)}, u32[]{:S(2)}, u32[]{:S(2)}) %collective-permute-start.4) | collective-permute-done | bytes 524320 | tf_op jit(solution)/shard_map/ppermute | solution.py:1183
  240.8 0.0 collective-permute-done.5.refs_4_
  240.8 0.0 copy-start
  240.8 1.0 copy-done
  241.9 1.0 copy-done.1
  242.9 2.9 %assemble.1.whole = f32[512,4096]{1,0:T(8,128)} custom-call(s32[1]{0:T(128)} %bitcast.own, bf16[64,4096]{1,0:T(8,128)(2,1)S(1)} %copy-done, bf16[64,4096]{1,0:T(8,128)(2,1)S(1)} %collective-permute-done.refs_1_, bf16[64,4096]{1,0:T(8,128)(2,1)S(1)} %collective-permute-done.4.refs_2_, bf16[64,4096]{1,0:T(8,128)(2,1)S(1)} %copy-done.1, ...), custom_call_target="tpu_custom_call" | custom-call | flops 1000000 | bytes 10485760 | tf_op jit(solution)/shard_map/assemble/pallas_call | solution.py:1131
  245.8 4.5 %collective-permute-done.1.upper = bf16[64,4096]{1,0:T(8,128)(2,1)S(1)} collective-permute-done((bf16[64,4096]{1,0:T(8,128)(2,1)S(1)}, bf16[64,4096]{1,0:T(8,128)(2,1)S(1)}, u32[]{:S(2)}, u32[]{:S(2)}) %collective-permute-start.1) | collective-permute-done | bytes 524320 | tf_op jit(solution)/shard_map/ppermute | solution.py:1183
  250.4 0.0 collective-permute-done.3.lower
  250.4 1.9 complete.1
  (38 shorter events, 0.7 us)
Async XLA Ops:
  8.4 56.9 %all-to-all-start = ((bf16[8,528,256]{2,1,0:T(8,128)(2,1)}), bf16[8,528,256]{2,1,0:T(8,128)(2,1)}, u32[]{:S(2)}, u32[]{:S(2)}) async-start(bf16[8,528,256]{2,1,0:T(8,128)(2,1)} %bitcast.91), calls=%async_computation | async-start | bytes 4325376 | tf_op jit(solution)/shard_map/all_to_all | solution.py:1212
  78.2 32.2 %all-to-all-start.1 = ((bf16[16,128,512]{2,1,0:T(8,128)(2,1)}), bf16[16,128,512]{2,1,0:T(8,128)(2,1)}, u32[]{:S(2)}, u32[]{:S(2)}) async-start(bf16[16,128,512]{2,1,0:T(8,128)(2,1)} %bitcast.90), calls=%async_computation.1 | async-start | bytes 4194304 | tf_op jit(solution)/shard_map/all_to_all | solution.py:1227
  110.4 56.9 %all-to-all-start.2 = ((bf16[16,128,1024]{2,1,0:T(8,128)(2,1)}), bf16[16,128,1024]{2,1,0:T(8,128)(2,1)}, u32[]{:S(2)}, u32[]{:S(2)}) async-start(bf16[16,128,1024]{2,1,0:T(8,128)(2,1)} %bitcast.88), calls=%async_computation.2 | async-start | bytes 8388608 | tf_op jit(solution)/shard_map/all_to_all | solution.py:1227
  124.7 5.2 %copy-start.2 = (bf16[2,2,2,2,128,512]{5,4,3,2,1,0:T(8,128)(2,1)S(1)}, bf16[2,2,2,2,128,512]{5,4,3,2,1,0:T(8,128)(2,1)}, u32[]{:S(2)}) copy-start(bf16[2,2,2,2,128,512]{5,4,3,2,1,0:T(8,128)(2,1)} %get-tuple-element.28) | copy-start | bytes 6291460
  167.3 36.1 %all-to-all-start.3 = ((bf16[16,144,512]{2,1,0:T(8,128)(2,1)}), bf16[16,144,512]{2,1,0:T(8,128)(2,1)}, u32[]{:S(2)}, u32[]{:S(2)}) async-start(bf16[16,144,512]{2,1,0:T(8,128)(2,1)} %pad_maximum_fusion), calls=%async_computation.3 | async-start | bytes 4718592 | tf_op jit(solution)/shard_map/all_to_all | solution.py:1227
  211.9 15.6 %collective-permute-start = (bf16[64,4096]{1,0:T(8,128)(2,1)}, bf16[64,4096]{1,0:T(8,128)(2,1)S(1)}, u32[]{:S(2)}, u32[]{:S(2)}) collective-permute-start(bf16[64,4096]{1,0:T(8,128)(2,1)} %get-tuple-element.47.refs_0_), channel_id=1, source_target_pairs={{0,8},{8,0},{16,24},{24,16},{1,9},{9,1},{17,25},{25,17},{2,10},{10... | collective-permute-start | bytes 1572872 | tf_op jit(solution)/shard_map/ppermute | solution.py:1182
  214.5 15.1 %collective-permute-start.2 = (bf16[64,4096]{1,0:T(8,128)(2,1)}, bf16[64,4096]{1,0:T(8,128)(2,1)S(1)}, u32[]{:S(2)}, u32[]{:S(2)}) collective-permute-start(bf16[64,4096]{1,0:T(8,128)(2,1)} %get-tuple-element.48.refs_3_), channel_id=1, source_target_pairs={{0,16},{8,24},{16,0},{24,8},{1,17},{9,25},{17,1},{25,9},{2,18},{10... | collective-permute-start | bytes 1572872 | tf_op jit(solution)/shard_map/ppermute | solution.py:1182
  216.0 24.8 %collective-permute-start.4 = (bf16[64,4096]{1,0:T(8,128)(2,1)}, bf16[64,4096]{1,0:T(8,128)(2,1)S(1)}, u32[]{:S(2)}, u32[]{:S(2)}) collective-permute-start(bf16[64,4096]{1,0:T(8,128)(2,1)} %get-tuple-element.47.refs_0_), channel_id=1, source_target_pairs={{0,16},{8,24},{16,0},{24,8},{1,17},{9,25},{17,1},{25,9},{2,18},{10... | collective-permute-start | bytes 1572872 | tf_op jit(solution)/shard_map/ppermute | solution.py:1183
  216.5 24.3 %collective-permute-start.5 = (bf16[64,4096]{1,0:T(8,128)(2,1)}, bf16[64,4096]{1,0:T(8,128)(2,1)S(1)}, u32[]{:S(2)}, u32[]{:S(2)}) collective-permute-start(bf16[64,4096]{1,0:T(8,128)(2,1)} %get-tuple-element.48.refs_3_), channel_id=1, source_target_pairs={{0,8},{8,0},{16,24},{24,16},{1,9},{9,1},{17,25},{25,17},{2,10},{10... | collective-permute-start | bytes 1572872 | tf_op jit(solution)/shard_map/ppermute | solution.py:1184
  227.5 22.9 %collective-permute-start.1 = (bf16[64,4096]{1,0:T(8,128)(2,1)S(1)}, bf16[64,4096]{1,0:T(8,128)(2,1)S(1)}, u32[]{:S(2)}, u32[]{:S(2)}) collective-permute-start(bf16[64,4096]{1,0:T(8,128)(2,1)S(1)} %collective-permute-done.refs_1_), channel_id=1, source_target_pairs={{0,16},{8,24},{16,0},{24,8},{1,17},{9,25},{17,1},{25,9},{2,18},{10... | collective-permute-start | bytes 1572872 | tf_op jit(solution)/shard_map/ppermute | solution.py:1183
  229.6 20.8 %collective-permute-start.3 = (bf16[64,4096]{1,0:T(8,128)(2,1)S(1)}, bf16[64,4096]{1,0:T(8,128)(2,1)S(1)}, u32[]{:S(2)}, u32[]{:S(2)}) collective-permute-start(bf16[64,4096]{1,0:T(8,128)(2,1)S(1)} %collective-permute-done.2.refs_5_), channel_id=1, source_target_pairs={{0,8},{8,0},{16,24},{24,16},{1,9},{9,1},{17,25},{25,17},{2,10},{10... | collective-permute-start | bytes 1572872 | tf_op jit(solution)/shard_map/ppermute | solution.py:1184
  240.8 1.0 copy-start
  241.9 1.0 copy-start.1

commit v7 on v6

--- a/solution.py
+++ b/solution.py
@@ -380,7 +380,7 @@
                 inverse = pl.reciprocal(below, approx=True)
                 inverse = inverse * (2.0 - below * inverse)
                 value = holo_buf[here, there].astype(jnp.float32) * inverse
-                return (value - 1.0).astype(jnp.bfloat16).astype(jnp.float32)
+                return value - 1.0
 
             sums = sixteen_sums(term, lambda n: weights[group * 16 + n])
             for q in range(4):

time: 253 us -> 253 us (level)
  no operation moved by 1% of the time
where the time goes in v7:
time: 253 us; the launch traced here: 252 us
  waiting for transfers between devices  113 us (45%)
  Pallas kernels  98.7 us (39%)
  starting transfers between devices  28.9 us (11%)
  local copies, waits for them, and re-layouts  6.95 us (3%)
  other arithmetic  4.03 us (2%)
    all_to_all x3, waiting for transfers between devices, to_rows(): lax.all_to_all(halfway.reshape(16, -1, halfway.shape[-1]), ('depth', 'low...  48 us
    all_to_all x1, waiting for transfers between devices, half_spectrum_shards(): lax.all_to_all(sections.reshape(8, rows + 16, 2 * LANE), ('high', 'low',...  39 us
    pallas_call x2, Pallas kernels, next_columns(): pl.pallas_call(next_columns_kernel, grid_spec=pltpu.PrefetchScalarGridSpe...  24.1 us
    all_to_all x3, starting transfers between devices, to_rows(): lax.all_to_all(halfway.reshape(16, -1, halfway.shape[-1]), ('depth', 'low...  15 us
    pallas_call x2, Pallas kernels, row_inverse(): pl.pallas_call(functools.partial(row_inverse_kernel, plane), grid=(count,...  13.4 us
    pallas_call x1, Pallas kernels, first_columns(): pl.pallas_call(first_columns_kernel, grid_spec=pltpu.PrefetchScalarGridSp...  12.8 us
    pallas_call x1, Pallas kernels, propagators(): pl.pallas_call(functools.partial(propagator_kernel, planes), grid=(OUT,),...  10.9 us
    ppermute x1, waiting for transfers between devices, exchange_depth(): lax.ppermute(a, 'depth', OVER_X)  10.9 us
  transfers between devices with their start and end apart: 10, of which 8 were waited for; matrix products, arithmetic and copies ran while one was open for 4% of the time, Pallas kernels for 27%

profile of v7, /device:TPU:0, one launch (start us, length us, event | category | flops | bytes accessed | tf_op | source)
XLA Modules:
  0.0 251.9 jit_solution(3354704955489569050)
XLA Ops:
  0.0 8.1 %row_forward.1 = bf16[2,2,2,528,256]{4,3,2,1,0:T(8,128)(2,1)} custom-call(s32[1]{0:T(128)} %bitcast.own, f32[64]{0:T(128)} %constant.58.clone.weights, bf16[512,4096]{1,0:T(8,128)(2,1)} %holo.1, bf16[512,4096]{1,0:T(8,128)(2,1)} %back.3, bf16[8,512,512]{2,1,0:T(8,128)(2,1)} %constant.57.clone.table), custom_call_target="tpu_custom_call" | custom-call | flops 10000000000 | bytes 12582912 | tf_op jit(solution)/shard_map/row_forward/pallas_call | solution.py:431
  8.1 6.3 %all-to-all-start = ((bf16[8,528,256]{2,1,0:T(8,128)(2,1)}), bf16[8,528,256]{2,1,0:T(8,128)(2,1)}, u32[]{:S(2)}, u32[]{:S(2)}) async-start(bf16[8,528,256]{2,1,0:T(8,128)(2,1)} %bitcast.91), calls=%async_computation | async-start | bytes 4325376 | tf_op jit(solution)/shard_map/all_to_all | solution.py:1212
  14.4 0.6 multiply_multiply_fusion.fx2
  15.0 10.9 %propagators.1.kernels = bf16[4,16,256,256]{3,2,1,0:T(8,128)(2,1)} custom-call(f32[1,128]{1,0:T(1,128)} %multiply_multiply_fusion.fx2), custom_call_target="tpu_custom_call" | custom-call | flops 1000000000 | bytes 16777216 | tf_op jit(solution)/shard_map/propagators/pallas_call | solution.py:471
  26.0 39.0 %all-to-all-done.data = bf16[8,528,256]{2,1,0:T(8,128)(2,1)} async-done(((bf16[8,528,256]{2,1,0:T(8,128)(2,1)}), bf16[8,528,256]{2,1,0:T(8,128)(2,1)}, u32[]{:S(2)}, u32[]{:S(2)}) %all-to-all-start) | async-done | bytes 2162720 | tf_op jit(solution)/shard_map/all_to_all | solution.py:1212
  65.0 12.8 %first_columns.1 = (bf16[2,2,2,2,128,512]{5,4,3,2,1,0:T(8,128)(2,1)}, bf16[8,512,256]{2,1,0:T(8,128)(2,1)}, bf16[1,16,512]{2,1,0:T(8,128)(2,1)}) custom-call(s32[1]{0:T(128)} %bitcast.1.half, bf16[8,528,256]{2,1,0:T(8,128)(2,1)} %all-to-all-done.data, bf16[4,16,256,256]{3,2,1,0:T(8,128)(2,1)} %propagators.1.kernels, ...), custom_call_target="tpu_custom_call" | custom-call | flops 10000000000 | bytes 16777216 | tf_op jit(solution)/shard_map/first_columns/pallas_call | solution.py:661
  77.9 4.6 %all-to-all-start.1 = ((bf16[16,128,512]{2,1,0:T(8,128)(2,1)}), bf16[16,128,512]{2,1,0:T(8,128)(2,1)}, u32[]{:S(2)}, u32[]{:S(2)}) async-start(bf16[16,128,512]{2,1,0:T(8,128)(2,1)} %bitcast.90), calls=%async_computation.1 | async-start | bytes 4194304 | tf_op jit(solution)/shard_map/all_to_all | solution.py:1227
  82.5 0.6 pad_add_fusion.own
  83.2 6.9 %nyquist.1.nyquist_in = f32[256,128]{1,0:T(8,128)} custom-call(s32[2]{0:T(128)} %pad_add_fusion.own, bf16[8,528,256]{2,1,0:T(8,128)(2,1)} %all-to-all-done.data), custom_call_target="tpu_custom_call" | custom-call | flops 1000000000 | bytes 262144 | tf_op jit(solution)/shard_map/nyquist/pallas_call | solution.py:908
  90.1 15.7 %next_columns.3 = (bf16[2,2,2,2,128,1024]{5,4,3,2,1,0:T(8,128)(2,1)}, bf16[2,16,512]{2,1,0:T(8,128)(2,1)}) custom-call(s32[1]{0:T(128)} %bitcast.1.half, bf16[8,512,256]{2,1,0:T(8,128)(2,1)} %get-tuple-element.27.spectrum, bf16[4,16,256,256]{3,2,1,0:T(8,128)(2,1)} %propagators.1.kernels, bf16[512,512]{1,0:T(8,128)(2,1)} %constant.61.clone.inner_back_in.inner_back, ...), custom_call_target="tpu_custom_call" | custom-call | flops 14000000000 | bytes 33554432 | tf_op jit(solution)/shard_map/next_columns/pallas_call | solution.py:701
  105.7 4.3 %all-to-all-done.1 = bf16[16,128,512]{2,1,0:T(8,128)(2,1)} async-done(((bf16[16,128,512]{2,1,0:T(8,128)(2,1)}), bf16[16,128,512]{2,1,0:T(8,128)(2,1)}, u32[]{:S(2)}, u32[]{:S(2)}) %all-to-all-start.1) | async-done | bytes 2097184 | tf_op jit(solution)/shard_map/all_to_all | solution.py:1227
  110.0 4.8 %all-to-all-start.2 = ((bf16[16,128,1024]{2,1,0:T(8,128)(2,1)}), bf16[16,128,1024]{2,1,0:T(8,128)(2,1)}, u32[]{:S(2)}, u32[]{:S(2)}) async-start(bf16[16,128,1024]{2,1,0:T(8,128)(2,1)} %bitcast.88), calls=%async_computation.2 | async-start | bytes 8388608 | tf_op jit(solution)/shard_map/all_to_all | solution.py:1227
  114.8 1.0 fusion.9
  116.0 8.4 %next_columns.2 = (bf16[2,2,2,2,128,512]{5,4,3,2,1,0:T(8,128)(2,1)}, bf16[1,16,512]{2,1,0:T(8,128)(2,1)}) custom-call(s32[1]{0:T(128)} %bitcast.1.half, bf16[8,512,256]{2,1,0:T(8,128)(2,1)} %get-tuple-element.27.spectrum, bf16[4,16,256,256]{3,2,1,0:T(8,128)(2,1)} %propagators.1.kernels, bf16[512,512]{1,0:T(8,128)(2,1)} %constant.61.clone.inner_back_in.inner_back, ...), custom_call_target="tpu_custom_call" | custom-call | flops 7000000000 | bytes 16777216 | tf_op jit(solution)/shard_map/next_columns/pallas_call | solution.py:701
  124.4 0.0 copy-start.2
  124.4 1.2 fusion.10
  125.7 0.8 fusion.5
  126.8 1.4 slice_reduce_fusion.1
  128.3 0.7 fusion.11
  129.2 0.1 pad_maximum_fusion.1
  129.4 0.1 copy.77
  129.4 0.1 fusion.4
  129.6 0.0 copy-done.2
  129.6 1.6 pad_maximum_fusion
  131.2 5.4 %row_inverse.2 = (bf16[1,128,4096]{2,1,0:T(8,128)(2,1)}, f32[1,16,4096]{2,1,0:T(8,128)}) custom-call(bf16[4,2,2,128,512]{4,3,2,1,0:T(8,128)(2,1)} %bitcast.26.parts, f32[256,128]{1,0:T(8,128)} %nyquist.1.nyquist_in, bf16[2,512,512]{2,1,0:T(8,128)(2,1)} %constant.65.clone.table.table_in, f32[16,256]{1,0:T(8,128)} %constant.66.clone.turn.turn_in), custom_call_target="tpu_custom_call" | custom-call | flops 3000000000 | bytes 8388608 | tf_op jit(solution)/shard_map/row_inverse/pallas_call | solution.py:830
  136.6 30.4 %all-to-all-done.2 = bf16[16,128,1024]{2,1,0:T(8,128)(2,1)} async-done(((bf16[16,128,1024]{2,1,0:T(8,128)(2,1)}), bf16[16,128,1024]{2,1,0:T(8,128)(2,1)}, u32[]{:S(2)}, u32[]{:S(2)}) %all-to-all-start.2) | async-done | bytes 4194336 | tf_op jit(solution)/shard_map/all_to_all | solution.py:1227
  167.0 5.6 %all-to-all-start.3 = ((bf16[16,144,512]{2,1,0:T(8,128)(2,1)}), bf16[16,144,512]{2,1,0:T(8,128)(2,1)}, u32[]{:S(2)}, u32[]{:S(2)}) async-start(bf16[16,144,512]{2,1,0:T(8,128)(2,1)} %pad_maximum_fusion), calls=%async_computation.3 | async-start | bytes 4718592 | tf_op jit(solution)/shard_map/all_to_all | solution.py:1227
  172.5 8.0 %row_inverse.3 = (bf16[2,128,4096]{2,1,0:T(8,128)(2,1)}, f32[2,16,4096]{2,1,0:T(8,128)}) custom-call(bf16[4,2,2,128,1024]{4,3,2,1,0:T(8,128)(2,1)} %bitcast.28.parts, f32[256,128]{1,0:T(8,128)} %nyquist.1.nyquist_in, bf16[2,512,512]{2,1,0:T(8,128)(2,1)} %constant.65.clone.table.table_in, f32[16,256]{1,0:T(8,128)} %constant.66.clone.turn.turn_in), custom_call_target="tpu_custom_call" | custom-call | flops 6000000000 | bytes 16777216 | tf_op jit(solution)/shard_map/row_inverse/pallas_call | solution.py:830
  180.5 9.3 %early_focus.1 = (bf16[128,4096]{1,0:T(8,128)(2,1)}, bf16[128,4096]{1,0:T(8,128)(2,1)}) custom-call(bf16[1,128,4096]{2,1,0:T(8,128)(2,1)} %get-tuple-element.40.first, bf16[2,128,4096]{2,1,0:T(8,128)(2,1)} %get-tuple-element.42.others), custom_call_target="tpu_custom_call" | custom-call | flops 1000000000 | bytes 12582912 | tf_op jit(solution)/shard_map/early_focus/pallas_call | solution.py:971
  189.8 13.3 %all-to-all-done.3 = bf16[16,144,512]{2,1,0:T(8,128)(2,1)} async-done(((bf16[16,144,512]{2,1,0:T(8,128)(2,1)}), bf16[16,144,512]{2,1,0:T(8,128)(2,1)}, u32[]{:S(2)}, u32[]{:S(2)}) %all-to-all-start.3) | async-done | bytes 2359328 | tf_op jit(solution)/shard_map/all_to_all | solution.py:1227
  203.1 8.4 %last_rows.1 = (bf16[64,4096]{1,0:T(8,128)(2,1)}, bf16[64,4096]{1,0:T(8,128)(2,1)}) custom-call(bf16[4,2,2,144,512]{4,3,2,1,0:T(8,128)(2,1)} %bitcast.29.parts, bf16[128,4096]{1,0:T(8,128)(2,1)} %get-tuple-element.43.best, bf16[128,4096]{1,0:T(8,128)(2,1)} %get-tuple-element.44.spatial, bf16[2,128,4096]{2,1,0:T(8,128)(2,1)} %get-tuple-element.42.others, ...), custom_call_target="tpu_custom_call" | custom-call | flops 3000000000 | bytes 16777216 | tf_op jit(solution)/shard_map/last_rows/pallas_call | solution.py:1089
  211.5 2.6 %collective-permute-start = (bf16[64,4096]{1,0:T(8,128)(2,1)}, bf16[64,4096]{1,0:T(8,128)(2,1)S(1)}, u32[]{:S(2)}, u32[]{:S(2)}) collective-permute-start(bf16[64,4096]{1,0:T(8,128)(2,1)} %get-tuple-element.47.refs_0_), channel_id=1, source_target_pairs={{0,8},{8,0},{16,24},{24,16},{1,9},{9,1},{17,25},{25,17},{2,10},{10... | collective-permute-start | bytes 1572872 | tf_op jit(solution)/shard_map/ppermute | solution.py:1182
  214.1 1.5 collective-permute-start.2
  215.6 0.6 collective-permute-start.4
  216.2 0.1 collective-permute-start.5
  216.2 10.9 %collective-permute-done.refs_1_ = bf16[64,4096]{1,0:T(8,128)(2,1)S(1)} collective-permute-done((bf16[64,4096]{1,0:T(8,128)(2,1)}, bf16[64,4096]{1,0:T(8,128)(2,1)S(1)}, u32[]{:S(2)}, u32[]{:S(2)}) %collective-permute-start) | collective-permute-done | bytes 524320 | tf_op jit(solution)/shard_map/ppermute | solution.py:1182
  227.1 1.5 collective-permute-start.1
  228.6 0.6 collective-permute-done.2.refs_5_
  229.2 1.4 collective-permute-start.3
  230.7 9.8 %collective-permute-done.4.refs_2_ = bf16[64,4096]{1,0:T(8,128)(2,1)S(1)} collective-permute-done((bf16[64,4096]{1,0:T(8,128)(2,1)}, bf16[64,4096]{1,0:T(8,128)(2,1)S(1)}, u32[]{:S(2)}, u32[]{:S(2)}) %collective-permute-start.4) | collective-permute-done | bytes 524320 | tf_op jit(solution)/shard_map/ppermute | solution.py:1183
  240.5 0.0 collective-permute-done.5.refs_4_
  240.5 0.0 copy-start
  240.5 1.0 copy-done
  241.5 1.0 copy-done.1
  242.5 2.9 %assemble.1.whole = f32[512,4096]{1,0:T(8,128)} custom-call(s32[1]{0:T(128)} %bitcast.own, bf16[64,4096]{1,0:T(8,128)(2,1)S(1)} %copy-done, bf16[64,4096]{1,0:T(8,128)(2,1)S(1)} %collective-permute-done.refs_1_, bf16[64,4096]{1,0:T(8,128)(2,1)S(1)} %collective-permute-done.4.refs_2_, bf16[64,4096]{1,0:T(8,128)(2,1)S(1)} %copy-done.1, ...), custom_call_target="tpu_custom_call" | custom-call | flops 1000000 | bytes 10485760 | tf_op jit(solution)/shard_map/assemble/pallas_call | solution.py:1131
  245.5 4.5 %collective-permute-done.1.upper = bf16[64,4096]{1,0:T(8,128)(2,1)S(1)} collective-permute-done((bf16[64,4096]{1,0:T(8,128)(2,1)S(1)}, bf16[64,4096]{1,0:T(8,128)(2,1)S(1)}, u32[]{:S(2)}, u32[]{:S(2)}) %collective-permute-start.1) | collective-permute-done | bytes 524320 | tf_op jit(solution)/shard_map/ppermute | solution.py:1183
  250.0 0.0 collective-permute-done.3.lower
  250.0 1.9 complete.1
  (38 shorter events, 0.7 us)
Async XLA Ops:
  8.1 56.9 %all-to-all-start = ((bf16[8,528,256]{2,1,0:T(8,128)(2,1)}), bf16[8,528,256]{2,1,0:T(8,128)(2,1)}, u32[]{:S(2)}, u32[]{:S(2)}) async-start(bf16[8,528,256]{2,1,0:T(8,128)(2,1)} %bitcast.91), calls=%async_computation | async-start | bytes 4325376 | tf_op jit(solution)/shard_map/all_to_all | solution.py:1212
  77.9 32.2 %all-to-all-start.1 = ((bf16[16,128,512]{2,1,0:T(8,128)(2,1)}), bf16[16,128,512]{2,1,0:T(8,128)(2,1)}, u32[]{:S(2)}, u32[]{:S(2)}) async-start(bf16[16,128,512]{2,1,0:T(8,128)(2,1)} %bitcast.90), calls=%async_computation.1 | async-start | bytes 4194304 | tf_op jit(solution)/shard_map/all_to_all | solution.py:1227
  110.0 56.9 %all-to-all-start.2 = ((bf16[16,128,1024]{2,1,0:T(8,128)(2,1)}), bf16[16,128,1024]{2,1,0:T(8,128)(2,1)}, u32[]{:S(2)}, u32[]{:S(2)}) async-start(bf16[16,128,1024]{2,1,0:T(8,128)(2,1)} %bitcast.88), calls=%async_computation.2 | async-start | bytes 8388608 | tf_op jit(solution)/shard_map/all_to_all | solution.py:1227
  124.4 5.2 %copy-start.2 = (bf16[2,2,2,2,128,512]{5,4,3,2,1,0:T(8,128)(2,1)S(1)}, bf16[2,2,2,2,128,512]{5,4,3,2,1,0:T(8,128)(2,1)}, u32[]{:S(2)}) copy-start(bf16[2,2,2,2,128,512]{5,4,3,2,1,0:T(8,128)(2,1)} %get-tuple-element.28) | copy-start | bytes 6291460
  167.0 36.1 %all-to-all-start.3 = ((bf16[16,144,512]{2,1,0:T(8,128)(2,1)}), bf16[16,144,512]{2,1,0:T(8,128)(2,1)}, u32[]{:S(2)}, u32[]{:S(2)}) async-start(bf16[16,144,512]{2,1,0:T(8,128)(2,1)} %pad_maximum_fusion), calls=%async_computation.3 | async-start | bytes 4718592 | tf_op jit(solution)/shard_map/all_to_all | solution.py:1227
  211.5 15.6 %collective-permute-start = (bf16[64,4096]{1,0:T(8,128)(2,1)}, bf16[64,4096]{1,0:T(8,128)(2,1)S(1)}, u32[]{:S(2)}, u32[]{:S(2)}) collective-permute-start(bf16[64,4096]{1,0:T(8,128)(2,1)} %get-tuple-element.47.refs_0_), channel_id=1, source_target_pairs={{0,8},{8,0},{16,24},{24,16},{1,9},{9,1},{17,25},{25,17},{2,10},{10... | collective-permute-start | bytes 1572872 | tf_op jit(solution)/shard_map/ppermute | solution.py:1182
  214.1 15.1 %collective-permute-start.2 = (bf16[64,4096]{1,0:T(8,128)(2,1)}, bf16[64,4096]{1,0:T(8,128)(2,1)S(1)}, u32[]{:S(2)}, u32[]{:S(2)}) collective-permute-start(bf16[64,4096]{1,0:T(8,128)(2,1)} %get-tuple-element.48.refs_3_), channel_id=1, source_target_pairs={{0,16},{8,24},{16,0},{24,8},{1,17},{9,25},{17,1},{25,9},{2,18},{10... | collective-permute-start | bytes 1572872 | tf_op jit(solution)/shard_map/ppermute | solution.py:1182
  215.6 24.8 %collective-permute-start.4 = (bf16[64,4096]{1,0:T(8,128)(2,1)}, bf16[64,4096]{1,0:T(8,128)(2,1)S(1)}, u32[]{:S(2)}, u32[]{:S(2)}) collective-permute-start(bf16[64,4096]{1,0:T(8,128)(2,1)} %get-tuple-element.47.refs_0_), channel_id=1, source_target_pairs={{0,16},{8,24},{16,0},{24,8},{1,17},{9,25},{17,1},{25,9},{2,18},{10... | collective-permute-start | bytes 1572872 | tf_op jit(solution)/shard_map/ppermute | solution.py:1183
  216.2 24.3 %collective-permute-start.5 = (bf16[64,4096]{1,0:T(8,128)(2,1)}, bf16[64,4096]{1,0:T(8,128)(2,1)S(1)}, u32[]{:S(2)}, u32[]{:S(2)}) collective-permute-start(bf16[64,4096]{1,0:T(8,128)(2,1)} %get-tuple-element.48.refs_3_), channel_id=1, source_target_pairs={{0,8},{8,0},{16,24},{24,16},{1,9},{9,1},{17,25},{25,17},{2,10},{10... | collective-permute-start | bytes 1572872 | tf_op jit(solution)/shard_map/ppermute | solution.py:1184
  227.1 22.9 %collective-permute-start.1 = (bf16[64,4096]{1,0:T(8,128)(2,1)S(1)}, bf16[64,4096]{1,0:T(8,128)(2,1)S(1)}, u32[]{:S(2)}, u32[]{:S(2)}) collective-permute-start(bf16[64,4096]{1,0:T(8,128)(2,1)S(1)} %collective-permute-done.refs_1_), channel_id=1, source_target_pairs={{0,16},{8,24},{16,0},{24,8},{1,17},{9,25},{17,1},{25,9},{2,18},{10... | collective-permute-start | bytes 1572872 | tf_op jit(solution)/shard_map/ppermute | solution.py:1183
  229.2 20.8 %collective-permute-start.3 = (bf16[64,4096]{1,0:T(8,128)(2,1)S(1)}, bf16[64,4096]{1,0:T(8,128)(2,1)S(1)}, u32[]{:S(2)}, u32[]{:S(2)}) collective-permute-start(bf16[64,4096]{1,0:T(8,128)(2,1)S(1)} %collective-permute-done.2.refs_5_), channel_id=1, source_target_pairs={{0,8},{8,0},{16,24},{24,16},{1,9},{9,1},{17,25},{25,17},{2,10},{10... | collective-permute-start | bytes 1572872 | tf_op jit(solution)/shard_map/ppermute | solution.py:1184
  240.5 1.0 copy-start
  241.5 1.0 copy-start.1

commit v8 on v6

--- a/solution.py
+++ b/solution.py
@@ -317,7 +317,7 @@
 
 
 CHUNK = 64
-BATCHES = ((0,), (1, 2), (3, 4), (5, 6, 7))
+BATCHES = ((1, 2), (3, 4), (5, 6, 7), (0,))
 
 
 def sixteen_sums(term, w):
@@ -1012,25 +1012,29 @@
     late += (edge0_in, edge0), (edge12_in, edge12)
     for i, (source, target) in enumerate(late):
         loads.append(pltpu.make_async_copy(source, target, sems.at[1, i]))
-    early = (nyquist_in, nyquist), (table_in, table), (turn_in, turn)
+    early = (turn_in, turn), (table_in.at[1], table.at[1])
+    early += (table_in.at[0], table.at[0]), (nyquist_in, nyquist)
     early = [pltpu.make_async_copy(a, b, sems.at[2, i]) for i, (a, b) in enumerate(early)]
-    for load in early + loads:
+    for load in early[:2] + loads[1:CLS] + early[2:] + loads[:1] + loads[CLS:]:
         load.start()
-    for load in early:
+    for load in early[:2]:
         load.wait()
     lane = lax.broadcasted_iota(jnp.int32, (rows, LANE), 1)
     few_lane = lax.broadcasted_iota(jnp.int32, (16, LANE), 1)
     few_row = lax.broadcasted_iota(jnp.int32, (16, LANE), 0)
-    beside = jnp.where(few_row % 2 == 0, nyquist[rows : rows + 1, :], nyquist[rows + 1 : rows + 2, :])
     columns = []
-    for part in range(2):
-        mine = jnp.where(lane == 6 + part, nyquist[:rows, :], 0.0)
-        few = jnp.where(few_lane == (few_row // 2) * 2 + part, beside, 0.0)
-        column = jnp.sum(jnp.concatenate([mine, few], axis=0), axis=1, keepdims=True)
-        columns.append(column.astype(jnp.bfloat16))
     for groups in BATCHES:
         for group in groups:
             loads[group].wait()
+        if groups[0] == 0:
+            for load in early[2:]:
+                load.wait()
+            beside = jnp.where(few_row % 2 == 0, nyquist[rows : rows + 1, :], nyquist[rows + 1 : rows + 2, :])
+            for part in range(2):
+                mine = jnp.where(lane == 6 + part, nyquist[:rows, :], 0.0)
+                few = jnp.where(few_lane == (few_row // 2) * 2 + part, beside, 0.0)
+                column = jnp.sum(jnp.concatenate([mine, few], axis=0), axis=1, keepdims=True)
+                columns.append(column.astype(jnp.bfloat16))
         halves = [[part_buf[g, i] for i in range(2)] for g in groups]
         open_classes(groups, halves, columns, table, turn, opened)
 
@@ -1075,7 +1079,7 @@
         value = jnp.where(index == 15 * side, ends[side : side + 1], both[here].astype(jnp.float32))
         both[here] = value.astype(jnp.bfloat16)
         source = both.at[pl.ds(side * half, half)]
-        stores.append(pltpu.make_async_copy(source, out, sems.at[2, 3 + side]))
+        stores.append(pltpu.make_async_copy(source, out, sems.at[2, 4 + side]))
         stores[-1].start()
     for store in stores:
         store.wait()
@@ -1144,27 +1148,25 @@
 
 
 def complete_kernel(own, upper, lower, whole, out):
-    half = lower.shape[0] // 2
     step = pl.program_id(0)
     for s, ref in enumerate((upper, lower)):
-        for part in range(2):
-
-            @pl.when(step == 2 * s + part)
-            def _():
-                out[...] = ref[part * half : (part + 1) * half].astype(jnp.float32)
+
+        @pl.when(step == s)
+        def _():
+            out[...] = ref[...].astype(jnp.float32)
 
 
 def complete(depth_index, upper, lower, whole):
     half = upper.shape[0]
     both = pl.BlockSpec((half, N), lambda i, o: (0, 0))
-    place = lambda i, o: (jnp.bitwise_xor(3, o[0]) * 4 + i, 0)
+    place = lambda i, o: (jnp.bitwise_xor(3, o[0]) * 2 + i, 0)
     return pl.pallas_call(
         complete_kernel,
         grid_spec=pltpu.PrefetchScalarGridSpec(
             num_scalar_prefetch=1,
-            grid=(4,),
+            grid=(2,),
             in_specs=[both, both, pl.BlockSpec(memory_space=pl.ANY)],
-            out_specs=pl.BlockSpec((half // 2, N), place),
+            out_specs=pl.BlockSpec((half, N), place),
         ),
         out_shape=jax.ShapeDtypeStruct(whole.shape, jnp.float32),
         input_output_aliases={3: 0},

time: 253 us -> 252 us (level)
  no operation moved by 1% of the time
where the time goes in v8:
time: 252 us
  waiting for transfers between devices  113 us (45%)
  Pallas kernels  98.3 us (39%)
  starting transfers between devices  28.9 us (11%)
  local copies, waits for them, and re-layouts  6.95 us (3%)
  other arithmetic  4.03 us (2%)
    all_to_all x3, waiting for transfers between devices, to_rows(): lax.all_to_all(halfway.reshape(16, -1, halfway.shape[-1]), ('depth', 'low...  48.1 us
    all_to_all x1, waiting for transfers between devices, half_spectrum_shards(): lax.all_to_all(sections.reshape(8, rows + 16, 2 * LANE), ('high', 'low',...  39 us
    pallas_call x2, Pallas kernels, next_columns(): pl.pallas_call(next_columns_kernel, grid_spec=pltpu.PrefetchScalarGridSpe...  24.1 us
    all_to_all x3, starting transfers between devices, to_rows(): lax.all_to_all(halfway.reshape(16, -1, halfway.shape[-1]), ('depth', 'low...  15 us
    pallas_call x2, Pallas kernels, row_inverse(): pl.pallas_call(functools.partial(row_inverse_kernel, plane), grid=(count,...  13.3 us
    pallas_call x1, Pallas kernels, first_columns(): pl.pallas_call(first_columns_kernel, grid_spec=pltpu.PrefetchScalarGridSp...  12.8 us
    pallas_call x1, Pallas kernels, propagators(): pl.pallas_call(functools.partial(propagator_kernel, planes), grid=(OUT,),...  10.9 us
    ppermute x1, waiting for transfers between devices, exchange_depth(): lax.ppermute(a, 'depth', OVER_X)  10.9 us
  transfers between devices with their start and end apart: 10, of which 8 were waited for; matrix products, arithmetic and copies ran while one was open for 4% of the time, Pallas kernels for 27%

profile of v8, /device:TPU:0, one launch (start us, length us, event | category | flops | bytes accessed | tf_op | source)
XLA Modules:
  0.0 251.6 jit_solution(17805782626133790846)
XLA Ops:
  0.0 8.4 %row_forward.1 = bf16[2,2,2,528,256]{4,3,2,1,0:T(8,128)(2,1)} custom-call(s32[1]{0:T(128)} %bitcast.own, f32[64]{0:T(128)} %constant.58.clone.weights, bf16[512,4096]{1,0:T(8,128)(2,1)} %holo.1, bf16[512,4096]{1,0:T(8,128)(2,1)} %back.3, bf16[8,512,512]{2,1,0:T(8,128)(2,1)} %constant.57.clone.table), custom_call_target="tpu_custom_call" | custom-call | flops 10000000000 | bytes 12582912 | tf_op jit(solution)/shard_map/row_forward/pallas_call | solution.py:431
  8.4 6.3 %all-to-all-start = ((bf16[8,528,256]{2,1,0:T(8,128)(2,1)}), bf16[8,528,256]{2,1,0:T(8,128)(2,1)}, u32[]{:S(2)}, u32[]{:S(2)}) async-start(bf16[8,528,256]{2,1,0:T(8,128)(2,1)} %bitcast.91), calls=%async_computation | async-start | bytes 4325376 | tf_op jit(solution)/shard_map/all_to_all | solution.py:1214
  14.8 0.6 multiply_multiply_fusion.fx2
  15.4 10.9 %propagators.1.kernels = bf16[4,16,256,256]{3,2,1,0:T(8,128)(2,1)} custom-call(f32[1,128]{1,0:T(1,128)} %multiply_multiply_fusion.fx2), custom_call_target="tpu_custom_call" | custom-call | flops 1000000000 | bytes 16777216 | tf_op jit(solution)/shard_map/propagators/pallas_call | solution.py:471
  26.3 39.0 %all-to-all-done.data = bf16[8,528,256]{2,1,0:T(8,128)(2,1)} async-done(((bf16[8,528,256]{2,1,0:T(8,128)(2,1)}), bf16[8,528,256]{2,1,0:T(8,128)(2,1)}, u32[]{:S(2)}, u32[]{:S(2)}) %all-to-all-start) | async-done | bytes 2162720 | tf_op jit(solution)/shard_map/all_to_all | solution.py:1214
  65.4 12.8 %first_columns.1 = (bf16[2,2,2,2,128,512]{5,4,3,2,1,0:T(8,128)(2,1)}, bf16[8,512,256]{2,1,0:T(8,128)(2,1)}, bf16[1,16,512]{2,1,0:T(8,128)(2,1)}) custom-call(s32[1]{0:T(128)} %bitcast.1.half, bf16[8,528,256]{2,1,0:T(8,128)(2,1)} %all-to-all-done.data, bf16[4,16,256,256]{3,2,1,0:T(8,128)(2,1)} %propagators.1.kernels, ...), custom_call_target="tpu_custom_call" | custom-call | flops 10000000000 | bytes 16777216 | tf_op jit(solution)/shard_map/first_columns/pallas_call | solution.py:661
  78.2 4.6 %all-to-all-start.1 = ((bf16[16,128,512]{2,1,0:T(8,128)(2,1)}), bf16[16,128,512]{2,1,0:T(8,128)(2,1)}, u32[]{:S(2)}, u32[]{:S(2)}) async-start(bf16[16,128,512]{2,1,0:T(8,128)(2,1)} %bitcast.90), calls=%async_computation.1 | async-start | bytes 4194304 | tf_op jit(solution)/shard_map/all_to_all | solution.py:1229
  82.9 0.6 pad_add_fusion.own
  83.5 6.9 %nyquist.1.nyquist_in = f32[256,128]{1,0:T(8,128)} custom-call(s32[2]{0:T(128)} %pad_add_fusion.own, bf16[8,528,256]{2,1,0:T(8,128)(2,1)} %all-to-all-done.data), custom_call_target="tpu_custom_call" | custom-call | flops 1000000000 | bytes 262144 | tf_op jit(solution)/shard_map/nyquist/pallas_call | solution.py:908
  90.4 15.7 %next_columns.3 = (bf16[2,2,2,2,128,1024]{5,4,3,2,1,0:T(8,128)(2,1)}, bf16[2,16,512]{2,1,0:T(8,128)(2,1)}) custom-call(s32[1]{0:T(128)} %bitcast.1.half, bf16[8,512,256]{2,1,0:T(8,128)(2,1)} %get-tuple-element.27.spectrum, bf16[4,16,256,256]{3,2,1,0:T(8,128)(2,1)} %propagators.1.kernels, bf16[512,512]{1,0:T(8,128)(2,1)} %constant.61.clone.inner_back_in.inner_back, ...), custom_call_target="tpu_custom_call" | custom-call | flops 14000000000 | bytes 33554432 | tf_op jit(solution)/shard_map/next_columns/pallas_call | solution.py:701
  106.1 4.3 %all-to-all-done.1 = bf16[16,128,512]{2,1,0:T(8,128)(2,1)} async-done(((bf16[16,128,512]{2,1,0:T(8,128)(2,1)}), bf16[16,128,512]{2,1,0:T(8,128)(2,1)}, u32[]{:S(2)}, u32[]{:S(2)}) %all-to-all-start.1) | async-done | bytes 2097184 | tf_op jit(solution)/shard_map/all_to_all | solution.py:1229
  110.4 4.8 %all-to-all-start.2 = ((bf16[16,128,1024]{2,1,0:T(8,128)(2,1)}), bf16[16,128,1024]{2,1,0:T(8,128)(2,1)}, u32[]{:S(2)}, u32[]{:S(2)}) async-start(bf16[16,128,1024]{2,1,0:T(8,128)(2,1)} %bitcast.88), calls=%async_computation.2 | async-start | bytes 8388608 | tf_op jit(solution)/shard_map/all_to_all | solution.py:1229
  115.2 1.0 fusion.9
  116.3 8.4 %next_columns.2 = (bf16[2,2,2,2,128,512]{5,4,3,2,1,0:T(8,128)(2,1)}, bf16[1,16,512]{2,1,0:T(8,128)(2,1)}) custom-call(s32[1]{0:T(128)} %bitcast.1.half, bf16[8,512,256]{2,1,0:T(8,128)(2,1)} %get-tuple-element.27.spectrum, bf16[4,16,256,256]{3,2,1,0:T(8,128)(2,1)} %propagators.1.kernels, bf16[512,512]{1,0:T(8,128)(2,1)} %constant.61.clone.inner_back_in.inner_back, ...), custom_call_target="tpu_custom_call" | custom-call | flops 7000000000 | bytes 16777216 | tf_op jit(solution)/shard_map/next_columns/pallas_call | solution.py:701
  124.7 0.0 copy-start.2
  124.7 1.2 fusion.10
  126.0 0.8 fusion.5
  127.1 1.4 slice_reduce_fusion.1
  128.7 0.7 fusion.11
  129.6 0.1 pad_maximum_fusion.1
  129.7 0.1 copy.77
  129.8 0.1 fusion.4
  129.9 0.0 copy-done.2
  129.9 1.6 pad_maximum_fusion
  131.5 5.4 %row_inverse.2 = (bf16[1,128,4096]{2,1,0:T(8,128)(2,1)}, f32[1,16,4096]{2,1,0:T(8,128)}) custom-call(bf16[4,2,2,128,512]{4,3,2,1,0:T(8,128)(2,1)} %bitcast.26.parts, f32[256,128]{1,0:T(8,128)} %nyquist.1.nyquist_in, bf16[2,512,512]{2,1,0:T(8,128)(2,1)} %constant.65.clone.table.table_in, f32[16,256]{1,0:T(8,128)} %constant.66.clone.turn.turn_in), custom_call_target="tpu_custom_call" | custom-call | flops 3000000000 | bytes 8388608 | tf_op jit(solution)/shard_map/row_inverse/pallas_call | solution.py:830
  136.9 30.4 %all-to-all-done.2 = bf16[16,128,1024]{2,1,0:T(8,128)(2,1)} async-done(((bf16[16,128,1024]{2,1,0:T(8,128)(2,1)}), bf16[16,128,1024]{2,1,0:T(8,128)(2,1)}, u32[]{:S(2)}, u32[]{:S(2)}) %all-to-all-start.2) | async-done | bytes 4194336 | tf_op jit(solution)/shard_map/all_to_all | solution.py:1229
  167.3 5.6 %all-to-all-start.3 = ((bf16[16,144,512]{2,1,0:T(8,128)(2,1)}), bf16[16,144,512]{2,1,0:T(8,128)(2,1)}, u32[]{:S(2)}, u32[]{:S(2)}) async-start(bf16[16,144,512]{2,1,0:T(8,128)(2,1)} %pad_maximum_fusion), calls=%async_computation.3 | async-start | bytes 4718592 | tf_op jit(solution)/shard_map/all_to_all | solution.py:1229
  172.9 7.9 %row_inverse.3 = (bf16[2,128,4096]{2,1,0:T(8,128)(2,1)}, f32[2,16,4096]{2,1,0:T(8,128)}) custom-call(bf16[4,2,2,128,1024]{4,3,2,1,0:T(8,128)(2,1)} %bitcast.28.parts, f32[256,128]{1,0:T(8,128)} %nyquist.1.nyquist_in, bf16[2,512,512]{2,1,0:T(8,128)(2,1)} %constant.65.clone.table.table_in, f32[16,256]{1,0:T(8,128)} %constant.66.clone.turn.turn_in), custom_call_target="tpu_custom_call" | custom-call | flops 6000000000 | bytes 16777216 | tf_op jit(solution)/shard_map/row_inverse/pallas_call | solution.py:830
  180.8 9.3 %early_focus.1 = (bf16[128,4096]{1,0:T(8,128)(2,1)}, bf16[128,4096]{1,0:T(8,128)(2,1)}) custom-call(bf16[1,128,4096]{2,1,0:T(8,128)(2,1)} %get-tuple-element.40.first, bf16[2,128,4096]{2,1,0:T(8,128)(2,1)} %get-tuple-element.42.others), custom_call_target="tpu_custom_call" | custom-call | flops 1000000000 | bytes 12582912 | tf_op jit(solution)/shard_map/early_focus/pallas_call | solution.py:971
  190.1 13.4 %all-to-all-done.3 = bf16[16,144,512]{2,1,0:T(8,128)(2,1)} async-done(((bf16[16,144,512]{2,1,0:T(8,128)(2,1)}), bf16[16,144,512]{2,1,0:T(8,128)(2,1)}, u32[]{:S(2)}, u32[]{:S(2)}) %all-to-all-start.3) | async-done | bytes 2359328 | tf_op jit(solution)/shard_map/all_to_all | solution.py:1229
  203.5 8.3 %last_rows.1 = (bf16[64,4096]{1,0:T(8,128)(2,1)}, bf16[64,4096]{1,0:T(8,128)(2,1)}) custom-call(bf16[4,2,2,144,512]{4,3,2,1,0:T(8,128)(2,1)} %bitcast.29.parts, bf16[128,4096]{1,0:T(8,128)(2,1)} %get-tuple-element.43.best, bf16[128,4096]{1,0:T(8,128)(2,1)} %get-tuple-element.44.spatial, bf16[2,128,4096]{2,1,0:T(8,128)(2,1)} %get-tuple-element.42.others, ...), custom_call_target="tpu_custom_call" | custom-call | flops 3000000000 | bytes 16777216 | tf_op jit(solution)/shard_map/last_rows/pallas_call | solution.py:1093
  211.7 2.6 %collective-permute-start = (bf16[64,4096]{1,0:T(8,128)(2,1)}, bf16[64,4096]{1,0:T(8,128)(2,1)S(1)}, u32[]{:S(2)}, u32[]{:S(2)}) collective-permute-start(bf16[64,4096]{1,0:T(8,128)(2,1)} %get-tuple-element.47.refs_0_), channel_id=1, source_target_pairs={{0,8},{8,0},{16,24},{24,16},{1,9},{9,1},{17,25},{25,17},{2,10},{10... | collective-permute-start | bytes 1572872 | tf_op jit(solution)/shard_map/ppermute | solution.py:1184
  214.3 1.5 collective-permute-start.2
  215.8 0.6 collective-permute-start.4
  216.4 0.1 collective-permute-start.5
  216.4 10.9 %collective-permute-done.refs_1_ = bf16[64,4096]{1,0:T(8,128)(2,1)S(1)} collective-permute-done((bf16[64,4096]{1,0:T(8,128)(2,1)}, bf16[64,4096]{1,0:T(8,128)(2,1)S(1)}, u32[]{:S(2)}, u32[]{:S(2)}) %collective-permute-start) | collective-permute-done | bytes 524320 | tf_op jit(solution)/shard_map/ppermute | solution.py:1184
  227.3 1.5 collective-permute-start.1
  228.8 0.6 collective-permute-done.2.refs_5_
  229.4 1.5 collective-permute-start.3
  230.9 9.8 %collective-permute-done.4.refs_2_ = bf16[64,4096]{1,0:T(8,128)(2,1)S(1)} collective-permute-done((bf16[64,4096]{1,0:T(8,128)(2,1)}, bf16[64,4096]{1,0:T(8,128)(2,1)S(1)}, u32[]{:S(2)}, u32[]{:S(2)}) %collective-permute-start.4) | collective-permute-done | bytes 524320 | tf_op jit(solution)/shard_map/ppermute | solution.py:1185
  240.6 0.0 collective-permute-done.5.refs_4_
  240.7 0.0 copy-start
  240.7 1.0 copy-done
  241.7 1.0 copy-done.1
  242.7 2.9 %assemble.1.whole = f32[512,4096]{1,0:T(8,128)} custom-call(s32[1]{0:T(128)} %bitcast.own, bf16[64,4096]{1,0:T(8,128)(2,1)S(1)} %copy-done, bf16[64,4096]{1,0:T(8,128)(2,1)S(1)} %collective-permute-done.refs_1_, bf16[64,4096]{1,0:T(8,128)(2,1)S(1)} %collective-permute-done.4.refs_2_, bf16[64,4096]{1,0:T(8,128)(2,1)S(1)} %copy-done.1, ...), custom_call_target="tpu_custom_call" | custom-call | flops 1000000 | bytes 10485760 | tf_op jit(solution)/shard_map/assemble/pallas_call | solution.py:1135
  245.7 4.6 %collective-permute-done.1.upper = bf16[64,4096]{1,0:T(8,128)(2,1)S(1)} collective-permute-done((bf16[64,4096]{1,0:T(8,128)(2,1)S(1)}, bf16[64,4096]{1,0:T(8,128)(2,1)S(1)}, u32[]{:S(2)}, u32[]{:S(2)}) %collective-permute-start.1) | collective-permute-done | bytes 524320 | tf_op jit(solution)/shard_map/ppermute | solution.py:1185
  250.2 0.0 collective-permute-done.3.lower
  250.2 1.4 complete.1
  (38 shorter events, 0.7 us)
Async XLA Ops:
  8.4 56.9 %all-to-all-start = ((bf16[8,528,256]{2,1,0:T(8,128)(2,1)}), bf16[8,528,256]{2,1,0:T(8,128)(2,1)}, u32[]{:S(2)}, u32[]{:S(2)}) async-start(bf16[8,528,256]{2,1,0:T(8,128)(2,1)} %bitcast.91), calls=%async_computation | async-start | bytes 4325376 | tf_op jit(solution)/shard_map/all_to_all | solution.py:1214
  78.2 32.2 %all-to-all-start.1 = ((bf16[16,128,512]{2,1,0:T(8,128)(2,1)}), bf16[16,128,512]{2,1,0:T(8,128)(2,1)}, u32[]{:S(2)}, u32[]{:S(2)}) async-start(bf16[16,128,512]{2,1,0:T(8,128)(2,1)} %bitcast.90), calls=%async_computation.1 | async-start | bytes 4194304 | tf_op jit(solution)/shard_map/all_to_all | solution.py:1229
  110.4 56.9 %all-to-all-start.2 = ((bf16[16,128,1024]{2,1,0:T(8,128)(2,1)}), bf16[16,128,1024]{2,1,0:T(8,128)(2,1)}, u32[]{:S(2)}, u32[]{:S(2)}) async-start(bf16[16,128,1024]{2,1,0:T(8,128)(2,1)} %bitcast.88), calls=%async_computation.2 | async-start | bytes 8388608 | tf_op jit(solution)/shard_map/all_to_all | solution.py:1229
  124.7 5.2 %copy-start.2 = (bf16[2,2,2,2,128,512]{5,4,3,2,1,0:T(8,128)(2,1)S(1)}, bf16[2,2,2,2,128,512]{5,4,3,2,1,0:T(8,128)(2,1)}, u32[]{:S(2)}) copy-start(bf16[2,2,2,2,128,512]{5,4,3,2,1,0:T(8,128)(2,1)} %get-tuple-element.28) | copy-start | bytes 6291460
  167.3 36.1 %all-to-all-start.3 = ((bf16[16,144,512]{2,1,0:T(8,128)(2,1)}), bf16[16,144,512]{2,1,0:T(8,128)(2,1)}, u32[]{:S(2)}, u32[]{:S(2)}) async-start(bf16[16,144,512]{2,1,0:T(8,128)(2,1)} %pad_maximum_fusion), calls=%async_computation.3 | async-start | bytes 4718592 | tf_op jit(solution)/shard_map/all_to_all | solution.py:1229
  211.7 15.6 %collective-permute-start = (bf16[64,4096]{1,0:T(8,128)(2,1)}, bf16[64,4096]{1,0:T(8,128)(2,1)S(1)}, u32[]{:S(2)}, u32[]{:S(2)}) collective-permute-start(bf16[64,4096]{1,0:T(8,128)(2,1)} %get-tuple-element.47.refs_0_), channel_id=1, source_target_pairs={{0,8},{8,0},{16,24},{24,16},{1,9},{9,1},{17,25},{25,17},{2,10},{10... | collective-permute-start | bytes 1572872 | tf_op jit(solution)/shard_map/ppermute | solution.py:1184
  214.3 15.1 %collective-permute-start.2 = (bf16[64,4096]{1,0:T(8,128)(2,1)}, bf16[64,4096]{1,0:T(8,128)(2,1)S(1)}, u32[]{:S(2)}, u32[]{:S(2)}) collective-permute-start(bf16[64,4096]{1,0:T(8,128)(2,1)} %get-tuple-element.48.refs_3_), channel_id=1, source_target_pairs={{0,16},{8,24},{16,0},{24,8},{1,17},{9,25},{17,1},{25,9},{2,18},{10... | collective-permute-start | bytes 1572872 | tf_op jit(solution)/shard_map/ppermute | solution.py:1184
  215.8 24.8 %collective-permute-start.4 = (bf16[64,4096]{1,0:T(8,128)(2,1)}, bf16[64,4096]{1,0:T(8,128)(2,1)S(1)}, u32[]{:S(2)}, u32[]{:S(2)}) collective-permute-start(bf16[64,4096]{1,0:T(8,128)(2,1)} %get-tuple-element.47.refs_0_), channel_id=1, source_target_pairs={{0,16},{8,24},{16,0},{24,8},{1,17},{9,25},{17,1},{25,9},{2,18},{10... | collective-permute-start | bytes 1572872 | tf_op jit(solution)/shard_map/ppermute | solution.py:1185
  216.4 24.3 %collective-permute-start.5 = (bf16[64,4096]{1,0:T(8,128)(2,1)}, bf16[64,4096]{1,0:T(8,128)(2,1)S(1)}, u32[]{:S(2)}, u32[]{:S(2)}) collective-permute-start(bf16[64,4096]{1,0:T(8,128)(2,1)} %get-tuple-element.48.refs_3_), channel_id=1, source_target_pairs={{0,8},{8,0},{16,24},{24,16},{1,9},{9,1},{17,25},{25,17},{2,10},{10... | collective-permute-start | bytes 1572872 | tf_op jit(solution)/shard_map/ppermute | solution.py:1186
  227.3 22.9 %collective-permute-start.1 = (bf16[64,4096]{1,0:T(8,128)(2,1)S(1)}, bf16[64,4096]{1,0:T(8,128)(2,1)S(1)}, u32[]{:S(2)}, u32[]{:S(2)}) collective-permute-start(bf16[64,4096]{1,0:T(8,128)(2,1)S(1)} %collective-permute-done.refs_1_), channel_id=1, source_target_pairs={{0,16},{8,24},{16,0},{24,8},{1,17},{9,25},{17,1},{25,9},{2,18},{10... | collective-permute-start | bytes 1572872 | tf_op jit(solution)/shard_map/ppermute | solution.py:1185
  229.4 20.8 %collective-permute-start.3 = (bf16[64,4096]{1,0:T(8,128)(2,1)S(1)}, bf16[64,4096]{1,0:T(8,128)(2,1)S(1)}, u32[]{:S(2)}, u32[]{:S(2)}) collective-permute-start(bf16[64,4096]{1,0:T(8,128)(2,1)S(1)} %collective-permute-done.2.refs_5_), channel_id=1, source_target_pairs={{0,8},{8,0},{16,24},{24,16},{1,9},{9,1},{17,25},{25,17},{2,10},{10... | collective-permute-start | bytes 1572872 | tf_op jit(solution)/shard_map/ppermute | solution.py:1186
  240.7 1.0 copy-start
  241.7 1.0 copy-start.1

commit v9 on v8

--- a/solution.py
+++ b/solution.py
@@ -380,7 +380,7 @@
                 inverse = pl.reciprocal(below, approx=True)
                 inverse = inverse * (2.0 - below * inverse)
                 value = holo_buf[here, there].astype(jnp.float32) * inverse
-                return (value - 1.0).astype(jnp.bfloat16).astype(jnp.float32)
+                return value - 1.0
 
             sums = sixteen_sums(term, lambda n: weights[group * 16 + n])
             for q in range(4):

time: 252 us -> 252 us (level)
  no operation moved by 1% of the time
where the time goes in v9:
time: 252 us; the launch traced here: 251 us
  waiting for transfers between devices  113 us (45%)
  Pallas kernels  97.9 us (39%)
  starting transfers between devices  28.9 us (11%)
  local copies, waits for them, and re-layouts  6.95 us (3%)
  other arithmetic  4.03 us (2%)
    all_to_all x3, waiting for transfers between devices, to_rows(): lax.all_to_all(halfway.reshape(16, -1, halfway.shape[-1]), ('depth', 'low...  48.1 us
    all_to_all x1, waiting for transfers between devices, half_spectrum_shards(): lax.all_to_all(sections.reshape(8, rows + 16, 2 * LANE), ('high', 'low',...  39 us
    pallas_call x2, Pallas kernels, next_columns(): pl.pallas_call(next_columns_kernel, grid_spec=pltpu.PrefetchScalarGridSpe...  24.1 us
    all_to_all x3, starting transfers between devices, to_rows(): lax.all_to_all(halfway.reshape(16, -1, halfway.shape[-1]), ('depth', 'low...  15 us
    pallas_call x2, Pallas kernels, row_inverse(): pl.pallas_call(functools.partial(row_inverse_kernel, plane), grid=(count,...  13.3 us
    pallas_call x1, Pallas kernels, first_columns(): pl.pallas_call(first_columns_kernel, grid_spec=pltpu.PrefetchScalarGridSp...  12.8 us
    pallas_call x1, Pallas kernels, propagators(): pl.pallas_call(functools.partial(propagator_kernel, planes), grid=(OUT,),...  10.9 us
    ppermute x1, waiting for transfers between devices, exchange_depth(): lax.ppermute(a, 'depth', OVER_X)  10.9 us
  transfers between devices with their start and end apart: 10, of which 8 were waited for; matrix products, arithmetic and copies ran while one was open for 4% of the time, Pallas kernels for 27%

profile of v9, /device:TPU:0, one launch (start us, length us, event | category | flops | bytes accessed | tf_op | source)
XLA Modules:
  0.0 251.3 jit_solution(7821047835163880169)
XLA Ops:
  0.0 8.1 %row_forward.1 = bf16[2,2,2,528,256]{4,3,2,1,0:T(8,128)(2,1)} custom-call(s32[1]{0:T(128)} %bitcast.own, f32[64]{0:T(128)} %constant.58.clone.weights, bf16[512,4096]{1,0:T(8,128)(2,1)} %holo.1, bf16[512,4096]{1,0:T(8,128)(2,1)} %back.3, bf16[8,512,512]{2,1,0:T(8,128)(2,1)} %constant.57.clone.table), custom_call_target="tpu_custom_call" | custom-call | flops 10000000000 | bytes 12582912 | tf_op jit(solution)/shard_map/row_forward/pallas_call | solution.py:431
  8.1 6.3 %all-to-all-start = ((bf16[8,528,256]{2,1,0:T(8,128)(2,1)}), bf16[8,528,256]{2,1,0:T(8,128)(2,1)}, u32[]{:S(2)}, u32[]{:S(2)}) async-start(bf16[8,528,256]{2,1,0:T(8,128)(2,1)} %bitcast.91), calls=%async_computation | async-start | bytes 4325376 | tf_op jit(solution)/shard_map/all_to_all | solution.py:1214
  14.4 0.6 multiply_multiply_fusion.fx2
  15.0 10.9 %propagators.1.kernels = bf16[4,16,256,256]{3,2,1,0:T(8,128)(2,1)} custom-call(f32[1,128]{1,0:T(1,128)} %multiply_multiply_fusion.fx2), custom_call_target="tpu_custom_call" | custom-call | flops 1000000000 | bytes 16777216 | tf_op jit(solution)/shard_map/propagators/pallas_call | solution.py:471
  26.0 39.0 %all-to-all-done.data = bf16[8,528,256]{2,1,0:T(8,128)(2,1)} async-done(((bf16[8,528,256]{2,1,0:T(8,128)(2,1)}), bf16[8,528,256]{2,1,0:T(8,128)(2,1)}, u32[]{:S(2)}, u32[]{:S(2)}) %all-to-all-start) | async-done | bytes 2162720 | tf_op jit(solution)/shard_map/all_to_all | solution.py:1214
  65.0 12.8 %first_columns.1 = (bf16[2,2,2,2,128,512]{5,4,3,2,1,0:T(8,128)(2,1)}, bf16[8,512,256]{2,1,0:T(8,128)(2,1)}, bf16[1,16,512]{2,1,0:T(8,128)(2,1)}) custom-call(s32[1]{0:T(128)} %bitcast.1.half, bf16[8,528,256]{2,1,0:T(8,128)(2,1)} %all-to-all-done.data, bf16[4,16,256,256]{3,2,1,0:T(8,128)(2,1)} %propagators.1.kernels, ...), custom_call_target="tpu_custom_call" | custom-call | flops 10000000000 | bytes 16777216 | tf_op jit(solution)/shard_map/first_columns/pallas_call | solution.py:661
  77.9 4.6 %all-to-all-start.1 = ((bf16[16,128,512]{2,1,0:T(8,128)(2,1)}), bf16[16,128,512]{2,1,0:T(8,128)(2,1)}, u32[]{:S(2)}, u32[]{:S(2)}) async-start(bf16[16,128,512]{2,1,0:T(8,128)(2,1)} %bitcast.90), calls=%async_computation.1 | async-start | bytes 4194304 | tf_op jit(solution)/shard_map/all_to_all | solution.py:1229
  82.5 0.6 pad_add_fusion.own
  83.2 6.9 %nyquist.1.nyquist_in = f32[256,128]{1,0:T(8,128)} custom-call(s32[2]{0:T(128)} %pad_add_fusion.own, bf16[8,528,256]{2,1,0:T(8,128)(2,1)} %all-to-all-done.data), custom_call_target="tpu_custom_call" | custom-call | flops 1000000000 | bytes 262144 | tf_op jit(solution)/shard_map/nyquist/pallas_call | solution.py:908
  90.1 15.7 %next_columns.3 = (bf16[2,2,2,2,128,1024]{5,4,3,2,1,0:T(8,128)(2,1)}, bf16[2,16,512]{2,1,0:T(8,128)(2,1)}) custom-call(s32[1]{0:T(128)} %bitcast.1.half, bf16[8,512,256]{2,1,0:T(8,128)(2,1)} %get-tuple-element.27.spectrum, bf16[4,16,256,256]{3,2,1,0:T(8,128)(2,1)} %propagators.1.kernels, bf16[512,512]{1,0:T(8,128)(2,1)} %constant.61.clone.inner_back_in.inner_back, ...), custom_call_target="tpu_custom_call" | custom-call | flops 14000000000 | bytes 33554432 | tf_op jit(solution)/shard_map/next_columns/pallas_call | solution.py:701
  105.7 4.3 %all-to-all-done.1 = bf16[16,128,512]{2,1,0:T(8,128)(2,1)} async-done(((bf16[16,128,512]{2,1,0:T(8,128)(2,1)}), bf16[16,128,512]{2,1,0:T(8,128)(2,1)}, u32[]{:S(2)}, u32[]{:S(2)}) %all-to-all-start.1) | async-done | bytes 2097184 | tf_op jit(solution)/shard_map/all_to_all | solution.py:1229
  110.0 4.8 %all-to-all-start.2 = ((bf16[16,128,1024]{2,1,0:T(8,128)(2,1)}), bf16[16,128,1024]{2,1,0:T(8,128)(2,1)}, u32[]{:S(2)}, u32[]{:S(2)}) async-start(bf16[16,128,1024]{2,1,0:T(8,128)(2,1)} %bitcast.88), calls=%async_computation.2 | async-start | bytes 8388608 | tf_op jit(solution)/shard_map/all_to_all | solution.py:1229
  114.8 1.0 fusion.9
  116.0 8.4 %next_columns.2 = (bf16[2,2,2,2,128,512]{5,4,3,2,1,0:T(8,128)(2,1)}, bf16[1,16,512]{2,1,0:T(8,128)(2,1)}) custom-call(s32[1]{0:T(128)} %bitcast.1.half, bf16[8,512,256]{2,1,0:T(8,128)(2,1)} %get-tuple-element.27.spectrum, bf16[4,16,256,256]{3,2,1,0:T(8,128)(2,1)} %propagators.1.kernels, bf16[512,512]{1,0:T(8,128)(2,1)} %constant.61.clone.inner_back_in.inner_back, ...), custom_call_target="tpu_custom_call" | custom-call | flops 7000000000 | bytes 16777216 | tf_op jit(solution)/shard_map/next_columns/pallas_call | solution.py:701
  124.4 0.0 copy-start.2
  124.4 1.2 fusion.10
  125.7 0.8 fusion.5
  126.8 1.4 slice_reduce_fusion.1
  128.3 0.7 fusion.11
  129.2 0.1 pad_maximum_fusion.1
  129.4 0.1 copy.77
  129.4 0.1 fusion.4
  129.6 0.0 copy-done.2
  129.6 1.6 pad_maximum_fusion
  131.2 5.4 %row_inverse.2 = (bf16[1,128,4096]{2,1,0:T(8,128)(2,1)}, f32[1,16,4096]{2,1,0:T(8,128)}) custom-call(bf16[4,2,2,128,512]{4,3,2,1,0:T(8,128)(2,1)} %bitcast.26.parts, f32[256,128]{1,0:T(8,128)} %nyquist.1.nyquist_in, bf16[2,512,512]{2,1,0:T(8,128)(2,1)} %constant.65.clone.table.table_in, f32[16,256]{1,0:T(8,128)} %constant.66.clone.turn.turn_in), custom_call_target="tpu_custom_call" | custom-call | flops 3000000000 | bytes 8388608 | tf_op jit(solution)/shard_map/row_inverse/pallas_call | solution.py:830
  136.5 30.4 %all-to-all-done.2 = bf16[16,128,1024]{2,1,0:T(8,128)(2,1)} async-done(((bf16[16,128,1024]{2,1,0:T(8,128)(2,1)}), bf16[16,128,1024]{2,1,0:T(8,128)(2,1)}, u32[]{:S(2)}, u32[]{:S(2)}) %all-to-all-start.2) | async-done | bytes 4194336 | tf_op jit(solution)/shard_map/all_to_all | solution.py:1229
  167.0 5.6 %all-to-all-start.3 = ((bf16[16,144,512]{2,1,0:T(8,128)(2,1)}), bf16[16,144,512]{2,1,0:T(8,128)(2,1)}, u32[]{:S(2)}, u32[]{:S(2)}) async-start(bf16[16,144,512]{2,1,0:T(8,128)(2,1)} %pad_maximum_fusion), calls=%async_computation.3 | async-start | bytes 4718592 | tf_op jit(solution)/shard_map/all_to_all | solution.py:1229
  172.5 7.9 %row_inverse.3 = (bf16[2,128,4096]{2,1,0:T(8,128)(2,1)}, f32[2,16,4096]{2,1,0:T(8,128)}) custom-call(bf16[4,2,2,128,1024]{4,3,2,1,0:T(8,128)(2,1)} %bitcast.28.parts, f32[256,128]{1,0:T(8,128)} %nyquist.1.nyquist_in, bf16[2,512,512]{2,1,0:T(8,128)(2,1)} %constant.65.clone.table.table_in, f32[16,256]{1,0:T(8,128)} %constant.66.clone.turn.turn_in), custom_call_target="tpu_custom_call" | custom-call | flops 6000000000 | bytes 16777216 | tf_op jit(solution)/shard_map/row_inverse/pallas_call | solution.py:830
  180.4 9.3 %early_focus.1 = (bf16[128,4096]{1,0:T(8,128)(2,1)}, bf16[128,4096]{1,0:T(8,128)(2,1)}) custom-call(bf16[1,128,4096]{2,1,0:T(8,128)(2,1)} %get-tuple-element.40.first, bf16[2,128,4096]{2,1,0:T(8,128)(2,1)} %get-tuple-element.42.others), custom_call_target="tpu_custom_call" | custom-call | flops 1000000000 | bytes 12582912 | tf_op jit(solution)/shard_map/early_focus/pallas_call | solution.py:971
  189.7 13.4 %all-to-all-done.3 = bf16[16,144,512]{2,1,0:T(8,128)(2,1)} async-done(((bf16[16,144,512]{2,1,0:T(8,128)(2,1)}), bf16[16,144,512]{2,1,0:T(8,128)(2,1)}, u32[]{:S(2)}, u32[]{:S(2)}) %all-to-all-start.3) | async-done | bytes 2359328 | tf_op jit(solution)/shard_map/all_to_all | solution.py:1229
  203.1 8.3 %last_rows.1 = (bf16[64,4096]{1,0:T(8,128)(2,1)}, bf16[64,4096]{1,0:T(8,128)(2,1)}) custom-call(bf16[4,2,2,144,512]{4,3,2,1,0:T(8,128)(2,1)} %bitcast.29.parts, bf16[128,4096]{1,0:T(8,128)(2,1)} %get-tuple-element.43.best, bf16[128,4096]{1,0:T(8,128)(2,1)} %get-tuple-element.44.spatial, bf16[2,128,4096]{2,1,0:T(8,128)(2,1)} %get-tuple-element.42.others, ...), custom_call_target="tpu_custom_call" | custom-call | flops 3000000000 | bytes 16777216 | tf_op jit(solution)/shard_map/last_rows/pallas_call | solution.py:1093
  211.4 2.6 %collective-permute-start = (bf16[64,4096]{1,0:T(8,128)(2,1)}, bf16[64,4096]{1,0:T(8,128)(2,1)S(1)}, u32[]{:S(2)}, u32[]{:S(2)}) collective-permute-start(bf16[64,4096]{1,0:T(8,128)(2,1)} %get-tuple-element.47.refs_0_), channel_id=1, source_target_pairs={{0,8},{8,0},{16,24},{24,16},{1,9},{9,1},{17,25},{25,17},{2,10},{10... | collective-permute-start | bytes 1572872 | tf_op jit(solution)/shard_map/ppermute | solution.py:1184
  214.0 1.5 collective-permute-start.2
  215.5 0.6 collective-permute-start.4
  216.0 0.1 collective-permute-start.5
  216.1 10.9 %collective-permute-done.refs_1_ = bf16[64,4096]{1,0:T(8,128)(2,1)S(1)} collective-permute-done((bf16[64,4096]{1,0:T(8,128)(2,1)}, bf16[64,4096]{1,0:T(8,128)(2,1)S(1)}, u32[]{:S(2)}, u32[]{:S(2)}) %collective-permute-start) | collective-permute-done | bytes 524320 | tf_op jit(solution)/shard_map/ppermute | solution.py:1184
  227.0 1.5 collective-permute-start.1
  228.5 0.6 collective-permute-done.2.refs_5_
  229.1 1.5 collective-permute-start.3
  230.5 9.8 %collective-permute-done.4.refs_2_ = bf16[64,4096]{1,0:T(8,128)(2,1)S(1)} collective-permute-done((bf16[64,4096]{1,0:T(8,128)(2,1)}, bf16[64,4096]{1,0:T(8,128)(2,1)S(1)}, u32[]{:S(2)}, u32[]{:S(2)}) %collective-permute-start.4) | collective-permute-done | bytes 524320 | tf_op jit(solution)/shard_map/ppermute | solution.py:1185
  240.3 0.0 collective-permute-done.5.refs_4_
  240.3 0.0 copy-start
  240.3 1.0 copy-done
  241.3 1.0 copy-done.1
  242.4 2.9 %assemble.1.whole = f32[512,4096]{1,0:T(8,128)} custom-call(s32[1]{0:T(128)} %bitcast.own, bf16[64,4096]{1,0:T(8,128)(2,1)S(1)} %copy-done, bf16[64,4096]{1,0:T(8,128)(2,1)S(1)} %collective-permute-done.refs_1_, bf16[64,4096]{1,0:T(8,128)(2,1)S(1)} %collective-permute-done.4.refs_2_, bf16[64,4096]{1,0:T(8,128)(2,1)S(1)} %copy-done.1, ...), custom_call_target="tpu_custom_call" | custom-call | flops 1000000 | bytes 10485760 | tf_op jit(solution)/shard_map/assemble/pallas_call | solution.py:1135
  245.3 4.6 %collective-permute-done.1.upper = bf16[64,4096]{1,0:T(8,128)(2,1)S(1)} collective-permute-done((bf16[64,4096]{1,0:T(8,128)(2,1)S(1)}, bf16[64,4096]{1,0:T(8,128)(2,1)S(1)}, u32[]{:S(2)}, u32[]{:S(2)}) %collective-permute-start.1) | collective-permute-done | bytes 524320 | tf_op jit(solution)/shard_map/ppermute | solution.py:1185
  249.9 0.0 collective-permute-done.3.lower
  249.9 1.4 complete.1
  (38 shorter events, 0.7 us)
Async XLA Ops:
  8.1 56.9 %all-to-all-start = ((bf16[8,528,256]{2,1,0:T(8,128)(2,1)}), bf16[8,528,256]{2,1,0:T(8,128)(2,1)}, u32[]{:S(2)}, u32[]{:S(2)}) async-start(bf16[8,528,256]{2,1,0:T(8,128)(2,1)} %bitcast.91), calls=%async_computation | async-start | bytes 4325376 | tf_op jit(solution)/shard_map/all_to_all | solution.py:1214
  77.9 32.2 %all-to-all-start.1 = ((bf16[16,128,512]{2,1,0:T(8,128)(2,1)}), bf16[16,128,512]{2,1,0:T(8,128)(2,1)}, u32[]{:S(2)}, u32[]{:S(2)}) async-start(bf16[16,128,512]{2,1,0:T(8,128)(2,1)} %bitcast.90), calls=%async_computation.1 | async-start | bytes 4194304 | tf_op jit(solution)/shard_map/all_to_all | solution.py:1229
  110.0 56.9 %all-to-all-start.2 = ((bf16[16,128,1024]{2,1,0:T(8,128)(2,1)}), bf16[16,128,1024]{2,1,0:T(8,128)(2,1)}, u32[]{:S(2)}, u32[]{:S(2)}) async-start(bf16[16,128,1024]{2,1,0:T(8,128)(2,1)} %bitcast.88), calls=%async_computation.2 | async-start | bytes 8388608 | tf_op jit(solution)/shard_map/all_to_all | solution.py:1229
  124.4 5.2 %copy-start.2 = (bf16[2,2,2,2,128,512]{5,4,3,2,1,0:T(8,128)(2,1)S(1)}, bf16[2,2,2,2,128,512]{5,4,3,2,1,0:T(8,128)(2,1)}, u32[]{:S(2)}) copy-start(bf16[2,2,2,2,128,512]{5,4,3,2,1,0:T(8,128)(2,1)} %get-tuple-element.28) | copy-start | bytes 6291460
  167.0 36.1 %all-to-all-start.3 = ((bf16[16,144,512]{2,1,0:T(8,128)(2,1)}), bf16[16,144,512]{2,1,0:T(8,128)(2,1)}, u32[]{:S(2)}, u32[]{:S(2)}) async-start(bf16[16,144,512]{2,1,0:T(8,128)(2,1)} %pad_maximum_fusion), calls=%async_computation.3 | async-start | bytes 4718592 | tf_op jit(solution)/shard_map/all_to_all | solution.py:1229
  211.4 15.6 %collective-permute-start = (bf16[64,4096]{1,0:T(8,128)(2,1)}, bf16[64,4096]{1,0:T(8,128)(2,1)S(1)}, u32[]{:S(2)}, u32[]{:S(2)}) collective-permute-start(bf16[64,4096]{1,0:T(8,128)(2,1)} %get-tuple-element.47.refs_0_), channel_id=1, source_target_pairs={{0,8},{8,0},{16,24},{24,16},{1,9},{9,1},{17,25},{25,17},{2,10},{10... | collective-permute-start | bytes 1572872 | tf_op jit(solution)/shard_map/ppermute | solution.py:1184
  214.0 15.1 %collective-permute-start.2 = (bf16[64,4096]{1,0:T(8,128)(2,1)}, bf16[64,4096]{1,0:T(8,128)(2,1)S(1)}, u32[]{:S(2)}, u32[]{:S(2)}) collective-permute-start(bf16[64,4096]{1,0:T(8,128)(2,1)} %get-tuple-element.48.refs_3_), channel_id=1, source_target_pairs={{0,16},{8,24},{16,0},{24,8},{1,17},{9,25},{17,1},{25,9},{2,18},{10... | collective-permute-start | bytes 1572872 | tf_op jit(solution)/shard_map/ppermute | solution.py:1184
  215.5 24.8 %collective-permute-start.4 = (bf16[64,4096]{1,0:T(8,128)(2,1)}, bf16[64,4096]{1,0:T(8,128)(2,1)S(1)}, u32[]{:S(2)}, u32[]{:S(2)}) collective-permute-start(bf16[64,4096]{1,0:T(8,128)(2,1)} %get-tuple-element.47.refs_0_), channel_id=1, source_target_pairs={{0,16},{8,24},{16,0},{24,8},{1,17},{9,25},{17,1},{25,9},{2,18},{10... | collective-permute-start | bytes 1572872 | tf_op jit(solution)/shard_map/ppermute | solution.py:1185
  216.0 24.3 %collective-permute-start.5 = (bf16[64,4096]{1,0:T(8,128)(2,1)}, bf16[64,4096]{1,0:T(8,128)(2,1)S(1)}, u32[]{:S(2)}, u32[]{:S(2)}) collective-permute-start(bf16[64,4096]{1,0:T(8,128)(2,1)} %get-tuple-element.48.refs_3_), channel_id=1, source_target_pairs={{0,8},{8,0},{16,24},{24,16},{1,9},{9,1},{17,25},{25,17},{2,10},{10... | collective-permute-start | bytes 1572872 | tf_op jit(solution)/shard_map/ppermute | solution.py:1186
  227.0 22.9 %collective-permute-start.1 = (bf16[64,4096]{1,0:T(8,128)(2,1)S(1)}, bf16[64,4096]{1,0:T(8,128)(2,1)S(1)}, u32[]{:S(2)}, u32[]{:S(2)}) collective-permute-start(bf16[64,4096]{1,0:T(8,128)(2,1)S(1)} %collective-permute-done.refs_1_), channel_id=1, source_target_pairs={{0,16},{8,24},{16,0},{24,8},{1,17},{9,25},{17,1},{25,9},{2,18},{10... | collective-permute-start | bytes 1572872 | tf_op jit(solution)/shard_map/ppermute | solution.py:1185
  229.1 20.8 %collective-permute-start.3 = (bf16[64,4096]{1,0:T(8,128)(2,1)S(1)}, bf16[64,4096]{1,0:T(8,128)(2,1)S(1)}, u32[]{:S(2)}, u32[]{:S(2)}) collective-permute-start(bf16[64,4096]{1,0:T(8,128)(2,1)S(1)} %collective-permute-done.2.refs_5_), channel_id=1, source_target_pairs={{0,8},{8,0},{16,24},{24,16},{1,9},{9,1},{17,25},{25,17},{2,10},{10... | collective-permute-start | bytes 1572872 | tf_op jit(solution)/shard_map/ppermute | solution.py:1186
  240.3 1.0 copy-start
  241.3 1.0 copy-start.1
